TPU v7x, 512 devices: a whole 4x4x16 slice. The times are simulated.
512 devices in a mesh: narrow: 8 (over z_lo), wide: 64 (over x, y, z_hi, core).
Axes of the slice: x: 4, y: 4, z: 16 (z_hi: 2, z_lo: 8; z = z_hi * 8 + z_lo), core: 2. Of those that a mesh axis runs over, the one named last changes fastest.
Arguments:
- state: float32 [5120, 5120], P('wide', 'narrow'), may hold values from 0 to 10, as said below
- in_pattern: int32 [20, 20], replicated, may hold values from 0 to 1, as said below
- out_pattern: int32 [20, 20], replicated, may hold values from 0 to 1, as said below
Outputs:
- clustered: float32 [5120, 5120], P('wide', 'narrow')
Inputs may be any that keep to these rules, and one draw needn't show every extreme that they name: `in_pattern`: entries are 0 or 1 and every diagonal block is 1. `out_pattern`: entries are 0 or 1 and every diagonal block is 1. `state`: nonnegative; the diagonal lies between 0.5 and 1.
All inputs are finite; a program needn't handle non-finite values.
Results may differ from a plain program's by a relative error of at most 0.00011.
Values sent between devices are 32-bit elements; how exact they have to be, the bound alone decides.
No kernel may reach another device: no remote copies, remote signals or barrier semaphores. Data moves between devices by JAX's collectives and lax.ppermute only.
A program may use at most 64 MiB of HBM per device.

v0:
```python
import jax
import jax.numpy as jnp
from jax import lax
from jax.sharding import PartitionSpec as P

BLK = 256


def tile_mask(pattern, row_start, rows, col_start, cols):
    blocks = pattern.shape[0]
    row_blk = (row_start + jnp.arange(rows)) // BLK
    col_blk = (col_start + jnp.arange(cols)) // BLK
    row_pick = (row_blk[:, None] == jnp.arange(blocks)[None, :]).astype(jnp.float32)
    col_pick = (col_blk[:, None] == jnp.arange(blocks)[None, :]).astype(jnp.float32)
    picked = jnp.dot(row_pick, pattern.astype(jnp.float32), preferred_element_type=jnp.float32)
    return jnp.dot(picked, col_pick.T, preferred_element_type=jnp.float32)


def body(state, in_pattern, out_pattern):
    rows, cols = state.shape
    nodes_all = cols * lax.axis_size("narrow")
    row_start = lax.axis_index("wide") * rows
    col_start = lax.axis_index("narrow") * cols
    masked = state * tile_mask(in_pattern, row_start, rows, col_start, cols)
    column_block = lax.all_gather(masked, "wide", axis=0, tiled=True)
    expanded = jnp.dot(
        lax.all_gather(masked, "narrow", axis=1, tiled=True),
        column_block,
        preferred_element_type=jnp.float32,
        precision=lax.Precision.HIGHEST,
    )
    inflated = expanded * expanded * tile_mask(out_pattern, row_start, rows, col_start, cols)
    totals = lax.psum(jnp.sum(inflated, axis=1), "narrow")
    return inflated * (nodes_all / totals)[:, None]


def solution(mesh):
    return jax.shard_map(
        body,
        mesh=mesh,
        in_specs=(P("wide", "narrow"), P(), P()),
        out_specs=P("wide", "narrow"),
        check_vma=False,
    )
```

profile of v0, /device:TPU:6, one launch (start us, length us, event | category | flops | bytes accessed | tf_op | source)
XLA Modules:
  0.0 345.2 jit_solution(17521195521909558858)
XLA Ops:
  6.5 0.0 all-gather.3.cloned.1.call-start
  6.6 2.0 convolution_multiply_fusion.1
  8.6 0.0 all-gather.3.cloned.1.call-update
  8.6 0.0 all-gather.5.cloned.1.call-start
  8.6 0.7 all-gather.5.cloned.1.call-update
  9.3 1.1 fusion.3
  10.4 72.6 %all-gather.3.cloned.1.call-done = f32[80,5120]{1,0:T(8,128)} async-done(((f32[80,640]{1,0:T(8,128)}), f32[80,5120]{1,0:T(8,128)}) %all-gather.3.cloned.1.call-update) | async-done | bytes 1638416 | tf_op jit(solution)/shard_map/all_gather | solution.py:27
  83.0 216.3 %all-gather.5.cloned.1.call-done = f32[5120,640]{1,0:T(8,128)} async-done(((f32[80,640]{1,0:T(8,128)}), f32[5120,640]{1,0:T(8,128)}) %all-gather.5.cloned.1.call-update) | async-done | bytes 13107216 | tf_op jit(solution)/shard_map/all_gather | solution.py:25
  299.3 13.3 %fusion.19 = (f32[80]{0:T(128)S(1)}, f32[80,640]{1,0:T(8,128)S(1)}) fusion(f32[80,640]{1,0:T(8,128)S(1)} %fusion.3, f32[80,5120]{1,0:T(8,128)} %all-gather.3.cloned.1.call-done, f32[5120,640]{1,0:T(8,128)} %all-gather.5.cloned.1.call-done), kind=kOutput, calls=%fused_computation.29 | convolution fusion | flops 3145881600 | bytes 15155520 | tf_op jit(solution)/shard_map/dot_general | solution.py:26
  312.5 25.1 %psum.7 = f32[80]{0:T(128)S(1)} all-reduce(f32[80]{0:T(128)S(1)} %get-tuple-element.5), channel_id=1, replica_groups=mesh['narrow'=8,'wide'=64] {'narrow'}, use_global_device_ids=true, to_apply=%region_1.2 | all-reduce | flops 80 | bytes 640 | tf_op jit(solution)/shard_map/psum | solution.py:33
  337.6 0.8 broadcast_multiply_fusion
  (3 shorter events, 0.0 us)
Async XLA Ops:
  6.5 76.5 %all-gather.3.cloned.1.call-start = ((), (), s32[]{:S(2)}) async-start(), calls=%async_computation | async-start | bytes 1843200 | tf_op jit(solution)/shard_map/all_gather | solution.py:27
  8.6 290.7 %all-gather.5.cloned.1.call-start = ((), (), s32[]{:S(2)}) async-start(), calls=%async_computation.1 | async-start | bytes 13312000 | tf_op jit(solution)/shard_map/all_gather | solution.py:25
Sparse Core Ops, SparseCore 0:
  9.4 73.5 all-gather.2
  87.3 211.8 all-gather.4
where the time goes:
time: 346 us; the launch traced here: 345 us
  waiting for transfers between devices  290 us (84%)
  blocking collectives  25.1 us (7%)
  matrix products  16.3 us (5%)
  between operations  13.4 us (4%)
    all_gather x1, waiting for transfers between devices, body(): column_block = lax.all_gather(masked, 'wide', axis=0, tiled=True)  216 us
    all_gather x1, waiting for transfers between devices, body(): lax.all_gather(masked, 'narrow', axis=1, tiled=True)  72.6 us
    psum x1, blocking collectives, body(): totals = lax.psum(jnp.sum(inflated, axis=1), 'narrow')  25.1 us
    dot_general x1, matrix products, body(): jnp.dot(lax.all_gather(masked, 'narrow', axis=1, tiled=True), column_bloc...  13.3 us
  transfers between devices with their start and end apart: 2, of which 2 were waited for; matrix products, arithmetic and copies ran while one was open for 0% of the time, Pallas kernels for 0%

commit v1 on v0

v1 whole, which is shorter than its diff:
```python
import jax
import jax.numpy as jnp
from jax import lax
from jax.sharding import Mesh, PartitionSpec as P

BLK = 256
ROWS = ("x", "y", "zh", "c")


def tile_mask(pattern, row_start, rows, col_start, cols):
    blocks = pattern.shape[0]
    pattern = pattern.astype(jnp.float32)
    row_blk = (row_start + jnp.arange(rows)) // BLK
    first = row_start // BLK
    low = lax.dynamic_slice_in_dim(pattern, first, 1, 0)[0]
    high = lax.dynamic_slice_in_dim(pattern, jnp.minimum(first + 1, blocks - 1), 1, 0)[0]
    col_blk = (col_start + jnp.arange(cols)) // BLK
    pick = col_blk[:, None] == jnp.arange(blocks)[None, :]
    low = jnp.sum(jnp.where(pick, low[None, :], 0.0), axis=1)
    high = jnp.sum(jnp.where(pick, high[None, :], 0.0), axis=1)
    return jnp.where((row_blk == first)[:, None], low[None, :], high[None, :])


def body(state, in_pattern, out_pattern):
    rows, cols = state.shape
    n_y, n_zl = lax.axis_size("y"), lax.axis_size("zl")
    part = rows // n_y
    nodes_all = cols * n_zl
    row_start = lax.axis_index(ROWS) * rows
    col_start = lax.axis_index("zl") * cols
    masked = state * tile_mask(in_pattern, row_start, rows, col_start, cols)

    pieces = masked.reshape(rows, 2, 2, 2, n_y, part)
    pieces = pieces.transpose(4, 0, 3, 2, 1, 5).reshape(n_y, rows, cols // n_y)
    left = lax.all_to_all(pieces, "y", 0, 0).reshape(n_y * rows, cols // n_y)
    left = lax.all_gather(left, "zl", axis=0)

    right = lax.all_to_all(masked.reshape(n_y, part, cols), "y", 0, 0)
    right = right.reshape(2, 2 * part, cols)
    right = lax.all_gather(right, "zh", axis=1)
    right = lax.all_gather(right, "x", axis=0)
    right = lax.all_gather(right, "c", axis=2)
    right = right.reshape(n_zl, cols // n_y, cols)

    partial = jnp.einsum(
        "zik,zkj->ij",
        left,
        right,
        preferred_element_type=jnp.float32,
        precision=lax.Precision.HIGH,
    )
    shares = lax.all_to_all(partial.reshape(n_y, rows, cols), "y", 0, 0)
    expanded = jnp.sum(shares, axis=0)
    inflated = expanded * expanded * tile_mask(out_pattern, row_start, rows, col_start, cols)
    sums = jnp.broadcast_to(jnp.sum(inflated, axis=1)[None, :], (n_zl, rows))
    totals = jnp.sum(lax.all_to_all(sums, "zl", 0, 0), axis=0)
    return inflated * (nodes_all / totals)[:, None]


def solution(mesh):
    fine = Mesh(
        mesh.devices.reshape(8, 4, 4, 2, 2), ("zl", "x", "y", "zh", "c")
    )
    return jax.shard_map(
        body,
        mesh=fine,
        in_specs=(P(ROWS, "zl"), P(), P()),
        out_specs=P(ROWS, "zl"),
        check_vma=False,
    )
```

time: 346 us -> 228 us (0.66)
  waiting for transfers between devices: 290 us -> 112 us
  blocking collectives: 25.1 us -> 86.8 us
  matrix products: 16.3 us -> 4.87 us
  local copies, waits for them, and re-layouts: 0 us -> 7.27 us
    all_gather x2 -> x3, waiting for transfers between devices: 289 us -> 112 us  [the longest x1 71.1 us: body(): left = lax.all_gather(left, 'zl', axis=0)]
    all_to_all x0 -> x4, blocking collectives: none -> 57.6 us  [the longest x1 20.2 us: body(): totals = jnp.sum(lax.all_to_all(sums, 'zl', 0, 0), axis=0)]
    all_gather x0 -> x1, blocking collectives: none -> 29.2 us  [body(): right = lax.all_gather(right, 'zh', axis=1)]
    psum x1 -> x0, blocking collectives: 25.1 us -> none  [body(): totals = lax.psum(jnp.sum(inflated, axis=1), 'narrow')]
    dot_general x3 -> x1, matrix products: 16.3 us -> 4.87 us  [body(): jnp.einsum('zik,zkj->ij', left, right, preferred_element_type=jnp.float32...]
  transfers between devices with their start and end apart: 2 -> 3, of which waited for: 2 -> 3; matrix products, arithmetic and copies ran while one was open for 0% -> 3% of each run, Pallas kernels for 0% -> 0%
where the time goes in v1:
time: 228 us
  waiting for transfers between devices  112 us (49%)
  blocking collectives  86.8 us (38%)
  between operations  13.2 us (6%)
  local copies, waits for them, and re-layouts  7.27 us (3%)
  matrix products  4.87 us (2%)
  other arithmetic  3.61 us (2%)
    all_gather x1, waiting for transfers between devices, body(): left = lax.all_gather(left, 'zl', axis=0)  71.1 us
    all_gather x1, blocking collectives, body(): right = lax.all_gather(right, 'zh', axis=1)  29.2 us
    all_gather x1, waiting for transfers between devices, body(): right = lax.all_gather(right, 'x', axis=0)  23.6 us
    all_to_all x1, blocking collectives, body(): totals = jnp.sum(lax.all_to_all(sums, 'zl', 0, 0), axis=0)  20.2 us
    all_gather x1, waiting for transfers between devices, body(): right = lax.all_gather(right, 'c', axis=2)  17.3 us
    all_to_all x1, blocking collectives, body(): shares = lax.all_to_all(partial.reshape(n_y, rows, cols), 'y', 0, 0)  17.2 us
    all_to_all x1, blocking collectives, body(): right = lax.all_to_all(masked.reshape(n_y, part, cols), 'y', 0, 0)  10.9 us
    all_to_all x1, blocking collectives, body(): left = lax.all_to_all(pieces, 'y', 0, 0).reshape(n_y * rows, cols // n_y)  9.4 us
  transfers between devices with their start and end apart: 3, of which 3 were waited for; matrix products, arithmetic and copies ran while one was open for 3% of the time, Pallas kernels for 0%

profile of v1, /device:TPU:6, one launch (start us, length us, event | category | flops | bytes accessed | tf_op | source)
XLA Modules:
  0.0 227.9 jit_solution(11328832699408419571)
XLA Ops:
  6.6 0.7 convert_element_type.6
  7.3 0.7 convert_element_type.7
  8.0 0.1 select_reduce_fusion.1
  8.1 1.0 select_multiply_fusion.1
  9.2 10.9 %all_to_all.21 = f32[4,20,640]{2,1,0:T(8,128)S(1)} all-to-all(f32[4,20,640]{2,1,0:T(8,128)S(1)} %reshape.68), channel_id=1, replica_groups=mesh['zl'=8,'x'=4,'y'=4,'zh'=2,'c'=2] {'y'}, dimensions={0} | all-to-all | bytes 409600 | tf_op jit(solution)/shard_map/all_to_all | solution.py:38
  20.1 29.2 %all_gather.19 = f32[2,2,40,640]{3,2,0,1:T(8,128)} all-gather(f32[2,1,40,640]{3,2,0,1:T(8,128)S(1)} %all_gather_reshape.7), channel_id=1, replica_groups=mesh['zl'=8,'x'=4,'y'=4,'zh'=2,'c'=2] {'zh'}, dimensions={1}, use_global_device_ids=true | all-gather | bytes 614400 | tf_op jit(solution)/shard_map/all_gather | solution.py:40
  49.2 0.0 all-gather.8.cloned.1.call-update
  49.2 0.0 all-gather.6.cloned.1.call-start
  49.3 0.2 copy.30
  49.5 0.1 copy.31
  49.6 9.4 %all_to_all.22 = f32[4,80,160]{1,2,0:T(8,128)S(1)} all-to-all(f32[4,80,160]{1,2,0:T(8,128)S(1)} %copy.32), channel_id=1, replica_groups=mesh['zl'=8,'x'=4,'y'=4,'zh'=2,'c'=2] {'y'}, dimensions={0} | all-to-all | bytes 409600 | tf_op jit(solution)/shard_map/all_to_all | solution.py:35
  59.0 0.2 copy.33
  59.2 0.9 all_gather_reshape.6
  60.2 0.0 all-gather.10.cloned.1.call-start
  60.2 23.6 %all-gather.8.cloned.1.call-done = f32[8,2,40,640]{3,2,0,1:T(8,128)} async-done(((f32[2,2,40,640]{3,2,0,1:T(8,128)}), f32[8,2,40,640]{3,2,0,1:T(8,128)}) %all-gather.8.cloned.1.call-update) | async-done | bytes 1638416 | tf_op jit(solution)/shard_map/all_gather | solution.py:41
  83.8 2.8 %copy.35 = f32[4,2,2,40,640]{4,3,2,1,0:T(8,128)} copy(f32[4,2,2,40,640]{4,3,1,0,2:T(8,128)} %bitcast.28) | data formatting | bytes 3276800 | tf_op jit(solution)/shard_map/all_gather | solution.py:41
  86.6 71.1 %all-gather.6.cloned.1.call-done = f32[8,320,160]{1,2,0:T(8,128)} async-done(((f32[1,320,160]{1,2,0:T(8,128)}), f32[8,320,160]{1,2,0:T(8,128)}) %all-gather.6.cloned.1.call-update) | async-done | bytes 1638416 | tf_op jit(solution)/shard_map/all_gather | solution.py:36
  157.7 3.0 %reshape.75 = f32[4,80,160,8]{1,0,2,3:T(4,128)S(1)} reshape(f32[320,160,8]{0,1,2:T(8,128)} %bitcast.27) | data formatting | bytes 3276800 | tf_op jit(solution)/shard_map/zik,zkj->ij/dot_general | solution.py:45
  160.7 17.3 %all-gather.10.cloned.1.call-done = f32[4,2,4,40,640]{4,3,2,1,0:T(8,128)} async-done(((f32[4,2,2,40,640]{4,3,2,1,0:T(8,128)}), f32[4,2,4,40,640]{4,3,2,1,0:T(8,128)}) %all-gather.10.cloned.1.call-update) | async-done | bytes 3276816 | tf_op jit(solution)/shard_map/all_gather | solution.py:42
  178.1 4.9 %fusion.2 = f32[4,80,640]{2,1,0:T(8,128)S(1)} fusion(f32[8,160,640,1]{2,1,0,3:T(8,128)} %bitcast.26, f32[4,80,160,8]{1,0,2,3:T(4,128)S(1)} %reshape.75), kind=kOutput, calls=%fused_computation.2 | convolution fusion | flops 1572864000 | bytes 5734400 | tf_op jit(solution)/shard_map/zik,zkj->ij/dot_general | solution.py:45
  182.9 17.2 %all_to_all.23 = f32[4,80,640]{2,1,0:T(8,128)S(1)} all-to-all(f32[4,80,640]{2,1,0:T(8,128)S(1)} %fusion.2), channel_id=1, replica_groups=mesh['zl'=8,'x'=4,'y'=4,'zh'=2,'c'=2] {'y'}, dimensions={0} | all-to-all | bytes 1638400 | tf_op jit(solution)/shard_map/all_to_all | solution.py:52
  200.2 0.2 fusion.6
  200.4 20.2 %all_to_all.24 = f32[8,1,80]{2,1,0:T(1,128)S(1)} all-to-all(f32[8,1,80]{2,1,0:T(1,128)S(1)} %broadcast_in_dim.106), channel_id=1, replica_groups=mesh['zl'=8,'x'=4,'y'=4,'zh'=2,'c'=2] {'zl'}, dimensions={0} | all-to-all | bytes 5120 | tf_op jit(solution)/shard_map/all_to_all | solution.py:56
  220.5 0.8 fusion.5
  (14 shorter events, 0.2 us)
Async XLA Ops:
  6.5 77.2 %all-gather.8.cloned.1.call-start = ((), (), s32[]{:S(2)}) async-start(), calls=%async_computation.5 | async-start | bytes 2048000 | tf_op jit(solution)/shard_map/all_gather | solution.py:41
  49.2 108.4 %all-gather.6.cloned.1.call-start = ((), (), s32[]{:S(2)}) async-start(), calls=%async_computation.4 | async-start | bytes 2211840 | tf_op jit(solution)/shard_map/all_gather | solution.py:36
  60.2 117.9 %all-gather.10.cloned.1.call-start = ((), (), s32[]{:S(2)}) async-start(), calls=%async_computation.6 | async-start | bytes 4915200 | tf_op jit(solution)/shard_map/all_gather | solution.py:42
Sparse Core Ops, SparseCore 0:
  49.4 34.3 all-gather.7
  85.9 71.7 all-gather.5
  159.8 18.2 all-gather.9

commit v2 on v1

--- a/solution.py
+++ b/solution.py
@@ -21,6 +21,12 @@
     return jnp.where((row_blk == first)[:, None], low[None, :], high[None, :])
 
 
+def gather(block, axis_name, axis):
+    size = lax.axis_size(axis_name)
+    copies = jnp.broadcast_to(block[None], (size,) + block.shape)
+    return jnp.moveaxis(lax.all_to_all(copies, axis_name, 0, 0), 0, axis)
+
+
 def body(state, in_pattern, out_pattern):
     rows, cols = state.shape
     n_y, n_zl = lax.axis_size("y"), lax.axis_size("zl")
@@ -33,13 +39,14 @@
     pieces = masked.reshape(rows, 2, 2, 2, n_y, part)
     pieces = pieces.transpose(4, 0, 3, 2, 1, 5).reshape(n_y, rows, cols // n_y)
     left = lax.all_to_all(pieces, "y", 0, 0).reshape(n_y * rows, cols // n_y)
+
+    mine, left = lax.optimization_barrier((masked, left))
     left = lax.all_gather(left, "zl", axis=0)
-
-    right = lax.all_to_all(masked.reshape(n_y, part, cols), "y", 0, 0)
+    right = lax.all_to_all(mine.reshape(n_y, part, cols), "y", 0, 0)
     right = right.reshape(2, 2 * part, cols)
-    right = lax.all_gather(right, "zh", axis=1)
-    right = lax.all_gather(right, "x", axis=0)
-    right = lax.all_gather(right, "c", axis=2)
+    right = gather(right, "zh", 1)
+    right = gather(right, "x", 0)
+    right = gather(right, "c", 2)
     right = right.reshape(n_zl, cols // n_y, cols)
 
     partial = jnp.einsum(

time: 228 us -> 157 us (0.69)
  waiting for transfers between devices: 112 us -> 10.2 us
  blocking collectives: 86.8 us -> 118 us
    all_to_all x1 -> x4, blocking collectives: 10.9 us -> 75.1 us  [the longest x3 66.1 us: gather(): return jnp.moveaxis(lax.all_to_all(copies, axis_name, 0, 0), 0, axis)]
    all_gather x1, waiting for transfers between devices: 71.1 us -> 10.2 us  [body(): left = lax.all_gather(left, 'zl', axis=0)]
    all_gather x2 -> x0, waiting for transfers between devices: 40.9 us -> none  [the longest x1 23.6 us: body(): right = lax.all_gather(right, 'x', axis=0)]
    all_gather x1 -> x0, blocking collectives: 29.2 us -> none  [body(): right = lax.all_gather(right, 'zh', axis=1)]
    all_to_all x1, blocking collectives: 17.2 us -> 13.4 us  [body(): shares = lax.all_to_all(partial.reshape(n_y, rows, cols), 'y', 0, 0)]
    all_gather x1 -> x0, local copies, waits for them, and re-layouts: 2.76 us -> none  [body(): right = lax.all_gather(right, 'x', axis=0)]
    all_to_all x1, blocking collectives: 20.2 us -> 17.5 us  [body(): totals = jnp.sum(lax.all_to_all(sums, 'zl', 0, 0), axis=0)]
  transfers between devices with their start and end apart: 3 -> 1, of which waited for: 3 -> 1; matrix products, arithmetic and copies ran while one was open for 3% -> 0% of each run, Pallas kernels for 0% -> 0%
where the time goes in v2:
time: 157 us; the launch traced here: 156 us
  blocking collectives  118 us (75%)
  between operations  13.5 us (9%)
  waiting for transfers between devices  10.2 us (6%)
  local copies, waits for them, and re-layouts  6 us (4%)
  matrix products  4.73 us (3%)
  other arithmetic  3.61 us (2%)
    all_to_all x3, blocking collectives, gather(): return jnp.moveaxis(lax.all_to_all(copies, axis_name, 0, 0), 0, axis)  66.1 us
    all_to_all x1, blocking collectives, body(): totals = jnp.sum(lax.all_to_all(sums, 'zl', 0, 0), axis=0)  17.5 us
    all_to_all x1, blocking collectives, body(): shares = lax.all_to_all(partial.reshape(n_y, rows, cols), 'y', 0, 0)  13.4 us
    all_to_all x1, blocking collectives, body(): left = lax.all_to_all(pieces, 'y', 0, 0).reshape(n_y * rows, cols // n_y)  11.6 us
    all_gather x1, waiting for transfers between devices, body(): left = lax.all_gather(left, 'zl', axis=0)  10.2 us
    all_to_all x1, blocking collectives, body(): right = lax.all_to_all(mine.reshape(n_y, part, cols), 'y', 0, 0)  8.97 us
    dot_general x1, matrix products, body(): jnp.einsum('zik,zkj->ij', left, right, preferred_element_type=jnp.float32...  4.73 us
    dot_general x1, local copies, waits for them, and re-layouts, body(): jnp.einsum('zik,zkj->ij', left, right, preferred_element_type=jnp.float32...  3.87 us
  transfers between devices with their start and end apart: 1, of which 1 were waited for; matrix products, arithmetic and copies ran while one was open for 0% of the time, Pallas kernels for 0%

profile of v2, /device:TPU:6, one launch (start us, length us, event | category | flops | bytes accessed | tf_op | source)
XLA Modules:
  0.0 155.6 jit_solution(12291882310343842438)
XLA Ops:
  6.6 0.7 convert_element_type.6
  7.3 0.7 convert_element_type.7
  8.0 0.1 select_reduce_fusion.1
  8.1 1.0 select_multiply_fusion.1
  9.2 0.2 copy.30
  9.4 0.1 copy.31
  9.5 11.6 %all_to_all.36 = f32[4,80,160]{1,2,0:T(8,128)S(1)} all-to-all(f32[4,80,160]{1,2,0:T(8,128)S(1)} %copy.32), channel_id=1, replica_groups=mesh['zl'=8,'x'=4,'y'=4,'zh'=2,'c'=2] {'y'}, dimensions={0} | all-to-all | bytes 409600 | tf_op jit(solution)/shard_map/all_to_all | solution.py:41
  21.1 0.2 copy.33
  21.3 0.9 reshape.74
  22.2 0.0 all-gather.4.cloned.1.call-update
  22.3 9.0 %all_to_all.37 = f32[4,20,640]{2,1,0:T(8,128)S(1)} all-to-all(f32[4,20,640]{2,1,0:T(8,128)S(1)} %reshape.75), channel_id=1, replica_groups=mesh['zl'=8,'x'=4,'y'=4,'zh'=2,'c'=2] {'y'}, dimensions={0} | all-to-all | bytes 409600 | tf_op jit(solution)/shard_map/all_to_all | solution.py:45
  31.3 41.6 %all_to_all.38 = f32[2,2,40,640]{3,2,1,0:T(8,128)S(1)} all-to-all(f32[2,2,40,640]{3,2,1,0:T(8,128)S(1)} %broadcast_in_dim.120), channel_id=1, replica_groups=mesh['zl'=8,'x'=4,'y'=4,'zh'=2,'c'=2] {'zh'}, dimensions={0} | all-to-all | bytes 819200 | tf_op jit(solution)/shard_map/all_to_all | solution.py:27
  72.9 0.1 broadcast_in_dim.121
  73.0 18.1 %all_to_all.39 = f32[4,2,2,40,640]{4,3,2,1,0:T(8,128)S(1)} all-to-all(f32[4,2,2,40,640]{4,3,2,1,0:T(8,128)S(1)} %broadcast_in_dim.121), channel_id=1, replica_groups=mesh['zl'=8,'x'=4,'y'=4,'zh'=2,'c'=2] {'x'}, dimensions={0} | all-to-all | bytes 3276800 | tf_op jit(solution)/shard_map/all_to_all | solution.py:27
  91.2 0.3 broadcast_in_dim.122
  91.4 6.4 %all_to_all.40 = f32[2,4,2,2,40,640]{5,4,3,2,1,0:T(8,128)S(1)} all-to-all(f32[2,4,2,2,40,640]{5,4,3,2,1,0:T(8,128)S(1)} %broadcast_in_dim.122), channel_id=1, replica_groups=mesh['zl'=8,'x'=4,'y'=4,'zh'=2,'c'=2] {'c'}, dimensions={0} | all-to-all | bytes 6553600 | tf_op jit(solution)/shard_map/all_to_all | solution.py:27
  97.8 0.3 copy.36
  98.1 10.2 %all-gather.4.cloned.1.call-done = f32[8,320,160]{1,2,0:T(8,128)} async-done(((f32[1,320,160]{1,2,0:T(8,128)}), f32[8,320,160]{1,2,0:T(8,128)}) %all-gather.4.cloned.1.call-update) | async-done | bytes 1638416 | tf_op jit(solution)/shard_map/all_gather | solution.py:44
  108.3 3.9 %reshape.83 = f32[4,80,160,8]{1,0,2,3:T(4,128)} reshape(f32[320,160,8]{0,1,2:T(8,128)} %bitcast.30) | data formatting | bytes 3276800 | tf_op jit(solution)/shard_map/zik,zkj->ij/dot_general | solution.py:52
  112.1 4.7 %fusion.2 = f32[4,80,640]{2,1,0:T(8,128)S(1)} fusion(f32[8,160,640,1]{2,1,0,3:T(8,128)S(1)} %bitcast.28, f32[4,80,160,8]{1,0,2,3:T(4,128)} %reshape.83), kind=kOutput, calls=%fused_computation.2 | convolution fusion | flops 1572864000 | bytes 5734400 | tf_op jit(solution)/shard_map/zik,zkj->ij/dot_general | solution.py:52
  116.9 13.4 %all_to_all.41 = f32[4,80,640]{2,1,0:T(8,128)S(1)} all-to-all(f32[4,80,640]{2,1,0:T(8,128)S(1)} %fusion.2), channel_id=1, replica_groups=mesh['zl'=8,'x'=4,'y'=4,'zh'=2,'c'=2] {'y'}, dimensions={0} | all-to-all | bytes 1638400 | tf_op jit(solution)/shard_map/all_to_all | solution.py:59
  130.3 0.2 fusion.6
  130.5 17.5 %all_to_all.42 = f32[8,1,80]{2,1,0:T(1,128)S(1)} all-to-all(f32[8,1,80]{2,1,0:T(1,128)S(1)} %broadcast_in_dim.129), channel_id=1, replica_groups=mesh['zl'=8,'x'=4,'y'=4,'zh'=2,'c'=2] {'zl'}, dimensions={0} | all-to-all | bytes 5120 | tf_op jit(solution)/shard_map/all_to_all | solution.py:63
  148.0 0.8 fusion.5
  (14 shorter events, 0.3 us)
Async XLA Ops:
  6.5 101.7 %all-gather.4.cloned.1.call-start = ((), (), s32[]{:S(2)}) async-start(), calls=%async_computation.7 | async-start | bytes 2211840 | tf_op jit(solution)/shard_map/all_gather | solution.py:44
Sparse Core Ops, SparseCore 0:
  22.4 85.8 all-gather.3

commit v3 on v2

--- a/solution.py
+++ b/solution.py
@@ -36,15 +36,21 @@
     col_start = lax.axis_index("zl") * cols
     masked = state * tile_mask(in_pattern, row_start, rows, col_start, cols)
 
+    other = lax.ppermute(masked, "zh", [(0, 1), (1, 0)])
+
     pieces = masked.reshape(rows, 2, 2, 2, n_y, part)
     pieces = pieces.transpose(4, 0, 3, 2, 1, 5).reshape(n_y, rows, cols // n_y)
     left = lax.all_to_all(pieces, "y", 0, 0).reshape(n_y * rows, cols // n_y)
 
     mine, left = lax.optimization_barrier((masked, left))
     left = lax.all_gather(left, "zl", axis=0)
-    right = lax.all_to_all(mine.reshape(n_y, part, cols), "y", 0, 0)
-    right = right.reshape(2, 2 * part, cols)
-    right = gather(right, "zh", 1)
+    mine = lax.all_to_all(mine.reshape(n_y, part, cols), "y", 0, 0)
+    other, mine = lax.optimization_barrier((other, mine))
+    other = lax.all_to_all(other.reshape(n_y, part, cols), "y", 0, 0)
+    mine = mine.reshape(2, 2 * part, cols)
+    other = other.reshape(2, 2 * part, cols)
+    low = lax.axis_index("zh") == 0
+    right = jnp.where(low, jnp.stack([mine, other], 1), jnp.stack([other, mine], 1))
     right = gather(right, "x", 0)
     right = gather(right, "c", 2)
     right = right.reshape(n_zl, cols // n_y, cols)

time: 157 us -> 150 us (0.955)
  blocking collectives: 118 us -> 69.4 us
  starting transfers between devices: 0.01 us -> 22.5 us
  waiting for transfers between devices: 10.2 us -> 27.2 us
    all_to_all x3 -> x2, blocking collectives: 66.1 us -> 26.3 us  [gather(): return jnp.moveaxis(lax.all_to_all(copies, axis_name, 0, 0), 0, axis)]
    ppermute x0 -> x1, starting transfers between devices: none -> 15.7 us  [body(): other = lax.ppermute(masked, 'zh', [(0, 1), (1, 0)])]
    all_to_all x1 -> x0, blocking collectives: 8.97 us -> none  [body(): right = lax.all_to_all(mine.reshape(n_y, part, cols), 'y', 0, 0)]
    ppermute x0 -> x1, waiting for transfers between devices: none -> 6.82 us  [body(): other = lax.ppermute(masked, 'zh', [(0, 1), (1, 0)])]
    all_to_all x0 -> x2, starting transfers between devices: none -> 6.8 us  [the longest x1 3.4 us: body(): mine = lax.all_to_all(mine.reshape(n_y, part, cols), 'y', 0, 0)]
    all_to_all x0 -> x2, waiting for transfers between devices: none -> 6.52 us  [the longest x1 6.52 us: body(): other = lax.all_to_all(other.reshape(n_y, part, cols), 'y', 0, 0)]
    all_gather x1, waiting for transfers between devices: 10.2 us -> 13.9 us  [body(): left = lax.all_gather(left, 'zl', axis=0)]
    all_to_all x1, blocking collectives: 17.5 us -> 19.4 us  [body(): totals = jnp.sum(lax.all_to_all(sums, 'zl', 0, 0), axis=0)]
  transfers between devices with their start and end apart: 1 -> 4, of which waited for: 1 -> 3; matrix products, arithmetic and copies ran while one was open for 0% -> 1% of each run, Pallas kernels for 0% -> 0%
where the time goes in v3:
time: 150 us; the launch traced here: 148 us
  blocking collectives  69.4 us (46%)
  waiting for transfers between devices  27.2 us (18%)
  starting transfers between devices  22.5 us (15%)
  between operations  13.6 us (9%)
  local copies, waits for them, and re-layouts  7.39 us (5%)
  matrix products  4.73 us (3%)
  other arithmetic  3.64 us (2%)
    all_to_all x2, blocking collectives, gather(): return jnp.moveaxis(lax.all_to_all(copies, axis_name, 0, 0), 0, axis)  26.3 us
    all_to_all x1, blocking collectives, body(): totals = jnp.sum(lax.all_to_all(sums, 'zl', 0, 0), axis=0)  19.4 us
    ppermute x1, starting transfers between devices, body(): other = lax.ppermute(masked, 'zh', [(0, 1), (1, 0)])  15.7 us
    all_gather x1, waiting for transfers between devices, body(): left = lax.all_gather(left, 'zl', axis=0)  13.9 us
    all_to_all x1, blocking collectives, body(): shares = lax.all_to_all(partial.reshape(n_y, rows, cols), 'y', 0, 0)  12 us
    all_to_all x1, blocking collectives, body(): left = lax.all_to_all(pieces, 'y', 0, 0).reshape(n_y * rows, cols // n_y)  11.6 us
    ppermute x1, waiting for transfers between devices, body(): other = lax.ppermute(masked, 'zh', [(0, 1), (1, 0)])  6.82 us
    all_to_all x1, waiting for transfers between devices, body(): other = lax.all_to_all(other.reshape(n_y, part, cols), 'y', 0, 0)  6.52 us
  transfers between devices with their start and end apart: 4, of which 3 were waited for; matrix products, arithmetic and copies ran while one was open for 1% of the time, Pallas kernels for 0%

profile of v3, /device:TPU:6, one launch (start us, length us, event | category | flops | bytes accessed | tf_op | source)
XLA Modules:
  0.0 148.5 jit_solution(6588865952599308480)
XLA Ops:
  6.6 0.7 convert_element_type.6
  7.3 0.7 convert_element_type.7
  8.1 1.0 select_multiply_fusion.1
  9.5 11.6 %all_to_all.36 = f32[4,80,160]{1,2,0:T(8,128)S(1)} all-to-all(f32[4,80,160]{1,2,0:T(8,128)S(1)} %copy.34), channel_id=1, replica_groups=mesh['zl'=8,'x'=4,'y'=4,'zh'=2,'c'=2] {'y'}, dimensions={0} | all-to-all | bytes 409600 | tf_op jit(solution)/shard_map/all_to_all | solution.py:43
  21.1 0.2 copy.35
  21.3 0.9 reshape.108
  22.2 15.7 %collective-permute-start = (f32[80,640]{1,0:T(8,128)S(1)}, f32[80,640]{1,0:T(8,128)S(1)}, u32[]{:S(2)}, u32[]{:S(2)}) collective-permute-start(f32[80,640]{1,0:T(8,128)S(1)} %select_multiply_fusion.1), channel_id=1, source_target_pairs={{0,2},{2,0},{1,3},{3,1},{4,6},{6,4},{5,7},{7,5},{8,10},{10,8},{9,1... | collective-permute-start | bytes 614408 | tf_op jit(solution)/shard_map/ppermute | solution.py:39
  38.0 0.7 reshape.109
  38.7 3.4 %all-to-all-start.1 = ((f32[4,20,640]{2,1,0:T(8,128)}), f32[4,20,640]{2,1,0:T(8,128)S(1)}, u32[]{:S(2)}, u32[]{:S(2)}) async-start(f32[4,20,640]{2,1,0:T(8,128)} %reshape.109), calls=%async_computation.1 | async-start | bytes 491520 | tf_op jit(solution)/shard_map/all_to_all | solution.py:47
  42.1 6.8 %collective-permute-done = f32[80,640]{1,0:T(8,128)S(1)} collective-permute-done((f32[80,640]{1,0:T(8,128)S(1)}, f32[80,640]{1,0:T(8,128)S(1)}, u32[]{:S(2)}, u32[]{:S(2)}) %collective-permute-start) | collective-permute-done | bytes 204832 | tf_op jit(solution)/shard_map/ppermute | solution.py:39
  48.9 0.7 reshape.110
  49.6 3.4 %all-to-all-start.2 = ((f32[4,20,640]{2,1,0:T(8,128)}), f32[4,20,640]{2,1,0:T(8,128)S(1)}, u32[]{:S(2)}, u32[]{:S(2)}) async-start(f32[4,20,640]{2,1,0:T(8,128)} %reshape.110), calls=%async_computation.2 | async-start | bytes 491520 | tf_op jit(solution)/shard_map/all_to_all | solution.py:49
  53.1 6.5 %all-to-all-done.2 = f32[4,20,640]{2,1,0:T(8,128)S(1)} async-done(((f32[4,20,640]{2,1,0:T(8,128)}), f32[4,20,640]{2,1,0:T(8,128)S(1)}, u32[]{:S(2)}, u32[]{:S(2)}) %all-to-all-start.2) | async-done | bytes 204832 | tf_op jit(solution)/shard_map/all_to_all | solution.py:49
  59.8 20.0 %all_to_all.37 = f32[4,2,2,40,640]{4,3,2,1,0:T(8,128)S(1)} all-to-all(f32[4,2,2,40,640]{4,3,2,1,0:T(8,128)S(1)} %broadcast_in_dim.112), channel_id=1, replica_groups=mesh['zl'=8,'x'=4,'y'=4,'zh'=2,'c'=2] {'x'}, dimensions={0} | all-to-all | bytes 3276800 | tf_op jit(solution)/shard_map/all_to_all | solution.py:27
  79.8 0.3 broadcast_in_dim.113
  80.0 6.4 %all_to_all.38 = f32[2,4,2,2,40,640]{5,4,3,2,1,0:T(8,128)S(1)} all-to-all(f32[2,4,2,2,40,640]{5,4,3,2,1,0:T(8,128)S(1)} %broadcast_in_dim.113), channel_id=1, replica_groups=mesh['zl'=8,'x'=4,'y'=4,'zh'=2,'c'=2] {'c'}, dimensions={0} | all-to-all | bytes 6553600 | tf_op jit(solution)/shard_map/all_to_all | solution.py:27
  86.4 0.3 copy.38
  86.7 13.9 %all-gather.4.cloned.1.call-done = f32[8,320,160]{1,2,0:T(8,128)} async-done(((f32[1,320,160]{1,2,0:T(8,128)}), f32[8,320,160]{1,2,0:T(8,128)}) %all-gather.4.cloned.1.call-update) | async-done | bytes 1638416 | tf_op jit(solution)/shard_map/all_gather | solution.py:46
  100.5 3.9 %reshape.118 = f32[4,80,160,8]{1,0,2,3:T(4,128)} reshape(f32[320,160,8]{0,1,2:T(8,128)} %bitcast.29) | data formatting | bytes 3276800 | tf_op jit(solution)/shard_map/zik,zkj->ij/dot_general | solution.py:58
  104.4 4.7 %fusion.2 = f32[4,80,640]{2,1,0:T(8,128)S(1)} fusion(f32[8,160,640,1]{2,1,0,3:T(8,128)S(1)} %bitcast.27, f32[4,80,160,8]{1,0,2,3:T(4,128)} %reshape.118), kind=kOutput, calls=%fused_computation.2 | convolution fusion | flops 1572864000 | bytes 5734400 | tf_op jit(solution)/shard_map/zik,zkj->ij/dot_general | solution.py:58
  109.1 12.0 %all_to_all.39 = f32[4,80,640]{2,1,0:T(8,128)S(1)} all-to-all(f32[4,80,640]{2,1,0:T(8,128)S(1)} %fusion.2), channel_id=1, replica_groups=mesh['zl'=8,'x'=4,'y'=4,'zh'=2,'c'=2] {'y'}, dimensions={0} | all-to-all | bytes 1638400 | tf_op jit(solution)/shard_map/all_to_all | solution.py:65
  121.2 0.2 fusion.6
  121.4 19.4 %all_to_all.40 = f32[8,1,80]{2,1,0:T(1,128)S(1)} all-to-all(f32[8,1,80]{2,1,0:T(1,128)S(1)} %broadcast_in_dim.120), channel_id=1, replica_groups=mesh['zl'=8,'x'=4,'y'=4,'zh'=2,'c'=2] {'zl'}, dimensions={0} | all-to-all | bytes 5120 | tf_op jit(solution)/shard_map/all_to_all | solution.py:69
  140.8 0.8 fusion.5
  (20 shorter events, 0.8 us)
Async XLA Ops:
  6.5 94.0 %all-gather.4.cloned.1.call-start = ((), (), s32[]{:S(2)}) async-start(), calls=%async_computation.7 | async-start | bytes 2211840 | tf_op jit(solution)/shard_map/all_gather | solution.py:46
  22.2 26.7 %collective-permute-start = (f32[80,640]{1,0:T(8,128)S(1)}, f32[80,640]{1,0:T(8,128)S(1)}, u32[]{:S(2)}, u32[]{:S(2)}) collective-permute-start(f32[80,640]{1,0:T(8,128)S(1)} %select_multiply_fusion.1), channel_id=1, source_target_pairs={{0,2},{2,0},{1,3},{3,1},{4,6},{6,4},{5,7},{7,5},{8,10},{10,8},{9,1... | collective-permute-start | bytes 614408 | tf_op jit(solution)/shard_map/ppermute | solution.py:39
  38.7 10.2 %all-to-all-start.1 = ((f32[4,20,640]{2,1,0:T(8,128)}), f32[4,20,640]{2,1,0:T(8,128)S(1)}, u32[]{:S(2)}, u32[]{:S(2)}) async-start(f32[4,20,640]{2,1,0:T(8,128)} %reshape.109), calls=%async_computation.1 | async-start | bytes 491520 | tf_op jit(solution)/shard_map/all_to_all | solution.py:47
  49.6 10.0 %all-to-all-start.2 = ((f32[4,20,640]{2,1,0:T(8,128)}), f32[4,20,640]{2,1,0:T(8,128)S(1)}, u32[]{:S(2)}, u32[]{:S(2)}) async-start(f32[4,20,640]{2,1,0:T(8,128)} %reshape.110), calls=%async_computation.2 | async-start | bytes 491520 | tf_op jit(solution)/shard_map/all_to_all | solution.py:49
Sparse Core Ops, SparseCore 0:
  22.4 78.1 all-gather.3

commit v4 on v2

v4 whole, which is shorter than its diff:
```python
import functools

import jax
import jax.numpy as jnp
from jax import lax
from jax.experimental import pallas as pl
from jax.experimental.pallas import tpu as pltpu
from jax.sharding import Mesh, PartitionSpec as P

BLK = 256
ROWS = ("x", "y", "zh", "c")
SLOTS = 256
EXACT = lax.Precision.HIGHEST


def tile_mask(pattern, row_start, rows, col_start, cols):
    blocks = pattern.shape[0]
    row_blk = (row_start + jnp.arange(rows)) // BLK
    first = row_start // BLK
    low = lax.dynamic_slice_in_dim(pattern, first, 1, 0)[0]
    high = lax.dynamic_slice_in_dim(pattern, jnp.minimum(first + 1, blocks - 1), 1, 0)[0]
    col_blk = (col_start + jnp.arange(cols)) // BLK
    pick = col_blk[:, None] == jnp.arange(blocks)[None, :]
    low = jnp.sum(jnp.where(pick, low[None, :], 0.0), axis=1)
    high = jnp.sum(jnp.where(pick, high[None, :], 0.0), axis=1)
    return jnp.where((row_blk == first)[:, None], low[None, :], high[None, :])


def places(pattern, zh, c):
    q = jnp.arange(80)
    chunk = 20 * (q // 5) + 10 * zh + 5 * c + q % 5
    half = jnp.arange(40)
    row_pick = (chunk[:, None] // 16 == jnp.arange(20)[None, :]).astype(jnp.float32)
    col_pick = (half[None, :] // 2 == jnp.arange(20)[:, None]).astype(jnp.float32)
    live = row_pick @ pattern @ col_pick
    before = (q[:, None] > q[None, :]).astype(jnp.float32) @ live
    same = (half[:, None] // 5 == half[None, :] // 5) & (half[:, None] < half[None, :])
    earlier = jnp.sum(live, axis=0, keepdims=True) @ same.astype(jnp.float32)
    return jnp.where(live > 0, before + earlier, -1.0), live


def most_live(pattern):
    g = jnp.arange(16)[:, None] * 20 + jnp.arange(5)[None, :]
    chunk = (jnp.arange(4) * 5)[:, None, None] + g[None]
    weight = jnp.sum((chunk[..., None] // 16 == jnp.arange(20)).astype(jnp.float32), (1, 2))
    half = jnp.arange(40).reshape(8, 5)
    wide = jnp.sum((half[..., None] // 2 == jnp.arange(20)).astype(jnp.float32), 1)
    return jnp.max(weight @ pattern @ wide.T)


def split(x):
    hi = x.astype(jnp.bfloat16)
    return hi, (x - hi.astype(jnp.float32)).astype(jnp.bfloat16)


def dot(a, b):
    return jnp.dot(a, b, preferred_element_type=jnp.float32)


def product_kernel(slots, place_ref, packed_ref, right_ref, out_ref, left_ref):
    lane = lax.broadcasted_iota(jnp.int32, (80, 128), 1) // 32
    slot = lax.broadcasted_iota(jnp.int32, (80, slots), 1).astype(jnp.float32)
    place = place_ref[...]
    units, group = [], 0
    for z in range(8):
        hi, lo = split(packed_ref[z])
        both = jnp.concatenate([hi, lo], axis=1)
        pick = jnp.concatenate(
            [
                (place[:, 5 * z + h : 5 * z + h + 1] == slot).astype(jnp.bfloat16)
                for h in range(5)
            ],
            axis=0,
        )
        got = dot(pick, both)
        got = got[:, :128] + got[:, 128:]
        units += [got[80 * h : 80 * h + 80] for h in range(5)]
        while len(units) >= 4:
            four, units = units[:4], units[4:]
            for r in range(4):
                tile = jnp.zeros((80, 128), jnp.float32)
                for j in range(4):
                    moved = four[j]
                    if j != r:
                        moved = pltpu.roll(moved, 32 * ((j - r) % 4), 1)
                    tile = jnp.where(lane == j, moved, tile)
                left_ref[80 * r : 80 * r + 80, 128 * group : 128 * group + 128] = tile
            group += 1
    to = lax.broadcasted_iota(jnp.int32, (320, 1), 0)
    source = (to % 20) // 5 * 80 + to // 20 * 5 + to % 5
    order = (source == lax.broadcasted_iota(jnp.int32, (320, 320), 1)).astype(jnp.bfloat16)
    left_hi, left_lo = split(left_ref[...])
    left_hi = dot(order, left_hi).astype(jnp.bfloat16)
    left_lo = dot(order, left_lo).astype(jnp.bfloat16)
    right_hi, right_lo = split(right_ref[...])
    out_ref[...] = dot(left_hi, right_hi) + (dot(left_hi, right_lo) + dot(left_lo, right_hi))


def product(place, packed, right):
    slots = packed.shape[1]
    vmem = pl.BlockSpec(memory_space=pltpu.VMEM)
    return pl.pallas_call(
        functools.partial(product_kernel, slots),
        out_shape=jax.ShapeDtypeStruct((320, 640), jnp.float32),
        in_specs=[vmem] * 3,
        out_specs=vmem,
        scratch_shapes=[pltpu.VMEM((320, 1280), jnp.float32)],
        compiler_params=pltpu.CompilerParams(vmem_limit_bytes=48 * 2**20),
        cost_estimate=pl.CostEstimate(
            flops=3 * 10**9, bytes_accessed=6 * 10**6, transcendentals=0
        ),
    )(place, packed, right)


def gather(block, axis_name, axis):
    size = lax.axis_size(axis_name)
    copies = jnp.broadcast_to(block[None], (size,) + block.shape)
    return jnp.moveaxis(lax.all_to_all(copies, axis_name, 0, 0), 0, axis)


def partial_product(slots, units, place, masked):
    zl = lax.axis_index("zl")
    mine = lax.dynamic_slice_in_dim(place, 5 * zl, 5, 1).reshape(400, 1)
    pick = (mine == jnp.arange(slots, dtype=jnp.float32)[None, :]).astype(jnp.float32)
    packed = jnp.dot(pick.T, units, precision=EXACT)
    masked, packed = lax.optimization_barrier((masked, packed))
    packed = lax.all_gather(packed, "zl", axis=0)

    right = masked.reshape(5, 4, 4, 640).transpose(1, 0, 2, 3).reshape(4, 1, 20, 640)
    right = jnp.broadcast_to(right, (4, 2, 20, 640)).reshape(8, 20, 640)
    right = lax.all_to_all(right, ("y", "zh"), 0, 0)
    right = right.reshape(2, 2, 2, 20, 640)
    right = gather(right, "x", 0)
    right = gather(right, "c", 4).reshape(1280, 640)
    return product(place, packed, right)


def body(state, in_pattern, out_pattern):
    rows, cols = state.shape
    nodes_all = cols * lax.axis_size("zl")
    row_start = lax.axis_index(ROWS) * rows
    col_start = lax.axis_index("zl") * cols
    in_pattern = in_pattern.astype(jnp.float32)
    out_pattern = out_pattern.astype(jnp.float32)
    masked = state * tile_mask(in_pattern, row_start, rows, col_start, cols)
    place, _ = places(in_pattern, lax.axis_index("zh"), lax.axis_index("c"))

    units = masked.reshape(5, 4, 4, 5, 8, 4, 4)
    units = units.transpose(1, 5, 0, 3, 2, 4, 6).reshape(16, 25, 128)
    units = lax.all_to_all(units, ("x", "y"), 0, 0).reshape(400, 128)

    shares = lax.cond(
        most_live(in_pattern) <= SLOTS,
        functools.partial(partial_product, SLOTS),
        functools.partial(partial_product, 400),
        units,
        place,
        masked,
    )
    shares = lax.all_to_all(shares.reshape(16, 20, 640), ("x", "y"), 0, 0)
    expanded = jnp.sum(shares.reshape(4, 4, 4, 5, 640), axis=1)
    expanded = expanded.transpose(2, 0, 1, 3).reshape(rows, cols)
    inflated = expanded * expanded * tile_mask(out_pattern, row_start, rows, col_start, cols)
    sums = jnp.broadcast_to(jnp.sum(inflated, axis=1)[None, :], (8, rows))
    totals = jnp.sum(lax.all_to_all(sums, "zl", 0, 0), axis=0)
    return inflated * (nodes_all / totals)[:, None]


def solution(mesh):
    fine = Mesh(
        mesh.devices.reshape(8, 4, 4, 2, 2), ("zl", "x", "y", "zh", "c")
    )
    return jax.shard_map(
        body,
        mesh=fine,
        in_specs=(P(ROWS, "zl"), P(), P()),
        out_specs=P(ROWS, "zl"),
        check_vma=False,
    )
```

time: 157 us -> 192 us (1.22)
  blocking collectives: 118 us -> 28.3 us
  waiting for transfers between devices: 10.2 us -> 61.6 us
  starting transfers between devices: 0.01 us -> 36.8 us
  local copies, waits for them, and re-layouts: 6 us -> 36.9 us
  Pallas kernels: 0 us -> 5.97 us
    all_to_all x4 -> x0, blocking collectives: 51.5 us -> none  [the longest x1 17.5 us: body(): totals = jnp.sum(lax.all_to_all(sums, 'zl', 0, 0), axis=0)]
    all_to_all x0 -> x4, waiting for transfers between devices: none -> 41.7 us  [the longest x1 17.1 us: partial_product(): right = lax.all_to_all(right, ('y', 'zh'), 0, 0)]
    all_to_all x3 -> x2, blocking collectives: 66.1 us -> 28.3 us  [gather(): return jnp.moveaxis(lax.all_to_all(copies, axis_name, 0, 0), 0, axis)]
    all_to_all x0 -> x4, starting transfers between devices: none -> 36.8 us  [the longest x1 14.1 us: partial_product(): right = lax.all_to_all(right, ('y', 'zh'), 0, 0)]
    reshape x4 -> x8, local copies, waits for them, and re-layouts: 0.95 us -> 29.1 us  [the longest x2 13.8 us: body(): units = units.transpose(1, 5, 0, 3, 2, 4, 6).reshape(16, 25, 128)]
    all_gather x1, waiting for transfers between devices: 10.2 us -> 19.3 us  [partial_product(): packed = lax.all_gather(packed, 'zl', axis=0)]
    pallas_call x0 -> x1, Pallas kernels: none -> 5.97 us  [product(): pl.pallas_call(functools.partial(product_kernel, slots), out_shape=jax.Sh...]
    dot_general x1 -> x0, local copies, waits for them, and re-layouts: 3.87 us -> none  [body(): jnp.einsum('zik,zkj->ij', left, right, preferred_element_type=jnp.float32...]
  transfers between devices with their start and end apart: 1 -> 5, of which waited for: 1 -> 5; matrix products, arithmetic and copies ran while one was open for 0% -> 5% of each run, Pallas kernels for 0% -> 0%
where the time goes in v4:
time: 192 us; the launch traced here: 191 us
  waiting for transfers between devices  61.6 us (32%)
  local copies, waits for them, and re-layouts  36.9 us (19%)
  starting transfers between devices  36.8 us (19%)
  blocking collectives  28.3 us (15%)
  between operations  14.2 us (7%)
  Pallas kernels  5.97 us (3%)
  other arithmetic  4.02 us (2%)
  matrix products  2.93 us (2%)
    all_to_all x2, blocking collectives, gather(): return jnp.moveaxis(lax.all_to_all(copies, axis_name, 0, 0), 0, axis)  28.3 us
    all_gather x1, waiting for transfers between devices, partial_product(): packed = lax.all_gather(packed, 'zl', axis=0)  19.3 us
    all_to_all x1, waiting for transfers between devices, partial_product(): right = lax.all_to_all(right, ('y', 'zh'), 0, 0)  17.1 us
    all_to_all x1, starting transfers between devices, partial_product(): right = lax.all_to_all(right, ('y', 'zh'), 0, 0)  14.1 us
    reshape x2, local copies, waits for them, and re-layouts, body(): units = units.transpose(1, 5, 0, 3, 2, 4, 6).reshape(16, 25, 128)  13.8 us
    all_to_all x1, waiting for transfers between devices, body(): shares = lax.all_to_all(shares.reshape(16, 20, 640), ('x', 'y'), 0, 0)  10.6 us
    all_to_all x1, waiting for transfers between devices, body(): totals = jnp.sum(lax.all_to_all(sums, 'zl', 0, 0), axis=0)  10.2 us
    reshape x1, local copies, waits for them, and re-layouts, body(): units = masked.reshape(5, 4, 4, 5, 8, 4, 4)  10.1 us
  transfers between devices with their start and end apart: 5, of which 5 were waited for; matrix products, arithmetic and copies ran while one was open for 5% of the time, Pallas kernels for 0%

profile of v4, /device:TPU:6, one launch (start us, length us, event | category | flops | bytes accessed | tf_op | source)
XLA Modules:
  0.0 191.1 jit_solution(11226516434898215739)
XLA Ops:
  8.1 1.0 select_multiply_fusion
  9.2 10.1 %reshape.360 = f32[5,4,4,5,8,4,4]{6,5,4,3,2,1,0:T(4,128)} reshape(f32[80,640]{1,0:T(8,128)S(1)} %select_multiply_fusion) | data formatting | bytes 409600 | tf_op jit(solution)/shard_map/reshape | solution.py:148
  19.3 6.5 %copy.104 = f32[4,4,5,5,4,8,4]{6,5,4,3,2,1,0:T(8,128)} copy(f32[4,4,5,5,4,8,4]{6,1,5,3,4,0,2:T(4,128)} %bitcast.45) | data formatting | bytes 409600 | tf_op jit(solution)/shard_map/reshape | solution.py:149
  25.8 7.2 %reshape.369 = f32[16,25,128]{2,1,0:T(8,128)} reshape(f32[4,4,5,5,4,8,4]{6,5,4,3,2,1,0:T(8,128)} %copy.104) | data formatting | bytes 409600 | tf_op jit(solution)/shard_map/reshape | solution.py:149
  33.0 9.2 %all-to-all-start.6 = ((f32[16,25,128]{2,1,0:T(8,128)}), f32[16,25,128]{2,1,0:T(8,128)S(1)}, u32[]{:S(2)}, u32[]{:S(2)}) async-start(f32[16,25,128]{2,1,0:T(8,128)} %reshape.369), calls=%async_computation.6 | async-start | bytes 524288 | tf_op jit(solution)/shard_map/all_to_all | solution.py:150
  42.7 0.8 fusion.11
  44.9 3.8 %all-to-all-done.6 = f32[16,25,128]{2,1,0:T(8,128)S(1)} async-done(((f32[16,25,128]{2,1,0:T(8,128)}), f32[16,25,128]{2,1,0:T(8,128)S(1)}, u32[]{:S(2)}, u32[]{:S(2)}) %all-to-all-start.6) | async-done | bytes 204832 | tf_op jit(solution)/shard_map/all_to_all | solution.py:150
  48.7 97.0 %conditional.1 = (f32[320,640]{1,0:T(8,128)}) conditional(s32[]{:T(128)} %convert_element_type.24, (f32[80,40]{0,1:T(8,128)S(1)}, f32[400,128]{1,0:T(8,128)S(1)}, f32[80,640]{1,0:T(8,128)S(1)}) %tuple.13, (f32[80,40]{0,1:T(8,128)S(1)}, f32[400,128]{1,0:T(8,128)S(1)}, f32[80,640]{1,0:T(8,128)S(1)}) %tuple.13), branch_computations={%region_6.7_spmd, %region_7.8_spmd} | conditional | flops 3245920000 | bytes 55185760 | solution.py:152
  49.3 1.4 fusion.2
  51.6 14.1 %all-to-all-start.3 = ((f32[8,20,640]{2,1,0:T(8,128)}), f32[8,20,640]{2,1,0:T(8,128)S(1)}, u32[]{:S(2)}, u32[]{:S(2)}) async-start(f32[8,20,640]{2,1,0:T(8,128)} %bitcast.9), calls=%async_computation.3 | async-start | bytes 983040 | tf_op jit(solution)/shard_map/cond/branch_1_fun/all_to_all | solution.py:131
  66.5 17.1 %all-to-all-done.3 = f32[8,20,640]{2,1,0:T(8,128)S(1)} async-done(((f32[8,20,640]{2,1,0:T(8,128)}), f32[8,20,640]{2,1,0:T(8,128)S(1)}, u32[]{:S(2)}, u32[]{:S(2)}) %all-to-all-start.3) | async-done | bytes 409632 | tf_op jit(solution)/shard_map/cond/branch_1_fun/all_to_all | solution.py:131
  84.3 21.9 %all_to_all.43 = f32[4,2,2,2,20,640]{5,3,4,2,1,0:T(2,128)S(1)} all-to-all(f32[4,2,2,2,20,640]{5,3,4,2,1,0:T(2,128)S(1)} %broadcast_in_dim.142), channel_id=1, replica_groups=mesh['zl'=8,'x'=4,'y'=4,'zh'=2,'c'=2] {'x'}, dimensions={0} | all-to-all | bytes 3276800 | tf_op jit(solution)/shard_map/cond/branch_1_fun/all_to_all | solution.py:118
  106.2 1.1 copy.90
  107.7 6.4 %all_to_all.44 = f32[2,4,2,2,2,20,640]{6,1,5,4,3,2,0:T(4,128)S(1)} all-to-all(f32[2,4,2,2,2,20,640]{6,1,5,4,3,2,0:T(4,128)S(1)} %broadcast_in_dim.143), channel_id=1, replica_groups=mesh['zl'=8,'x'=4,'y'=4,'zh'=2,'c'=2] {'c'}, dimensions={0} | all-to-all | bytes 6553600 | tf_op jit(solution)/shard_map/cond/branch_1_fun/all_to_all | solution.py:118
  114.0 2.3 %copy.91 = f32[4,2,2,2,2,20,640]{6,5,4,3,2,1,0:T(8,128)} copy(f32[4,2,2,2,2,20,640]{6,0,5,3,2,1,4:T(4,128)S(1)} %bitcast.47) | data formatting | bytes 6553600 | tf_op jit(solution)/shard_map/cond/branch_1_fun/transpose | solution.py:118
  116.3 2.9 %reshape.354.right_ref = f32[1280,640]{1,0:T(8,128)S(1)} reshape(f32[4,2,2,2,2,20,640]{6,5,4,3,2,1,0:T(8,128)} %copy.91) | data formatting | bytes 6553600 | tf_op jit(solution)/shard_map/cond/branch_1_fun/reshape | solution.py:134
  119.3 19.3 %all-gather.7.cloned.1.call-done = f32[2048,128]{1,0:T(8,128)} async-done(((f32[256,128]{1,0:T(8,128)}), f32[2048,128]{1,0:T(8,128)}) %all-gather.7.cloned.1.call-update) | async-done | bytes 1048592 | tf_op jit(solution)/shard_map/cond/branch_1_fun/all_gather | solution.py:127
  138.5 1.2 copy-done.1
  139.8 6.0 %branch_1_fun.1 = f32[320,640]{1,0:T(8,128)} custom-call(f32[80,40]{1,0:T(8,128)S(1)} %copy.95.place_ref, f32[8,256,128]{2,1,0:T(8,128)S(1)} %bitcast.44, f32[1280,640]{1,0:T(8,128)S(1)} %reshape.354.right_ref), custom_call_target="tpu_custom_call" | custom-call | flops 3000000000 | bytes 6000000 | tf_op jit(solution)/shard_map/cond/branch_1_fun/pallas_call | solution.py:102
  145.7 2.2 %reshape.363 = f32[16,20,640]{2,1,0:T(8,128)} reshape(f32[320,640]{1,0:T(8,128)} %get-tuple-element.86) | data formatting | bytes 1638400 | tf_op jit(solution)/shard_map/reshape | solution.py:160
  147.9 7.2 %all-to-all-start.7 = ((f32[16,20,640]{2,1,0:T(8,128)}), f32[16,20,640]{2,1,0:T(8,128)S(1)}, u32[]{:S(2)}, u32[]{:S(2)}) async-start(f32[16,20,640]{2,1,0:T(8,128)} %reshape.363), calls=%async_computation.7 | async-start | bytes 1966080 | tf_op jit(solution)/shard_map/all_to_all | solution.py:160
  155.1 10.6 %all-to-all-done.7 = f32[16,20,640]{2,1,0:T(8,128)S(1)} async-done(((f32[16,20,640]{2,1,0:T(8,128)}), f32[16,20,640]{2,1,0:T(8,128)S(1)}, u32[]{:S(2)}, u32[]{:S(2)}) %all-to-all-start.7) | async-done | bytes 819232 | tf_op jit(solution)/shard_map/all_to_all | solution.py:160
  166.9 6.2 %all-to-all-start.8 = ((f32[8,1,80]{2,1,0:T(1,128)}), f32[8,1,80]{2,1,0:T(1,128)S(1)}, u32[]{:S(2)}, u32[]{:S(2)}) async-start(f32[8,1,80]{2,1,0:T(1,128)} %broadcast_in_dim.183), calls=%async_computation.8 | async-start | bytes 8192 | tf_op jit(solution)/shard_map/all_to_all | solution.py:165
  173.2 10.2 %all-to-all-done.8 = f32[8,1,80]{2,1,0:T(1,128)S(1)} async-done(((f32[8,1,80]{2,1,0:T(1,128)}), f32[8,1,80]{2,1,0:T(1,128)S(1)}, u32[]{:S(2)}, u32[]{:S(2)}) %all-to-all-start.8) | async-done | bytes 2592 | tf_op jit(solution)/shard_map/all_to_all | solution.py:165
  (47 shorter events, 7.8 us)
Async XLA Ops:
  25.8 16.9 %copy-start.2 = (s32[20,20]{1,0:T(8,128)S(1)}, s32[20,20]{1,0:T(8,128)}, u32[]{:S(2)}) copy-start(s32[20,20]{1,0:T(8,128)} %param.6) | copy-start | bytes 4804
  33.0 15.6 %all-to-all-start.6 = ((f32[16,25,128]{2,1,0:T(8,128)}), f32[16,25,128]{2,1,0:T(8,128)S(1)}, u32[]{:S(2)}, u32[]{:S(2)}) async-start(f32[16,25,128]{2,1,0:T(8,128)} %reshape.369), calls=%async_computation.6 | async-start | bytes 524288 | tf_op jit(solution)/shard_map/all_to_all | solution.py:150
  51.6 32.0 %all-to-all-start.3 = ((f32[8,20,640]{2,1,0:T(8,128)}), f32[8,20,640]{2,1,0:T(8,128)S(1)}, u32[]{:S(2)}, u32[]{:S(2)}) async-start(f32[8,20,640]{2,1,0:T(8,128)} %bitcast.9), calls=%async_computation.3 | async-start | bytes 983040 | tf_op jit(solution)/shard_map/cond/branch_1_fun/all_to_all | solution.py:131
  65.8 72.8 %all-gather.7.cloned.1.call-start = ((), (), s32[]{:S(2)}) async-start(), calls=%async_computation.10 | async-start | bytes 1179648 | tf_op jit(solution)/shard_map/cond/branch_1_fun/all_gather | solution.py:127
  138.5 1.2 copy-start.1
  147.9 17.8 %all-to-all-start.7 = ((f32[16,20,640]{2,1,0:T(8,128)}), f32[16,20,640]{2,1,0:T(8,128)S(1)}, u32[]{:S(2)}, u32[]{:S(2)}) async-start(f32[16,20,640]{2,1,0:T(8,128)} %reshape.363), calls=%async_computation.7 | async-start | bytes 1966080 | tf_op jit(solution)/shard_map/all_to_all | solution.py:160
  166.9 16.5 %all-to-all-start.8 = ((f32[8,1,80]{2,1,0:T(1,128)}), f32[8,1,80]{2,1,0:T(1,128)S(1)}, u32[]{:S(2)}, u32[]{:S(2)}) async-start(f32[8,1,80]{2,1,0:T(1,128)} %broadcast_in_dim.183), calls=%async_computation.8 | async-start | bytes 8192 | tf_op jit(solution)/shard_map/all_to_all | solution.py:165
Sparse Core Ops, SparseCore 0:
  68.7 69.8 all-gather.6

commit v5 on v0

v5 whole, which is shorter than its diff:
```python
import functools

import jax
import jax.numpy as jnp
from jax import lax
from jax.experimental import pallas as pl
from jax.experimental.pallas import tpu as pltpu
from jax.sharding import Mesh, PartitionSpec as P

BLK = 256
ROWS = ("x", "y", "zh", "c")
MAIN, REST = 80, 24
LEFT = MAIN + REST
RUN, PAD = 20, 24
PIECE = LEFT + 5 * PAD
VMEM = pl.BlockSpec(memory_space=pltpu.VMEM)
SMEM = pl.BlockSpec(memory_space=pltpu.SMEM)


def split(x):
    hi = x.astype(jnp.bfloat16)
    return hi, (x - hi.astype(jnp.float32)).astype(jnp.bfloat16)


def dot(a, b):
    return jnp.dot(a, b, preferred_element_type=jnp.float32)


def call(kernel, outs, in_specs, args, scratch=(), flops=10**6, size=10**6):
    return pl.pallas_call(
        kernel,
        out_shape=outs,
        in_specs=in_specs,
        out_specs=jax.tree.map(lambda _: VMEM, outs),
        scratch_shapes=scratch,
        compiler_params=pltpu.CompilerParams(vmem_limit_bytes=40 * 2**20),
        cost_estimate=pl.CostEstimate(
            flops=flops, bytes_accessed=size, transcendentals=0
        ),
    )(*args)


def masked_block(at_ref, pattern_ref, h, x):
    row = at_ref[0] * 80
    col = (5 * at_ref[1] + h) // 2
    first = row // BLK
    low = pattern_ref[first, col].astype(jnp.float32)
    high = pattern_ref[jnp.minimum(first + 1, 19), col].astype(jnp.float32)
    here = lax.broadcasted_iota(jnp.int32, (80, 128), 0) + row < (first + 1) * BLK
    return x * jnp.where(here, low, high)


def pieces_kernel(at_ref, pattern_ref, state_ref, out_ref, masked_ref):
    zh, c = at_ref[2], at_ref[3]
    for h in range(5):
        lanes = slice(128 * h, 128 * h + 128)
        masked_ref[:, lanes] = masked_block(at_ref, pattern_ref, h, state_ref[:, lanes])
    out_ref[...] = jnp.zeros_like(out_ref)
    for y in range(4):
        for h in range(5):
            out_ref[y, LEFT + PAD * h : LEFT + PAD * h + RUN] = masked_ref[
                RUN * y : RUN * y + RUN, 128 * h : 128 * h + 128
            ]
    n = lax.broadcasted_iota(jnp.int32, (1, 640), 1)
    late = n >= 512
    y = jnp.where(late, (n - 512) // 32, n // 128)
    m = jnp.where(late, 128 + n % 32, n % 128)
    dzh, dc, y0, t = m // 80, m // 40 % 2, m // 20 % 2, m % 20
    zh_of = jnp.where(dzh == 0, zh, 1 - zh)
    c_of = jnp.where(dc == 0, c, 1 - c)
    source = 80 * (4 * y0 + 2 * zh_of + c_of) + 20 * y + t
    order = lax.broadcasted_iota(jnp.int32, (640, 640), 0) == source
    order = order.astype(jnp.float32).astype(jnp.bfloat16)
    x = masked_ref[...]
    hi, rest = x.astype(jnp.bfloat16), x
    rest = x - hi.astype(jnp.float32)
    mid, low = split(rest)
    moved = (dot(hi, order) + dot(mid, order)) + dot(low, order)
    lane = lax.broadcasted_iota(jnp.int32, (8, 128), 1) // 32
    for y in range(4):
        out_ref[y, :MAIN] = moved[:, 128 * y : 128 * y + 128]
        for slot in range(3):
            tile = jnp.zeros((8, 128), jnp.float32)
            for j in range(min(4, 10 - 4 * slot)):
                rows = 8 * (4 * slot + j)
                part = moved[rows : rows + 8, 512:]
                if j != y:
                    part = pltpu.roll(part, 32 * ((j - y) % 4), 1)
                tile = jnp.where(lane == j, part, tile)
            out_ref[y, MAIN + 8 * slot : MAIN + 8 * slot + 8] = tile


def unpack_kernel(got_ref, left_ref, right_ref):
    left_ref[...] = got_ref[:, :LEFT]
    for y in range(4):
        for h in range(5):
            right_ref[y // 2, RUN * (y % 2) : RUN * (y % 2) + RUN, 128 * h : 128 * h + 128] = (
                got_ref[y, LEFT + PAD * h : LEFT + PAD * h + RUN]
            )


def product_kernel(at_ref, *refs):
    lefts, rights, out_ref, hi_ref, lo_ref = refs[:8], refs[8:12], *refs[12:]
    for part, ref in enumerate(rights):
        for dx in range(4):
            for y1 in range(2):
                hi, lo = split(ref[dx, y1])
                rows = slice(40 * part, 40 * part + 40)
                hi_ref[2 * dx + y1, rows] = hi
                lo_ref[2 * dx + y1, rows] = lo
    lane = lax.broadcasted_iota(jnp.int32, (8, 128), 1) // 32
    zl, x = at_ref[1], at_ref[4]
    total = jnp.zeros((320, 640), jnp.float32)
    for d, ref in enumerate(lefts):
        source = lax.rem(zl - d + 8, 8)
        block = 2 * lax.rem(x - source // 2 + 4, 4) + lax.rem(source, 2)
        whole = []
        for y in range(4):
            rest = []
            for tile in range(10):
                rows = MAIN + 8 * (tile // 4)
                rest.append(jnp.where(lane == tile % 4, ref[y, rows : rows + 8], 0.0))
            rest = jnp.concatenate(rest, axis=0)
            whole.append(jnp.concatenate([ref[y, :MAIN], rest], axis=1))
        left_hi, left_lo = split(jnp.concatenate(whole, axis=0))
        right_hi, right_lo = hi_ref[block], lo_ref[block]
        right_hi = jnp.concatenate([right_hi] + [right_hi[128:]] * 3, axis=0)
        right_lo = jnp.concatenate([right_lo] + [right_lo[128:]] * 3, axis=0)
        total += dot(left_hi, right_hi) + (dot(left_hi, right_lo) + dot(left_lo, right_hi))
    out_ref[...] = total.reshape(4, 80, 640)


def inflate_kernel(at_ref, pattern_ref, shares_ref, out_ref, sums_ref):
    for h in range(5):
        lanes = slice(128 * h, 128 * h + 128)
        x = (shares_ref[0, :, lanes] + shares_ref[1, :, lanes]) + (
            shares_ref[2, :, lanes] + shares_ref[3, :, lanes]
        )
        out_ref[:, lanes] = masked_block(at_ref, pattern_ref, h, x * x)
    sums_ref[...] = lax.dot_general(
        jnp.ones((8, 640), jnp.float32),
        out_ref[...],
        (((1,), (1,)), ((), ())),
        precision=lax.Precision.HIGHEST,
        preferred_element_type=jnp.float32,
    )


def scale_kernel(nodes, inflated_ref, sums_ref, out_ref):
    totals = lax.dot_general(
        sums_ref[...],
        jnp.ones((8, 128), jnp.float32),
        (((0,), (0,)), ((), ())),
        precision=lax.Precision.HIGHEST,
        preferred_element_type=jnp.float32,
    )
    scale = nodes / totals
    for h in range(5):
        lanes = slice(128 * h, 128 * h + 128)
        out_ref[:, lanes] = inflated_ref[:, lanes] * scale


def shift(x, axis_name, by):
    size = lax.axis_size(axis_name)
    return lax.ppermute(x, axis_name, [(i, (i + by) % size) for i in range(size)])


def across_x(block):
    return jnp.stack([block] + [shift(block, "x", by) for by in (1, 2, 3)], 0)


def f32(*shape):
    return jax.ShapeDtypeStruct(shape, jnp.float32)


def body(state, in_pattern, out_pattern):
    rows, cols = state.shape
    nodes = cols * lax.axis_size("zl")
    at = jnp.stack(
        [lax.axis_index(ROWS)] + [lax.axis_index(a) for a in ("zl", "zh", "c", "x")]
    ).astype(jnp.int32)

    pieces = call(
        pieces_kernel,
        f32(4, PIECE, 128),
        [SMEM, SMEM, VMEM],
        (at, in_pattern, state),
        [pltpu.VMEM((rows, cols), jnp.float32)],
    )
    got = lax.all_to_all(pieces, "y", 0, 0)
    left, right = call(
        unpack_kernel, (f32(4, LEFT, 128), f32(2, 2 * RUN, cols)), [VMEM], (got,)
    )

    tie = lax.optimization_barrier
    up, down = shift(left, "zl", 1), shift(left, "zl", -1)
    far = shift(right, "zh", 1)
    near = across_x(right)
    lefts = [left, up, None, None, None, None, None, down]
    up, down, near, far = tie((up, down, near, far))
    up, down = shift(up, "zl", 1), shift(down, "zl", -1)
    far = across_x(far)
    near_swapped = shift(near, "c", 1)
    lefts[2], lefts[6] = up, down
    up, down, far, near_swapped = tie((up, down, far, near_swapped))
    up, down = shift(up, "zl", 1), shift(down, "zl", -1)
    far_swapped = shift(far, "c", 1)
    lefts[3], lefts[5] = up, down
    lefts[4] = shift(up, "zl", 1)

    partial = call(
        product_kernel,
        f32(4, rows, cols),
        [SMEM] + [VMEM] * 12,
        (at, *lefts, near, near_swapped, far, far_swapped),
        [pltpu.VMEM((8, 160, cols), jnp.bfloat16)] * 2,
        flops=3 * 10**9,
        size=6 * 10**6,
    )
    shares = lax.all_to_all(partial, "y", 0, 0)
    inflated, sums = call(
        inflate_kernel,
        (f32(rows, cols), f32(8, rows)),
        [SMEM, SMEM, VMEM],
        (at, out_pattern, shares),
    )
    sums = lax.all_to_all(sums.reshape(8, 1, rows), "zl", 0, 0).reshape(8, rows)
    return call(
        functools.partial(scale_kernel, float(nodes)),
        f32(rows, cols),
        [VMEM, VMEM],
        (inflated, sums),
    )


def solution(mesh):
    fine = Mesh(
        mesh.devices.reshape(8, 4, 4, 2, 2), ("zl", "x", "y", "zh", "c")
    )
    return jax.shard_map(
        body,
        mesh=fine,
        in_specs=(P(ROWS, "zl"), P(), P()),
        out_specs=P(ROWS, "zl"),
        check_vma=False,
    )
```

time: 346 us -> 168 us (0.49)
  waiting for transfers between devices: 290 us -> 39.9 us
  starting transfers between devices: 0.04 us -> 77.3 us
  matrix products: 16.3 us -> 0 us
  blocking collectives: 25.1 us -> 40.1 us
  between operations: 13.4 us -> 0.22 us
  Pallas kernels: 0 us -> 7.8 us
    all_gather x2 -> x0, waiting for transfers between devices: 289 us -> none  [the longest x1 216 us: body(): column_block = lax.all_gather(masked, 'wide', axis=0, tiled=True)]
    ppermute x0 -> x16, starting transfers between devices: none -> 77.3 us  [shift(): lax.ppermute(x, axis_name, [(i, (i + by) % size) for i in range(size)])]
    all_to_all x0 -> x3, blocking collectives: none -> 40.1 us  [the longest x1 14.3 us: body(): shares = lax.all_to_all(partial, 'y', 0, 0)]
    ppermute x0 -> x16, waiting for transfers between devices: none -> 39.9 us  [shift(): lax.ppermute(x, axis_name, [(i, (i + by) % size) for i in range(size)])]
    psum x1 -> x0, blocking collectives: 25.1 us -> none  [body(): totals = lax.psum(jnp.sum(inflated, axis=1), 'narrow')]
    dot_general x3 -> x0, matrix products: 16.3 us -> none  [the longest x1 13.3 us: body(): jnp.dot(lax.all_gather(masked, 'narrow', axis=1, tiled=True), column_bloc...]
    pallas_call x0 -> x5, Pallas kernels: none -> 7.8 us  [call(): pl.pallas_call(kernel, out_shape=outs, in_specs=in_specs, out_specs=jax.t...]
  transfers between devices with their start and end apart: 2 -> 16, of which waited for: 2 -> 7; matrix products, arithmetic and copies ran while one was open for 0% -> 0% of each run, Pallas kernels for 0% -> 0%
where the time goes in v5:
time: 168 us; the launch traced here: 167 us
  starting transfers between devices  77.3 us (46%)
  blocking collectives  40.1 us (24%)
  waiting for transfers between devices  39.9 us (24%)
  Pallas kernels  7.8 us (5%)
    ppermute x16, starting transfers between devices, shift(): lax.ppermute(x, axis_name, [(i, (i + by) % size) for i in range(size)])  77.3 us
    ppermute x16, waiting for transfers between devices, shift(): lax.ppermute(x, axis_name, [(i, (i + by) % size) for i in range(size)])  39.9 us
    all_to_all x1, blocking collectives, body(): shares = lax.all_to_all(partial, 'y', 0, 0)  14.3 us
    all_to_all x1, blocking collectives, body(): got = lax.all_to_all(pieces, 'y', 0, 0)  13 us
    all_to_all x1, blocking collectives, body(): sums = lax.all_to_all(sums.reshape(8, 1, rows), 'zl', 0, 0).reshape(8, rows)  12.8 us
    pallas_call x5, Pallas kernels, call(): pl.pallas_call(kernel, out_shape=outs, in_specs=in_specs, out_specs=jax.t...  7.8 us
  transfers between devices with their start and end apart: 16, of which 7 were waited for; matrix products, arithmetic and copies ran while one was open for 0% of the time, Pallas kernels for 0%

profile of v5, /device:TPU:6, one launch (start us, length us, event | category | flops | bytes accessed | tf_op | source)
XLA Modules:
  0.0 167.1 jit_solution(8805764972448058752)
XLA Ops:
  3.2 13.0 %all_to_all.15.got_ref = f32[4,224,128]{2,1,0:T(8,128)S(1)} all-to-all(f32[4,224,128]{2,1,0:T(8,128)S(1)} %shard_map.37), channel_id=1, replica_groups=mesh['zl'=8,'x'=4,'y'=4,'zh'=2,'c'=2] {'y'}, dimensions={0} | all-to-all | bytes 917504 | tf_op jit(solution)/shard_map/all_to_all | solution.py:190
  16.2 2.7 %collective-permute-start.4 = (f32[2,40,640]{2,1,0:T(8,128)S(1)}, f32[2,40,640]{2,1,0:T(8,128)S(1)}, u32[]{:S(2)}, u32[]{:S(2)}) collective-permute-start(f32[2,40,640]{2,1,0:T(8,128)S(1)} %get-tuple-element.18), channel_id=1, source_target_pairs={{0,48},{16,0},{32,16},{48,32},{1,49},{17,1},{33,17},{49,33},{2,50}... | collective-permute-start | bytes 614408 | tf_op jit(solution)/shard_map/ppermute | solution.py:165
  19.0 5.5 %collective-permute-start.3 = (f32[2,40,640]{2,1,0:T(8,128)S(1)}, f32[2,40,640]{2,1,0:T(8,128)S(1)}, u32[]{:S(2)}, u32[]{:S(2)}) collective-permute-start(f32[2,40,640]{2,1,0:T(8,128)S(1)} %get-tuple-element.18), channel_id=1, source_target_pairs={{0,32},{16,48},{32,0},{48,16},{1,33},{17,49},{33,1},{49,17},{2,34}... | collective-permute-start | bytes 614408 | tf_op jit(solution)/shard_map/ppermute | solution.py:165
  24.5 1.9 %collective-permute-start.2 = (f32[2,40,640]{2,1,0:T(8,128)S(1)}, f32[2,40,640]{2,1,0:T(8,128)S(1)}, u32[]{:S(2)}, u32[]{:S(2)}) collective-permute-start(f32[2,40,640]{2,1,0:T(8,128)S(1)} %get-tuple-element.18), channel_id=1, source_target_pairs={{0,16},{16,32},{32,48},{48,0},{1,17},{17,33},{33,49},{49,1},{2,18}... | collective-permute-start | bytes 614408 | tf_op jit(solution)/shard_map/ppermute | solution.py:165
  26.4 12.8 %collective-permute-start.1 = (f32[4,104,128]{2,1,0:T(8,128)S(1)}, f32[4,104,128]{2,1,0:T(8,128)S(1)}, u32[]{:S(2)}, u32[]{:S(2)}) collective-permute-start(f32[4,104,128]{2,1,0:T(8,128)S(1)} %get-tuple-element.17.refs_0_), channel_id=1, source_target_pairs={{0,448},{64,0},{128,64},{192,128},{256,192},{320,256},{384,320},{4... | collective-permute-start | bytes 638984 | tf_op jit(solution)/shard_map/ppermute | solution.py:165
  39.2 1.9 %collective-permute-start = (f32[4,104,128]{2,1,0:T(8,128)S(1)}, f32[4,104,128]{2,1,0:T(8,128)S(1)}, u32[]{:S(2)}, u32[]{:S(2)}) collective-permute-start(f32[4,104,128]{2,1,0:T(8,128)S(1)} %get-tuple-element.17.refs_0_), channel_id=1, source_target_pairs={{0,64},{64,128},{128,192},{192,256},{256,320},{320,384},{384,448},... | collective-permute-start | bytes 638984 | tf_op jit(solution)/shard_map/ppermute | solution.py:165
  41.1 8.2 %collective-permute-start.5 = (f32[2,40,640]{2,1,0:T(8,128)S(1)}, f32[2,40,640]{2,1,0:T(8,128)S(1)}, u32[]{:S(2)}, u32[]{:S(2)}) collective-permute-start(f32[2,40,640]{2,1,0:T(8,128)S(1)} %get-tuple-element.18), channel_id=1, source_target_pairs={{0,2},{2,0},{1,3},{3,1},{4,6},{6,4},{5,7},{7,5},{8,10},{10,8},{9,1... | collective-permute-start | bytes 614408 | tf_op jit(solution)/shard_map/ppermute | solution.py:165
  49.4 15.1 %collective-permute-done.5 = f32[2,40,640]{2,1,0:T(8,128)S(1)} collective-permute-done((f32[2,40,640]{2,1,0:T(8,128)S(1)}, f32[2,40,640]{2,1,0:T(8,128)S(1)}, u32[]{:S(2)}, u32[]{:S(2)}) %collective-permute-start.5) | collective-permute-done | bytes 204832 | tf_op jit(solution)/shard_map/ppermute | solution.py:165
  64.8 1.9 %collective-permute-start.11 = (f32[4,2,40,640]{3,2,1,0:T(8,128)S(1)}, f32[4,2,40,640]{3,2,1,0:T(8,128)S(1)}, u32[]{:S(2)}, u32[]{:S(2)}) collective-permute-start(f32[4,2,40,640]{3,2,1,0:T(8,128)S(1)} %pad_maximum_fusion.refs_8_), channel_id=1, source_target_pairs={{0,1},{1,0},{2,3},{3,2},{4,5},{5,4},{6,7},{7,6},{8,9},{9,8},{10,11... | collective-permute-start | bytes 2457608 | tf_op jit(solution)/shard_map/ppermute | solution.py:165
  66.8 3.5 %collective-permute-start.10 = (f32[2,40,640]{2,1,0:T(8,128)S(1)}, f32[2,40,640]{2,1,0:T(8,128)S(1)}, u32[]{:S(2)}, u32[]{:S(2)}) collective-permute-start(f32[2,40,640]{2,1,0:T(8,128)S(1)} %collective-permute-done.5), channel_id=1, source_target_pairs={{0,48},{16,0},{32,16},{48,32},{1,49},{17,1},{33,17},{49,33},{2,50}... | collective-permute-start | bytes 614408 | tf_op jit(solution)/shard_map/ppermute | solution.py:165
  70.3 2.7 %collective-permute-start.9 = (f32[2,40,640]{2,1,0:T(8,128)S(1)}, f32[2,40,640]{2,1,0:T(8,128)S(1)}, u32[]{:S(2)}, u32[]{:S(2)}) collective-permute-start(f32[2,40,640]{2,1,0:T(8,128)S(1)} %collective-permute-done.5), channel_id=1, source_target_pairs={{0,32},{16,48},{32,0},{48,16},{1,33},{17,49},{33,1},{49,17},{2,34}... | collective-permute-start | bytes 614408 | tf_op jit(solution)/shard_map/ppermute | solution.py:165
  72.9 4.3 %collective-permute-start.8 = (f32[2,40,640]{2,1,0:T(8,128)S(1)}, f32[2,40,640]{2,1,0:T(8,128)S(1)}, u32[]{:S(2)}, u32[]{:S(2)}) collective-permute-start(f32[2,40,640]{2,1,0:T(8,128)S(1)} %collective-permute-done.5), channel_id=1, source_target_pairs={{0,16},{16,32},{32,48},{48,0},{1,17},{17,33},{33,49},{49,1},{2,18}... | collective-permute-start | bytes 614408 | tf_op jit(solution)/shard_map/ppermute | solution.py:165
  77.2 1.9 %collective-permute-start.6 = (f32[4,104,128]{2,1,0:T(8,128)S(1)}, f32[4,104,128]{2,1,0:T(8,128)S(1)}, u32[]{:S(2)}, u32[]{:S(2)}) collective-permute-start(f32[4,104,128]{2,1,0:T(8,128)S(1)} %collective-permute-done.refs_1_), channel_id=1, source_target_pairs={{0,64},{64,128},{128,192},{192,256},{256,320},{320,384},{384,448},... | collective-permute-start | bytes 638984 | tf_op jit(solution)/shard_map/ppermute | solution.py:165
  79.2 2.5 %collective-permute-done.10 = f32[2,40,640]{2,1,0:T(8,128)S(1)} collective-permute-done((f32[2,40,640]{2,1,0:T(8,128)S(1)}, f32[2,40,640]{2,1,0:T(8,128)S(1)}, u32[]{:S(2)}, u32[]{:S(2)}) %collective-permute-start.10) | collective-permute-done | bytes 204832 | tf_op jit(solution)/shard_map/ppermute | solution.py:165
  81.7 13.2 %collective-permute-start.7 = (f32[4,104,128]{2,1,0:T(8,128)S(1)}, f32[4,104,128]{2,1,0:T(8,128)S(1)}, u32[]{:S(2)}, u32[]{:S(2)}) collective-permute-start(f32[4,104,128]{2,1,0:T(8,128)S(1)} %collective-permute-done.1.refs_7_), channel_id=1, source_target_pairs={{0,448},{64,0},{128,64},{192,128},{256,192},{320,256},{384,320},{4... | collective-permute-start | bytes 638984 | tf_op jit(solution)/shard_map/ppermute | solution.py:165
  95.9 3.4 %collective-permute-done.7.refs_6_ = f32[4,104,128]{2,1,0:T(8,128)S(1)} collective-permute-done((f32[4,104,128]{2,1,0:T(8,128)S(1)}, f32[4,104,128]{2,1,0:T(8,128)S(1)}, u32[]{:S(2)}, u32[]{:S(2)}) %collective-permute-start.7) | collective-permute-done | bytes 213024 | tf_op jit(solution)/shard_map/ppermute | solution.py:165
  99.3 1.9 %collective-permute-start.15 = (f32[4,2,40,640]{3,2,1,0:T(8,128)S(1)}, f32[4,2,40,640]{3,2,1,0:T(8,128)S(1)}, u32[]{:S(2)}, u32[]{:S(2)}) collective-permute-start(f32[4,2,40,640]{3,2,1,0:T(8,128)S(1)} %pad_maximum_fusion.1.refs_10_), channel_id=1, source_target_pairs={{0,1},{1,0},{2,3},{3,2},{4,5},{5,4},{6,7},{7,6},{8,9},{9,8},{10,11... | collective-permute-start | bytes 2457608 | tf_op jit(solution)/shard_map/ppermute | solution.py:165
  101.2 1.9 %collective-permute-start.12 = (f32[4,104,128]{2,1,0:T(8,128)S(1)}, f32[4,104,128]{2,1,0:T(8,128)S(1)}, u32[]{:S(2)}, u32[]{:S(2)}) collective-permute-start(f32[4,104,128]{2,1,0:T(8,128)S(1)} %collective-permute-done.6.refs_2_), channel_id=1, source_target_pairs={{0,64},{64,128},{128,192},{192,256},{256,320},{320,384},{384,448},... | collective-permute-start | bytes 638984 | tf_op jit(solution)/shard_map/ppermute | solution.py:165
  103.1 11.0 %collective-permute-start.14 = (f32[4,104,128]{2,1,0:T(8,128)S(1)}, f32[4,104,128]{2,1,0:T(8,128)S(1)}, u32[]{:S(2)}, u32[]{:S(2)}) collective-permute-start(f32[4,104,128]{2,1,0:T(8,128)S(1)} %collective-permute-done.7.refs_6_), channel_id=1, source_target_pairs={{0,448},{64,0},{128,64},{192,128},{256,192},{320,256},{384,320},{4... | collective-permute-start | bytes 638984 | tf_op jit(solution)/shard_map/ppermute | solution.py:165
  114.1 4.3 %collective-permute-done.12.refs_3_ = f32[4,104,128]{2,1,0:T(8,128)S(1)} collective-permute-done((f32[4,104,128]{2,1,0:T(8,128)S(1)}, f32[4,104,128]{2,1,0:T(8,128)S(1)}, u32[]{:S(2)}, u32[]{:S(2)}) %collective-permute-start.12) | collective-permute-done | bytes 213024 | tf_op jit(solution)/shard_map/ppermute | solution.py:165
  120.3 13.4 %collective-permute-done.13.refs_4_ = f32[4,104,128]{2,1,0:T(8,128)S(1)} collective-permute-done((f32[4,104,128]{2,1,0:T(8,128)S(1)}, f32[4,104,128]{2,1,0:T(8,128)S(1)}, u32[]{:S(2)}, u32[]{:S(2)}) %collective-permute-start.13) | collective-permute-done | bytes 213024 | tf_op jit(solution)/shard_map/ppermute | solution.py:165
  133.8 4.3 %shard_map.39 = f32[4,80,640]{2,1,0:T(8,128)S(1)} custom-call(s32[5]{0:T(128)S(1)} %stack.53.at_ref, f32[4,104,128]{2,1,0:T(8,128)S(1)} %get-tuple-element.17.refs_0_, f32[4,104,128]{2,1,0:T(8,128)S(1)} %collective-permute-done.refs_1_, f32[4,104,128]{2,1,0:T(8,128)S(1)} %collective-permute-done.6.refs_2_, ...), custom_call_target="tpu_custom_call" | custom-call | flops 3000000000 | bytes 6000000 | tf_op jit(solution)/shard_map/pallas_call | solution.py:30
  138.0 14.3 %all_to_all.16.shares_ref = f32[4,80,640]{2,1,0:T(8,128)S(1)} all-to-all(f32[4,80,640]{2,1,0:T(8,128)S(1)} %shard_map.39), channel_id=1, replica_groups=mesh['zl'=8,'x'=4,'y'=4,'zh'=2,'c'=2] {'y'}, dimensions={0} | all-to-all | bytes 1638400 | tf_op jit(solution)/shard_map/all_to_all | solution.py:220
  153.4 12.8 %all_to_all.17 = f32[8,1,80]{2,1,0:T(1,128)S(1)} all-to-all(f32[8,1,80]{2,1,0:T(1,128)S(1)} %bitcast.19), channel_id=1, replica_groups=mesh['zl'=8,'x'=4,'y'=4,'zh'=2,'c'=2] {'zl'}, dimensions={0} | all-to-all | bytes 5120 | tf_op jit(solution)/shard_map/all_to_all | solution.py:227
  (25 shorter events, 8.4 us)
Async XLA Ops:
  0.0 0.7 copy-start.1
  0.7 0.9 copy-start
  16.2 24.9 %collective-permute-start.4 = (f32[2,40,640]{2,1,0:T(8,128)S(1)}, f32[2,40,640]{2,1,0:T(8,128)S(1)}, u32[]{:S(2)}, u32[]{:S(2)}) collective-permute-start(f32[2,40,640]{2,1,0:T(8,128)S(1)} %get-tuple-element.18), channel_id=1, source_target_pairs={{0,48},{16,0},{32,16},{48,32},{1,49},{17,1},{33,17},{49,33},{2,50}... | collective-permute-start | bytes 614408 | tf_op jit(solution)/shard_map/ppermute | solution.py:165
  19.0 30.4 %collective-permute-start.3 = (f32[2,40,640]{2,1,0:T(8,128)S(1)}, f32[2,40,640]{2,1,0:T(8,128)S(1)}, u32[]{:S(2)}, u32[]{:S(2)}) collective-permute-start(f32[2,40,640]{2,1,0:T(8,128)S(1)} %get-tuple-element.18), channel_id=1, source_target_pairs={{0,32},{16,48},{32,0},{48,16},{1,33},{17,49},{33,1},{49,17},{2,34}... | collective-permute-start | bytes 614408 | tf_op jit(solution)/shard_map/ppermute | solution.py:165
  24.5 24.9 %collective-permute-start.2 = (f32[2,40,640]{2,1,0:T(8,128)S(1)}, f32[2,40,640]{2,1,0:T(8,128)S(1)}, u32[]{:S(2)}, u32[]{:S(2)}) collective-permute-start(f32[2,40,640]{2,1,0:T(8,128)S(1)} %get-tuple-element.18), channel_id=1, source_target_pairs={{0,16},{16,32},{32,48},{48,0},{1,17},{17,33},{33,49},{49,1},{2,18}... | collective-permute-start | bytes 614408 | tf_op jit(solution)/shard_map/ppermute | solution.py:165
  26.4 38.2 %collective-permute-start.1 = (f32[4,104,128]{2,1,0:T(8,128)S(1)}, f32[4,104,128]{2,1,0:T(8,128)S(1)}, u32[]{:S(2)}, u32[]{:S(2)}) collective-permute-start(f32[4,104,128]{2,1,0:T(8,128)S(1)} %get-tuple-element.17.refs_0_), channel_id=1, source_target_pairs={{0,448},{64,0},{128,64},{192,128},{256,192},{320,256},{384,320},{4... | collective-permute-start | bytes 638984 | tf_op jit(solution)/shard_map/ppermute | solution.py:165
  39.2 25.6 %collective-permute-start = (f32[4,104,128]{2,1,0:T(8,128)S(1)}, f32[4,104,128]{2,1,0:T(8,128)S(1)}, u32[]{:S(2)}, u32[]{:S(2)}) collective-permute-start(f32[4,104,128]{2,1,0:T(8,128)S(1)} %get-tuple-element.17.refs_0_), channel_id=1, source_target_pairs={{0,64},{64,128},{128,192},{192,256},{256,320},{320,384},{384,448},... | collective-permute-start | bytes 638984 | tf_op jit(solution)/shard_map/ppermute | solution.py:165
  41.1 23.4 %collective-permute-start.5 = (f32[2,40,640]{2,1,0:T(8,128)S(1)}, f32[2,40,640]{2,1,0:T(8,128)S(1)}, u32[]{:S(2)}, u32[]{:S(2)}) collective-permute-start(f32[2,40,640]{2,1,0:T(8,128)S(1)} %get-tuple-element.18), channel_id=1, source_target_pairs={{0,2},{2,0},{1,3},{3,1},{4,6},{6,4},{5,7},{7,5},{8,10},{10,8},{9,1... | collective-permute-start | bytes 614408 | tf_op jit(solution)/shard_map/ppermute | solution.py:165
  64.8 34.5 %collective-permute-start.11 = (f32[4,2,40,640]{3,2,1,0:T(8,128)S(1)}, f32[4,2,40,640]{3,2,1,0:T(8,128)S(1)}, u32[]{:S(2)}, u32[]{:S(2)}) collective-permute-start(f32[4,2,40,640]{3,2,1,0:T(8,128)S(1)} %pad_maximum_fusion.refs_8_), channel_id=1, source_target_pairs={{0,1},{1,0},{2,3},{3,2},{4,5},{5,4},{6,7},{7,6},{8,9},{9,8},{10,11... | collective-permute-start | bytes 2457608 | tf_op jit(solution)/shard_map/ppermute | solution.py:165
  66.8 15.0 %collective-permute-start.10 = (f32[2,40,640]{2,1,0:T(8,128)S(1)}, f32[2,40,640]{2,1,0:T(8,128)S(1)}, u32[]{:S(2)}, u32[]{:S(2)}) collective-permute-start(f32[2,40,640]{2,1,0:T(8,128)S(1)} %collective-permute-done.5), channel_id=1, source_target_pairs={{0,48},{16,0},{32,16},{48,32},{1,49},{17,1},{33,17},{49,33},{2,50}... | collective-permute-start | bytes 614408 | tf_op jit(solution)/shard_map/ppermute | solution.py:165
  70.3 24.7 %collective-permute-start.9 = (f32[2,40,640]{2,1,0:T(8,128)S(1)}, f32[2,40,640]{2,1,0:T(8,128)S(1)}, u32[]{:S(2)}, u32[]{:S(2)}) collective-permute-start(f32[2,40,640]{2,1,0:T(8,128)S(1)} %collective-permute-done.5), channel_id=1, source_target_pairs={{0,32},{16,48},{32,0},{48,16},{1,33},{17,49},{33,1},{49,17},{2,34}... | collective-permute-start | bytes 614408 | tf_op jit(solution)/shard_map/ppermute | solution.py:165
  72.9 22.0 %collective-permute-start.8 = (f32[2,40,640]{2,1,0:T(8,128)S(1)}, f32[2,40,640]{2,1,0:T(8,128)S(1)}, u32[]{:S(2)}, u32[]{:S(2)}) collective-permute-start(f32[2,40,640]{2,1,0:T(8,128)S(1)} %collective-permute-done.5), channel_id=1, source_target_pairs={{0,16},{16,32},{32,48},{48,0},{1,17},{17,33},{33,49},{49,1},{2,18}... | collective-permute-start | bytes 614408 | tf_op jit(solution)/shard_map/ppermute | solution.py:165
  77.2 18.6 %collective-permute-start.6 = (f32[4,104,128]{2,1,0:T(8,128)S(1)}, f32[4,104,128]{2,1,0:T(8,128)S(1)}, u32[]{:S(2)}, u32[]{:S(2)}) collective-permute-start(f32[4,104,128]{2,1,0:T(8,128)S(1)} %collective-permute-done.refs_1_), channel_id=1, source_target_pairs={{0,64},{64,128},{128,192},{192,256},{256,320},{320,384},{384,448},... | collective-permute-start | bytes 638984 | tf_op jit(solution)/shard_map/ppermute | solution.py:165
  81.7 17.6 %collective-permute-start.7 = (f32[4,104,128]{2,1,0:T(8,128)S(1)}, f32[4,104,128]{2,1,0:T(8,128)S(1)}, u32[]{:S(2)}, u32[]{:S(2)}) collective-permute-start(f32[4,104,128]{2,1,0:T(8,128)S(1)} %collective-permute-done.1.refs_7_), channel_id=1, source_target_pairs={{0,448},{64,0},{128,64},{192,128},{256,192},{320,256},{384,320},{4... | collective-permute-start | bytes 638984 | tf_op jit(solution)/shard_map/ppermute | solution.py:165
  99.3 34.5 %collective-permute-start.15 = (f32[4,2,40,640]{3,2,1,0:T(8,128)S(1)}, f32[4,2,40,640]{3,2,1,0:T(8,128)S(1)}, u32[]{:S(2)}, u32[]{:S(2)}) collective-permute-start(f32[4,2,40,640]{3,2,1,0:T(8,128)S(1)} %pad_maximum_fusion.1.refs_10_), channel_id=1, source_target_pairs={{0,1},{1,0},{2,3},{3,2},{4,5},{5,4},{6,7},{7,6},{8,9},{9,8},{10,11... | collective-permute-start | bytes 2457608 | tf_op jit(solution)/shard_map/ppermute | solution.py:165
  101.2 17.2 %collective-permute-start.12 = (f32[4,104,128]{2,1,0:T(8,128)S(1)}, f32[4,104,128]{2,1,0:T(8,128)S(1)}, u32[]{:S(2)}, u32[]{:S(2)}) collective-permute-start(f32[4,104,128]{2,1,0:T(8,128)S(1)} %collective-permute-done.6.refs_2_), channel_id=1, source_target_pairs={{0,64},{64,128},{128,192},{192,256},{256,320},{320,384},{384,448},... | collective-permute-start | bytes 638984 | tf_op jit(solution)/shard_map/ppermute | solution.py:165
  103.1 17.2 %collective-permute-start.14 = (f32[4,104,128]{2,1,0:T(8,128)S(1)}, f32[4,104,128]{2,1,0:T(8,128)S(1)}, u32[]{:S(2)}, u32[]{:S(2)}) collective-permute-start(f32[4,104,128]{2,1,0:T(8,128)S(1)} %collective-permute-done.7.refs_6_), channel_id=1, source_target_pairs={{0,448},{64,0},{128,64},{192,128},{256,192},{320,256},{384,320},{4... | collective-permute-start | bytes 638984 | tf_op jit(solution)/shard_map/ppermute | solution.py:165
  118.4 15.4 %collective-permute-start.13 = (f32[4,104,128]{2,1,0:T(8,128)S(1)}, f32[4,104,128]{2,1,0:T(8,128)S(1)}, u32[]{:S(2)}, u32[]{:S(2)}) collective-permute-start(f32[4,104,128]{2,1,0:T(8,128)S(1)} %collective-permute-done.12.refs_3_), channel_id=1, source_target_pairs={{0,64},{64,128},{128,192},{192,256},{256,320},{320,384},{384,448},... | collective-permute-start | bytes 638984 | tf_op jit(solution)/shard_map/ppermute | solution.py:165
  138.0 14.3 %copy-start.2 = (s32[20,20]{1,0:T(8,128)S(1)}, s32[20,20]{1,0:T(8,128)}, u32[]{:S(2)}) copy-start(s32[20,20]{1,0:T(8,128)} %pattern_ref.3) | copy-start | bytes 4804

commit v6 on v5

--- a/solution.py
+++ b/solution.py
@@ -40,8 +40,8 @@
     )(*args)
 
 
-def masked_block(at_ref, pattern_ref, h, x):
-    row = at_ref[0] * 80
+def masked_block(at_ref, owner, pattern_ref, h, x):
+    row = owner * 80
     col = (5 * at_ref[1] + h) // 2
     first = row // BLK
     low = pattern_ref[first, col].astype(jnp.float32)
@@ -50,17 +50,25 @@
     return x * jnp.where(here, low, high)
 
 
-def pieces_kernel(at_ref, pattern_ref, state_ref, out_ref, masked_ref):
-    zh, c = at_ref[2], at_ref[3]
+def pack_right(at_ref, owner, pattern_ref, state_ref, masked_ref, out_ref, base):
     for h in range(5):
         lanes = slice(128 * h, 128 * h + 128)
-        masked_ref[:, lanes] = masked_block(at_ref, pattern_ref, h, state_ref[:, lanes])
+        masked_ref[:, lanes] = masked_block(at_ref, owner, pattern_ref, h, state_ref[:, lanes])
     out_ref[...] = jnp.zeros_like(out_ref)
     for y in range(4):
         for h in range(5):
-            out_ref[y, LEFT + PAD * h : LEFT + PAD * h + RUN] = masked_ref[
-                RUN * y : RUN * y + RUN, 128 * h : 128 * h + 128
-            ]
+            rows = slice(base + PAD * h, base + PAD * h + RUN)
+            out_ref[y, rows] = masked_ref[RUN * y : RUN * y + RUN, 128 * h : 128 * h + 128]
+
+
+def far_kernel(at_ref, pattern_ref, state_ref, out_ref, masked_ref):
+    owner = at_ref[0] + 2 - 4 * at_ref[2]
+    pack_right(at_ref, owner, pattern_ref, state_ref, masked_ref, out_ref, 0)
+
+
+def pieces_kernel(at_ref, pattern_ref, state_ref, out_ref, masked_ref):
+    zh, c = at_ref[2], at_ref[3]
+    pack_right(at_ref, at_ref[0], pattern_ref, state_ref, masked_ref, out_ref, LEFT)
     n = lax.broadcasted_iota(jnp.int32, (1, 640), 1)
     late = n >= 512
     y = jnp.where(late, (n - 512) // 32, n // 128)
@@ -90,38 +98,45 @@
             out_ref[y, MAIN + 8 * slot : MAIN + 8 * slot + 8] = tile
 
 
-def unpack_kernel(got_ref, left_ref, right_ref):
-    left_ref[...] = got_ref[:, :LEFT]
+def unpack_right(got_ref, right_ref, base):
     for y in range(4):
         for h in range(5):
             right_ref[y // 2, RUN * (y % 2) : RUN * (y % 2) + RUN, 128 * h : 128 * h + 128] = (
-                got_ref[y, LEFT + PAD * h : LEFT + PAD * h + RUN]
+                got_ref[y, base + PAD * h : base + PAD * h + RUN]
             )
 
 
-def product_kernel(at_ref, *refs):
-    lefts, rights, out_ref, hi_ref, lo_ref = refs[:8], refs[8:12], *refs[12:]
-    for part, ref in enumerate(rights):
-        for dx in range(4):
-            for y1 in range(2):
-                hi, lo = split(ref[dx, y1])
-                rows = slice(40 * part, 40 * part + 40)
-                hi_ref[2 * dx + y1, rows] = hi
-                lo_ref[2 * dx + y1, rows] = lo
+def unpack_kernel(got_ref, left_ref, right_ref):
+    left_ref[...] = got_ref[:, :LEFT]
+    unpack_right(got_ref, right_ref, LEFT)
+
+
+def unpack_far_kernel(got_ref, right_ref):
+    unpack_right(got_ref, right_ref, 0)
+
+
+def product_kernel(at_ref, left_ref, right_ref, out_ref, hi_ref, lo_ref):
+    for dc in range(2):
+        c = lax.rem(at_ref[3] + dc, 2)
+        for dzh in range(2):
+            rows = slice(40 * (2 * dzh + dc), 40 * (2 * dzh + dc) + 40)
+            for x in range(4):
+                for y1 in range(2):
+                    hi, lo = split(right_ref[c, x, dzh, y1])
+                    hi_ref[2 * x + y1, rows] = hi
+                    lo_ref[2 * x + y1, rows] = lo
     lane = lax.broadcasted_iota(jnp.int32, (8, 128), 1) // 32
-    zl, x = at_ref[1], at_ref[4]
     total = jnp.zeros((320, 640), jnp.float32)
-    for d, ref in enumerate(lefts):
-        source = lax.rem(zl - d + 8, 8)
-        block = 2 * lax.rem(x - source // 2 + 4, 4) + lax.rem(source, 2)
+    for block in range(8):
         whole = []
         for y in range(4):
             rest = []
             for tile in range(10):
                 rows = MAIN + 8 * (tile // 4)
-                rest.append(jnp.where(lane == tile % 4, ref[y, rows : rows + 8], 0.0))
+                part = left_ref[block, y, rows : rows + 8]
+                rest.append(jnp.where(lane == tile % 4, part, 0.0))
             rest = jnp.concatenate(rest, axis=0)
-            whole.append(jnp.concatenate([ref[y, :MAIN], rest], axis=1))
+            whole.append(jnp.concatenate([left_ref[block, y, :MAIN], rest], axis=1))
         left_hi, left_lo = split(jnp.concatenate(whole, axis=0))
         right_hi, right_lo = hi_ref[block], lo_ref[block]
         right_hi = jnp.concatenate([right_hi] + [right_hi[128:]] * 3, axis=0)
@@ -136,7 +151,7 @@
         x = (shares_ref[0, :, lanes] + shares_ref[1, :, lanes]) + (
             shares_ref[2, :, lanes] + shares_ref[3, :, lanes]
         )
-        out_ref[:, lanes] = masked_block(at_ref, pattern_ref, h, x * x)
+        out_ref[:, lanes] = masked_block(at_ref, at_ref[0], pattern_ref, h, x * x)
     sums_ref[...] = lax.dot_general(
         jnp.ones((8, 640), jnp.float32),
         out_ref[...],
@@ -160,13 +175,10 @@
         out_ref[:, lanes] = inflated_ref[:, lanes] * scale
 
 
-def shift(x, axis_name, by):
+def gather(block, axis_name):
     size = lax.axis_size(axis_name)
-    return lax.ppermute(x, axis_name, [(i, (i + by) % size) for i in range(size)])
-
-
-def across_x(block):
-    return jnp.stack([block] + [shift(block, "x", by) for by in (1, 2, 3)], 0)
+    copies = jnp.broadcast_to(block[None], (size,) + block.shape)
+    return lax.all_to_all(copies, axis_name, 0, 0)
 
 
 def f32(*shape):
@@ -177,42 +189,37 @@
     rows, cols = state.shape
     nodes = cols * lax.axis_size("zl")
     at = jnp.stack(
-        [lax.axis_index(ROWS)] + [lax.axis_index(a) for a in ("zl", "zh", "c", "x")]
+        [lax.axis_index(ROWS)] + [lax.axis_index(a) for a in ("zl", "zh", "c")]
     ).astype(jnp.int32)
 
+    other = lax.ppermute(state, "zh", [(0, 1), (1, 0)])
+    work = [pltpu.VMEM((rows, cols), jnp.float32)]
     pieces = call(
         pieces_kernel,
         f32(4, PIECE, 128),
         [SMEM, SMEM, VMEM],
         (at, in_pattern, state),
-        [pltpu.VMEM((rows, cols), jnp.float32)],
+        work,
     )
     got = lax.all_to_all(pieces, "y", 0, 0)
-    left, right = call(
+    got, other = lax.optimization_barrier((got, other))
+    left, near = call(
         unpack_kernel, (f32(4, LEFT, 128), f32(2, 2 * RUN, cols)), [VMEM], (got,)
     )
-
-    tie = lax.optimization_barrier
-    up, down = shift(left, "zl", 1), shift(left, "zl", -1)
-    far = shift(right, "zh", 1)
-    near = across_x(right)
-    lefts = [left, up, None, None, None, None, None, down]
-    up, down, near, far = tie((up, down, near, far))
-    up, down = shift(up, "zl", 1), shift(down, "zl", -1)
-    far = across_x(far)
-    near_swapped = shift(near, "c", 1)
-    lefts[2], lefts[6] = up, down
-    up, down, far, near_swapped = tie((up, down, far, near_swapped))
-    up, down = shift(up, "zl", 1), shift(down, "zl", -1)
-    far_swapped = shift(far, "c", 1)
-    lefts[3], lefts[5] = up, down
-    lefts[4] = shift(up, "zl", 1)
+    far = call(
+        far_kernel, f32(4, 5 * PAD, 128), [SMEM, SMEM, VMEM], (at, in_pattern, other), work
+    )
+    left, far = lax.optimization_barrier((left, far))
+    left = lax.all_gather(left, "zl", axis=0)
+    far = lax.all_to_all(far, "y", 0, 0)
+    far = call(unpack_far_kernel, f32(2, 2 * RUN, cols), [VMEM], (far,))
+    right = gather(gather(jnp.stack([near, far]), "x"), "c")
 
     partial = call(
         product_kernel,
         f32(4, rows, cols),
-        [SMEM] + [VMEM] * 12,
-        (at, *lefts, near, near_swapped, far, far_swapped),
+        [SMEM, VMEM, VMEM],
+        (at, left, right),
         [pltpu.VMEM((8, 160, cols), jnp.bfloat16)] * 2,
         flops=3 * 10**9,
         size=6 * 10**6,

time: 168 us -> 165 us (0.982)
  starting transfers between devices: 77.3 us -> 20.2 us
  blocking collectives: 40.1 us -> 65.9 us
  between operations: 0.22 us -> 13.4 us
  waiting for transfers between devices: 39.9 us -> 50.9 us
  local copies, waits for them, and re-layouts: 1.64 us -> 4.18 us
  Pallas kernels: 7.8 us -> 9.59 us
    ppermute x16 -> x1, starting transfers between devices: 77.3 us -> 15.7 us  [body(): other = lax.ppermute(state, 'zh', [(0, 1), (1, 0)])]
    all_gather x0 -> x1, waiting for transfers between devices: none -> 45.6 us  [body(): left = lax.all_gather(left, 'zl', axis=0)]
    ppermute x16 -> x1, waiting for transfers between devices: 39.9 us -> 5.29 us  [body(): other = lax.ppermute(state, 'zh', [(0, 1), (1, 0)])]
    all_to_all x1 -> x3, blocking collectives: 13 us -> 38.3 us  [the longest x2 27.4 us: gather(): return lax.all_to_all(copies, axis_name, 0, 0)]
    all_to_all x0 -> x1, starting transfers between devices: none -> 4.46 us  [body(): got = lax.all_to_all(pieces, 'y', 0, 0)]
    unnamed x6 -> x10, local copies, waits for them, and re-layouts: 1.56 us -> 3.8 us
    pallas_call x5 -> x7, Pallas kernels: 7.8 us -> 9.59 us  [call(): pl.pallas_call(kernel, out_shape=outs, in_specs=in_specs, out_specs=jax.t...]
  transfers between devices with their start and end apart: 16 -> 3, of which waited for: 7 -> 2; matrix products, arithmetic and copies ran while one was open for 0% -> 0% of each run, Pallas kernels for 0% -> 0%
where the time goes in v6:
time: 165 us; the launch traced here: 164 us
  blocking collectives  65.9 us (40%)
  waiting for transfers between devices  50.9 us (31%)
  starting transfers between devices  20.2 us (12%)
  between operations  13.4 us (8%)
  Pallas kernels  9.59 us (6%)
  local copies, waits for them, and re-layouts  4.18 us (3%)
    all_gather x1, waiting for transfers between devices, body(): left = lax.all_gather(left, 'zl', axis=0)  45.6 us
    all_to_all x2, blocking collectives, gather(): return lax.all_to_all(copies, axis_name, 0, 0)  27.4 us
    ppermute x1, starting transfers between devices, body(): other = lax.ppermute(state, 'zh', [(0, 1), (1, 0)])  15.7 us
    all_to_all x1, blocking collectives, body(): sums = lax.all_to_all(sums.reshape(8, 1, rows), 'zl', 0, 0).reshape(8, rows)  13.9 us
    all_to_all x1, blocking collectives, body(): shares = lax.all_to_all(partial, 'y', 0, 0)  13.7 us
    all_to_all x1, blocking collectives, body(): far = lax.all_to_all(far, 'y', 0, 0)  10.9 us
    pallas_call x7, Pallas kernels, call(): pl.pallas_call(kernel, out_shape=outs, in_specs=in_specs, out_specs=jax.t...  9.59 us
    ppermute x1, waiting for transfers between devices, body(): other = lax.ppermute(state, 'zh', [(0, 1), (1, 0)])  5.29 us
  transfers between devices with their start and end apart: 3, of which 2 were waited for; matrix products, arithmetic and copies ran while one was open for 0% of the time, Pallas kernels for 0%

profile of v6, /device:TPU:6, one launch (start us, length us, event | category | flops | bytes accessed | tf_op | source)
XLA Modules:
  0.0 164.3 jit_solution(13977181478522199882)
XLA Ops:
  6.5 0.1 pad_add_fusion.at_ref
  6.6 0.9 copy-done
  7.5 0.7 copy-done.1
  8.3 2.3 %shard_map.37 = f32[4,224,128]{2,1,0:T(8,128)} custom-call(s32[4]{0:T(128)S(1)} %pad_add_fusion.at_ref, s32[20,20]{1,0:T(8,128)S(1)} %copy-done.1, f32[80,640]{1,0:T(8,128)S(1)} %copy-done), custom_call_target="tpu_custom_call" | custom-call | flops 1000000 | bytes 1000000 | tf_op jit(solution)/shard_map/pallas_call | solution.py:30
  10.5 4.5 %all-to-all-start = ((f32[4,224,128]{2,1,0:T(8,128)}), f32[4,224,128]{2,1,0:T(8,128)S(1)}, u32[]{:S(2)}, u32[]{:S(2)}) async-start(f32[4,224,128]{2,1,0:T(8,128)} %shard_map.37), calls=%async_computation | async-start | bytes 917504 | tf_op jit(solution)/shard_map/all_to_all | solution.py:204
  15.0 15.7 %collective-permute-start = (f32[80,640]{1,0:T(8,128)}, f32[80,640]{1,0:T(8,128)S(1)}, u32[]{:S(2)}, u32[]{:S(2)}) collective-permute-start(f32[80,640]{1,0:T(8,128)} %state_ref.1), channel_id=1, source_target_pairs={{0,2},{2,0},{1,3},{3,1},{4,6},{6,4},{5,7},{7,5},{8,10},{10,8},{9,1... | collective-permute-start | bytes 614408 | tf_op jit(solution)/shard_map/ppermute | solution.py:195
  30.7 5.3 %collective-permute-done.state_ref = f32[80,640]{1,0:T(8,128)S(1)} collective-permute-done((f32[80,640]{1,0:T(8,128)}, f32[80,640]{1,0:T(8,128)S(1)}, u32[]{:S(2)}, u32[]{:S(2)}) %collective-permute-start) | collective-permute-done | bytes 204832 | tf_op jit(solution)/shard_map/ppermute | solution.py:195
  36.0 0.0 all-to-all-done.got_ref
  36.0 0.7 copy-done.2
  36.7 0.8 shard_map.39
  37.5 0.7 shard_map.38
  38.3 0.0 all-gather.3.cloned.1.call-update
  38.3 10.9 %all_to_all.30.got_ref = f32[4,120,128]{2,1,0:T(8,128)S(1)} all-to-all(f32[4,120,128]{2,1,0:T(8,128)S(1)} %shard_map.39), channel_id=1, replica_groups=mesh['zl'=8,'x'=4,'y'=4,'zh'=2,'c'=2] {'y'}, dimensions={0} | all-to-all | bytes 491520 | tf_op jit(solution)/shard_map/all_to_all | solution.py:214
  49.3 0.1 broadcast_in_dim.4
  49.4 21.0 %all_to_all.31 = f32[4,2,2,40,640]{4,3,2,1,0:T(8,128)S(1)} all-to-all(f32[4,2,2,40,640]{4,3,2,1,0:T(8,128)S(1)} %broadcast_in_dim.4), channel_id=1, replica_groups=mesh['zl'=8,'x'=4,'y'=4,'zh'=2,'c'=2] {'x'}, dimensions={0} | all-to-all | bytes 3276800 | tf_op jit(solution)/shard_map/all_to_all | solution.py:181
  70.4 0.3 broadcast_in_dim.5
  70.6 6.4 %all_to_all.32.right_ref = f32[2,4,2,2,40,640]{5,4,3,2,1,0:T(8,128)S(1)} all-to-all(f32[2,4,2,2,40,640]{5,4,3,2,1,0:T(8,128)S(1)} %broadcast_in_dim.5), channel_id=1, replica_groups=mesh['zl'=8,'x'=4,'y'=4,'zh'=2,'c'=2] {'c'}, dimensions={0} | all-to-all | bytes 6553600 | tf_op jit(solution)/shard_map/all_to_all | solution.py:181
  77.0 45.6 %all-gather.3.cloned.1.call-done = f32[32,104,128]{2,1,0:T(8,128)} async-done(((f32[4,104,128]{2,1,0:T(8,128)}), f32[32,104,128]{2,1,0:T(8,128)}) %all-gather.3.cloned.1.call-update) | async-done | bytes 1703952 | tf_op jit(solution)/shard_map/all_gather | solution.py:213
  122.6 1.5 copy-done.4
  124.1 3.8 %shard_map.41 = f32[4,80,640]{2,1,0:T(8,128)S(1)} custom-call(s32[4]{0:T(128)S(1)} %pad_add_fusion.at_ref, f32[8,4,104,128]{3,2,1,0:T(8,128)S(1)} %bitcast.15, f32[2,4,2,2,40,640]{5,4,3,2,1,0:T(8,128)S(1)} %all_to_all.32.right_ref), custom_call_target="tpu_custom_call" | custom-call | flops 3000000000 | bytes 6000000 | tf_op jit(solution)/shard_map/pallas_call | solution.py:30
  127.8 13.7 %all_to_all.33.shares_ref = f32[4,80,640]{2,1,0:T(8,128)S(1)} all-to-all(f32[4,80,640]{2,1,0:T(8,128)S(1)} %shard_map.41), channel_id=1, replica_groups=mesh['zl'=8,'x'=4,'y'=4,'zh'=2,'c'=2] {'y'}, dimensions={0} | all-to-all | bytes 1638400 | tf_op jit(solution)/shard_map/all_to_all | solution.py:227
  141.5 1.1 shard_map.42
  142.6 13.9 %all_to_all.34 = f32[8,1,80]{2,1,0:T(1,128)S(1)} all-to-all(f32[8,1,80]{2,1,0:T(1,128)S(1)} %bitcast.14), channel_id=1, replica_groups=mesh['zl'=8,'x'=4,'y'=4,'zh'=2,'c'=2] {'zl'}, dimensions={0} | all-to-all | bytes 5120 | tf_op jit(solution)/shard_map/all_to_all | solution.py:234
  156.5 0.9 shard_map.43
  (9 shorter events, 0.1 us)
Async XLA Ops:
  6.6 0.9 copy-start
  7.5 0.7 copy-start.1
  10.5 25.5 %all-to-all-start = ((f32[4,224,128]{2,1,0:T(8,128)}), f32[4,224,128]{2,1,0:T(8,128)S(1)}, u32[]{:S(2)}, u32[]{:S(2)}) async-start(f32[4,224,128]{2,1,0:T(8,128)} %shard_map.37), calls=%async_computation | async-start | bytes 917504 | tf_op jit(solution)/shard_map/all_to_all | solution.py:204
  15.0 107.6 %all-gather.3.cloned.1.call-start = ((), (), s32[]{:S(2)}) async-start(), calls=%async_computation.6 | async-start | bytes 1916928 | tf_op jit(solution)/shard_map/all_gather | solution.py:213
  15.0 21.0 %collective-permute-start = (f32[80,640]{1,0:T(8,128)}, f32[80,640]{1,0:T(8,128)S(1)}, u32[]{:S(2)}, u32[]{:S(2)}) collective-permute-start(f32[80,640]{1,0:T(8,128)} %state_ref.1), channel_id=1, source_target_pairs={{0,2},{2,0},{1,3},{3,1},{4,6},{6,4},{5,7},{7,5},{8,10},{10,8},{9,1... | collective-permute-start | bytes 614408 | tf_op jit(solution)/shard_map/ppermute | solution.py:195
  36.0 0.7 copy-start.2
  122.6 1.5 copy-start.4
  124.1 17.4 %copy-start.3 = (s32[20,20]{1,0:T(8,128)S(1)}, s32[20,20]{1,0:T(8,128)}, u32[]{:S(2)}) copy-start(s32[20,20]{1,0:T(8,128)} %pattern_ref.5) | copy-start | bytes 4804
Sparse Core Ops, SparseCore 0:
  38.4 84.1 all-gather.2

commit v7 on v5

--- a/solution.py
+++ b/solution.py
@@ -40,8 +40,8 @@
     )(*args)
 
 
-def masked_block(at_ref, pattern_ref, h, x):
-    row = at_ref[0] * 80
+def masked_block(at_ref, owner, pattern_ref, h, x):
+    row = owner * 80
     col = (5 * at_ref[1] + h) // 2
     first = row // BLK
     low = pattern_ref[first, col].astype(jnp.float32)
@@ -50,17 +50,25 @@
     return x * jnp.where(here, low, high)
 
 
-def pieces_kernel(at_ref, pattern_ref, state_ref, out_ref, masked_ref):
-    zh, c = at_ref[2], at_ref[3]
+def pack_right(at_ref, owner, pattern_ref, state_ref, masked_ref, out_ref, base):
     for h in range(5):
         lanes = slice(128 * h, 128 * h + 128)
-        masked_ref[:, lanes] = masked_block(at_ref, pattern_ref, h, state_ref[:, lanes])
+        masked_ref[:, lanes] = masked_block(at_ref, owner, pattern_ref, h, state_ref[:, lanes])
     out_ref[...] = jnp.zeros_like(out_ref)
     for y in range(4):
         for h in range(5):
-            out_ref[y, LEFT + PAD * h : LEFT + PAD * h + RUN] = masked_ref[
-                RUN * y : RUN * y + RUN, 128 * h : 128 * h + 128
-            ]
+            rows = slice(base + PAD * h, base + PAD * h + RUN)
+            out_ref[y, rows] = masked_ref[RUN * y : RUN * y + RUN, 128 * h : 128 * h + 128]
+
+
+def far_kernel(at_ref, pattern_ref, state_ref, out_ref, masked_ref):
+    owner = at_ref[0] + 2 - 4 * at_ref[2]
+    pack_right(at_ref, owner, pattern_ref, state_ref, masked_ref, out_ref, 0)
+
+
+def pieces_kernel(at_ref, pattern_ref, state_ref, out_ref, masked_ref):
+    zh, c = at_ref[2], at_ref[3]
+    pack_right(at_ref, at_ref[0], pattern_ref, state_ref, masked_ref, out_ref, LEFT)
     n = lax.broadcasted_iota(jnp.int32, (1, 640), 1)
     late = n >= 512
     y = jnp.where(late, (n - 512) // 32, n // 128)
@@ -90,13 +98,21 @@
             out_ref[y, MAIN + 8 * slot : MAIN + 8 * slot + 8] = tile
 
 
-def unpack_kernel(got_ref, left_ref, right_ref):
-    left_ref[...] = got_ref[:, :LEFT]
+def unpack_right(got_ref, right_ref, base):
     for y in range(4):
         for h in range(5):
             right_ref[y // 2, RUN * (y % 2) : RUN * (y % 2) + RUN, 128 * h : 128 * h + 128] = (
-                got_ref[y, LEFT + PAD * h : LEFT + PAD * h + RUN]
+                got_ref[y, base + PAD * h : base + PAD * h + RUN]
             )
+
+
+def unpack_kernel(got_ref, left_ref, right_ref):
+    left_ref[...] = got_ref[:, :LEFT]
+    unpack_right(got_ref, right_ref, LEFT)
+
+
+def unpack_far_kernel(got_ref, right_ref):
+    unpack_right(got_ref, right_ref, 0)
 
 
 def product_kernel(at_ref, *refs):
@@ -136,7 +152,7 @@
         x = (shares_ref[0, :, lanes] + shares_ref[1, :, lanes]) + (
             shares_ref[2, :, lanes] + shares_ref[3, :, lanes]
         )
-        out_ref[:, lanes] = masked_block(at_ref, pattern_ref, h, x * x)
+        out_ref[:, lanes] = masked_block(at_ref, at_ref[0], pattern_ref, h, x * x)
     sums_ref[...] = lax.dot_general(
         jnp.ones((8, 640), jnp.float32),
         out_ref[...],
@@ -180,31 +196,39 @@
         [lax.axis_index(ROWS)] + [lax.axis_index(a) for a in ("zl", "zh", "c", "x")]
     ).astype(jnp.int32)
 
+    tie = lax.optimization_barrier
+    work = [pltpu.VMEM((rows, cols), jnp.float32)]
+    far = shift(state, "zh", 1)
     pieces = call(
         pieces_kernel,
         f32(4, PIECE, 128),
         [SMEM, SMEM, VMEM],
         (at, in_pattern, state),
-        [pltpu.VMEM((rows, cols), jnp.float32)],
+        work,
     )
     got = lax.all_to_all(pieces, "y", 0, 0)
-    left, right = call(
+    left, near = call(
         unpack_kernel, (f32(4, LEFT, 128), f32(2, 2 * RUN, cols)), [VMEM], (got,)
     )
-
-    tie = lax.optimization_barrier
+    near = across_x(near)
+    left, near, far = tie((left, near, far))
+
     up, down = shift(left, "zl", 1), shift(left, "zl", -1)
-    far = shift(right, "zh", 1)
-    near = across_x(right)
+    far = call(
+        far_kernel, f32(4, 5 * PAD, 128), [SMEM, SMEM, VMEM], (at, in_pattern, far), work
+    )
+    far = lax.all_to_all(far, "y", 0, 0)
+    far = call(unpack_far_kernel, f32(2, 2 * RUN, cols), [VMEM], (far,))
     lefts = [left, up, None, None, None, None, None, down]
-    up, down, near, far = tie((up, down, near, far))
+    up, down, far = tie((up, down, far))
+
     up, down = shift(up, "zl", 1), shift(down, "zl", -1)
     far = across_x(far)
-    near_swapped = shift(near, "c", 1)
     lefts[2], lefts[6] = up, down
-    up, down, far, near_swapped = tie((up, down, far, near_swapped))
+    up, down, far = tie((up, down, far))
+
     up, down = shift(up, "zl", 1), shift(down, "zl", -1)
-    far_swapped = shift(far, "c", 1)
+    near_swapped, far_swapped = shift(near, "c", 1), shift(far, "c", 1)
     lefts[3], lefts[5] = up, down
     lefts[4] = shift(up, "zl", 1)
 

time: 168 us -> 172 us (1.024)
  waiting for transfers between devices: 39.9 us -> 25.5 us
  blocking collectives: 40.1 us -> 49.1 us
  starting transfers between devices: 77.3 us -> 85.5 us
    ppermute x16, waiting for transfers between devices: 39.9 us -> 25.5 us  [shift(): lax.ppermute(x, axis_name, [(i, (i + by) % size) for i in range(size)])]
    all_to_all x0 -> x1, blocking collectives: none -> 8.97 us  [body(): far = lax.all_to_all(far, 'y', 0, 0)]
    ppermute x16, starting transfers between devices: 77.3 us -> 85.5 us  [shift(): lax.ppermute(x, axis_name, [(i, (i + by) % size) for i in range(size)])]
    pallas_call x5 -> x7, Pallas kernels: 7.8 us -> 8.61 us  [call(): pl.pallas_call(kernel, out_shape=outs, in_specs=in_specs, out_specs=jax.t...]
  transfers between devices with their start and end apart: 16 -> 16, of which waited for: 7 -> 6; matrix products, arithmetic and copies ran while one was open for 0% -> 0% of each run, Pallas kernels for 0% -> 0%
where the time goes in v7:
time: 172 us; the launch traced here: 171 us
  starting transfers between devices  85.5 us (50%)
  blocking collectives  49.1 us (29%)
  waiting for transfers between devices  25.5 us (15%)
  Pallas kernels  8.61 us (5%)
    ppermute x16, starting transfers between devices, shift(): lax.ppermute(x, axis_name, [(i, (i + by) % size) for i in range(size)])  85.5 us
    ppermute x16, waiting for transfers between devices, shift(): lax.ppermute(x, axis_name, [(i, (i + by) % size) for i in range(size)])  25.5 us
    all_to_all x1, blocking collectives, body(): shares = lax.all_to_all(partial, 'y', 0, 0)  14.3 us
    all_to_all x1, blocking collectives, body(): got = lax.all_to_all(pieces, 'y', 0, 0)  13 us
    all_to_all x1, blocking collectives, body(): sums = lax.all_to_all(sums.reshape(8, 1, rows), 'zl', 0, 0).reshape(8, rows)  12.8 us
    all_to_all x1, blocking collectives, body(): far = lax.all_to_all(far, 'y', 0, 0)  8.97 us
    pallas_call x7, Pallas kernels, call(): pl.pallas_call(kernel, out_shape=outs, in_specs=in_specs, out_specs=jax.t...  8.61 us
  transfers between devices with their start and end apart: 16, of which 6 were waited for; matrix products, arithmetic and copies ran while one was open for 0% of the time, Pallas kernels for 0%

profile of v7, /device:TPU:6, one launch (start us, length us, event | category | flops | bytes accessed | tf_op | source)
XLA Modules:
  0.0 170.7 jit_solution(10263906514941817780)
XLA Ops:
  3.1 13.0 %all_to_all.20.got_ref = f32[4,224,128]{2,1,0:T(8,128)S(1)} all-to-all(f32[4,224,128]{2,1,0:T(8,128)S(1)} %shard_map.37), channel_id=1, replica_groups=mesh['zl'=8,'x'=4,'y'=4,'zh'=2,'c'=2] {'y'}, dimensions={0} | all-to-all | bytes 917504 | tf_op jit(solution)/shard_map/all_to_all | solution.py:209
  16.2 2.9 %collective-permute-start.2 = (f32[2,40,640]{2,1,0:T(8,128)S(1)}, f32[2,40,640]{2,1,0:T(8,128)S(1)}, u32[]{:S(2)}, u32[]{:S(2)}) collective-permute-start(f32[2,40,640]{2,1,0:T(8,128)S(1)} %get-tuple-element.19), channel_id=1, source_target_pairs={{0,48},{16,0},{32,16},{48,32},{1,49},{17,1},{33,17},{49,33},{2,50}... | collective-permute-start | bytes 614408 | tf_op jit(solution)/shard_map/ppermute | solution.py:181
  19.1 5.5 %collective-permute-start.1 = (f32[2,40,640]{2,1,0:T(8,128)S(1)}, f32[2,40,640]{2,1,0:T(8,128)S(1)}, u32[]{:S(2)}, u32[]{:S(2)}) collective-permute-start(f32[2,40,640]{2,1,0:T(8,128)S(1)} %get-tuple-element.19), channel_id=1, source_target_pairs={{0,32},{16,48},{32,0},{48,16},{1,33},{17,49},{33,1},{49,17},{2,34}... | collective-permute-start | bytes 614408 | tf_op jit(solution)/shard_map/ppermute | solution.py:181
  24.6 1.9 %collective-permute-start = (f32[2,40,640]{2,1,0:T(8,128)S(1)}, f32[2,40,640]{2,1,0:T(8,128)S(1)}, u32[]{:S(2)}, u32[]{:S(2)}) collective-permute-start(f32[2,40,640]{2,1,0:T(8,128)S(1)} %get-tuple-element.19), channel_id=1, source_target_pairs={{0,16},{16,32},{32,48},{48,0},{1,17},{17,33},{33,49},{49,1},{2,18}... | collective-permute-start | bytes 614408 | tf_op jit(solution)/shard_map/ppermute | solution.py:181
  26.5 15.4 %collective-permute-start.3 = (f32[80,640]{1,0:T(8,128)S(1)}, f32[80,640]{1,0:T(8,128)S(1)}, u32[]{:S(2)}, u32[]{:S(2)}) collective-permute-start(f32[80,640]{1,0:T(8,128)S(1)} %copy-done.1), channel_id=1, source_target_pairs={{0,2},{2,0},{1,3},{3,1},{4,6},{6,4},{5,7},{7,5},{8,10},{10,8},{9,1... | collective-permute-start | bytes 614408 | tf_op jit(solution)/shard_map/ppermute | solution.py:181
  42.0 3.9 %collective-permute-done.3.state_ref = f32[80,640]{1,0:T(8,128)S(1)} collective-permute-done((f32[80,640]{1,0:T(8,128)S(1)}, f32[80,640]{1,0:T(8,128)S(1)}, u32[]{:S(2)}, u32[]{:S(2)}) %collective-permute-start.3) | collective-permute-done | bytes 204832 | tf_op jit(solution)/shard_map/ppermute | solution.py:181
  45.9 16.2 %collective-permute-start.5 = (f32[4,104,128]{2,1,0:T(8,128)S(1)}, f32[4,104,128]{2,1,0:T(8,128)S(1)}, u32[]{:S(2)}, u32[]{:S(2)}) collective-permute-start(f32[4,104,128]{2,1,0:T(8,128)S(1)} %get-tuple-element.20.refs_0_), channel_id=1, source_target_pairs={{0,448},{64,0},{128,64},{192,128},{256,192},{320,256},{384,320},{4... | collective-permute-start | bytes 638984 | tf_op jit(solution)/shard_map/ppermute | solution.py:181
  62.1 1.9 %collective-permute-start.4 = (f32[4,104,128]{2,1,0:T(8,128)S(1)}, f32[4,104,128]{2,1,0:T(8,128)S(1)}, u32[]{:S(2)}, u32[]{:S(2)}) collective-permute-start(f32[4,104,128]{2,1,0:T(8,128)S(1)} %get-tuple-element.20.refs_0_), channel_id=1, source_target_pairs={{0,64},{64,128},{128,192},{192,256},{256,320},{320,384},{384,448},... | collective-permute-start | bytes 638984 | tf_op jit(solution)/shard_map/ppermute | solution.py:181
  64.9 9.0 %all_to_all.21.got_ref = f32[4,120,128]{2,1,0:T(8,128)S(1)} all-to-all(f32[4,120,128]{2,1,0:T(8,128)S(1)} %shard_map.39), channel_id=1, replica_groups=mesh['zl'=8,'x'=4,'y'=4,'zh'=2,'c'=2] {'y'}, dimensions={0} | all-to-all | bytes 491520 | tf_op jit(solution)/shard_map/all_to_all | solution.py:220
  73.9 2.6 %collective-permute-done.4.refs_1_ = f32[4,104,128]{2,1,0:T(8,128)S(1)} collective-permute-done((f32[4,104,128]{2,1,0:T(8,128)S(1)}, f32[4,104,128]{2,1,0:T(8,128)S(1)}, u32[]{:S(2)}, u32[]{:S(2)}) %collective-permute-start.4) | collective-permute-done | bytes 213024 | tf_op jit(solution)/shard_map/ppermute | solution.py:181
  76.5 2.2 %collective-permute-start.10 = (f32[2,40,640]{2,1,0:T(8,128)S(1)}, f32[2,40,640]{2,1,0:T(8,128)S(1)}, u32[]{:S(2)}, u32[]{:S(2)}) collective-permute-start(f32[2,40,640]{2,1,0:T(8,128)S(1)} %shard_map.40), channel_id=1, source_target_pairs={{0,48},{16,0},{32,16},{48,32},{1,49},{17,1},{33,17},{49,33},{2,50}... | collective-permute-start | bytes 614408 | tf_op jit(solution)/shard_map/ppermute | solution.py:181
  78.7 3.9 %collective-permute-start.9 = (f32[2,40,640]{2,1,0:T(8,128)S(1)}, f32[2,40,640]{2,1,0:T(8,128)S(1)}, u32[]{:S(2)}, u32[]{:S(2)}) collective-permute-start(f32[2,40,640]{2,1,0:T(8,128)S(1)} %shard_map.40), channel_id=1, source_target_pairs={{0,32},{16,48},{32,0},{48,16},{1,33},{17,49},{33,1},{49,17},{2,34}... | collective-permute-start | bytes 614408 | tf_op jit(solution)/shard_map/ppermute | solution.py:181
  82.7 4.3 %collective-permute-start.8 = (f32[2,40,640]{2,1,0:T(8,128)S(1)}, f32[2,40,640]{2,1,0:T(8,128)S(1)}, u32[]{:S(2)}, u32[]{:S(2)}) collective-permute-start(f32[2,40,640]{2,1,0:T(8,128)S(1)} %shard_map.40), channel_id=1, source_target_pairs={{0,16},{16,32},{32,48},{48,0},{1,17},{17,33},{33,49},{49,1},{2,18}... | collective-permute-start | bytes 614408 | tf_op jit(solution)/shard_map/ppermute | solution.py:181
  87.0 1.9 %collective-permute-start.6 = (f32[4,104,128]{2,1,0:T(8,128)S(1)}, f32[4,104,128]{2,1,0:T(8,128)S(1)}, u32[]{:S(2)}, u32[]{:S(2)}) collective-permute-start(f32[4,104,128]{2,1,0:T(8,128)S(1)} %collective-permute-done.4.refs_1_), channel_id=1, source_target_pairs={{0,64},{64,128},{128,192},{192,256},{256,320},{320,384},{384,448},... | collective-permute-start | bytes 638984 | tf_op jit(solution)/shard_map/ppermute | solution.py:181
  88.9 10.5 %collective-permute-start.7 = (f32[4,104,128]{2,1,0:T(8,128)S(1)}, f32[4,104,128]{2,1,0:T(8,128)S(1)}, u32[]{:S(2)}, u32[]{:S(2)}) collective-permute-start(f32[4,104,128]{2,1,0:T(8,128)S(1)} %collective-permute-done.5.refs_7_), channel_id=1, source_target_pairs={{0,448},{64,0},{128,64},{192,128},{256,192},{320,256},{384,320},{4... | collective-permute-start | bytes 638984 | tf_op jit(solution)/shard_map/ppermute | solution.py:181
  99.4 1.9 %collective-permute-start.14 = (f32[4,2,40,640]{3,2,1,0:T(8,128)S(1)}, f32[4,2,40,640]{3,2,1,0:T(8,128)S(1)}, u32[]{:S(2)}, u32[]{:S(2)}) collective-permute-start(f32[4,2,40,640]{3,2,1,0:T(8,128)S(1)} %pad_maximum_fusion.refs_8_), channel_id=1, source_target_pairs={{0,1},{1,0},{2,3},{3,2},{4,5},{5,4},{6,7},{7,6},{8,9},{9,8},{10,11... | collective-permute-start | bytes 2457608 | tf_op jit(solution)/shard_map/ppermute | solution.py:181
  104.7 1.9 %collective-permute-start.11 = (f32[4,104,128]{2,1,0:T(8,128)S(1)}, f32[4,104,128]{2,1,0:T(8,128)S(1)}, u32[]{:S(2)}, u32[]{:S(2)}) collective-permute-start(f32[4,104,128]{2,1,0:T(8,128)S(1)} %collective-permute-done.6.refs_2_), channel_id=1, source_target_pairs={{0,64},{64,128},{128,192},{192,256},{256,320},{320,384},{384,448},... | collective-permute-start | bytes 638984 | tf_op jit(solution)/shard_map/ppermute | solution.py:181
  106.6 11.2 %collective-permute-start.13 = (f32[4,104,128]{2,1,0:T(8,128)S(1)}, f32[4,104,128]{2,1,0:T(8,128)S(1)}, u32[]{:S(2)}, u32[]{:S(2)}) collective-permute-start(f32[4,104,128]{2,1,0:T(8,128)S(1)} %collective-permute-done.7.refs_6_), channel_id=1, source_target_pairs={{0,448},{64,0},{128,64},{192,128},{256,192},{320,256},{384,320},{4... | collective-permute-start | bytes 638984 | tf_op jit(solution)/shard_map/ppermute | solution.py:181
  117.8 4.2 %collective-permute-done.11.refs_3_ = f32[4,104,128]{2,1,0:T(8,128)S(1)} collective-permute-done((f32[4,104,128]{2,1,0:T(8,128)S(1)}, f32[4,104,128]{2,1,0:T(8,128)S(1)}, u32[]{:S(2)}, u32[]{:S(2)}) %collective-permute-start.11) | collective-permute-done | bytes 213024 | tf_op jit(solution)/shard_map/ppermute | solution.py:181
  122.0 1.9 %collective-permute-start.12 = (f32[4,104,128]{2,1,0:T(8,128)S(1)}, f32[4,104,128]{2,1,0:T(8,128)S(1)}, u32[]{:S(2)}, u32[]{:S(2)}) collective-permute-start(f32[4,104,128]{2,1,0:T(8,128)S(1)} %collective-permute-done.11.refs_3_), channel_id=1, source_target_pairs={{0,64},{64,128},{128,192},{192,256},{256,320},{320,384},{384,448},... | collective-permute-start | bytes 638984 | tf_op jit(solution)/shard_map/ppermute | solution.py:181
  124.0 13.4 %collective-permute-done.12.refs_4_ = f32[4,104,128]{2,1,0:T(8,128)S(1)} collective-permute-done((f32[4,104,128]{2,1,0:T(8,128)S(1)}, f32[4,104,128]{2,1,0:T(8,128)S(1)}, u32[]{:S(2)}, u32[]{:S(2)}) %collective-permute-start.12) | collective-permute-done | bytes 213024 | tf_op jit(solution)/shard_map/ppermute | solution.py:181
  137.4 4.3 %shard_map.41 = f32[4,80,640]{2,1,0:T(8,128)S(1)} custom-call(s32[5]{0:T(128)S(1)} %stack.53.at_ref, f32[4,104,128]{2,1,0:T(8,128)S(1)} %get-tuple-element.20.refs_0_, f32[4,104,128]{2,1,0:T(8,128)S(1)} %collective-permute-done.4.refs_1_, f32[4,104,128]{2,1,0:T(8,128)S(1)} %collective-permute-done.6.refs_2_, ...), custom_call_target="tpu_custom_call" | custom-call | flops 3000000000 | bytes 6000000 | tf_op jit(solution)/shard_map/pallas_call | solution.py:30
  141.7 14.3 %all_to_all.22.shares_ref = f32[4,80,640]{2,1,0:T(8,128)S(1)} all-to-all(f32[4,80,640]{2,1,0:T(8,128)S(1)} %shard_map.41), channel_id=1, replica_groups=mesh['zl'=8,'x'=4,'y'=4,'zh'=2,'c'=2] {'y'}, dimensions={0} | all-to-all | bytes 1638400 | tf_op jit(solution)/shard_map/all_to_all | solution.py:244
  157.1 12.8 %all_to_all.23 = f32[8,1,80]{2,1,0:T(1,128)S(1)} all-to-all(f32[8,1,80]{2,1,0:T(1,128)S(1)} %bitcast.20), channel_id=1, replica_groups=mesh['zl'=8,'x'=4,'y'=4,'zh'=2,'c'=2] {'zl'}, dimensions={0} | all-to-all | bytes 5120 | tf_op jit(solution)/shard_map/all_to_all | solution.py:251
  (30 shorter events, 9.4 us)
Async XLA Ops:
  0.0 0.7 copy-start.2
  0.7 0.9 copy-start
  16.2 10.3 %copy-start.1 = (f32[80,640]{1,0:T(8,128)S(1)}, f32[80,640]{1,0:T(8,128)}, u32[]{:S(2)}) copy-start(f32[80,640]{1,0:T(8,128)} %state_ref.1) | copy-start | bytes 614404
  16.2 25.7 %collective-permute-start.2 = (f32[2,40,640]{2,1,0:T(8,128)S(1)}, f32[2,40,640]{2,1,0:T(8,128)S(1)}, u32[]{:S(2)}, u32[]{:S(2)}) collective-permute-start(f32[2,40,640]{2,1,0:T(8,128)S(1)} %get-tuple-element.19), channel_id=1, source_target_pairs={{0,48},{16,0},{32,16},{48,32},{1,49},{17,1},{33,17},{49,33},{2,50}... | collective-permute-start | bytes 614408 | tf_op jit(solution)/shard_map/ppermute | solution.py:181
  19.1 22.8 %collective-permute-start.1 = (f32[2,40,640]{2,1,0:T(8,128)S(1)}, f32[2,40,640]{2,1,0:T(8,128)S(1)}, u32[]{:S(2)}, u32[]{:S(2)}) collective-permute-start(f32[2,40,640]{2,1,0:T(8,128)S(1)} %get-tuple-element.19), channel_id=1, source_target_pairs={{0,32},{16,48},{32,0},{48,16},{1,33},{17,49},{33,1},{49,17},{2,34}... | collective-permute-start | bytes 614408 | tf_op jit(solution)/shard_map/ppermute | solution.py:181
  24.6 17.3 %collective-permute-start = (f32[2,40,640]{2,1,0:T(8,128)S(1)}, f32[2,40,640]{2,1,0:T(8,128)S(1)}, u32[]{:S(2)}, u32[]{:S(2)}) collective-permute-start(f32[2,40,640]{2,1,0:T(8,128)S(1)} %get-tuple-element.19), channel_id=1, source_target_pairs={{0,16},{16,32},{32,48},{48,0},{1,17},{17,33},{33,49},{49,1},{2,18}... | collective-permute-start | bytes 614408 | tf_op jit(solution)/shard_map/ppermute | solution.py:181
  26.5 19.4 %collective-permute-start.3 = (f32[80,640]{1,0:T(8,128)S(1)}, f32[80,640]{1,0:T(8,128)S(1)}, u32[]{:S(2)}, u32[]{:S(2)}) collective-permute-start(f32[80,640]{1,0:T(8,128)S(1)} %copy-done.1), channel_id=1, source_target_pairs={{0,2},{2,0},{1,3},{3,1},{4,6},{6,4},{5,7},{7,5},{8,10},{10,8},{9,1... | collective-permute-start | bytes 614408 | tf_op jit(solution)/shard_map/ppermute | solution.py:181
  45.9 28.0 %collective-permute-start.5 = (f32[4,104,128]{2,1,0:T(8,128)S(1)}, f32[4,104,128]{2,1,0:T(8,128)S(1)}, u32[]{:S(2)}, u32[]{:S(2)}) collective-permute-start(f32[4,104,128]{2,1,0:T(8,128)S(1)} %get-tuple-element.20.refs_0_), channel_id=1, source_target_pairs={{0,448},{64,0},{128,64},{192,128},{256,192},{320,256},{384,320},{4... | collective-permute-start | bytes 638984 | tf_op jit(solution)/shard_map/ppermute | solution.py:181
  62.1 14.3 %collective-permute-start.4 = (f32[4,104,128]{2,1,0:T(8,128)S(1)}, f32[4,104,128]{2,1,0:T(8,128)S(1)}, u32[]{:S(2)}, u32[]{:S(2)}) collective-permute-start(f32[4,104,128]{2,1,0:T(8,128)S(1)} %get-tuple-element.20.refs_0_), channel_id=1, source_target_pairs={{0,64},{64,128},{128,192},{192,256},{256,320},{320,384},{384,448},... | collective-permute-start | bytes 638984 | tf_op jit(solution)/shard_map/ppermute | solution.py:181
  76.5 23.0 %collective-permute-start.10 = (f32[2,40,640]{2,1,0:T(8,128)S(1)}, f32[2,40,640]{2,1,0:T(8,128)S(1)}, u32[]{:S(2)}, u32[]{:S(2)}) collective-permute-start(f32[2,40,640]{2,1,0:T(8,128)S(1)} %shard_map.40), channel_id=1, source_target_pairs={{0,48},{16,0},{32,16},{48,32},{1,49},{17,1},{33,17},{49,33},{2,50}... | collective-permute-start | bytes 614408 | tf_op jit(solution)/shard_map/ppermute | solution.py:181
  78.7 22.6 %collective-permute-start.9 = (f32[2,40,640]{2,1,0:T(8,128)S(1)}, f32[2,40,640]{2,1,0:T(8,128)S(1)}, u32[]{:S(2)}, u32[]{:S(2)}) collective-permute-start(f32[2,40,640]{2,1,0:T(8,128)S(1)} %shard_map.40), channel_id=1, source_target_pairs={{0,32},{16,48},{32,0},{48,16},{1,33},{17,49},{33,1},{49,17},{2,34}... | collective-permute-start | bytes 614408 | tf_op jit(solution)/shard_map/ppermute | solution.py:181
  82.7 18.7 %collective-permute-start.8 = (f32[2,40,640]{2,1,0:T(8,128)S(1)}, f32[2,40,640]{2,1,0:T(8,128)S(1)}, u32[]{:S(2)}, u32[]{:S(2)}) collective-permute-start(f32[2,40,640]{2,1,0:T(8,128)S(1)} %shard_map.40), channel_id=1, source_target_pairs={{0,16},{16,32},{32,48},{48,0},{1,17},{17,33},{33,49},{49,1},{2,18}... | collective-permute-start | bytes 614408 | tf_op jit(solution)/shard_map/ppermute | solution.py:181
  87.0 14.8 %collective-permute-start.6 = (f32[4,104,128]{2,1,0:T(8,128)S(1)}, f32[4,104,128]{2,1,0:T(8,128)S(1)}, u32[]{:S(2)}, u32[]{:S(2)}) collective-permute-start(f32[4,104,128]{2,1,0:T(8,128)S(1)} %collective-permute-done.4.refs_1_), channel_id=1, source_target_pairs={{0,64},{64,128},{128,192},{192,256},{256,320},{320,384},{384,448},... | collective-permute-start | bytes 638984 | tf_op jit(solution)/shard_map/ppermute | solution.py:181
  88.9 13.9 %collective-permute-start.7 = (f32[4,104,128]{2,1,0:T(8,128)S(1)}, f32[4,104,128]{2,1,0:T(8,128)S(1)}, u32[]{:S(2)}, u32[]{:S(2)}) collective-permute-start(f32[4,104,128]{2,1,0:T(8,128)S(1)} %collective-permute-done.5.refs_7_), channel_id=1, source_target_pairs={{0,448},{64,0},{128,64},{192,128},{256,192},{320,256},{384,320},{4... | collective-permute-start | bytes 638984 | tf_op jit(solution)/shard_map/ppermute | solution.py:181
  99.4 24.5 %collective-permute-start.14 = (f32[4,2,40,640]{3,2,1,0:T(8,128)S(1)}, f32[4,2,40,640]{3,2,1,0:T(8,128)S(1)}, u32[]{:S(2)}, u32[]{:S(2)}) collective-permute-start(f32[4,2,40,640]{3,2,1,0:T(8,128)S(1)} %pad_maximum_fusion.refs_8_), channel_id=1, source_target_pairs={{0,1},{1,0},{2,3},{3,2},{4,5},{5,4},{6,7},{7,6},{8,9},{9,8},{10,11... | collective-permute-start | bytes 2457608 | tf_op jit(solution)/shard_map/ppermute | solution.py:181
  102.8 34.6 %collective-permute-start.15 = (f32[4,2,40,640]{3,2,1,0:T(8,128)S(1)}, f32[4,2,40,640]{3,2,1,0:T(8,128)S(1)}, u32[]{:S(2)}, u32[]{:S(2)}) collective-permute-start(f32[4,2,40,640]{3,2,1,0:T(8,128)S(1)} %pad_maximum_fusion.1.refs_10_), channel_id=1, source_target_pairs={{0,1},{1,0},{2,3},{3,2},{4,5},{5,4},{6,7},{7,6},{8,9},{9,8},{10,11... | collective-permute-start | bytes 2457608 | tf_op jit(solution)/shard_map/ppermute | solution.py:181
  104.7 17.4 %collective-permute-start.11 = (f32[4,104,128]{2,1,0:T(8,128)S(1)}, f32[4,104,128]{2,1,0:T(8,128)S(1)}, u32[]{:S(2)}, u32[]{:S(2)}) collective-permute-start(f32[4,104,128]{2,1,0:T(8,128)S(1)} %collective-permute-done.6.refs_2_), channel_id=1, source_target_pairs={{0,64},{64,128},{128,192},{192,256},{256,320},{320,384},{384,448},... | collective-permute-start | bytes 638984 | tf_op jit(solution)/shard_map/ppermute | solution.py:181
  106.6 17.3 %collective-permute-start.13 = (f32[4,104,128]{2,1,0:T(8,128)S(1)}, f32[4,104,128]{2,1,0:T(8,128)S(1)}, u32[]{:S(2)}, u32[]{:S(2)}) collective-permute-start(f32[4,104,128]{2,1,0:T(8,128)S(1)} %collective-permute-done.7.refs_6_), channel_id=1, source_target_pairs={{0,448},{64,0},{128,64},{192,128},{256,192},{320,256},{384,320},{4... | collective-permute-start | bytes 638984 | tf_op jit(solution)/shard_map/ppermute | solution.py:181
  122.0 15.4 %collective-permute-start.12 = (f32[4,104,128]{2,1,0:T(8,128)S(1)}, f32[4,104,128]{2,1,0:T(8,128)S(1)}, u32[]{:S(2)}, u32[]{:S(2)}) collective-permute-start(f32[4,104,128]{2,1,0:T(8,128)S(1)} %collective-permute-done.11.refs_3_), channel_id=1, source_target_pairs={{0,64},{64,128},{128,192},{192,256},{256,320},{320,384},{384,448},... | collective-permute-start | bytes 638984 | tf_op jit(solution)/shard_map/ppermute | solution.py:181
  141.7 14.3 %copy-start.3 = (s32[20,20]{1,0:T(8,128)S(1)}, s32[20,20]{1,0:T(8,128)}, u32[]{:S(2)}) copy-start(s32[20,20]{1,0:T(8,128)} %pattern_ref.5) | copy-start | bytes 4804

commit v8 on v6

--- a/solution.py
+++ b/solution.py
@@ -59,11 +59,6 @@
         for h in range(5):
             rows = slice(base + PAD * h, base + PAD * h + RUN)
             out_ref[y, rows] = masked_ref[RUN * y : RUN * y + RUN, 128 * h : 128 * h + 128]
-
-
-def far_kernel(at_ref, pattern_ref, state_ref, out_ref, masked_ref):
-    owner = at_ref[0] + 2 - 4 * at_ref[2]
-    pack_right(at_ref, owner, pattern_ref, state_ref, masked_ref, out_ref, 0)
 
 
 def pieces_kernel(at_ref, pattern_ref, state_ref, out_ref, masked_ref):
@@ -111,32 +106,29 @@
     unpack_right(got_ref, right_ref, LEFT)
 
 
-def unpack_far_kernel(got_ref, right_ref):
-    unpack_right(got_ref, right_ref, 0)
-
-
-def product_kernel(at_ref, left_ref, right_ref, out_ref, hi_ref, lo_ref):
-    for dc in range(2):
-        c = lax.rem(at_ref[3] + dc, 2)
+def product_kernel(at_ref, *refs):
+    lefts, rights, out_ref, hi_ref, lo_ref = refs[:8], refs[8:10], *refs[10:]
+    zl, zh = at_ref[1], at_ref[2]
+    for dc, ref in enumerate(rights):
         for dzh in range(2):
             rows = slice(40 * (2 * dzh + dc), 40 * (2 * dzh + dc) + 40)
             for x in range(4):
                 for y1 in range(2):
-                    hi, lo = split(right_ref[c, x, dzh, y1])
+                    hi, lo = split(ref[2 * x + lax.rem(zh + dzh, 2), y1])
                     hi_ref[2 * x + y1, rows] = hi
                     lo_ref[2 * x + y1, rows] = lo
     lane = lax.broadcasted_iota(jnp.int32, (8, 128), 1) // 32
     total = jnp.zeros((320, 640), jnp.float32)
-    for block in range(8):
+    for d, ref in enumerate(lefts):
+        block = lax.rem(zl - d + 8, 8)
         whole = []
         for y in range(4):
             rest = []
             for tile in range(10):
                 rows = MAIN + 8 * (tile // 4)
-                part = left_ref[block, y, rows : rows + 8]
-                rest.append(jnp.where(lane == tile % 4, part, 0.0))
+                rest.append(jnp.where(lane == tile % 4, ref[y, rows : rows + 8], 0.0))
             rest = jnp.concatenate(rest, axis=0)
-            whole.append(jnp.concatenate([left_ref[block, y, :MAIN], rest], axis=1))
+            whole.append(jnp.concatenate([ref[y, :MAIN], rest], axis=1))
         left_hi, left_lo = split(jnp.concatenate(whole, axis=0))
         right_hi, right_lo = hi_ref[block], lo_ref[block]
         right_hi = jnp.concatenate([right_hi] + [right_hi[128:]] * 3, axis=0)
@@ -175,10 +167,9 @@
         out_ref[:, lanes] = inflated_ref[:, lanes] * scale
 
 
-def gather(block, axis_name):
+def shift(x, axis_name, by):
     size = lax.axis_size(axis_name)
-    copies = jnp.broadcast_to(block[None], (size,) + block.shape)
-    return lax.all_to_all(copies, axis_name, 0, 0)
+    return lax.ppermute(x, axis_name, [(i, (i + by) % size) for i in range(size)])
 
 
 def f32(*shape):
@@ -192,34 +183,32 @@
         [lax.axis_index(ROWS)] + [lax.axis_index(a) for a in ("zl", "zh", "c")]
     ).astype(jnp.int32)
 
-    other = lax.ppermute(state, "zh", [(0, 1), (1, 0)])
-    work = [pltpu.VMEM((rows, cols), jnp.float32)]
     pieces = call(
         pieces_kernel,
         f32(4, PIECE, 128),
         [SMEM, SMEM, VMEM],
         (at, in_pattern, state),
-        work,
+        [pltpu.VMEM((rows, cols), jnp.float32)],
     )
     got = lax.all_to_all(pieces, "y", 0, 0)
-    got, other = lax.optimization_barrier((got, other))
-    left, near = call(
+    left, right = call(
         unpack_kernel, (f32(4, LEFT, 128), f32(2, 2 * RUN, cols)), [VMEM], (got,)
     )
-    far = call(
-        far_kernel, f32(4, 5 * PAD, 128), [SMEM, SMEM, VMEM], (at, in_pattern, other), work
-    )
-    left, far = lax.optimization_barrier((left, far))
-    left = lax.all_gather(left, "zl", axis=0)
-    far = lax.all_to_all(far, "y", 0, 0)
-    far = call(unpack_far_kernel, f32(2, 2 * RUN, cols), [VMEM], (far,))
-    right = gather(gather(jnp.stack([near, far]), "x"), "c")
+
+    right = lax.all_gather(right, ("x", "zh"), axis=0)
+    lefts = [left] * 8
+    for d in (1, 2, 3):
+        lefts[d] = shift(lefts[d - 1], "zl", 1)
+        lefts[8 - d] = shift(lefts[(9 - d) % 8], "zl", -1)
+    lefts[3], lefts[5], right = lax.optimization_barrier((lefts[3], lefts[5], right))
+    lefts[4] = shift(lefts[3], "zl", 1)
+    swapped = shift(right, "c", 1)
 
     partial = call(
         product_kernel,
         f32(4, rows, cols),
-        [SMEM, VMEM, VMEM],
-        (at, left, right),
+        [SMEM] + [VMEM] * 10,
+        (at, *lefts, right, swapped),
         [pltpu.VMEM((8, 160, cols), jnp.bfloat16)] * 2,
         flops=3 * 10**9,
         size=6 * 10**6,

time: 165 us -> 201 us (1.22)
  waiting for transfers between devices: 50.9 us -> 91.7 us
  blocking collectives: 65.9 us -> 42.4 us
  starting transfers between devices: 20.2 us -> 40.9 us
    ppermute x1 -> x8, waiting for transfers between devices: 5.29 us -> 39.2 us  [shift(): lax.ppermute(x, axis_name, [(i, (i + by) % size) for i in range(size)])]
    all_to_all x3 -> x1, blocking collectives: 38.3 us -> 13 us  [body(): got = lax.all_to_all(pieces, 'y', 0, 0)]
    ppermute x1 -> x8, starting transfers between devices: 15.7 us -> 40.9 us  [shift(): lax.ppermute(x, axis_name, [(i, (i + by) % size) for i in range(size)])]
    all_gather x1, waiting for transfers between devices: 45.6 us -> 52.4 us  [body(): right = lax.all_gather(right, ('x', 'zh'), axis=0)]
    all_to_all x1 -> x0, starting transfers between devices: 4.46 us -> none  [body(): got = lax.all_to_all(pieces, 'y', 0, 0)]
    all_to_all x1, blocking collectives: 13.7 us -> 16.6 us  [body(): shares = lax.all_to_all(partial, 'y', 0, 0)]
    pallas_call x7 -> x5, Pallas kernels: 9.59 us -> 8.49 us  [call(): pl.pallas_call(kernel, out_shape=outs, in_specs=in_specs, out_specs=jax.t...]
  transfers between devices with their start and end apart: 3 -> 9, of which waited for: 2 -> 6; matrix products, arithmetic and copies ran while one was open for 0% -> 0% of each run, Pallas kernels for 0% -> 0%
where the time goes in v8:
time: 201 us; the launch traced here: 200 us
  waiting for transfers between devices  91.7 us (46%)
  blocking collectives  42.4 us (21%)
  starting transfers between devices  40.9 us (20%)
  between operations  13.5 us (7%)
  Pallas kernels  8.49 us (4%)
  local copies, waits for them, and re-layouts  3.08 us (2%)
    all_gather x1, waiting for transfers between devices, body(): right = lax.all_gather(right, ('x', 'zh'), axis=0)  52.4 us
    ppermute x8, starting transfers between devices, shift(): lax.ppermute(x, axis_name, [(i, (i + by) % size) for i in range(size)])  40.9 us
    ppermute x8, waiting for transfers between devices, shift(): lax.ppermute(x, axis_name, [(i, (i + by) % size) for i in range(size)])  39.2 us
    all_to_all x1, blocking collectives, body(): shares = lax.all_to_all(partial, 'y', 0, 0)  16.6 us
    all_to_all x1, blocking collectives, body(): got = lax.all_to_all(pieces, 'y', 0, 0)  13 us
    all_to_all x1, blocking collectives, body(): sums = lax.all_to_all(sums.reshape(8, 1, rows), 'zl', 0, 0).reshape(8, rows)  12.8 us
    pallas_call x5, Pallas kernels, call(): pl.pallas_call(kernel, out_shape=outs, in_specs=in_specs, out_specs=jax.t...  8.49 us
  transfers between devices with their start and end apart: 9, of which 6 were waited for; matrix products, arithmetic and copies ran while one was open for 0% of the time, Pallas kernels for 0%

profile of v8, /device:TPU:6, one launch (start us, length us, event | category | flops | bytes accessed | tf_op | source)
XLA Modules:
  0.0 200.1 jit_solution(10564231421714778782)
XLA Ops:
  6.6 0.9 copy-done
  8.3 1.5 shard_map.37
  9.8 13.0 %all_to_all.15.got_ref = f32[4,224,128]{2,1,0:T(8,128)S(1)} all-to-all(f32[4,224,128]{2,1,0:T(8,128)S(1)} %shard_map.37), channel_id=1, replica_groups=mesh['zl'=8,'x'=4,'y'=4,'zh'=2,'c'=2] {'y'}, dimensions={0} | all-to-all | bytes 917504 | tf_op jit(solution)/shard_map/all_to_all | solution.py:193
  22.8 0.7 shard_map.38
  23.5 13.2 %collective-permute-start.3 = (f32[4,104,128]{2,1,0:T(8,128)S(1)}, f32[4,104,128]{2,1,0:T(8,128)S(1)}, u32[]{:S(2)}, u32[]{:S(2)}) collective-permute-start(f32[4,104,128]{2,1,0:T(8,128)S(1)} %get-tuple-element.12.refs_0_), channel_id=1, source_target_pairs={{0,448},{64,0},{128,64},{192,128},{256,192},{320,256},{384,320},{4... | collective-permute-start | bytes 638984 | tf_op jit(solution)/shard_map/ppermute | solution.py:172
  36.7 1.9 collective-permute-start
  38.6 3.4 %collective-permute-done.3.refs_7_ = f32[4,104,128]{2,1,0:T(8,128)S(1)} collective-permute-done((f32[4,104,128]{2,1,0:T(8,128)S(1)}, f32[4,104,128]{2,1,0:T(8,128)S(1)}, u32[]{:S(2)}, u32[]{:S(2)}) %collective-permute-start.3) | collective-permute-done | bytes 213024 | tf_op jit(solution)/shard_map/ppermute | solution.py:172
  42.0 11.0 %collective-permute-start.4 = (f32[4,104,128]{2,1,0:T(8,128)S(1)}, f32[4,104,128]{2,1,0:T(8,128)S(1)}, u32[]{:S(2)}, u32[]{:S(2)}) collective-permute-start(f32[4,104,128]{2,1,0:T(8,128)S(1)} %collective-permute-done.3.refs_7_), channel_id=1, source_target_pairs={{0,448},{64,0},{128,64},{192,128},{256,192},{320,256},{384,320},{4... | collective-permute-start | bytes 638984 | tf_op jit(solution)/shard_map/ppermute | solution.py:172
  53.0 1.9 collective-permute-start.1
  55.0 9.2 %collective-permute-done.4.refs_6_ = f32[4,104,128]{2,1,0:T(8,128)S(1)} collective-permute-done((f32[4,104,128]{2,1,0:T(8,128)S(1)}, f32[4,104,128]{2,1,0:T(8,128)S(1)}, u32[]{:S(2)}, u32[]{:S(2)}) %collective-permute-start.4) | collective-permute-done | bytes 213024 | tf_op jit(solution)/shard_map/ppermute | solution.py:172
  64.1 7.1 %collective-permute-start.5 = (f32[4,104,128]{2,1,0:T(8,128)S(1)}, f32[4,104,128]{2,1,0:T(8,128)S(1)}, u32[]{:S(2)}, u32[]{:S(2)}) collective-permute-start(f32[4,104,128]{2,1,0:T(8,128)S(1)} %collective-permute-done.4.refs_6_), channel_id=1, source_target_pairs={{0,448},{64,0},{128,64},{192,128},{256,192},{320,256},{384,320},{4... | collective-permute-start | bytes 638984 | tf_op jit(solution)/shard_map/ppermute | solution.py:172
  71.3 1.9 collective-permute-start.2
  73.2 3.4 %collective-permute-done.5.refs_5_ = f32[4,104,128]{2,1,0:T(8,128)S(1)} collective-permute-done((f32[4,104,128]{2,1,0:T(8,128)S(1)}, f32[4,104,128]{2,1,0:T(8,128)S(1)}, u32[]{:S(2)}, u32[]{:S(2)}) %collective-permute-start.5) | collective-permute-done | bytes 213024 | tf_op jit(solution)/shard_map/ppermute | solution.py:172
  76.6 9.1 %collective-permute-done.2.refs_3_ = f32[4,104,128]{2,1,0:T(8,128)S(1)} collective-permute-done((f32[4,104,128]{2,1,0:T(8,128)S(1)}, f32[4,104,128]{2,1,0:T(8,128)S(1)}, u32[]{:S(2)}, u32[]{:S(2)}) %collective-permute-start.2) | collective-permute-done | bytes 213024 | tf_op jit(solution)/shard_map/ppermute | solution.py:172
  85.6 52.4 %all-gather.3.cloned.1.call-done = f32[16,40,640]{2,1,0:T(8,128)} async-done(((f32[2,40,640]{2,1,0:T(8,128)}), f32[16,40,640]{2,1,0:T(8,128)}) %all-gather.3.cloned.1.call-update) | async-done | bytes 1638416 | tf_op jit(solution)/shard_map/all_gather | solution.py:198
  138.1 1.9 collective-permute-start.7
  140.0 1.9 collective-permute-start.6
  141.9 14.2 %collective-permute-done.6.refs_4_ = f32[4,104,128]{2,1,0:T(8,128)S(1)} collective-permute-done((f32[4,104,128]{2,1,0:T(8,128)S(1)}, f32[4,104,128]{2,1,0:T(8,128)S(1)}, u32[]{:S(2)}, u32[]{:S(2)}) %collective-permute-start.6) | collective-permute-done | bytes 213024 | tf_op jit(solution)/shard_map/ppermute | solution.py:172
  156.2 1.4 copy-done.3
  157.6 4.3 %shard_map.39 = f32[4,80,640]{2,1,0:T(8,128)S(1)} custom-call(s32[4]{0:T(128)S(1)} %pad_add_fusion.at_ref, f32[4,104,128]{2,1,0:T(8,128)S(1)} %get-tuple-element.12.refs_0_, f32[4,104,128]{2,1,0:T(8,128)S(1)} %collective-permute-done.refs_1_, f32[4,104,128]{2,1,0:T(8,128)S(1)} %collective-permute-done.1.refs_2_, ...), custom_call_target="tpu_custom_call" | custom-call | flops 3000000000 | bytes 6000000 | tf_op jit(solution)/shard_map/pallas_call | solution.py:30
  161.9 16.6 %all_to_all.16.shares_ref = f32[4,80,640]{2,1,0:T(8,128)S(1)} all-to-all(f32[4,80,640]{2,1,0:T(8,128)S(1)} %shard_map.39), channel_id=1, replica_groups=mesh['zl'=8,'x'=4,'y'=4,'zh'=2,'c'=2] {'y'}, dimensions={0} | all-to-all | bytes 1638400 | tf_op jit(solution)/shard_map/all_to_all | solution.py:216
  178.5 1.1 shard_map.40
  179.6 12.8 %all_to_all.17 = f32[8,1,80]{2,1,0:T(1,128)S(1)} all-to-all(f32[8,1,80]{2,1,0:T(1,128)S(1)} %bitcast.10), channel_id=1, replica_groups=mesh['zl'=8,'x'=4,'y'=4,'zh'=2,'c'=2] {'zl'}, dimensions={0} | all-to-all | bytes 5120 | tf_op jit(solution)/shard_map/all_to_all | solution.py:223
  192.3 0.9 shard_map.41
  (12 shorter events, 0.8 us)
Async XLA Ops:
  6.5 131.6 %all-gather.3.cloned.1.call-start = ((), (), s32[]{:S(2)}) async-start(), calls=%async_computation.3 | async-start | bytes 1843200 | tf_op jit(solution)/shard_map/all_gather | solution.py:198
  6.6 0.9 copy-start
  7.5 0.7 copy-start.1
  23.5 18.5 %collective-permute-start.3 = (f32[4,104,128]{2,1,0:T(8,128)S(1)}, f32[4,104,128]{2,1,0:T(8,128)S(1)}, u32[]{:S(2)}, u32[]{:S(2)}) collective-permute-start(f32[4,104,128]{2,1,0:T(8,128)S(1)} %get-tuple-element.12.refs_0_), channel_id=1, source_target_pairs={{0,448},{64,0},{128,64},{192,128},{256,192},{320,256},{384,320},{4... | collective-permute-start | bytes 638984 | tf_op jit(solution)/shard_map/ppermute | solution.py:172
  36.7 16.3 %collective-permute-start = (f32[4,104,128]{2,1,0:T(8,128)S(1)}, f32[4,104,128]{2,1,0:T(8,128)S(1)}, u32[]{:S(2)}, u32[]{:S(2)}) collective-permute-start(f32[4,104,128]{2,1,0:T(8,128)S(1)} %get-tuple-element.12.refs_0_), channel_id=1, source_target_pairs={{0,64},{64,128},{128,192},{192,256},{256,320},{320,384},{384,448},... | collective-permute-start | bytes 638984 | tf_op jit(solution)/shard_map/ppermute | solution.py:172
  42.0 22.1 %collective-permute-start.4 = (f32[4,104,128]{2,1,0:T(8,128)S(1)}, f32[4,104,128]{2,1,0:T(8,128)S(1)}, u32[]{:S(2)}, u32[]{:S(2)}) collective-permute-start(f32[4,104,128]{2,1,0:T(8,128)S(1)} %collective-permute-done.3.refs_7_), channel_id=1, source_target_pairs={{0,448},{64,0},{128,64},{192,128},{256,192},{320,256},{384,320},{4... | collective-permute-start | bytes 638984 | tf_op jit(solution)/shard_map/ppermute | solution.py:172
  53.0 18.2 %collective-permute-start.1 = (f32[4,104,128]{2,1,0:T(8,128)S(1)}, f32[4,104,128]{2,1,0:T(8,128)S(1)}, u32[]{:S(2)}, u32[]{:S(2)}) collective-permute-start(f32[4,104,128]{2,1,0:T(8,128)S(1)} %collective-permute-done.refs_1_), channel_id=1, source_target_pairs={{0,64},{64,128},{128,192},{192,256},{256,320},{320,384},{384,448},... | collective-permute-start | bytes 638984 | tf_op jit(solution)/shard_map/ppermute | solution.py:172
  64.1 12.4 %collective-permute-start.5 = (f32[4,104,128]{2,1,0:T(8,128)S(1)}, f32[4,104,128]{2,1,0:T(8,128)S(1)}, u32[]{:S(2)}, u32[]{:S(2)}) collective-permute-start(f32[4,104,128]{2,1,0:T(8,128)S(1)} %collective-permute-done.4.refs_6_), channel_id=1, source_target_pairs={{0,448},{64,0},{128,64},{192,128},{256,192},{320,256},{384,320},{4... | collective-permute-start | bytes 638984 | tf_op jit(solution)/shard_map/ppermute | solution.py:172
  71.3 14.4 %collective-permute-start.2 = (f32[4,104,128]{2,1,0:T(8,128)S(1)}, f32[4,104,128]{2,1,0:T(8,128)S(1)}, u32[]{:S(2)}, u32[]{:S(2)}) collective-permute-start(f32[4,104,128]{2,1,0:T(8,128)S(1)} %collective-permute-done.1.refs_2_), channel_id=1, source_target_pairs={{0,64},{64,128},{128,192},{192,256},{256,320},{320,384},{384,448},... | collective-permute-start | bytes 638984 | tf_op jit(solution)/shard_map/ppermute | solution.py:172
  138.1 18.1 %collective-permute-start.7 = (f32[8,2,40,640]{3,2,1,0:T(8,128)}, f32[8,2,40,640]{3,2,1,0:T(8,128)S(1)}, u32[]{:S(2)}, u32[]{:S(2)}) collective-permute-start(f32[8,2,40,640]{3,2,1,0:T(8,128)} %bitcast.11), channel_id=1, source_target_pairs={{0,1},{1,0},{2,3},{3,2},{4,5},{5,4},{6,7},{7,6},{8,9},{9,8},{10,11... | collective-permute-start | bytes 4915208 | tf_op jit(solution)/shard_map/ppermute | solution.py:172
  140.0 16.2 %collective-permute-start.6 = (f32[4,104,128]{2,1,0:T(8,128)S(1)}, f32[4,104,128]{2,1,0:T(8,128)S(1)}, u32[]{:S(2)}, u32[]{:S(2)}) collective-permute-start(f32[4,104,128]{2,1,0:T(8,128)S(1)} %collective-permute-done.2.refs_3_), channel_id=1, source_target_pairs={{0,64},{64,128},{128,192},{192,256},{256,320},{320,384},{384,448},... | collective-permute-start | bytes 638984 | tf_op jit(solution)/shard_map/ppermute | solution.py:172
  156.2 1.4 copy-start.3
  161.9 16.6 %copy-start.2 = (s32[20,20]{1,0:T(8,128)S(1)}, s32[20,20]{1,0:T(8,128)}, u32[]{:S(2)}) copy-start(s32[20,20]{1,0:T(8,128)} %pattern_ref.3) | copy-start | bytes 4804
Sparse Core Ops, SparseCore 0:
  23.7 114.3 all-gather.2

commit v9 on v7

--- a/solution.py
+++ b/solution.py
@@ -61,7 +61,9 @@
             out_ref[y, rows] = masked_ref[RUN * y : RUN * y + RUN, 128 * h : 128 * h + 128]
 
 
-def far_kernel(at_ref, pattern_ref, state_ref, out_ref, masked_ref):
+def far_kernel(at_ref, pattern_ref, top_ref, bottom_ref, out_ref, state_ref, masked_ref):
+    state_ref[:40] = top_ref[...]
+    state_ref[40:] = bottom_ref[...]
     owner = at_ref[0] + 2 - 4 * at_ref[2]
     pack_right(at_ref, owner, pattern_ref, state_ref, masked_ref, out_ref, 0)
 
@@ -117,19 +119,18 @@
 
 def product_kernel(at_ref, *refs):
     lefts, rights, out_ref, hi_ref, lo_ref = refs[:8], refs[8:12], *refs[12:]
+    zl = at_ref[1]
     for part, ref in enumerate(rights):
-        for dx in range(4):
+        rows = slice(40 * part, 40 * part + 40)
+        for x in range(4):
             for y1 in range(2):
-                hi, lo = split(ref[dx, y1])
-                rows = slice(40 * part, 40 * part + 40)
-                hi_ref[2 * dx + y1, rows] = hi
-                lo_ref[2 * dx + y1, rows] = lo
+                hi, lo = split(ref[x, y1])
+                hi_ref[2 * x + y1, rows] = hi
+                lo_ref[2 * x + y1, rows] = lo
     lane = lax.broadcasted_iota(jnp.int32, (8, 128), 1) // 32
-    zl, x = at_ref[1], at_ref[4]
     total = jnp.zeros((320, 640), jnp.float32)
     for d, ref in enumerate(lefts):
-        source = lax.rem(zl - d + 8, 8)
-        block = 2 * lax.rem(x - source // 2 + 4, 4) + lax.rem(source, 2)
+        block = lax.rem(zl - d + 8, 8)
         whole = []
         for y in range(4):
             rest = []
@@ -181,8 +182,12 @@
     return lax.ppermute(x, axis_name, [(i, (i + by) % size) for i in range(size)])
 
 
-def across_x(block):
-    return jnp.stack([block] + [shift(block, "x", by) for by in (1, 2, 3)], 0)
+def shift_z(x, by):
+    pairs = []
+    for z in range(16):
+        to = (z + by) % 16
+        pairs.append((z % 8 * 2 + z // 8, to % 8 * 2 + to // 8))
+    return lax.ppermute(x, ("zl", "zh"), pairs)
 
 
 def f32(*shape):
@@ -193,42 +198,46 @@
     rows, cols = state.shape
     nodes = cols * lax.axis_size("zl")
     at = jnp.stack(
-        [lax.axis_index(ROWS)] + [lax.axis_index(a) for a in ("zl", "zh", "c", "x")]
+        [lax.axis_index(ROWS)] + [lax.axis_index(a) for a in ("zl", "zh", "c")]
     ).astype(jnp.int32)
 
     tie = lax.optimization_barrier
-    work = [pltpu.VMEM((rows, cols), jnp.float32)]
-    far = shift(state, "zh", 1)
+    work = pltpu.VMEM((rows, cols), jnp.float32)
+    top, bottom = shift_z(state[:40], 4), shift_z(state[40:], -4)
     pieces = call(
-        pieces_kernel,
-        f32(4, PIECE, 128),
-        [SMEM, SMEM, VMEM],
-        (at, in_pattern, state),
-        work,
+        pieces_kernel, f32(4, PIECE, 128), [SMEM, SMEM, VMEM], (at, in_pattern, state), [work]
     )
     got = lax.all_to_all(pieces, "y", 0, 0)
+    top, bottom, got = tie((top, bottom, got))
+
+    top, bottom = shift_z(top, 4), shift_z(bottom, -4)
     left, near = call(
         unpack_kernel, (f32(4, LEFT, 128), f32(2, 2 * RUN, cols)), [VMEM], (got,)
     )
-    near = across_x(near)
-    left, near, far = tie((left, near, far))
+    near = lax.all_gather(near, "x", axis=0)
+    top, bottom, left, near = tie((top, bottom, left, near))
 
     up, down = shift(left, "zl", 1), shift(left, "zl", -1)
     far = call(
-        far_kernel, f32(4, 5 * PAD, 128), [SMEM, SMEM, VMEM], (at, in_pattern, far), work
+        far_kernel,
+        f32(4, 5 * PAD, 128),
+        [SMEM, SMEM, VMEM, VMEM],
+        (at, in_pattern, top, bottom),
+        [work, work],
     )
     far = lax.all_to_all(far, "y", 0, 0)
     far = call(unpack_far_kernel, f32(2, 2 * RUN, cols), [VMEM], (far,))
     lefts = [left, up, None, None, None, None, None, down]
-    up, down, far = tie((up, down, far))
+    up, down, far, near = tie((up, down, far, near))
 
     up, down = shift(up, "zl", 1), shift(down, "zl", -1)
-    far = across_x(far)
+    far = lax.all_gather(far, "x", axis=0)
+    near_swapped = shift(near, "c", 1)
     lefts[2], lefts[6] = up, down
-    up, down, far = tie((up, down, far))
+    up, down, far, near_swapped = tie((up, down, far, near_swapped))
 
     up, down = shift(up, "zl", 1), shift(down, "zl", -1)
-    near_swapped, far_swapped = shift(near, "c", 1), shift(far, "c", 1)
+    far_swapped = shift(far, "c", 1)
     lefts[3], lefts[5] = up, down
     lefts[4] = shift(up, "zl", 1)
 

time: 172 us -> 177 us (1.029)
  blocking collectives: 49.1 us -> 67.4 us
  starting transfers between devices: 85.5 us -> 68.4 us
  waiting for transfers between devices: 25.5 us -> 29.7 us
    ppermute x16 -> x9, starting transfers between devices: 85.5 us -> 39.4 us  [shift(): lax.ppermute(x, axis_name, [(i, (i + by) % size) for i in range(size)])]
    all_gather x0 -> x2, blocking collectives: none -> 28.1 us  [the longest x1 14.4 us: body(): far = lax.all_gather(far, 'x', axis=0)]
    ppermute x0 -> x4, starting transfers between devices: none -> 24.4 us  [shift_z(): return lax.ppermute(x, ('zl', 'zh'), pairs)]
    all_to_all x1 -> x0, blocking collectives: 13 us -> none  [body(): got = lax.all_to_all(pieces, 'y', 0, 0)]
    ppermute x0 -> x4, waiting for transfers between devices: none -> 11.9 us  [shift_z(): return lax.ppermute(x, ('zl', 'zh'), pairs)]
    ppermute x16 -> x9, waiting for transfers between devices: 25.5 us -> 17.8 us  [shift(): lax.ppermute(x, axis_name, [(i, (i + by) % size) for i in range(size)])]
    all_to_all x0 -> x1, starting transfers between devices: none -> 4.6 us  [body(): got = lax.all_to_all(pieces, 'y', 0, 0)]
    all_to_all x1, blocking collectives: 8.97 us -> 10.9 us  [body(): far = lax.all_to_all(far, 'y', 0, 0)]
  transfers between devices with their start and end apart: 16 -> 14, of which waited for: 6 -> 5; matrix products, arithmetic and copies ran while one was open for 0% -> 0% of each run, Pallas kernels for 0% -> 0%
where the time goes in v9:
time: 177 us
  starting transfers between devices  68.4 us (39%)
  blocking collectives  67.4 us (38%)
  waiting for transfers between devices  29.7 us (17%)
  Pallas kernels  9.39 us (5%)
    ppermute x9, starting transfers between devices, shift(): lax.ppermute(x, axis_name, [(i, (i + by) % size) for i in range(size)])  39.4 us
    ppermute x4, starting transfers between devices, shift_z(): return lax.ppermute(x, ('zl', 'zh'), pairs)  24.4 us
    ppermute x9, waiting for transfers between devices, shift(): lax.ppermute(x, axis_name, [(i, (i + by) % size) for i in range(size)])  17.8 us
    all_to_all x1, blocking collectives, body(): shares = lax.all_to_all(partial, 'y', 0, 0)  15.5 us
    all_gather x1, blocking collectives, body(): far = lax.all_gather(far, 'x', axis=0)  14.4 us
    all_gather x1, blocking collectives, body(): near = lax.all_gather(near, 'x', axis=0)  13.8 us
    all_to_all x1, blocking collectives, body(): sums = lax.all_to_all(sums.reshape(8, 1, rows), 'zl', 0, 0).reshape(8, rows)  12.8 us
    ppermute x4, waiting for transfers between devices, shift_z(): return lax.ppermute(x, ('zl', 'zh'), pairs)  11.9 us
  transfers between devices with their start and end apart: 14, of which 5 were waited for; matrix products, arithmetic and copies ran while one was open for 0% of the time, Pallas kernels for 0%

profile of v9, /device:TPU:6, one launch (start us, length us, event | category | flops | bytes accessed | tf_op | source)
XLA Modules:
  0.0 176.7 jit_solution(5859127826165461882)
XLA Ops:
  1.6 2.3 %shard_map.37 = f32[4,224,128]{2,1,0:T(8,128)} custom-call(s32[4]{0:T(128)S(1)} %pad_add_fusion.at_ref, s32[20,20]{1,0:T(8,128)S(1)} %copy-done.2, f32[80,640]{1,0:T(8,128)S(1)} %copy-done), custom_call_target="tpu_custom_call" | custom-call | flops 1000000 | bytes 1000000 | tf_op jit(solution)/shard_map/pallas_call | solution.py:30
  3.9 4.6 %all-to-all-start = ((f32[4,224,128]{2,1,0:T(8,128)}), f32[4,224,128]{2,1,0:T(8,128)S(1)}, u32[]{:S(2)}, u32[]{:S(2)}) async-start(f32[4,224,128]{2,1,0:T(8,128)} %shard_map.37), calls=%async_computation | async-start | bytes 917504 | tf_op jit(solution)/shard_map/all_to_all | solution.py:210
  8.5 12.7 %collective-permute-start.1 = (f32[40,640]{1,0:T(8,128)S(1)}, f32[40,640]{1,0:T(8,128)S(1)}, u32[]{:S(2)}, u32[]{:S(2)}) collective-permute-start(f32[40,640]{1,0:T(8,128)S(1)} %get-tuple-element.43), channel_id=1, source_target_pairs={{0,258},{64,322},{128,386},{192,450},{256,0},{320,64},{384,128},{4... | collective-permute-start | bytes 307208 | tf_op jit(solution)/shard_map/ppermute | solution.py:190
  21.3 1.9 %collective-permute-start = (f32[40,640]{1,0:T(8,128)S(1)}, f32[40,640]{1,0:T(8,128)S(1)}, u32[]{:S(2)}, u32[]{:S(2)}) collective-permute-start(f32[40,640]{1,0:T(8,128)S(1)} %get-tuple-element.44), channel_id=1, source_target_pairs={{0,256},{64,320},{128,384},{192,448},{256,2},{320,66},{384,130},{4... | collective-permute-start | bytes 307208 | tf_op jit(solution)/shard_map/ppermute | solution.py:190
  23.2 6.5 %collective-permute-done.1 = f32[40,640]{1,0:T(8,128)S(1)} collective-permute-done((f32[40,640]{1,0:T(8,128)S(1)}, f32[40,640]{1,0:T(8,128)S(1)}, u32[]{:S(2)}, u32[]{:S(2)}) %collective-permute-start.1) | collective-permute-done | bytes 102432 | tf_op jit(solution)/shard_map/ppermute | solution.py:190
  29.7 5.3 %collective-permute-done = f32[40,640]{1,0:T(8,128)S(1)} collective-permute-done((f32[40,640]{1,0:T(8,128)S(1)}, f32[40,640]{1,0:T(8,128)S(1)}, u32[]{:S(2)}, u32[]{:S(2)}) %collective-permute-start) | collective-permute-done | bytes 102432 | tf_op jit(solution)/shard_map/ppermute | solution.py:190
  35.1 1.9 %collective-permute-start.2 = (f32[40,640]{1,0:T(8,128)S(1)}, f32[40,640]{1,0:T(8,128)S(1)}, u32[]{:S(2)}, u32[]{:S(2)}) collective-permute-start(f32[40,640]{1,0:T(8,128)S(1)} %collective-permute-done), channel_id=1, source_target_pairs={{0,256},{64,320},{128,384},{192,448},{256,2},{320,66},{384,130},{4... | collective-permute-start | bytes 307208 | tf_op jit(solution)/shard_map/ppermute | solution.py:190
  37.0 7.8 %collective-permute-start.3 = (f32[40,640]{1,0:T(8,128)S(1)}, f32[40,640]{1,0:T(8,128)S(1)}, u32[]{:S(2)}, u32[]{:S(2)}) collective-permute-start(f32[40,640]{1,0:T(8,128)S(1)} %collective-permute-done.1), channel_id=1, source_target_pairs={{0,258},{64,322},{128,386},{192,450},{256,0},{320,64},{384,128},{4... | collective-permute-start | bytes 307208 | tf_op jit(solution)/shard_map/ppermute | solution.py:190
  44.9 13.8 %all-gather = f32[8,40,640]{2,1,0:T(8,128)S(1)} all-gather(f32[2,40,640]{2,1,0:T(8,128)S(1)} %get-tuple-element.28), channel_id=2, replica_groups=mesh['zl'=8,'x'=4,'y'=4,'zh'=2,'c'=2] {'x'}, dimensions={0}, use_global_device_ids=true | all-gather | bytes 1024000 | tf_op jit(solution)/shard_map/all_gather | solution.py:217
  58.6 6.9 %collective-permute-start.5 = (f32[4,104,128]{2,1,0:T(8,128)S(1)}, f32[4,104,128]{2,1,0:T(8,128)S(1)}, u32[]{:S(2)}, u32[]{:S(2)}) collective-permute-start(f32[4,104,128]{2,1,0:T(8,128)S(1)} %get-tuple-element.29.refs_0_), channel_id=1, source_target_pairs={{0,448},{64,0},{128,64},{192,128},{256,192},{320,256},{384,320},{4... | collective-permute-start | bytes 638984 | tf_op jit(solution)/shard_map/ppermute | solution.py:182
  65.5 1.9 %collective-permute-start.4 = (f32[4,104,128]{2,1,0:T(8,128)S(1)}, f32[4,104,128]{2,1,0:T(8,128)S(1)}, u32[]{:S(2)}, u32[]{:S(2)}) collective-permute-start(f32[4,104,128]{2,1,0:T(8,128)S(1)} %get-tuple-element.29.refs_0_), channel_id=1, source_target_pairs={{0,64},{64,128},{128,192},{192,256},{256,320},{320,384},{384,448},... | collective-permute-start | bytes 638984 | tf_op jit(solution)/shard_map/ppermute | solution.py:182
  68.3 10.9 %all_to_all.20.got_ref = f32[4,120,128]{2,1,0:T(8,128)S(1)} all-to-all(f32[4,120,128]{2,1,0:T(8,128)S(1)} %shard_map.39), channel_id=1, replica_groups=mesh['zl'=8,'x'=4,'y'=4,'zh'=2,'c'=2] {'y'}, dimensions={0} | all-to-all | bytes 491520 | tf_op jit(solution)/shard_map/all_to_all | solution.py:228
  79.9 1.9 %collective-permute-start.8 = (f32[4,2,40,640]{3,2,1,0:T(8,128)S(1)}, f32[4,2,40,640]{3,2,1,0:T(8,128)S(1)}, u32[]{:S(2)}, u32[]{:S(2)}) collective-permute-start(f32[4,2,40,640]{3,2,1,0:T(8,128)S(1)} %bitcast.10), channel_id=1, source_target_pairs={{0,1},{1,0},{2,3},{3,2},{4,5},{5,4},{6,7},{7,6},{8,9},{9,8},{10,11... | collective-permute-start | bytes 2457608 | tf_op jit(solution)/shard_map/ppermute | solution.py:182
  81.8 1.9 %collective-permute-start.6 = (f32[4,104,128]{2,1,0:T(8,128)S(1)}, f32[4,104,128]{2,1,0:T(8,128)S(1)}, u32[]{:S(2)}, u32[]{:S(2)}) collective-permute-start(f32[4,104,128]{2,1,0:T(8,128)S(1)} %collective-permute-done.4.refs_1_), channel_id=1, source_target_pairs={{0,64},{64,128},{128,192},{192,256},{256,320},{320,384},{384,448},... | collective-permute-start | bytes 638984 | tf_op jit(solution)/shard_map/ppermute | solution.py:182
  83.7 10.5 %collective-permute-start.7 = (f32[4,104,128]{2,1,0:T(8,128)S(1)}, f32[4,104,128]{2,1,0:T(8,128)S(1)}, u32[]{:S(2)}, u32[]{:S(2)}) collective-permute-start(f32[4,104,128]{2,1,0:T(8,128)S(1)} %collective-permute-done.5.refs_7_), channel_id=1, source_target_pairs={{0,448},{64,0},{128,64},{192,128},{256,192},{320,256},{384,320},{4... | collective-permute-start | bytes 638984 | tf_op jit(solution)/shard_map/ppermute | solution.py:182
  94.2 14.4 %all-gather.1 = f32[8,40,640]{2,1,0:T(8,128)S(1)} all-gather(f32[2,40,640]{2,1,0:T(8,128)S(1)} %shard_map.40), channel_id=3, replica_groups=mesh['zl'=8,'x'=4,'y'=4,'zh'=2,'c'=2] {'x'}, dimensions={0}, use_global_device_ids=true | all-gather | bytes 1024000 | tf_op jit(solution)/shard_map/all_gather | solution.py:234
  108.6 1.9 %collective-permute-start.12 = (f32[4,2,40,640]{3,2,1,0:T(8,128)S(1)}, f32[4,2,40,640]{3,2,1,0:T(8,128)S(1)}, u32[]{:S(2)}, u32[]{:S(2)}) collective-permute-start(f32[4,2,40,640]{3,2,1,0:T(8,128)S(1)} %bitcast.12), channel_id=1, source_target_pairs={{0,1},{1,0},{2,3},{3,2},{4,5},{5,4},{6,7},{7,6},{8,9},{9,8},{10,11... | collective-permute-start | bytes 2457608 | tf_op jit(solution)/shard_map/ppermute | solution.py:182
  110.6 1.9 %collective-permute-start.9 = (f32[4,104,128]{2,1,0:T(8,128)S(1)}, f32[4,104,128]{2,1,0:T(8,128)S(1)}, u32[]{:S(2)}, u32[]{:S(2)}) collective-permute-start(f32[4,104,128]{2,1,0:T(8,128)S(1)} %collective-permute-done.6.refs_2_), channel_id=1, source_target_pairs={{0,64},{64,128},{128,192},{192,256},{256,320},{320,384},{384,448},... | collective-permute-start | bytes 638984 | tf_op jit(solution)/shard_map/ppermute | solution.py:182
  112.5 10.5 %collective-permute-start.11 = (f32[4,104,128]{2,1,0:T(8,128)S(1)}, f32[4,104,128]{2,1,0:T(8,128)S(1)}, u32[]{:S(2)}, u32[]{:S(2)}) collective-permute-start(f32[4,104,128]{2,1,0:T(8,128)S(1)} %collective-permute-done.7.refs_6_), channel_id=1, source_target_pairs={{0,448},{64,0},{128,64},{192,128},{256,192},{320,256},{384,320},{4... | collective-permute-start | bytes 638984 | tf_op jit(solution)/shard_map/ppermute | solution.py:182
  123.0 4.1 %collective-permute-done.9.refs_3_ = f32[4,104,128]{2,1,0:T(8,128)S(1)} collective-permute-done((f32[4,104,128]{2,1,0:T(8,128)S(1)}, f32[4,104,128]{2,1,0:T(8,128)S(1)}, u32[]{:S(2)}, u32[]{:S(2)}) %collective-permute-start.9) | collective-permute-done | bytes 213024 | tf_op jit(solution)/shard_map/ppermute | solution.py:182
  129.0 13.0 %collective-permute-done.10.refs_4_ = f32[4,104,128]{2,1,0:T(8,128)S(1)} collective-permute-done((f32[4,104,128]{2,1,0:T(8,128)S(1)}, f32[4,104,128]{2,1,0:T(8,128)S(1)}, u32[]{:S(2)}, u32[]{:S(2)}) %collective-permute-start.10) | collective-permute-done | bytes 213024 | tf_op jit(solution)/shard_map/ppermute | solution.py:182
  142.1 4.3 %shard_map.41 = f32[4,80,640]{2,1,0:T(8,128)S(1)} custom-call(s32[4]{0:T(128)S(1)} %pad_add_fusion.at_ref, f32[4,104,128]{2,1,0:T(8,128)S(1)} %get-tuple-element.29.refs_0_, f32[4,104,128]{2,1,0:T(8,128)S(1)} %collective-permute-done.4.refs_1_, f32[4,104,128]{2,1,0:T(8,128)S(1)} %collective-permute-done.6.refs_2_, ...), custom_call_target="tpu_custom_call" | custom-call | flops 3000000000 | bytes 6000000 | tf_op jit(solution)/shard_map/pallas_call | solution.py:30
  146.4 15.5 %all_to_all.21.shares_ref = f32[4,80,640]{2,1,0:T(8,128)S(1)} all-to-all(f32[4,80,640]{2,1,0:T(8,128)S(1)} %shard_map.41), channel_id=1, replica_groups=mesh['zl'=8,'x'=4,'y'=4,'zh'=2,'c'=2] {'y'}, dimensions={0} | all-to-all | bytes 1638400 | tf_op jit(solution)/shard_map/all_to_all | solution.py:253
  163.0 12.8 %all_to_all.22 = f32[8,1,80]{2,1,0:T(1,128)S(1)} all-to-all(f32[8,1,80]{2,1,0:T(1,128)S(1)} %bitcast.15), channel_id=1, replica_groups=mesh['zl'=8,'x'=4,'y'=4,'zh'=2,'c'=2] {'zl'}, dimensions={0} | all-to-all | bytes 5120 | tf_op jit(solution)/shard_map/all_to_all | solution.py:260
  (26 shorter events, 7.1 us)
Async XLA Ops:
  0.0 0.7 copy-start.2
  0.7 0.9 copy-start
  3.9 4.6 %copy-start.1 = (f32[80,640]{1,0:T(8,128)S(1)}, f32[80,640]{1,0:T(8,128)}, u32[]{:S(2)}) copy-start(f32[80,640]{1,0:T(8,128)} %state_ref.1) | copy-start | bytes 614404
  3.9 31.1 %all-to-all-start = ((f32[4,224,128]{2,1,0:T(8,128)}), f32[4,224,128]{2,1,0:T(8,128)S(1)}, u32[]{:S(2)}, u32[]{:S(2)}) async-start(f32[4,224,128]{2,1,0:T(8,128)} %shard_map.37), calls=%async_computation | async-start | bytes 917504 | tf_op jit(solution)/shard_map/all_to_all | solution.py:210
  8.5 21.2 %collective-permute-start.1 = (f32[40,640]{1,0:T(8,128)S(1)}, f32[40,640]{1,0:T(8,128)S(1)}, u32[]{:S(2)}, u32[]{:S(2)}) collective-permute-start(f32[40,640]{1,0:T(8,128)S(1)} %get-tuple-element.43), channel_id=1, source_target_pairs={{0,258},{64,322},{128,386},{192,450},{256,0},{320,64},{384,128},{4... | collective-permute-start | bytes 307208 | tf_op jit(solution)/shard_map/ppermute | solution.py:190
  21.3 13.8 %collective-permute-start = (f32[40,640]{1,0:T(8,128)S(1)}, f32[40,640]{1,0:T(8,128)S(1)}, u32[]{:S(2)}, u32[]{:S(2)}) collective-permute-start(f32[40,640]{1,0:T(8,128)S(1)} %get-tuple-element.44), channel_id=1, source_target_pairs={{0,256},{64,320},{128,384},{192,448},{256,2},{320,66},{384,130},{4... | collective-permute-start | bytes 307208 | tf_op jit(solution)/shard_map/ppermute | solution.py:190
  35.1 23.6 %collective-permute-start.2 = (f32[40,640]{1,0:T(8,128)S(1)}, f32[40,640]{1,0:T(8,128)S(1)}, u32[]{:S(2)}, u32[]{:S(2)}) collective-permute-start(f32[40,640]{1,0:T(8,128)S(1)} %collective-permute-done), channel_id=1, source_target_pairs={{0,256},{64,320},{128,384},{192,448},{256,2},{320,66},{384,130},{4... | collective-permute-start | bytes 307208 | tf_op jit(solution)/shard_map/ppermute | solution.py:190
  37.0 21.6 %collective-permute-start.3 = (f32[40,640]{1,0:T(8,128)S(1)}, f32[40,640]{1,0:T(8,128)S(1)}, u32[]{:S(2)}, u32[]{:S(2)}) collective-permute-start(f32[40,640]{1,0:T(8,128)S(1)} %collective-permute-done.1), channel_id=1, source_target_pairs={{0,258},{64,322},{128,386},{192,450},{256,0},{320,64},{384,128},{4... | collective-permute-start | bytes 307208 | tf_op jit(solution)/shard_map/ppermute | solution.py:190
  58.6 20.6 %collective-permute-start.5 = (f32[4,104,128]{2,1,0:T(8,128)S(1)}, f32[4,104,128]{2,1,0:T(8,128)S(1)}, u32[]{:S(2)}, u32[]{:S(2)}) collective-permute-start(f32[4,104,128]{2,1,0:T(8,128)S(1)} %get-tuple-element.29.refs_0_), channel_id=1, source_target_pairs={{0,448},{64,0},{128,64},{192,128},{256,192},{320,256},{384,320},{4... | collective-permute-start | bytes 638984 | tf_op jit(solution)/shard_map/ppermute | solution.py:182
  65.5 14.3 %collective-permute-start.4 = (f32[4,104,128]{2,1,0:T(8,128)S(1)}, f32[4,104,128]{2,1,0:T(8,128)S(1)}, u32[]{:S(2)}, u32[]{:S(2)}) collective-permute-start(f32[4,104,128]{2,1,0:T(8,128)S(1)} %get-tuple-element.29.refs_0_), channel_id=1, source_target_pairs={{0,64},{64,128},{128,192},{192,256},{256,320},{320,384},{384,448},... | collective-permute-start | bytes 638984 | tf_op jit(solution)/shard_map/ppermute | solution.py:182
  79.9 28.8 %collective-permute-start.8 = (f32[4,2,40,640]{3,2,1,0:T(8,128)S(1)}, f32[4,2,40,640]{3,2,1,0:T(8,128)S(1)}, u32[]{:S(2)}, u32[]{:S(2)}) collective-permute-start(f32[4,2,40,640]{3,2,1,0:T(8,128)S(1)} %bitcast.10), channel_id=1, source_target_pairs={{0,1},{1,0},{2,3},{3,2},{4,5},{5,4},{6,7},{7,6},{8,9},{9,8},{10,11... | collective-permute-start | bytes 2457608 | tf_op jit(solution)/shard_map/ppermute | solution.py:182
  81.8 26.9 %collective-permute-start.6 = (f32[4,104,128]{2,1,0:T(8,128)S(1)}, f32[4,104,128]{2,1,0:T(8,128)S(1)}, u32[]{:S(2)}, u32[]{:S(2)}) collective-permute-start(f32[4,104,128]{2,1,0:T(8,128)S(1)} %collective-permute-done.4.refs_1_), channel_id=1, source_target_pairs={{0,64},{64,128},{128,192},{192,256},{256,320},{320,384},{384,448},... | collective-permute-start | bytes 638984 | tf_op jit(solution)/shard_map/ppermute | solution.py:182
  83.7 24.9 %collective-permute-start.7 = (f32[4,104,128]{2,1,0:T(8,128)S(1)}, f32[4,104,128]{2,1,0:T(8,128)S(1)}, u32[]{:S(2)}, u32[]{:S(2)}) collective-permute-start(f32[4,104,128]{2,1,0:T(8,128)S(1)} %collective-permute-done.5.refs_7_), channel_id=1, source_target_pairs={{0,448},{64,0},{128,64},{192,128},{256,192},{320,256},{384,320},{4... | collective-permute-start | bytes 638984 | tf_op jit(solution)/shard_map/ppermute | solution.py:182
  108.6 33.4 %collective-permute-start.12 = (f32[4,2,40,640]{3,2,1,0:T(8,128)S(1)}, f32[4,2,40,640]{3,2,1,0:T(8,128)S(1)}, u32[]{:S(2)}, u32[]{:S(2)}) collective-permute-start(f32[4,2,40,640]{3,2,1,0:T(8,128)S(1)} %bitcast.12), channel_id=1, source_target_pairs={{0,1},{1,0},{2,3},{3,2},{4,5},{5,4},{6,7},{7,6},{8,9},{9,8},{10,11... | collective-permute-start | bytes 2457608 | tf_op jit(solution)/shard_map/ppermute | solution.py:182
  110.6 16.5 %collective-permute-start.9 = (f32[4,104,128]{2,1,0:T(8,128)S(1)}, f32[4,104,128]{2,1,0:T(8,128)S(1)}, u32[]{:S(2)}, u32[]{:S(2)}) collective-permute-start(f32[4,104,128]{2,1,0:T(8,128)S(1)} %collective-permute-done.6.refs_2_), channel_id=1, source_target_pairs={{0,64},{64,128},{128,192},{192,256},{256,320},{320,384},{384,448},... | collective-permute-start | bytes 638984 | tf_op jit(solution)/shard_map/ppermute | solution.py:182
  112.5 16.5 %collective-permute-start.11 = (f32[4,104,128]{2,1,0:T(8,128)S(1)}, f32[4,104,128]{2,1,0:T(8,128)S(1)}, u32[]{:S(2)}, u32[]{:S(2)}) collective-permute-start(f32[4,104,128]{2,1,0:T(8,128)S(1)} %collective-permute-done.7.refs_6_), channel_id=1, source_target_pairs={{0,448},{64,0},{128,64},{192,128},{256,192},{320,256},{384,320},{4... | collective-permute-start | bytes 638984 | tf_op jit(solution)/shard_map/ppermute | solution.py:182
  127.1 15.0 %collective-permute-start.10 = (f32[4,104,128]{2,1,0:T(8,128)S(1)}, f32[4,104,128]{2,1,0:T(8,128)S(1)}, u32[]{:S(2)}, u32[]{:S(2)}) collective-permute-start(f32[4,104,128]{2,1,0:T(8,128)S(1)} %collective-permute-done.9.refs_3_), channel_id=1, source_target_pairs={{0,64},{64,128},{128,192},{192,256},{256,320},{320,384},{384,448},... | collective-permute-start | bytes 638984 | tf_op jit(solution)/shard_map/ppermute | solution.py:182
  146.4 15.5 %copy-start.3 = (s32[20,20]{1,0:T(8,128)S(1)}, s32[20,20]{1,0:T(8,128)}, u32[]{:S(2)}) copy-start(s32[20,20]{1,0:T(8,128)} %pattern_ref.5) | copy-start | bytes 4804

commit v10 on v0

v10 whole, which is shorter than its diff:
```python
import functools

import jax
import jax.numpy as jnp
from jax import lax
from jax.experimental import pallas as pl
from jax.experimental.pallas import tpu as pltpu
from jax.sharding import Mesh, PartitionSpec as P

BLK = 256
ROWS = ("x", "y", "zh", "c")
SLOTS = 248
ALL = 400
UNITS = 56
VMEM = pl.BlockSpec(memory_space=pltpu.VMEM)
SMEM = pl.BlockSpec(memory_space=pltpu.SMEM)
EXACT = lax.Precision.HIGHEST


def iota(shape, axis):
    return lax.broadcasted_iota(jnp.int32, shape, axis)


def one_hot(mask):
    return mask.astype(jnp.float32).astype(jnp.bfloat16)


def split(x):
    hi = x.astype(jnp.bfloat16)
    return hi, (x - hi.astype(jnp.float32)).astype(jnp.bfloat16)


def split3(x):
    hi = x.astype(jnp.bfloat16)
    return (hi, *split(x - hi.astype(jnp.float32)))


def dot(a, b, precision=None):
    return jnp.dot(a, b, preferred_element_type=jnp.float32, precision=precision)


def dot_rows(a, b, precision=None):
    return lax.dot_general(
        a, b, (((1,), (1,)), ((), ())), precision=precision, preferred_element_type=jnp.float32
    )


def call(kernel, outs, in_specs, args, out_specs=None, scratch=(), flops=10**6, size=10**6):
    return pl.pallas_call(
        kernel,
        out_shape=outs,
        in_specs=in_specs,
        out_specs=out_specs or jax.tree.map(lambda _: VMEM, outs),
        scratch_shapes=scratch,
        compiler_params=pltpu.CompilerParams(vmem_limit_bytes=48 * 2**20),
        cost_estimate=pl.CostEstimate(flops=flops, bytes_accessed=size, transcendentals=0),
    )(*args)


def chunk_of(q, zh, c):
    return 20 * (q // 5) + 10 * zh + 5 * c + q % 5


def places(pattern, zh, c):
    rows = one_hot(chunk_of(iota((80, 1), 0), zh, c) // 16 == iota((80, 20), 1))
    cols = one_hot(iota((20, 40), 1) // 2 == iota((20, 40), 0))
    live = dot(dot(rows, pattern).astype(jnp.bfloat16), cols)
    before = dot(one_hot(iota((80, 80), 1) < iota((80, 80), 0)), live.astype(jnp.bfloat16))
    total = jnp.broadcast_to(jnp.sum(live, axis=0, keepdims=True), (80, 40))
    a, b = iota((40, 40), 0), iota((40, 40), 1)
    earlier = dot(total.astype(jnp.bfloat16), one_hot((a // 5 == b // 5) & (a < b)))
    return jnp.where(live > 0, before + earlier, -1.0)


def places_across(pattern, zh, c):
    rows = one_hot(chunk_of(iota((1, 80), 1), zh, c) // 16 == iota((20, 80), 0))
    cols = one_hot(iota((40, 20), 0) // 2 == iota((40, 20), 1))
    live = dot(dot_rows(cols, pattern).astype(jnp.bfloat16), rows)
    before = dot(live.astype(jnp.bfloat16), one_hot(iota((80, 80), 0) < iota((80, 80), 1)))
    total = jnp.broadcast_to(jnp.sum(live, axis=1, keepdims=True), (40, 80))
    a, b = iota((40, 40), 1), iota((40, 40), 0)
    earlier = dot(one_hot((a // 5 == b // 5) & (a < b)), total.astype(jnp.bfloat16))
    return jnp.where(live > 0, before + earlier, -1.0)


def units_kernel(pattern_ref, state_ref, out_ref, most_ref, moved_ref, plain_ref):
    pattern = pattern_ref[...].astype(jnp.float32).astype(jnp.bfloat16)
    counts = []
    for group in range(4):
        rows = chunk_of(iota((80, 1), 0), group // 2, group % 2) // 16 == iota((80, 20), 1)
        counts.append(jnp.sum(rows.astype(jnp.float32), axis=0, keepdims=True))
    counts = jnp.concatenate(counts * 2, axis=0).astype(jnp.bfloat16)
    wide = jnp.zeros((20, 8), jnp.float32)
    for h in range(5):
        wide += ((5 * iota((20, 8), 1) + h) // 2 == iota((20, 8), 0)).astype(jnp.float32)
    most = dot(dot(counts, pattern).astype(jnp.bfloat16), wide.astype(jnp.bfloat16))
    most_ref[0, 0] = jnp.max(most).astype(jnp.int32)

    n = iota((1, 128), 1)
    source = 16 * (n % 32 // 4) + 4 * (n // 32) + n % 4
    order = one_hot(iota((128, 128), 0) == source)
    for h in range(5):
        lanes = slice(128 * h, 128 * h + 128)
        plain_ref[h] = state_ref[:, lanes]
        hi, mid, low = split3(state_ref[:, lanes])
        moved_ref[h] = (dot(hi, order) + dot(mid, order)) + dot(low, order)
    lane = iota((5, 128), 1) // 32
    for x in range(4):
        for y in range(4):
            for h in range(5):
                unit = jnp.zeros((5, 128), jnp.float32)
                for r in range(4):
                    part = moved_ref[h, pl.ds(4 * x + r, 5, stride=16), :]
                    if r != y:
                        part = pltpu.roll(part, 32 * ((r - y) % 4), 1)
                    unit = jnp.where(lane == r, part, unit)
                out_ref[4 * x + y, 5 * h : 5 * h + 5] = unit
                out_ref[4 * x + y, 25 + 5 * h : 30 + 5 * h] = plain_ref[
                    h, pl.ds(4 * y + x, 5, stride=16), :
                ]
            out_ref[4 * x + y, 50:] = jnp.zeros((UNITS - 50, 128), jnp.float32)


def pack_kernel(slots, at_ref, pattern_ref, got_ref, left_ref, right_ref):
    pattern = pattern_ref[...].astype(jnp.float32).astype(jnp.bfloat16)
    place = places_across(pattern, at_ref[2], at_ref[3])
    count = 16 * UNITS
    units = jnp.concatenate(split3(got_ref[...].reshape(count, 128)), axis=1)
    row = iota((1, count), 1)
    for start, ref in ((0, left_ref), (25, right_ref)):
        j = row % UNITS - start
        inside = (j >= 0) & (j < 25)
        q = 5 * (row // UNITS) + j % 5
        expand = (q == iota((80, count), 0)).astype(jnp.float32)
        spread = dot(place, expand, EXACT)
        mine = 5 * at_ref[1] + j // 5 == iota((40, count), 0)
        slot = jnp.sum(jnp.where(mine, spread, 0.0), axis=0, keepdims=True)
        slot = jnp.where(inside, slot, -1.0)
        pick = one_hot(slot == iota((slots, count), 0).astype(jnp.float32))
        got = dot(pick, units)
        ref[...] = (got[:, :128] + got[:, 128:256]) + got[:, 256:]


def product_kernel(slots, at_ref, pattern_ref, packed_ref, own_ref, swap_ref, out_ref, left_ref, right_ref):
    pattern = pattern_ref[...].astype(jnp.float32).astype(jnp.bfloat16)
    zl, zh, c = at_ref[1], at_ref[2], at_ref[3]
    slot = iota((80, slots), 1).astype(jnp.float32)

    half = iota((80, 40), 1)
    for dc, ref in ((0, own_ref), (1, swap_ref)):
        for dzh in range(2):
            place = places(pattern, jnp.abs(zh - dzh), jnp.abs(c - dc))
            pick = []
            for h in range(5):
                at = jnp.sum(jnp.where(half == 5 * zl + h, place, 0.0), axis=1, keepdims=True)
                pick.append(one_hot(at == slot))
            pick = jnp.concatenate(pick, axis=0)
            for t in range(4):
                got = dot(pick, jnp.concatenate(split(ref[t, dzh]), axis=1))
                got = got[:, :128] + got[:, 128:]
                base = 40 * (4 * (2 * dzh + dc) + t)
                for h in range(5):
                    for g in range(2):
                        right_ref[g, base : base + 40, 128 * h : 128 * h + 128] = got[
                            80 * h + 40 * g : 80 * h + 40 * g + 40
                        ]

    place = places(pattern, zh, c)
    lane = iota((80, 128), 1) // 32
    units, group = [], 0
    for z in range(8):
        pick = jnp.concatenate(
            [one_hot(place[:, 5 * z + h : 5 * z + h + 1] == slot) for h in range(5)], axis=0
        )
        got = dot(pick, jnp.concatenate(split(packed_ref[z]), axis=1))
        got = got[:, :128] + got[:, 128:]
        units += [got[80 * h : 80 * h + 80] for h in range(5)]
        while len(units) >= 4:
            four, units = units[:4], units[4:]
            for r in range(4):
                tile = jnp.zeros((80, 128), jnp.float32)
                for j in range(4):
                    moved = four[j]
                    if j != r:
                        moved = pltpu.roll(moved, 32 * ((j - r) % 4), 1)
                    tile = jnp.where(lane == j, moved, tile)
                left_ref[80 * r : 80 * r + 80, 128 * group : 128 * group + 128] = tile
            group += 1

    to = iota((320, 1), 0)
    rows = one_hot(to % 20 // 5 * 80 + to // 20 * 5 + to % 5 == iota((320, 320), 1))
    m = iota((1, 640), 1)
    p, x0, y, e = m // 40, m % 40 // 20, m % 20 // 5, m % 5
    zh_of, c_of = jnp.abs(zh - p // 8), jnp.abs(c - p // 4 % 2)
    source = 160 * (2 * x0 + y // 2) + 4 * (20 * (y % 2) + 10 * zh_of + 5 * c_of + e) + p % 4
    cols = one_hot(iota((640, 640), 0) == source)
    total = jnp.zeros((320, 640), jnp.float32)
    for g in range(2):
        left = []
        for part in split(left_ref[:, 640 * g : 640 * g + 640]):
            part = dot(rows, part).astype(jnp.bfloat16)
            left.append(dot(part, cols).astype(jnp.bfloat16))
        right = split(right_ref[g])
        total += dot(left[0], right[0]) + (dot(left[0], right[1]) + dot(left[1], right[0]))
    out_ref[...] = total.reshape(16, 20, 640)


def inflate_kernel(at_ref, pattern_ref, shares_ref, out_ref, sums_ref, sum_ref):
    for x in range(4):
        total = (shares_ref[4 * x] + shares_ref[4 * x + 1]) + (
            shares_ref[4 * x + 2] + shares_ref[4 * x + 3]
        )
        for r in range(4):
            for h in range(5):
                lanes = slice(128 * h, 128 * h + 128)
                sum_ref[h, pl.ds(4 * x + r, 5, stride=16), :] = total[5 * r : 5 * r + 5, lanes]
    row = at_ref[0] * 80
    first = row // BLK
    here = iota((80, 128), 0) + row < (first + 1) * BLK
    for h in range(5):
        lanes = slice(128 * h, 128 * h + 128)
        col = (5 * at_ref[1] + h) // 2
        low = pattern_ref[first, col].astype(jnp.float32)
        high = pattern_ref[jnp.minimum(first + 1, 19), col].astype(jnp.float32)
        value = sum_ref[h]
        out_ref[:, lanes] = value * value * jnp.where(here, low, high)
    sums_ref[...] = dot_rows(jnp.ones((8, 640), jnp.float32), out_ref[...], EXACT)


def scale_kernel(nodes, inflated_ref, sums_ref, out_ref):
    totals = lax.dot_general(
        sums_ref[...],
        jnp.ones((8, 128), jnp.float32),
        (((0,), (0,)), ((), ())),
        precision=EXACT,
        preferred_element_type=jnp.float32,
    )
    scale = nodes / totals
    for h in range(5):
        lanes = slice(128 * h, 128 * h + 128)
        out_ref[:, lanes] = inflated_ref[:, lanes] * scale


def swap(x, axis_name):
    return lax.ppermute(x, axis_name, [(0, 1), (1, 0)])


def f32(*shape):
    return jax.ShapeDtypeStruct(shape, jnp.float32)


def gather(x, axis_name, limit):
    rows = x.shape[-2]
    parts = -(-rows // limit)
    size = rows // parts
    done = [
        lax.all_gather(x[..., i * size : (i + 1) * size, :], axis_name, axis=0)
        for i in range(parts)
    ]
    return done[0] if parts == 1 else jnp.concatenate(done, axis=-2)


def partial_product(slots, at, in_pattern, got):
    left, right = call(
        functools.partial(pack_kernel, slots),
        (f32(slots, 128), f32(slots, 128)),
        [SMEM, VMEM, VMEM],
        (at, in_pattern, got),
    )
    far = swap(right, "zh")
    left = gather(left, "zl", SLOTS)
    left, far = lax.optimization_barrier((left, far))
    own = gather(jnp.stack([right, far]), "x", SLOTS)
    return call(
        functools.partial(product_kernel, slots),
        f32(16, 20, 640),
        [SMEM] + [VMEM] * 4,
        (at, in_pattern, left, own, swap(own, "c")),
        scratch=[pltpu.VMEM((320, 1280), jnp.float32), pltpu.VMEM((2, 640, 640), jnp.float32)],
        flops=5 * 10**9,
        size=5 * 10**6,
    )


def body(state, in_pattern, out_pattern):
    rows, cols = state.shape
    nodes = cols * lax.axis_size("zl")
    at = jnp.stack([lax.axis_index(ROWS)] + [lax.axis_index(a) for a in ("zl", "zh", "c")])
    at = at.astype(jnp.int32)
    units, most = call(
        units_kernel,
        (f32(16, UNITS, 128), jax.ShapeDtypeStruct((1, 1), jnp.int32)),
        [VMEM, VMEM],
        (in_pattern, state),
        out_specs=(VMEM, SMEM),
        scratch=[pltpu.VMEM((5, rows, 128), jnp.float32)] * 2,
    )
    got = lax.all_to_all(units, ("x", "y"), 0, 0)
    shares = lax.cond(
        most[0, 0] <= SLOTS,
        functools.partial(partial_product, SLOTS),
        functools.partial(partial_product, ALL),
        at,
        in_pattern,
        got,
    )
    shares = lax.all_to_all(shares, ("x", "y"), 0, 0)
    inflated, sums = call(
        inflate_kernel,
        (f32(rows, cols), f32(8, rows)),
        [SMEM, SMEM, VMEM],
        (at, out_pattern, shares),
        scratch=[pltpu.VMEM((5, rows, 128), jnp.float32)],
    )
    sums = lax.all_to_all(sums.reshape(8, 1, rows), "zl", 0, 0).reshape(8, rows)
    return call(
        functools.partial(scale_kernel, float(nodes)),
        f32(rows, cols),
        [VMEM, VMEM],
        (inflated, sums),
    )


def solution(mesh):
    fine = Mesh(
        mesh.devices.reshape(8, 4, 4, 2, 2), ("zl", "x", "y", "zh", "c")
    )
    return jax.shard_map(
        body,
        mesh=fine,
        in_specs=(P(ROWS, "zl"), P(), P()),
        out_specs=P(ROWS, "zl"),
        check_vma=False,
    )
```

time: 346 us -> 158 us (0.46)
  waiting for transfers between devices: 290 us -> 9.54 us
  blocking collectives: 25.1 us -> 103 us
  starting transfers between devices: 0.04 us -> 26.1 us
  Pallas kernels: 0 us -> 16.7 us
  matrix products: 16.3 us -> 0 us
  between operations: 13.4 us -> 0.71 us
    all_gather x2 -> x0, waiting for transfers between devices: 289 us -> none  [the longest x1 216 us: body(): column_block = lax.all_gather(masked, 'wide', axis=0, tiled=True)]
    all_gather x0 -> x2, blocking collectives: none -> 65.9 us  [gather(): lax.all_gather(x[..., i * size:(i + 1) * size, :], axis_name, axis=0)]
    all_to_all x0 -> x2, blocking collectives: none -> 37.6 us  [the longest x1 20 us: body(): shares = lax.all_to_all(shares, ('x', 'y'), 0, 0)]
    psum x1 -> x0, blocking collectives: 25.1 us -> none  [body(): totals = lax.psum(jnp.sum(inflated, axis=1), 'narrow')]
    ppermute x0 -> x2, starting transfers between devices: none -> 16.9 us  [swap(): return lax.ppermute(x, axis_name, [(0, 1), (1, 0)])]
    pallas_call x0 -> x5, Pallas kernels: none -> 16.7 us  [call(): pl.pallas_call(kernel, out_shape=outs, in_specs=in_specs, out_specs=out_s...]
    dot_general x3 -> x0, matrix products: 16.3 us -> none  [the longest x1 13.3 us: body(): jnp.dot(lax.all_gather(masked, 'narrow', axis=1, tiled=True), column_bloc...]
    all_to_all x0 -> x1, starting transfers between devices: none -> 9.29 us  [body(): got = lax.all_to_all(units, ('x', 'y'), 0, 0)]
  transfers between devices with their start and end apart: 2 -> 3, of which waited for: 2 -> 2; matrix products, arithmetic and copies ran while one was open for 0% -> 0% of each run, Pallas kernels for 0% -> 0%
where the time goes in v10:
time: 158 us
  blocking collectives  103 us (65%)
  starting transfers between devices  26.1 us (17%)
  Pallas kernels  16.7 us (11%)
  waiting for transfers between devices  9.54 us (6%)
    all_gather x2, blocking collectives, gather(): lax.all_gather(x[..., i * size:(i + 1) * size, :], axis_name, axis=0)  65.9 us
    all_to_all x1, blocking collectives, body(): shares = lax.all_to_all(shares, ('x', 'y'), 0, 0)  20 us
    all_to_all x1, blocking collectives, body(): sums = lax.all_to_all(sums.reshape(8, 1, rows), 'zl', 0, 0).reshape(8, rows)  17.5 us
    ppermute x2, starting transfers between devices, swap(): return lax.ppermute(x, axis_name, [(0, 1), (1, 0)])  16.9 us
    pallas_call x5, Pallas kernels, call(): pl.pallas_call(kernel, out_shape=outs, in_specs=in_specs, out_specs=out_s...  16.7 us
    all_to_all x1, starting transfers between devices, body(): got = lax.all_to_all(units, ('x', 'y'), 0, 0)  9.29 us
    all_to_all x1, waiting for transfers between devices, body(): got = lax.all_to_all(units, ('x', 'y'), 0, 0)  6.95 us
  transfers between devices with their start and end apart: 3, of which 2 were waited for; matrix products, arithmetic and copies ran while one was open for 0% of the time, Pallas kernels for 0%

profile of v10, /device:TPU:6, one launch (start us, length us, event | category | flops | bytes accessed | tf_op | source)
XLA Modules:
  0.0 157.6 jit_solution(17107284441690368821)
XLA Ops:
  0.0 0.0 copy-start
  0.0 0.9 copy-done
  0.9 2.3 %shard_map.37 = (f32[16,56,128]{2,1,0:T(8,128)}, s32[1,1]{1,0:T(1,128)}) custom-call(s32[20,20]{1,0:T(8,128)} %pattern_ref.2, f32[80,640]{1,0:T(8,128)S(1)} %copy-done), custom_call_target="tpu_custom_call" | custom-call | flops 1000000 | bytes 1000000 | tf_op jit(solution)/shard_map/pallas_call | solution.py:49
  3.2 9.3 %all-to-all-start = ((f32[16,56,128]{2,1,0:T(8,128)}), f32[16,56,128]{2,1,0:T(8,128)S(1)}, u32[]{:S(2)}, u32[]{:S(2)}) async-start(f32[16,56,128]{2,1,0:T(8,128)} %get-tuple-element.39), calls=%async_computation | async-start | bytes 917504 | tf_op jit(solution)/shard_map/all_to_all | solution.py:298
  13.2 0.1 pad_add_fusion.at_ref
  13.3 7.0 %all-to-all-done = f32[16,56,128]{2,1,0:T(8,128)S(1)} async-done(((f32[16,56,128]{2,1,0:T(8,128)}), f32[16,56,128]{2,1,0:T(8,128)S(1)}, u32[]{:S(2)}, u32[]{:S(2)}) %all-to-all-start) | async-done | bytes 458784 | tf_op jit(solution)/shard_map/all_to_all | solution.py:298
  20.2 97.7 %conditional.1 = (f32[16,20,640]{2,1,0:T(8,128)S(1)}) conditional(s32[]{:T(128)} %bitcast.14, (s32[4]{0:T(128)S(1)}, s32[20,20]{1,0:T(8,128)}, f32[16,56,128]{2,1,0:T(8,128)S(1)}) %tuple.13, (s32[4]{0:T(128)S(1)}, s32[20,20]{1,0:T(8,128)}, f32[16,56,128]{2,1,0:T(8,128)S(1)}) %tuple.13), branch_computations={%region_0.0_spmd, %region_1.0_spmd} | conditional | flops 5001921536 | bytes 25052916 | solution.py:299
  20.2 0.0 copy-start.3
  20.2 2.3 %branch_1_fun.2 = (f32[248,128]{1,0:T(8,128)S(1)}, f32[248,128]{1,0:T(8,128)S(1)}) custom-call(s32[4]{0:T(128)S(1)} %get-tuple-element.27.at_ref, s32[20,20]{1,0:T(8,128)} %get-tuple-element.28.pattern_ref, f32[16,56,128]{2,1,0:T(8,128)S(1)} %get-tuple-element.29.got_ref), custom_call_target="tpu_custom_call" | custom-call | flops 1000000 | bytes 1000000 | tf_op jit(solution)/shard_map/cond/branch_1_fun/pallas_call | solution.py:49
  22.6 15.0 %collective-permute-start = (f32[248,128]{1,0:T(8,128)S(1)}, f32[248,128]{1,0:T(8,128)S(1)}, u32[]{:S(2)}, u32[]{:S(2)}) collective-permute-start(f32[248,128]{1,0:T(8,128)S(1)} %get-tuple-element.31), channel_id=1, source_target_pairs={{0,2},{2,0},{1,3},{3,1},{4,6},{6,4},{5,7},{7,5},{8,10},{10,8},{9,1... | collective-permute-start | bytes 380936 | tf_op jit(solution)/shard_map/cond/branch_1_fun/ppermute | solution.py:245
  37.5 52.1 %all-gather.4 = f32[1984,128]{1,0:T(8,128)S(1)} all-gather(f32[248,128]{1,0:T(8,128)S(1)} %get-tuple-element.30), channel_id=6, replica_groups=mesh['zl'=8,'x'=4,'y'=4,'zh'=2,'c'=2] {'zl'}, dimensions={0}, use_global_device_ids=true | all-gather | bytes 1142784 | tf_op jit(solution)/shard_map/cond/branch_1_fun/all_gather | solution.py:257
  89.6 0.0 collective-permute-done
  89.6 13.8 %all-gather.5 = f32[8,248,128]{2,1,0:T(8,128)S(1)} all-gather(f32[2,248,128]{2,1,0:T(8,128)S(1)} %pad_maximum_fusion.3), channel_id=7, replica_groups=mesh['zl'=8,'x'=4,'y'=4,'zh'=2,'c'=2] {'x'}, dimensions={0}, use_global_device_ids=true | all-gather | bytes 1269760 | tf_op jit(solution)/shard_map/cond/branch_1_fun/all_gather | solution.py:257
  103.4 1.9 %collective-permute-start.1 = (f32[4,2,248,128]{3,2,1,0:T(8,128)S(1)}, f32[4,2,248,128]{3,2,1,0:T(8,128)S(1)}, u32[]{:S(2)}, u32[]{:S(2)}) collective-permute-start(f32[4,2,248,128]{3,2,1,0:T(8,128)S(1)} %bitcast.19), channel_id=1, source_target_pairs={{0,1},{1,0},{2,3},{3,2},{4,5},{5,4},{6,7},{7,6},{8,9},{9,8},{10,11... | collective-permute-start | bytes 3047432 | tf_op jit(solution)/shard_map/cond/branch_1_fun/ppermute | solution.py:245
  105.3 2.6 %collective-permute-done.1.swap_ref = f32[4,2,248,128]{3,2,1,0:T(8,128)S(1)} collective-permute-done((f32[4,2,248,128]{3,2,1,0:T(8,128)S(1)}, f32[4,2,248,128]{3,2,1,0:T(8,128)S(1)}, u32[]{:S(2)}, u32[]{:S(2)}) %collective-permute-start.1) | collective-permute-done | bytes 1015840 | tf_op jit(solution)/shard_map/cond/branch_1_fun/ppermute | solution.py:245
  107.9 0.0 copy-done.3
  107.9 10.0 %branch_1_fun.3 = f32[16,20,640]{2,1,0:T(8,128)S(1)} custom-call(s32[4]{0:T(128)S(1)} %get-tuple-element.27.at_ref, s32[20,20]{1,0:T(8,128)S(1)} %copy-done.3, f32[8,248,128]{2,1,0:T(8,128)S(1)} %bitcast.21, f32[4,2,248,128]{3,2,1,0:T(8,128)S(1)} %bitcast.20, f32[4,2,248,128]{3,2,1,0:T(8,128)S(1)} %collective-permute-done.1.swap_ref), custom_call_target="tpu_custom_call" | custom-call | flops 5000000000 | bytes 5000000 | tf_op jit(solution)/shard_map/cond/branch_1_fun/pallas_call | solution.py:49
  117.9 0.0 copy-start.1
  118.0 20.0 %all_to_all.15.shares_ref = f32[16,20,640]{2,1,0:T(8,128)S(1)} all-to-all(f32[16,20,640]{2,1,0:T(8,128)S(1)} %get-tuple-element.46), channel_id=1, replica_groups=mesh['zl'=8,'x'=4,'y'=4,'zh'=2,'c'=2] {'x','y'}, dimensions={0} | all-to-all | bytes 1638400 | tf_op jit(solution)/shard_map/all_to_all | solution.py:307
  138.0 0.0 copy-done.1
  138.0 1.1 shard_map.38
  139.1 17.5 %all_to_all.16 = f32[8,1,80]{2,1,0:T(1,128)S(1)} all-to-all(f32[8,1,80]{2,1,0:T(1,128)S(1)} %bitcast.25), channel_id=1, replica_groups=mesh['zl'=8,'x'=4,'y'=4,'zh'=2,'c'=2] {'zl'}, dimensions={0} | all-to-all | bytes 5120 | tf_op jit(solution)/shard_map/all_to_all | solution.py:315
  156.7 0.9 shard_map.39
  (1 shorter events, 0.0 us)
Async XLA Ops:
  0.0 0.9 copy-start
  3.2 17.0 %all-to-all-start = ((f32[16,56,128]{2,1,0:T(8,128)}), f32[16,56,128]{2,1,0:T(8,128)S(1)}, u32[]{:S(2)}, u32[]{:S(2)}) async-start(f32[16,56,128]{2,1,0:T(8,128)} %get-tuple-element.39), calls=%async_computation | async-start | bytes 917504 | tf_op jit(solution)/shard_map/all_to_all | solution.py:298
  20.2 87.7 %copy-start.3 = (s32[20,20]{1,0:T(8,128)S(1)}, s32[20,20]{1,0:T(8,128)}, u32[]{:S(2)}) copy-start(s32[20,20]{1,0:T(8,128)} %get-tuple-element.28.pattern_ref) | copy-start | bytes 4804 | tf_op jit(solution)/shard_map/cond
  22.6 67.0 %collective-permute-start = (f32[248,128]{1,0:T(8,128)S(1)}, f32[248,128]{1,0:T(8,128)S(1)}, u32[]{:S(2)}, u32[]{:S(2)}) collective-permute-start(f32[248,128]{1,0:T(8,128)S(1)} %get-tuple-element.31), channel_id=1, source_target_pairs={{0,2},{2,0},{1,3},{3,1},{4,6},{6,4},{5,7},{7,5},{8,10},{10,8},{9,1... | collective-permute-start | bytes 380936 | tf_op jit(solution)/shard_map/cond/branch_1_fun/ppermute | solution.py:245
  103.4 4.5 %collective-permute-start.1 = (f32[4,2,248,128]{3,2,1,0:T(8,128)S(1)}, f32[4,2,248,128]{3,2,1,0:T(8,128)S(1)}, u32[]{:S(2)}, u32[]{:S(2)}) collective-permute-start(f32[4,2,248,128]{3,2,1,0:T(8,128)S(1)} %bitcast.19), channel_id=1, source_target_pairs={{0,1},{1,0},{2,3},{3,2},{4,5},{5,4},{6,7},{7,6},{8,9},{9,8},{10,11... | collective-permute-start | bytes 3047432 | tf_op jit(solution)/shard_map/cond/branch_1_fun/ppermute | solution.py:245
  117.9 20.1 %copy-start.1 = (s32[20,20]{1,0:T(8,128)S(1)}, s32[20,20]{1,0:T(8,128)}, u32[]{:S(2)}) copy-start(s32[20,20]{1,0:T(8,128)} %pattern_ref.3) | copy-start | bytes 4804

commit v11 on v10

--- a/solution.py
+++ b/solution.py
@@ -149,14 +149,15 @@
     half = iota((80, 40), 1)
     for dc, ref in ((0, own_ref), (1, swap_ref)):
         for dzh in range(2):
-            place = places(pattern, jnp.abs(zh - dzh), jnp.abs(c - dc))
+            there = jnp.abs(zh - dzh)
+            place = places(pattern, there, jnp.abs(c - dc))
             pick = []
             for h in range(5):
                 at = jnp.sum(jnp.where(half == 5 * zl + h, place, 0.0), axis=1, keepdims=True)
                 pick.append(one_hot(at == slot))
             pick = jnp.concatenate(pick, axis=0)
             for t in range(4):
-                got = dot(pick, jnp.concatenate(split(ref[t, dzh]), axis=1))
+                got = dot(pick, jnp.concatenate(split(ref[t, there]), axis=1))
                 got = got[:, :128] + got[:, 128:]
                 base = 40 * (4 * (2 * dzh + dc) + t)
                 for h in range(5):
@@ -267,10 +268,11 @@
         [SMEM, VMEM, VMEM],
         (at, in_pattern, got),
     )
-    far = swap(right, "zh")
+    right = gather(right, "zh", SLOTS)
+    left, right = lax.optimization_barrier((left, right))
     left = gather(left, "zl", SLOTS)
-    left, far = lax.optimization_barrier((left, far))
-    own = gather(jnp.stack([right, far]), "x", SLOTS)
+    right, left = lax.optimization_barrier((right, left))
+    own = gather(right, "x", SLOTS)
     return call(
         functools.partial(product_kernel, slots),
         f32(16, 20, 640),

time: 158 us -> 168 us (1.063)
  blocking collectives: 103 us -> 128 us
  starting transfers between devices: 26.1 us -> 11.2 us
    all_gather x2 -> x3, blocking collectives: 65.9 us -> 87.6 us  [gather(): lax.all_gather(x[..., i * size:(i + 1) * size, :], axis_name, axis=0)]
    ppermute x2 -> x1, starting transfers between devices: 16.9 us -> 1.91 us  [swap(): return lax.ppermute(x, axis_name, [(0, 1), (1, 0)])]
    all_to_all x1, blocking collectives: 17.5 us -> 20.4 us  [body(): sums = lax.all_to_all(sums.reshape(8, 1, rows), 'zl', 0, 0).reshape(8, rows)]
  transfers between devices with their start and end apart: 3 -> 2, of which waited for: 2 -> 2; matrix products, arithmetic and copies ran while one was open for 0% -> 0% of each run, Pallas kernels for 0% -> 0%
where the time goes in v11:
time: 168 us; the launch traced here: 167 us
  blocking collectives  128 us (76%)
  Pallas kernels  16.7 us (10%)
  starting transfers between devices  11.2 us (7%)
  waiting for transfers between devices  9.59 us (6%)
    all_gather x3, blocking collectives, gather(): lax.all_gather(x[..., i * size:(i + 1) * size, :], axis_name, axis=0)  87.6 us
    all_to_all x1, blocking collectives, body(): sums = lax.all_to_all(sums.reshape(8, 1, rows), 'zl', 0, 0).reshape(8, rows)  20.4 us
    all_to_all x1, blocking collectives, body(): shares = lax.all_to_all(shares, ('x', 'y'), 0, 0)  19.6 us
    pallas_call x5, Pallas kernels, call(): pl.pallas_call(kernel, out_shape=outs, in_specs=in_specs, out_specs=out_s...  16.7 us
    all_to_all x1, starting transfers between devices, body(): got = lax.all_to_all(units, ('x', 'y'), 0, 0)  9.29 us
    all_to_all x1, waiting for transfers between devices, body(): got = lax.all_to_all(units, ('x', 'y'), 0, 0)  7.01 us
  transfers between devices with their start and end apart: 2, of which 2 were waited for; matrix products, arithmetic and copies ran while one was open for 0% of the time, Pallas kernels for 0%

profile of v11, /device:TPU:6, one launch (start us, length us, event | category | flops | bytes accessed | tf_op | source)
XLA Modules:
  0.0 166.8 jit_solution(996488336667608477)
XLA Ops:
  0.0 0.0 copy-start
  0.0 0.9 copy-done
  0.9 2.3 %shard_map.37 = (f32[16,56,128]{2,1,0:T(8,128)}, s32[1,1]{1,0:T(1,128)}) custom-call(s32[20,20]{1,0:T(8,128)} %pattern_ref.2, f32[80,640]{1,0:T(8,128)S(1)} %copy-done), custom_call_target="tpu_custom_call" | custom-call | flops 1000000 | bytes 1000000 | tf_op jit(solution)/shard_map/pallas_call | solution.py:49
  3.2 9.3 %all-to-all-start = ((f32[16,56,128]{2,1,0:T(8,128)}), f32[16,56,128]{2,1,0:T(8,128)S(1)}, u32[]{:S(2)}, u32[]{:S(2)}) async-start(f32[16,56,128]{2,1,0:T(8,128)} %get-tuple-element.43), calls=%async_computation | async-start | bytes 917504 | tf_op jit(solution)/shard_map/all_to_all | solution.py:300
  13.1 0.1 pad_add_fusion.at_ref
  13.2 7.0 %all-to-all-done = f32[16,56,128]{2,1,0:T(8,128)S(1)} async-done(((f32[16,56,128]{2,1,0:T(8,128)}), f32[16,56,128]{2,1,0:T(8,128)S(1)}, u32[]{:S(2)}, u32[]{:S(2)}) %all-to-all-start) | async-done | bytes 458784 | tf_op jit(solution)/shard_map/all_to_all | solution.py:300
  20.2 104.5 %conditional.1 = (f32[16,20,640]{2,1,0:T(8,128)S(1)}) conditional(s32[]{:T(128)} %bitcast.13, (s32[4]{0:T(128)S(1)}, s32[20,20]{1,0:T(8,128)}, f32[16,56,128]{2,1,0:T(8,128)S(1)}) %tuple.15, (s32[4]{0:T(128)S(1)}, s32[20,20]{1,0:T(8,128)}, f32[16,56,128]{2,1,0:T(8,128)S(1)}) %tuple.15), branch_computations={%region_0.0_spmd, %region_1.0_spmd} | conditional | flops 5001921536 | bytes 26076876 | solution.py:301
  20.2 0.0 copy-start.3
  20.2 2.3 %branch_1_fun.2 = (f32[248,128]{1,0:T(8,128)S(1)}, f32[248,128]{1,0:T(8,128)S(1)}) custom-call(s32[4]{0:T(128)S(1)} %get-tuple-element.29.at_ref, s32[20,20]{1,0:T(8,128)} %get-tuple-element.30.pattern_ref, f32[16,56,128]{2,1,0:T(8,128)S(1)} %get-tuple-element.31.got_ref), custom_call_target="tpu_custom_call" | custom-call | flops 1000000 | bytes 1000000 | tf_op jit(solution)/shard_map/cond/branch_1_fun/pallas_call | solution.py:49
  22.6 21.8 %all-gather.6 = f32[496,128]{1,0:T(8,128)S(1)} all-gather(f32[248,128]{1,0:T(8,128)S(1)} %get-tuple-element.33), channel_id=8, replica_groups=mesh['zl'=8,'x'=4,'y'=4,'zh'=2,'c'=2] {'zh'}, dimensions={0}, use_global_device_ids=true | all-gather | bytes 380928 | tf_op jit(solution)/shard_map/cond/branch_1_fun/all_gather | solution.py:258
  44.3 52.1 %all-gather.7 = f32[1984,128]{1,0:T(8,128)S(1)} all-gather(f32[248,128]{1,0:T(8,128)S(1)} %get-tuple-element.35), channel_id=9, replica_groups=mesh['zl'=8,'x'=4,'y'=4,'zh'=2,'c'=2] {'zl'}, dimensions={0}, use_global_device_ids=true | all-gather | bytes 1142784 | tf_op jit(solution)/shard_map/cond/branch_1_fun/all_gather | solution.py:258
  96.4 13.8 %all-gather.8 = f32[8,248,128]{2,1,0:T(8,128)S(1)} all-gather(f32[2,248,128]{2,1,0:T(8,128)S(1)} %bitcast.27), channel_id=10, replica_groups=mesh['zl'=8,'x'=4,'y'=4,'zh'=2,'c'=2] {'x'}, dimensions={0}, use_global_device_ids=true | all-gather | bytes 1269760 | tf_op jit(solution)/shard_map/cond/branch_1_fun/all_gather | solution.py:258
  110.2 1.9 %collective-permute-start = (f32[4,2,248,128]{3,2,1,0:T(8,128)S(1)}, f32[4,2,248,128]{3,2,1,0:T(8,128)S(1)}, u32[]{:S(2)}, u32[]{:S(2)}) collective-permute-start(f32[4,2,248,128]{3,2,1,0:T(8,128)S(1)} %bitcast.18), channel_id=1, source_target_pairs={{0,1},{1,0},{2,3},{3,2},{4,5},{5,4},{6,7},{7,6},{8,9},{9,8},{10,11... | collective-permute-start | bytes 3047432 | tf_op jit(solution)/shard_map/cond/branch_1_fun/ppermute | solution.py:246
  112.1 2.6 %collective-permute-done.swap_ref = f32[4,2,248,128]{3,2,1,0:T(8,128)S(1)} collective-permute-done((f32[4,2,248,128]{3,2,1,0:T(8,128)S(1)}, f32[4,2,248,128]{3,2,1,0:T(8,128)S(1)}, u32[]{:S(2)}, u32[]{:S(2)}) %collective-permute-start) | collective-permute-done | bytes 1015840 | tf_op jit(solution)/shard_map/cond/branch_1_fun/ppermute | solution.py:246
  114.7 0.0 copy-done.3
  114.7 10.0 %branch_1_fun.3 = f32[16,20,640]{2,1,0:T(8,128)S(1)} custom-call(s32[4]{0:T(128)S(1)} %get-tuple-element.29.at_ref, s32[20,20]{1,0:T(8,128)S(1)} %copy-done.3, f32[8,248,128]{2,1,0:T(8,128)S(1)} %bitcast.20, f32[4,2,248,128]{3,2,1,0:T(8,128)S(1)} %bitcast.19, f32[4,2,248,128]{3,2,1,0:T(8,128)S(1)} %collective-permute-done.swap_ref), custom_call_target="tpu_custom_call" | custom-call | flops 5000000000 | bytes 5000000 | tf_op jit(solution)/shard_map/cond/branch_1_fun/pallas_call | solution.py:49
  124.7 0.0 copy-start.1
  124.7 19.6 %all_to_all.15.shares_ref = f32[16,20,640]{2,1,0:T(8,128)S(1)} all-to-all(f32[16,20,640]{2,1,0:T(8,128)S(1)} %get-tuple-element.52), channel_id=1, replica_groups=mesh['zl'=8,'x'=4,'y'=4,'zh'=2,'c'=2] {'x','y'}, dimensions={0} | all-to-all | bytes 1638400 | tf_op jit(solution)/shard_map/all_to_all | solution.py:309
  144.4 0.0 copy-done.1
  144.4 1.1 shard_map.38
  145.5 20.4 %all_to_all.16 = f32[8,1,80]{2,1,0:T(1,128)S(1)} all-to-all(f32[8,1,80]{2,1,0:T(1,128)S(1)} %bitcast.22), channel_id=1, replica_groups=mesh['zl'=8,'x'=4,'y'=4,'zh'=2,'c'=2] {'zl'}, dimensions={0} | all-to-all | bytes 5120 | tf_op jit(solution)/shard_map/all_to_all | solution.py:317
  165.9 0.9 shard_map.39
Async XLA Ops:
  0.0 0.9 copy-start
  3.2 17.0 %all-to-all-start = ((f32[16,56,128]{2,1,0:T(8,128)}), f32[16,56,128]{2,1,0:T(8,128)S(1)}, u32[]{:S(2)}, u32[]{:S(2)}) async-start(f32[16,56,128]{2,1,0:T(8,128)} %get-tuple-element.43), calls=%async_computation | async-start | bytes 917504 | tf_op jit(solution)/shard_map/all_to_all | solution.py:300
  20.2 94.5 %copy-start.3 = (s32[20,20]{1,0:T(8,128)S(1)}, s32[20,20]{1,0:T(8,128)}, u32[]{:S(2)}) copy-start(s32[20,20]{1,0:T(8,128)} %get-tuple-element.30.pattern_ref) | copy-start | bytes 4804 | tf_op jit(solution)/shard_map/cond
  110.2 4.5 %collective-permute-start = (f32[4,2,248,128]{3,2,1,0:T(8,128)S(1)}, f32[4,2,248,128]{3,2,1,0:T(8,128)S(1)}, u32[]{:S(2)}, u32[]{:S(2)}) collective-permute-start(f32[4,2,248,128]{3,2,1,0:T(8,128)S(1)} %bitcast.18), channel_id=1, source_target_pairs={{0,1},{1,0},{2,3},{3,2},{4,5},{5,4},{6,7},{7,6},{8,9},{9,8},{10,11... | collective-permute-start | bytes 3047432 | tf_op jit(solution)/shard_map/cond/branch_1_fun/ppermute | solution.py:246
  124.7 19.7 %copy-start.1 = (s32[20,20]{1,0:T(8,128)S(1)}, s32[20,20]{1,0:T(8,128)}, u32[]{:S(2)}) copy-start(s32[20,20]{1,0:T(8,128)} %pattern_ref.3) | copy-start | bytes 4804

commit v12 on v6

--- a/solution.py
+++ b/solution.py
@@ -59,11 +59,6 @@
         for h in range(5):
             rows = slice(base + PAD * h, base + PAD * h + RUN)
             out_ref[y, rows] = masked_ref[RUN * y : RUN * y + RUN, 128 * h : 128 * h + 128]
-
-
-def far_kernel(at_ref, pattern_ref, state_ref, out_ref, masked_ref):
-    owner = at_ref[0] + 2 - 4 * at_ref[2]
-    pack_right(at_ref, owner, pattern_ref, state_ref, masked_ref, out_ref, 0)
 
 
 def pieces_kernel(at_ref, pattern_ref, state_ref, out_ref, masked_ref):
@@ -111,10 +106,6 @@
     unpack_right(got_ref, right_ref, LEFT)
 
 
-def unpack_far_kernel(got_ref, right_ref):
-    unpack_right(got_ref, right_ref, 0)
-
-
 def product_kernel(at_ref, left_ref, right_ref, out_ref, hi_ref, lo_ref):
     for dc in range(2):
         c = lax.rem(at_ref[3] + dc, 2)
@@ -122,7 +113,7 @@
             rows = slice(40 * (2 * dzh + dc), 40 * (2 * dzh + dc) + 40)
             for x in range(4):
                 for y1 in range(2):
-                    hi, lo = split(right_ref[c, x, dzh, y1])
+                    hi, lo = split(right_ref[c, x, lax.rem(at_ref[2] + dzh, 2), y1])
                     hi_ref[2 * x + y1, rows] = hi
                     lo_ref[2 * x + y1, rows] = lo
     lane = lax.broadcasted_iota(jnp.int32, (8, 128), 1) // 32
@@ -192,28 +183,19 @@
         [lax.axis_index(ROWS)] + [lax.axis_index(a) for a in ("zl", "zh", "c")]
     ).astype(jnp.int32)
 
-    other = lax.ppermute(state, "zh", [(0, 1), (1, 0)])
-    work = [pltpu.VMEM((rows, cols), jnp.float32)]
     pieces = call(
         pieces_kernel,
         f32(4, PIECE, 128),
         [SMEM, SMEM, VMEM],
         (at, in_pattern, state),
-        work,
+        [pltpu.VMEM((rows, cols), jnp.float32)],
     )
     got = lax.all_to_all(pieces, "y", 0, 0)
-    got, other = lax.optimization_barrier((got, other))
     left, near = call(
         unpack_kernel, (f32(4, LEFT, 128), f32(2, 2 * RUN, cols)), [VMEM], (got,)
     )
-    far = call(
-        far_kernel, f32(4, 5 * PAD, 128), [SMEM, SMEM, VMEM], (at, in_pattern, other), work
-    )
-    left, far = lax.optimization_barrier((left, far))
     left = lax.all_gather(left, "zl", axis=0)
-    far = lax.all_to_all(far, "y", 0, 0)
-    far = call(unpack_far_kernel, f32(2, 2 * RUN, cols), [VMEM], (far,))
-    right = gather(gather(jnp.stack([near, far]), "x"), "c")
+    right = gather(gather(gather(near, "zh"), "x"), "c")
 
     partial = call(
         product_kernel,

time: 165 us -> 146 us (0.88)
  blocking collectives: 65.9 us -> 101 us
  waiting for transfers between devices: 50.9 us -> 18.8 us
  starting transfers between devices: 20.2 us -> 0.01 us
    all_to_all x2 -> x3, blocking collectives: 27.4 us -> 57.4 us  [gather(): return lax.all_to_all(copies, axis_name, 0, 0)]
    all_gather x1, waiting for transfers between devices: 45.6 us -> 18.8 us  [body(): left = lax.all_gather(left, 'zl', axis=0)]
    ppermute x1 -> x0, starting transfers between devices: 15.7 us -> none  [body(): other = lax.ppermute(state, 'zh', [(0, 1), (1, 0)])]
    ppermute x1 -> x0, waiting for transfers between devices: 5.29 us -> none  [body(): other = lax.ppermute(state, 'zh', [(0, 1), (1, 0)])]
    all_to_all x1 -> x0, starting transfers between devices: 4.46 us -> none  [body(): got = lax.all_to_all(pieces, 'y', 0, 0)]
    all_to_all x1, blocking collectives: 13.9 us -> 16.2 us  [body(): sums = lax.all_to_all(sums.reshape(8, 1, rows), 'zl', 0, 0).reshape(8, rows)]
    all_to_all x1, blocking collectives: 10.9 us -> 13 us  [body(): got = lax.all_to_all(pieces, 'y', 0, 0)]
    pallas_call x7 -> x5, Pallas kernels: 9.59 us -> 7.99 us  [call(): pl.pallas_call(kernel, out_shape=outs, in_specs=in_specs, out_specs=jax.t...]
  transfers between devices with their start and end apart: 3 -> 1, of which waited for: 2 -> 1; matrix products, arithmetic and copies ran while one was open for 0% -> 0% of each run, Pallas kernels for 0% -> 0%
where the time goes in v12:
time: 146 us; the launch traced here: 145 us
  blocking collectives  101 us (69%)
  waiting for transfers between devices  18.8 us (13%)
  between operations  13.4 us (9%)
  Pallas kernels  7.99 us (5%)
  local copies, waits for them, and re-layouts  3.5 us (2%)
    all_to_all x3, blocking collectives, gather(): return lax.all_to_all(copies, axis_name, 0, 0)  57.4 us
    all_gather x1, waiting for transfers between devices, body(): left = lax.all_gather(left, 'zl', axis=0)  18.8 us
    all_to_all x1, blocking collectives, body(): sums = lax.all_to_all(sums.reshape(8, 1, rows), 'zl', 0, 0).reshape(8, rows)  16.2 us
    all_to_all x1, blocking collectives, body(): shares = lax.all_to_all(partial, 'y', 0, 0)  14.8 us
    all_to_all x1, blocking collectives, body(): got = lax.all_to_all(pieces, 'y', 0, 0)  13 us
    pallas_call x5, Pallas kernels, call(): pl.pallas_call(kernel, out_shape=outs, in_specs=in_specs, out_specs=jax.t...  7.99 us
    unnamed x8, local copies, waits for them, and re-layouts  3.09 us
  transfers between devices with their start and end apart: 1, of which 1 were waited for; matrix products, arithmetic and copies ran while one was open for 0% of the time, Pallas kernels for 0%

profile of v12, /device:TPU:6, one launch (start us, length us, event | category | flops | bytes accessed | tf_op | source)
XLA Modules:
  0.0 145.3 jit_solution(18238298672498015330)
XLA Ops:
  6.5 0.0 all-gather.3.cloned.1.call-start
  6.5 0.1 pad_add_fusion.at_ref
  6.6 0.0 copy-start
  6.6 0.9 copy-done
  7.5 0.0 copy-start.1
  7.5 0.7 copy-done.1
  8.3 1.5 %shard_map.37 = f32[4,224,128]{2,1,0:T(8,128)S(1)} custom-call(s32[4]{0:T(128)S(1)} %pad_add_fusion.at_ref, s32[20,20]{1,0:T(8,128)S(1)} %copy-done.1, f32[80,640]{1,0:T(8,128)S(1)} %copy-done), custom_call_target="tpu_custom_call" | custom-call | flops 1000000 | bytes 1000000 | tf_op jit(solution)/shard_map/pallas_call | solution.py:30
  9.8 13.0 %all_to_all.30.got_ref = f32[4,224,128]{2,1,0:T(8,128)S(1)} all-to-all(f32[4,224,128]{2,1,0:T(8,128)S(1)} %shard_map.37), channel_id=1, replica_groups=mesh['zl'=8,'x'=4,'y'=4,'zh'=2,'c'=2] {'y'}, dimensions={0} | all-to-all | bytes 917504 | tf_op jit(solution)/shard_map/all_to_all | solution.py:193
  22.8 0.7 shard_map.38
  23.5 0.0 all-gather.3.cloned.1.call-update
  23.6 31.2 %all_to_all.31 = f32[2,2,40,640]{3,2,1,0:T(8,128)S(1)} all-to-all(f32[2,2,40,640]{3,2,1,0:T(8,128)S(1)} %broadcast_in_dim.6), channel_id=1, replica_groups=mesh['zl'=8,'x'=4,'y'=4,'zh'=2,'c'=2] {'zh'}, dimensions={0} | all-to-all | bytes 819200 | tf_op jit(solution)/shard_map/all_to_all | solution.py:172
  54.7 0.1 broadcast_in_dim.7
  54.9 19.9 %all_to_all.32 = f32[4,2,2,40,640]{4,3,2,1,0:T(8,128)S(1)} all-to-all(f32[4,2,2,40,640]{4,3,2,1,0:T(8,128)S(1)} %broadcast_in_dim.7), channel_id=1, replica_groups=mesh['zl'=8,'x'=4,'y'=4,'zh'=2,'c'=2] {'x'}, dimensions={0} | all-to-all | bytes 3276800 | tf_op jit(solution)/shard_map/all_to_all | solution.py:172
  74.7 0.3 broadcast_in_dim.8
  75.0 6.4 %all_to_all.33.right_ref = f32[2,4,2,2,40,640]{5,4,3,2,1,0:T(8,128)S(1)} all-to-all(f32[2,4,2,2,40,640]{5,4,3,2,1,0:T(8,128)S(1)} %broadcast_in_dim.8), channel_id=1, replica_groups=mesh['zl'=8,'x'=4,'y'=4,'zh'=2,'c'=2] {'c'}, dimensions={0} | all-to-all | bytes 6553600 | tf_op jit(solution)/shard_map/all_to_all | solution.py:172
  81.4 18.8 %all-gather.3.cloned.1.call-done = f32[32,104,128]{2,1,0:T(8,128)} async-done(((f32[4,104,128]{2,1,0:T(8,128)}), f32[32,104,128]{2,1,0:T(8,128)}) %all-gather.3.cloned.1.call-update) | async-done | bytes 1703952 | tf_op jit(solution)/shard_map/all_gather | solution.py:197
  100.2 0.0 copy-start.3
  100.2 1.5 copy-done.3
  101.7 3.8 %shard_map.39 = f32[4,80,640]{2,1,0:T(8,128)S(1)} custom-call(s32[4]{0:T(128)S(1)} %pad_add_fusion.at_ref, f32[8,4,104,128]{3,2,1,0:T(8,128)S(1)} %bitcast.11, f32[2,4,2,2,40,640]{5,4,3,2,1,0:T(8,128)S(1)} %all_to_all.33.right_ref), custom_call_target="tpu_custom_call" | custom-call | flops 3000000000 | bytes 6000000 | tf_op jit(solution)/shard_map/pallas_call | solution.py:30
  105.4 14.8 %all_to_all.34.shares_ref = f32[4,80,640]{2,1,0:T(8,128)S(1)} all-to-all(f32[4,80,640]{2,1,0:T(8,128)S(1)} %shard_map.39), channel_id=1, replica_groups=mesh['zl'=8,'x'=4,'y'=4,'zh'=2,'c'=2] {'y'}, dimensions={0} | all-to-all | bytes 1638400 | tf_op jit(solution)/shard_map/all_to_all | solution.py:209
  120.3 0.0 copy-done.2
  120.3 1.1 shard_map.40
  121.4 16.2 %all_to_all.35 = f32[8,1,80]{2,1,0:T(1,128)S(1)} all-to-all(f32[8,1,80]{2,1,0:T(1,128)S(1)} %bitcast.10), channel_id=1, replica_groups=mesh['zl'=8,'x'=4,'y'=4,'zh'=2,'c'=2] {'zl'}, dimensions={0} | all-to-all | bytes 5120 | tf_op jit(solution)/shard_map/all_to_all | solution.py:216
  137.5 0.9 shard_map.41
  (2 shorter events, 0.0 us)
Async XLA Ops:
  6.5 93.7 %all-gather.3.cloned.1.call-start = ((), (), s32[]{:S(2)}) async-start(), calls=%async_computation.6 | async-start | bytes 1916928 | tf_op jit(solution)/shard_map/all_gather | solution.py:197
  6.6 0.9 copy-start
  7.5 0.7 copy-start.1
  100.2 1.5 %copy-start.3 = (f32[32,104,128]{2,1,0:T(8,128)S(1)}, f32[32,104,128]{2,1,0:T(8,128)}, u32[]{:S(2)}) copy-start(f32[32,104,128]{2,1,0:T(8,128)} %all-gather.3.cloned.1.call-done) | copy-start | bytes 5111812
  101.7 18.6 %copy-start.2 = (s32[20,20]{1,0:T(8,128)S(1)}, s32[20,20]{1,0:T(8,128)}, u32[]{:S(2)}) copy-start(s32[20,20]{1,0:T(8,128)} %pattern_ref.3) | copy-start | bytes 4804
Sparse Core Ops, SparseCore 0:
  23.7 76.4 all-gather.2

commit v13 on v7

--- a/solution.py
+++ b/solution.py
@@ -59,11 +59,6 @@
         for h in range(5):
             rows = slice(base + PAD * h, base + PAD * h + RUN)
             out_ref[y, rows] = masked_ref[RUN * y : RUN * y + RUN, 128 * h : 128 * h + 128]
-
-
-def far_kernel(at_ref, pattern_ref, state_ref, out_ref, masked_ref):
-    owner = at_ref[0] + 2 - 4 * at_ref[2]
-    pack_right(at_ref, owner, pattern_ref, state_ref, masked_ref, out_ref, 0)
 
 
 def pieces_kernel(at_ref, pattern_ref, state_ref, out_ref, masked_ref):
@@ -111,12 +106,8 @@
     unpack_right(got_ref, right_ref, LEFT)
 
 
-def unpack_far_kernel(got_ref, right_ref):
-    unpack_right(got_ref, right_ref, 0)
-
-
 def product_kernel(at_ref, *refs):
-    lefts, rights, out_ref, hi_ref, lo_ref = refs[:8], refs[8:12], *refs[12:]
+    lefts, rights, out_ref, hi_ref, lo_ref = refs[:2], refs[2:6], *refs[6:]
     for part, ref in enumerate(rights):
         for dx in range(4):
             for y1 in range(2):
@@ -127,8 +118,9 @@
     lane = lax.broadcasted_iota(jnp.int32, (8, 128), 1) // 32
     zl, x = at_ref[1], at_ref[4]
     total = jnp.zeros((320, 640), jnp.float32)
-    for d, ref in enumerate(lefts):
-        source = lax.rem(zl - d + 8, 8)
+    for d in range(8):
+        ref = lefts[d // 4].at[d % 4]
+        source = 4 * lax.rem(zl // 4 + d // 4, 2) + d % 4
         block = 2 * lax.rem(x - source // 2 + 4, 4) + lax.rem(source, 2)
         whole = []
         for y in range(4):
@@ -196,47 +188,37 @@
         [lax.axis_index(ROWS)] + [lax.axis_index(a) for a in ("zl", "zh", "c", "x")]
     ).astype(jnp.int32)
 
-    tie = lax.optimization_barrier
-    work = [pltpu.VMEM((rows, cols), jnp.float32)]
-    far = shift(state, "zh", 1)
     pieces = call(
         pieces_kernel,
         f32(4, PIECE, 128),
         [SMEM, SMEM, VMEM],
         (at, in_pattern, state),
-        work,
+        [pltpu.VMEM((rows, cols), jnp.float32)],
     )
     got = lax.all_to_all(pieces, "y", 0, 0)
     left, near = call(
         unpack_kernel, (f32(4, LEFT, 128), f32(2, 2 * RUN, cols)), [VMEM], (got,)
     )
+
+    tie = lax.optimization_barrier
+    halves = [[0, 1, 2, 3], [4, 5, 6, 7]]
+    away = lax.ppermute(left, "zl", [(i, i ^ 4) for i in range(8)])
+    far = shift(near, "zh", 1)
     near = across_x(near)
-    left, near, far = tie((left, near, far))
-
-    up, down = shift(left, "zl", 1), shift(left, "zl", -1)
-    far = call(
-        far_kernel, f32(4, 5 * PAD, 128), [SMEM, SMEM, VMEM], (at, in_pattern, far), work
-    )
-    far = lax.all_to_all(far, "y", 0, 0)
-    far = call(unpack_far_kernel, f32(2, 2 * RUN, cols), [VMEM], (far,))
-    lefts = [left, up, None, None, None, None, None, down]
-    up, down, far = tie((up, down, far))
-
-    up, down = shift(up, "zl", 1), shift(down, "zl", -1)
+    here = lax.all_gather(left, "zl", axis=0, axis_index_groups=halves)
+    away, far, near, here = tie((away, far, near, here))
+
     far = across_x(far)
-    lefts[2], lefts[6] = up, down
-    up, down, far = tie((up, down, far))
-
-    up, down = shift(up, "zl", 1), shift(down, "zl", -1)
-    near_swapped, far_swapped = shift(near, "c", 1), shift(far, "c", 1)
-    lefts[3], lefts[5] = up, down
-    lefts[4] = shift(up, "zl", 1)
+    near_swapped = shift(near, "c", 1)
+    away = lax.all_gather(away, "zl", axis=0, axis_index_groups=halves)
+    away, far, near_swapped = tie((away, far, near_swapped))
+    far_swapped = shift(far, "c", 1)
 
     partial = call(
         product_kernel,
         f32(4, rows, cols),
-        [SMEM] + [VMEM] * 12,
-        (at, *lefts, near, near_swapped, far, far_swapped),
+        [SMEM] + [VMEM] * 6,
+        (at, here, away, near, near_swapped, far, far_swapped),
         [pltpu.VMEM((8, 160, cols), jnp.bfloat16)] * 2,
         flops=3 * 10**9,
         size=6 * 10**6,

time: 172 us -> 162 us (0.942)
  blocking collectives: 49.1 us -> 105 us
  starting transfers between devices: 85.5 us -> 44.1 us
  waiting for transfers between devices: 25.5 us -> 2.32 us
    all_gather x0 -> x2, blocking collectives: none -> 61.7 us  [the longest x1 41 us: body(): here = lax.all_gather(left, 'zl', axis=0, axis_index_groups=halves)]
    ppermute x16 -> x9, starting transfers between devices: 85.5 us -> 39.8 us  [shift(): lax.ppermute(x, axis_name, [(i, (i + by) % size) for i in range(size)])]
    ppermute x16 -> x9, waiting for transfers between devices: 25.5 us -> 2.32 us  [shift(): lax.ppermute(x, axis_name, [(i, (i + by) % size) for i in range(size)])]
    all_to_all x1 -> x0, blocking collectives: 8.97 us -> none  [body(): far = lax.all_to_all(far, 'y', 0, 0)]
    ppermute x0 -> x1, starting transfers between devices: none -> 4.29 us  [body(): away = lax.ppermute(left, 'zl', [(i, i ^ 4) for i in range(8)])]
    all_to_all x1, blocking collectives: 12.8 us -> 14.5 us  [body(): sums = lax.all_to_all(sums.reshape(8, 1, rows), 'zl', 0, 0).reshape(8, rows)]
    pallas_call x7 -> x5, Pallas kernels: 8.61 us -> 7.8 us  [call(): pl.pallas_call(kernel, out_shape=outs, in_specs=in_specs, out_specs=jax.t...]
  transfers between devices with their start and end apart: 16 -> 10, of which waited for: 6 -> 1; matrix products, arithmetic and copies ran while one was open for 0% -> 0% of each run, Pallas kernels for 0% -> 0%
where the time goes in v13:
time: 162 us; the launch traced here: 161 us
  blocking collectives  105 us (65%)
  starting transfers between devices  44.1 us (27%)
  Pallas kernels  7.8 us (5%)
  waiting for transfers between devices  2.32 us (1%)
  local copies, waits for them, and re-layouts  1.64 us (1%)
    all_gather x1, blocking collectives, body(): here = lax.all_gather(left, 'zl', axis=0, axis_index_groups=halves)  41 us
    ppermute x9, starting transfers between devices, shift(): lax.ppermute(x, axis_name, [(i, (i + by) % size) for i in range(size)])  39.8 us
    all_gather x1, blocking collectives, body(): away = lax.all_gather(away, 'zl', axis=0, axis_index_groups=halves)  20.6 us
    all_to_all x1, blocking collectives, body(): shares = lax.all_to_all(partial, 'y', 0, 0)  15.6 us
    all_to_all x1, blocking collectives, body(): sums = lax.all_to_all(sums.reshape(8, 1, rows), 'zl', 0, 0).reshape(8, rows)  14.5 us
    all_to_all x1, blocking collectives, body(): got = lax.all_to_all(pieces, 'y', 0, 0)  13 us
    pallas_call x5, Pallas kernels, call(): pl.pallas_call(kernel, out_shape=outs, in_specs=in_specs, out_specs=jax.t...  7.8 us
    ppermute x1, starting transfers between devices, body(): away = lax.ppermute(left, 'zl', [(i, i ^ 4) for i in range(8)])  4.29 us
  transfers between devices with their start and end apart: 10, of which 1 were waited for; matrix products, arithmetic and copies ran while one was open for 0% of the time, Pallas kernels for 0%

profile of v13, /device:TPU:6, one launch (start us, length us, event | category | flops | bytes accessed | tf_op | source)
XLA Modules:
  0.0 160.9 jit_solution(16982969238331697159)
XLA Ops:
  0.0 0.1 stack.53.at_ref
  0.1 0.6 copy-done.1
  0.7 0.9 copy-done
  1.6 1.5 shard_map.37
  3.1 13.0 %all_to_all.15.got_ref = f32[4,224,128]{2,1,0:T(8,128)S(1)} all-to-all(f32[4,224,128]{2,1,0:T(8,128)S(1)} %shard_map.37), channel_id=1, replica_groups=mesh['zl'=8,'x'=4,'y'=4,'zh'=2,'c'=2] {'y'}, dimensions={0} | all-to-all | bytes 917504 | tf_op jit(solution)/shard_map/all_to_all | solution.py:198
  16.2 2.7 %collective-permute-start.4 = (f32[2,40,640]{2,1,0:T(8,128)S(1)}, f32[2,40,640]{2,1,0:T(8,128)S(1)}, u32[]{:S(2)}, u32[]{:S(2)}) collective-permute-start(f32[2,40,640]{2,1,0:T(8,128)S(1)} %get-tuple-element.17), channel_id=1, source_target_pairs={{0,48},{16,0},{32,16},{48,32},{1,49},{17,1},{33,17},{49,33},{2,50}... | collective-permute-start | bytes 614408 | tf_op jit(solution)/shard_map/ppermute | solution.py:173
  19.0 5.5 %collective-permute-start.3 = (f32[2,40,640]{2,1,0:T(8,128)S(1)}, f32[2,40,640]{2,1,0:T(8,128)S(1)}, u32[]{:S(2)}, u32[]{:S(2)}) collective-permute-start(f32[2,40,640]{2,1,0:T(8,128)S(1)} %get-tuple-element.17), channel_id=1, source_target_pairs={{0,32},{16,48},{32,0},{48,16},{1,33},{17,49},{33,1},{49,17},{2,34}... | collective-permute-start | bytes 614408 | tf_op jit(solution)/shard_map/ppermute | solution.py:173
  24.4 1.9 %collective-permute-start.2 = (f32[2,40,640]{2,1,0:T(8,128)S(1)}, f32[2,40,640]{2,1,0:T(8,128)S(1)}, u32[]{:S(2)}, u32[]{:S(2)}) collective-permute-start(f32[2,40,640]{2,1,0:T(8,128)S(1)} %get-tuple-element.17), channel_id=1, source_target_pairs={{0,16},{16,32},{32,48},{48,0},{1,17},{17,33},{33,49},{49,1},{2,18}... | collective-permute-start | bytes 614408 | tf_op jit(solution)/shard_map/ppermute | solution.py:173
  26.4 15.4 %collective-permute-start.1 = (f32[2,40,640]{2,1,0:T(8,128)S(1)}, f32[2,40,640]{2,1,0:T(8,128)S(1)}, u32[]{:S(2)}, u32[]{:S(2)}) collective-permute-start(f32[2,40,640]{2,1,0:T(8,128)S(1)} %get-tuple-element.17), channel_id=1, source_target_pairs={{0,2},{2,0},{1,3},{3,1},{4,6},{6,4},{5,7},{7,5},{8,10},{10,8},{9,1... | collective-permute-start | bytes 614408 | tf_op jit(solution)/shard_map/ppermute | solution.py:173
  41.7 4.3 %collective-permute-start = (f32[4,104,128]{2,1,0:T(8,128)S(1)}, f32[4,104,128]{2,1,0:T(8,128)S(1)}, u32[]{:S(2)}, u32[]{:S(2)}) collective-permute-start(f32[4,104,128]{2,1,0:T(8,128)S(1)} %get-tuple-element.16), channel_id=1, source_target_pairs={{0,256},{64,320},{128,384},{192,448},{256,0},{320,64},{384,128},{4... | collective-permute-start | bytes 638984 | tf_op jit(solution)/shard_map/ppermute | solution.py:205
  46.0 41.0 %all-gather = f32[16,104,128]{2,1,0:T(8,128)S(1)} all-gather(f32[4,104,128]{2,1,0:T(8,128)S(1)} %get-tuple-element.16), channel_id=2, replica_groups={{0,64,128,192},{256,320,384,448},{1,65,129,193},{257,321,385,449},{2,66..., dimensions={0}, use_global_device_ids=true | all-gather | bytes 1064960 | tf_op jit(solution)/shard_map/all_gather | solution.py:208
  87.1 0.1 pad_maximum_fusion.refs_2_
  87.1 1.9 %collective-permute-start.8 = (f32[4,2,40,640]{3,2,1,0:T(8,128)S(1)}, f32[4,2,40,640]{3,2,1,0:T(8,128)S(1)}, u32[]{:S(2)}, u32[]{:S(2)}) collective-permute-start(f32[4,2,40,640]{3,2,1,0:T(8,128)S(1)} %pad_maximum_fusion.refs_2_), channel_id=1, source_target_pairs={{0,1},{1,0},{2,3},{3,2},{4,5},{5,4},{6,7},{7,6},{8,9},{9,8},{10,11... | collective-permute-start | bytes 2457608 | tf_op jit(solution)/shard_map/ppermute | solution.py:173
  89.1 2.5 %collective-permute-start.7 = (f32[2,40,640]{2,1,0:T(8,128)S(1)}, f32[2,40,640]{2,1,0:T(8,128)S(1)}, u32[]{:S(2)}, u32[]{:S(2)}) collective-permute-start(f32[2,40,640]{2,1,0:T(8,128)S(1)} %collective-permute-done.1), channel_id=1, source_target_pairs={{0,48},{16,0},{32,16},{48,32},{1,49},{17,1},{33,17},{49,33},{2,50}... | collective-permute-start | bytes 614408 | tf_op jit(solution)/shard_map/ppermute | solution.py:173
  91.5 3.7 %collective-permute-start.6 = (f32[2,40,640]{2,1,0:T(8,128)S(1)}, f32[2,40,640]{2,1,0:T(8,128)S(1)}, u32[]{:S(2)}, u32[]{:S(2)}) collective-permute-start(f32[2,40,640]{2,1,0:T(8,128)S(1)} %collective-permute-done.1), channel_id=1, source_target_pairs={{0,32},{16,48},{32,0},{48,16},{1,33},{17,49},{33,1},{49,17},{2,34}... | collective-permute-start | bytes 614408 | tf_op jit(solution)/shard_map/ppermute | solution.py:173
  95.3 4.3 %collective-permute-start.5 = (f32[2,40,640]{2,1,0:T(8,128)S(1)}, f32[2,40,640]{2,1,0:T(8,128)S(1)}, u32[]{:S(2)}, u32[]{:S(2)}) collective-permute-start(f32[2,40,640]{2,1,0:T(8,128)S(1)} %collective-permute-done.1), channel_id=1, source_target_pairs={{0,16},{16,32},{32,48},{48,0},{1,17},{17,33},{33,49},{49,1},{2,18}... | collective-permute-start | bytes 614408 | tf_op jit(solution)/shard_map/ppermute | solution.py:173
  99.6 20.6 %all-gather.1 = f32[16,104,128]{2,1,0:T(8,128)S(1)} all-gather(f32[4,104,128]{2,1,0:T(8,128)S(1)} %collective-permute-done), channel_id=3, replica_groups={{0,64,128,192},{256,320,384,448},{1,65,129,193},{257,321,385,449},{2,66..., dimensions={0}, use_global_device_ids=true | all-gather | bytes 1064960 | tf_op jit(solution)/shard_map/all_gather | solution.py:213
  120.3 1.9 %collective-permute-start.9 = (f32[4,2,40,640]{3,2,1,0:T(8,128)S(1)}, f32[4,2,40,640]{3,2,1,0:T(8,128)S(1)}, u32[]{:S(2)}, u32[]{:S(2)}) collective-permute-start(f32[4,2,40,640]{3,2,1,0:T(8,128)S(1)} %pad_maximum_fusion.1.refs_4_), channel_id=1, source_target_pairs={{0,1},{1,0},{2,3},{3,2},{4,5},{5,4},{6,7},{7,6},{8,9},{9,8},{10,11... | collective-permute-start | bytes 2457608 | tf_op jit(solution)/shard_map/ppermute | solution.py:173
  122.2 2.3 %collective-permute-done.9.refs_5_ = f32[4,2,40,640]{3,2,1,0:T(8,128)S(1)} collective-permute-done((f32[4,2,40,640]{3,2,1,0:T(8,128)S(1)}, f32[4,2,40,640]{3,2,1,0:T(8,128)S(1)}, u32[]{:S(2)}, u32[]{:S(2)}) %collective-permute-start.9) | collective-permute-done | bytes 819232 | tf_op jit(solution)/shard_map/ppermute | solution.py:173
  124.5 4.3 %shard_map.39 = f32[4,80,640]{2,1,0:T(8,128)S(1)} custom-call(s32[5]{0:T(128)S(1)} %stack.53.at_ref, f32[4,4,104,128]{3,2,1,0:T(8,128)S(1)} %bitcast.19, f32[4,4,104,128]{3,2,1,0:T(8,128)S(1)} %bitcast.20, f32[4,2,40,640]{3,2,1,0:T(8,128)S(1)} %pad_maximum_fusion.refs_2_, f32[4,2,40,640]{3,2,1,0:T(8,128)S(1)} %collective-permute-done.8.refs_3_, ...), custom_call_target="tpu_custom_call" | custom-call | flops 3000000000 | bytes 6000000 | tf_op jit(solution)/shard_map/pallas_call | solution.py:30
  128.8 15.6 %all_to_all.16.shares_ref = f32[4,80,640]{2,1,0:T(8,128)S(1)} all-to-all(f32[4,80,640]{2,1,0:T(8,128)S(1)} %shard_map.39), channel_id=1, replica_groups=mesh['zl'=8,'x'=4,'y'=4,'zh'=2,'c'=2] {'y'}, dimensions={0} | all-to-all | bytes 1638400 | tf_op jit(solution)/shard_map/all_to_all | solution.py:226
  144.4 1.1 shard_map.40
  145.5 14.5 %all_to_all.17 = f32[8,1,80]{2,1,0:T(1,128)S(1)} all-to-all(f32[8,1,80]{2,1,0:T(1,128)S(1)} %bitcast.23), channel_id=1, replica_groups=mesh['zl'=8,'x'=4,'y'=4,'zh'=2,'c'=2] {'zl'}, dimensions={0} | all-to-all | bytes 5120 | tf_op jit(solution)/shard_map/all_to_all | solution.py:233
  160.0 0.9 shard_map.41
  (15 shorter events, 0.1 us)
Async XLA Ops:
  0.0 0.7 copy-start.1
  0.7 0.9 copy-start
  16.2 70.8 %collective-permute-start.4 = (f32[2,40,640]{2,1,0:T(8,128)S(1)}, f32[2,40,640]{2,1,0:T(8,128)S(1)}, u32[]{:S(2)}, u32[]{:S(2)}) collective-permute-start(f32[2,40,640]{2,1,0:T(8,128)S(1)} %get-tuple-element.17), channel_id=1, source_target_pairs={{0,48},{16,0},{32,16},{48,32},{1,49},{17,1},{33,17},{49,33},{2,50}... | collective-permute-start | bytes 614408 | tf_op jit(solution)/shard_map/ppermute | solution.py:173
  19.0 68.1 %collective-permute-start.3 = (f32[2,40,640]{2,1,0:T(8,128)S(1)}, f32[2,40,640]{2,1,0:T(8,128)S(1)}, u32[]{:S(2)}, u32[]{:S(2)}) collective-permute-start(f32[2,40,640]{2,1,0:T(8,128)S(1)} %get-tuple-element.17), channel_id=1, source_target_pairs={{0,32},{16,48},{32,0},{48,16},{1,33},{17,49},{33,1},{49,17},{2,34}... | collective-permute-start | bytes 614408 | tf_op jit(solution)/shard_map/ppermute | solution.py:173
  24.4 62.6 %collective-permute-start.2 = (f32[2,40,640]{2,1,0:T(8,128)S(1)}, f32[2,40,640]{2,1,0:T(8,128)S(1)}, u32[]{:S(2)}, u32[]{:S(2)}) collective-permute-start(f32[2,40,640]{2,1,0:T(8,128)S(1)} %get-tuple-element.17), channel_id=1, source_target_pairs={{0,16},{16,32},{32,48},{48,0},{1,17},{17,33},{33,49},{49,1},{2,18}... | collective-permute-start | bytes 614408 | tf_op jit(solution)/shard_map/ppermute | solution.py:173
  26.4 60.8 %collective-permute-start.1 = (f32[2,40,640]{2,1,0:T(8,128)S(1)}, f32[2,40,640]{2,1,0:T(8,128)S(1)}, u32[]{:S(2)}, u32[]{:S(2)}) collective-permute-start(f32[2,40,640]{2,1,0:T(8,128)S(1)} %get-tuple-element.17), channel_id=1, source_target_pairs={{0,2},{2,0},{1,3},{3,1},{4,6},{6,4},{5,7},{7,5},{8,10},{10,8},{9,1... | collective-permute-start | bytes 614408 | tf_op jit(solution)/shard_map/ppermute | solution.py:173
  41.7 45.4 %collective-permute-start = (f32[4,104,128]{2,1,0:T(8,128)S(1)}, f32[4,104,128]{2,1,0:T(8,128)S(1)}, u32[]{:S(2)}, u32[]{:S(2)}) collective-permute-start(f32[4,104,128]{2,1,0:T(8,128)S(1)} %get-tuple-element.16), channel_id=1, source_target_pairs={{0,256},{64,320},{128,384},{192,448},{256,0},{320,64},{384,128},{4... | collective-permute-start | bytes 638984 | tf_op jit(solution)/shard_map/ppermute | solution.py:205
  87.1 33.2 %collective-permute-start.8 = (f32[4,2,40,640]{3,2,1,0:T(8,128)S(1)}, f32[4,2,40,640]{3,2,1,0:T(8,128)S(1)}, u32[]{:S(2)}, u32[]{:S(2)}) collective-permute-start(f32[4,2,40,640]{3,2,1,0:T(8,128)S(1)} %pad_maximum_fusion.refs_2_), channel_id=1, source_target_pairs={{0,1},{1,0},{2,3},{3,2},{4,5},{5,4},{6,7},{7,6},{8,9},{9,8},{10,11... | collective-permute-start | bytes 2457608 | tf_op jit(solution)/shard_map/ppermute | solution.py:173
  89.1 31.1 %collective-permute-start.7 = (f32[2,40,640]{2,1,0:T(8,128)S(1)}, f32[2,40,640]{2,1,0:T(8,128)S(1)}, u32[]{:S(2)}, u32[]{:S(2)}) collective-permute-start(f32[2,40,640]{2,1,0:T(8,128)S(1)} %collective-permute-done.1), channel_id=1, source_target_pairs={{0,48},{16,0},{32,16},{48,32},{1,49},{17,1},{33,17},{49,33},{2,50}... | collective-permute-start | bytes 614408 | tf_op jit(solution)/shard_map/ppermute | solution.py:173
  91.5 28.7 %collective-permute-start.6 = (f32[2,40,640]{2,1,0:T(8,128)S(1)}, f32[2,40,640]{2,1,0:T(8,128)S(1)}, u32[]{:S(2)}, u32[]{:S(2)}) collective-permute-start(f32[2,40,640]{2,1,0:T(8,128)S(1)} %collective-permute-done.1), channel_id=1, source_target_pairs={{0,32},{16,48},{32,0},{48,16},{1,33},{17,49},{33,1},{49,17},{2,34}... | collective-permute-start | bytes 614408 | tf_op jit(solution)/shard_map/ppermute | solution.py:173
  95.3 25.0 %collective-permute-start.5 = (f32[2,40,640]{2,1,0:T(8,128)S(1)}, f32[2,40,640]{2,1,0:T(8,128)S(1)}, u32[]{:S(2)}, u32[]{:S(2)}) collective-permute-start(f32[2,40,640]{2,1,0:T(8,128)S(1)} %collective-permute-done.1), channel_id=1, source_target_pairs={{0,16},{16,32},{32,48},{48,0},{1,17},{17,33},{33,49},{49,1},{2,18}... | collective-permute-start | bytes 614408 | tf_op jit(solution)/shard_map/ppermute | solution.py:173
  120.3 4.2 %collective-permute-start.9 = (f32[4,2,40,640]{3,2,1,0:T(8,128)S(1)}, f32[4,2,40,640]{3,2,1,0:T(8,128)S(1)}, u32[]{:S(2)}, u32[]{:S(2)}) collective-permute-start(f32[4,2,40,640]{3,2,1,0:T(8,128)S(1)} %pad_maximum_fusion.1.refs_4_), channel_id=1, source_target_pairs={{0,1},{1,0},{2,3},{3,2},{4,5},{5,4},{6,7},{7,6},{8,9},{9,8},{10,11... | collective-permute-start | bytes 2457608 | tf_op jit(solution)/shard_map/ppermute | solution.py:173
  128.8 15.6 %copy-start.2 = (s32[20,20]{1,0:T(8,128)S(1)}, s32[20,20]{1,0:T(8,128)}, u32[]{:S(2)}) copy-start(s32[20,20]{1,0:T(8,128)} %pattern_ref.3) | copy-start | bytes 4804

commit v14 on v12

--- a/solution.py
+++ b/solution.py
@@ -12,7 +12,6 @@
 MAIN, REST = 80, 24
 LEFT = MAIN + REST
 RUN, PAD = 20, 24
-PIECE = LEFT + 5 * PAD
 VMEM = pl.BlockSpec(memory_space=pltpu.VMEM)
 SMEM = pl.BlockSpec(memory_space=pltpu.SMEM)
 
@@ -50,20 +49,15 @@
     return x * jnp.where(here, low, high)
 
 
-def pack_right(at_ref, owner, pattern_ref, state_ref, masked_ref, out_ref, base):
+def mask(at_ref, pattern_ref, state_ref, masked_ref):
     for h in range(5):
         lanes = slice(128 * h, 128 * h + 128)
-        masked_ref[:, lanes] = masked_block(at_ref, owner, pattern_ref, h, state_ref[:, lanes])
-    out_ref[...] = jnp.zeros_like(out_ref)
-    for y in range(4):
-        for h in range(5):
-            rows = slice(base + PAD * h, base + PAD * h + RUN)
-            out_ref[y, rows] = masked_ref[RUN * y : RUN * y + RUN, 128 * h : 128 * h + 128]
-
-
-def pieces_kernel(at_ref, pattern_ref, state_ref, out_ref, masked_ref):
+        masked_ref[:, lanes] = masked_block(at_ref, at_ref[0], pattern_ref, h, state_ref[:, lanes])
+
+
+def left_kernel(at_ref, pattern_ref, state_ref, out_ref, masked_ref):
     zh, c = at_ref[2], at_ref[3]
-    pack_right(at_ref, at_ref[0], pattern_ref, state_ref, masked_ref, out_ref, LEFT)
+    mask(at_ref, pattern_ref, state_ref, masked_ref)
     n = lax.broadcasted_iota(jnp.int32, (1, 640), 1)
     late = n >= 512
     y = jnp.where(late, (n - 512) // 32, n // 128)
@@ -75,9 +69,8 @@
     order = lax.broadcasted_iota(jnp.int32, (640, 640), 0) == source
     order = order.astype(jnp.float32).astype(jnp.bfloat16)
     x = masked_ref[...]
-    hi, rest = x.astype(jnp.bfloat16), x
-    rest = x - hi.astype(jnp.float32)
-    mid, low = split(rest)
+    hi = x.astype(jnp.bfloat16)
+    mid, low = split(x - hi.astype(jnp.float32))
     moved = (dot(hi, order) + dot(mid, order)) + dot(low, order)
     lane = lax.broadcasted_iota(jnp.int32, (8, 128), 1) // 32
     for y in range(4):
@@ -93,32 +86,48 @@
             out_ref[y, MAIN + 8 * slot : MAIN + 8 * slot + 8] = tile
 
 
-def unpack_right(got_ref, right_ref, base):
+def right_kernel(at_ref, pattern_ref, state_ref, out_ref, masked_ref):
+    mask(at_ref, pattern_ref, state_ref, masked_ref)
+    out_ref[...] = jnp.zeros_like(out_ref)
+    for y in range(4):
+        for h in range(5):
+            out_ref[y, PAD * h : PAD * h + RUN] = masked_ref[
+                RUN * y : RUN * y + RUN, 128 * h : 128 * h + 128
+            ]
+
+
+def unpack_kernel(got_ref, right_ref):
     for y in range(4):
         for h in range(5):
             right_ref[y // 2, RUN * (y % 2) : RUN * (y % 2) + RUN, 128 * h : 128 * h + 128] = (
-                got_ref[y, base + PAD * h : base + PAD * h + RUN]
+                got_ref[y, PAD * h : PAD * h + RUN]
             )
 
 
-def unpack_kernel(got_ref, left_ref, right_ref):
-    left_ref[...] = got_ref[:, :LEFT]
-    unpack_right(got_ref, right_ref, LEFT)
-
-
-def product_kernel(at_ref, left_ref, right_ref, out_ref, hi_ref, lo_ref):
-    for dc in range(2):
-        c = lax.rem(at_ref[3] + dc, 2)
-        for dzh in range(2):
-            rows = slice(40 * (2 * dzh + dc), 40 * (2 * dzh + dc) + 40)
-            for x in range(4):
-                for y1 in range(2):
-                    hi, lo = split(right_ref[c, x, lax.rem(at_ref[2] + dzh, 2), y1])
-                    hi_ref[2 * x + y1, rows] = hi
-                    lo_ref[2 * x + y1, rows] = lo
+def halves_kernel(at_ref, right_ref, hi_ref, lo_ref):
+    zh, c = at_ref[2], at_ref[3]
+    for x in range(4):
+        for y1 in range(2):
+            rows = [
+                right_ref[lax.rem(c + dc, 2), x, lax.rem(zh + dzh, 2), y1]
+                for dzh in range(2)
+                for dc in range(2)
+            ]
+            rows = jnp.concatenate(rows + [rows[3][8:]] * 3, axis=0)
+            hi_ref[2 * x + y1], lo_ref[2 * x + y1] = split(rows)
+
+
+def product_kernel(left_hbm, hi_ref, lo_ref, out_ref, left_ref, sems):
+    copies = [
+        pltpu.make_async_copy(left_hbm.at[block], left_ref.at[block], sems.at[block])
+        for block in range(8)
+    ]
+    for copy in copies:
+        copy.start()
     lane = lax.broadcasted_iota(jnp.int32, (8, 128), 1) // 32
     total = jnp.zeros((320, 640), jnp.float32)
     for block in range(8):
+        copies[block].wait()
         whole = []
         for y in range(4):
             rest = []
@@ -130,8 +139,6 @@
             whole.append(jnp.concatenate([left_ref[block, y, :MAIN], rest], axis=1))
         left_hi, left_lo = split(jnp.concatenate(whole, axis=0))
         right_hi, right_lo = hi_ref[block], lo_ref[block]
-        right_hi = jnp.concatenate([right_hi] + [right_hi[128:]] * 3, axis=0)
-        right_lo = jnp.concatenate([right_lo] + [right_lo[128:]] * 3, axis=0)
         total += dot(left_hi, right_hi) + (dot(left_hi, right_lo) + dot(left_lo, right_hi))
     out_ref[...] = total.reshape(4, 80, 640)
 
@@ -183,26 +190,26 @@
         [lax.axis_index(ROWS)] + [lax.axis_index(a) for a in ("zl", "zh", "c")]
     ).astype(jnp.int32)
 
-    pieces = call(
-        pieces_kernel,
-        f32(4, PIECE, 128),
-        [SMEM, SMEM, VMEM],
-        (at, in_pattern, state),
-        [pltpu.VMEM((rows, cols), jnp.float32)],
-    )
-    got = lax.all_to_all(pieces, "y", 0, 0)
-    left, near = call(
-        unpack_kernel, (f32(4, LEFT, 128), f32(2, 2 * RUN, cols)), [VMEM], (got,)
-    )
+    work = [pltpu.VMEM((rows, cols), jnp.float32)]
+    specs = [SMEM, SMEM, VMEM]
+    left = call(left_kernel, f32(4, LEFT, 128), specs, (at, in_pattern, state), work)
+    left = lax.all_to_all(left, "y", 0, 0)
+    left, later = lax.optimization_barrier((left, state))
     left = lax.all_gather(left, "zl", axis=0)
-    right = gather(gather(gather(near, "zh"), "x"), "c")
+
+    right = call(right_kernel, f32(4, 5 * PAD, 128), specs, (at, in_pattern, later), work)
+    right = lax.all_to_all(right, "y", 0, 0)
+    right = call(unpack_kernel, f32(2, 2 * RUN, cols), [VMEM], (right,))
+    right = gather(gather(gather(right, "zh"), "x"), "c")
+    half = jax.ShapeDtypeStruct((8, 256, cols), jnp.bfloat16)
+    right_hi, right_lo = call(halves_kernel, (half, half), [SMEM, VMEM], (at, right))
 
     partial = call(
         product_kernel,
         f32(4, rows, cols),
-        [SMEM, VMEM, VMEM],
-        (at, left, right),
-        [pltpu.VMEM((8, 160, cols), jnp.bfloat16)] * 2,
+        [pl.BlockSpec(memory_space=pltpu.HBM), VMEM, VMEM],
+        (left, right_hi, right_lo),
+        [pltpu.VMEM((8, 4, LEFT, 128), jnp.float32), pltpu.SemaphoreType.DMA((8,))],
         flops=3 * 10**9,
         size=6 * 10**6,
     )

time: 146 us -> 163 us (1.12)
  blocking collectives: 101 us -> 125 us
  waiting for transfers between devices: 18.8 us -> 1.63 us
  Pallas kernels: 7.99 us -> 12.9 us
  local copies, waits for them, and re-layouts: 3.5 us -> 8.37 us
    all_gather x1, waiting for transfers between devices: 18.8 us -> 1.62 us  [body(): left = lax.all_gather(left, 'zl', axis=0)]
    all_to_all x3, blocking collectives: 57.4 us -> 67.4 us  [gather(): return lax.all_to_all(copies, axis_name, 0, 0)]
    all_to_all x1, blocking collectives: 16.2 us -> 23.4 us  [body(): sums = lax.all_to_all(sums.reshape(8, 1, rows), 'zl', 0, 0).reshape(8, rows)]
    all_to_all x1 -> x2, blocking collectives: 13 us -> 19.8 us  [the longest x1 10.8 us: body(): left = lax.all_to_all(left, 'y', 0, 0)]
    pallas_call x5 -> x7, Pallas kernels: 7.99 us -> 12.9 us  [call(): pl.pallas_call(kernel, out_shape=outs, in_specs=in_specs, out_specs=jax.t...]
    unnamed x8 -> x16, local copies, waits for them, and re-layouts: 3.09 us -> 7.97 us
  transfers between devices with their start and end apart: 1 -> 1, of which waited for: 1 -> 1; matrix products, arithmetic and copies ran while one was open for 0% -> 0% of each run, Pallas kernels for 0% -> 1%
where the time goes in v14:
time: 163 us; the launch traced here: 162 us
  blocking collectives  125 us (77%)
  between operations  13.5 us (8%)
  Pallas kernels  12.9 us (8%)
  local copies, waits for them, and re-layouts  8.37 us (5%)
    all_to_all x3, blocking collectives, gather(): return lax.all_to_all(copies, axis_name, 0, 0)  67.4 us
    all_to_all x1, blocking collectives, body(): sums = lax.all_to_all(sums.reshape(8, 1, rows), 'zl', 0, 0).reshape(8, rows)  23.4 us
    all_to_all x1, blocking collectives, body(): shares = lax.all_to_all(partial, 'y', 0, 0)  14.6 us
    pallas_call x7, Pallas kernels, call(): pl.pallas_call(kernel, out_shape=outs, in_specs=in_specs, out_specs=jax.t...  12.9 us
    all_to_all x1, blocking collectives, body(): left = lax.all_to_all(left, 'y', 0, 0)  10.8 us
    all_to_all x1, blocking collectives, body(): right = lax.all_to_all(right, 'y', 0, 0)  8.97 us
    unnamed x16, local copies, waits for them, and re-layouts  7.97 us
  transfers between devices with their start and end apart: 1, of which 1 were waited for; matrix products, arithmetic and copies ran while one was open for 0% of the time, Pallas kernels for 1%

profile of v14, /device:TPU:6, one launch (start us, length us, event | category | flops | bytes accessed | tf_op | source)
XLA Modules:
  0.0 161.7 jit_solution(346535875531155904)
XLA Ops:
  6.5 0.1 pad_add_fusion.at_ref
  6.6 0.9 copy-done
  7.5 0.7 copy-done.2
  8.3 1.5 shard_map.37
  9.8 10.8 %all_to_all.35 = f32[4,104,128]{2,1,0:T(8,128)} all-to-all(f32[4,104,128]{2,1,0:T(8,128)S(1)} %shard_map.37), channel_id=1, replica_groups=mesh['zl'=8,'x'=4,'y'=4,'zh'=2,'c'=2] {'y'}, dimensions={0} | all-to-all | bytes 425984 | tf_op jit(solution)/shard_map/all_to_all | solution.py:196
  20.6 0.9 copy-done.1
  21.5 0.7 copy-done.3
  22.2 0.8 shard_map.38
  23.0 9.0 %all_to_all.36.got_ref = f32[4,120,128]{2,1,0:T(8,128)S(1)} all-to-all(f32[4,120,128]{2,1,0:T(8,128)S(1)} %shard_map.38), channel_id=1, replica_groups=mesh['zl'=8,'x'=4,'y'=4,'zh'=2,'c'=2] {'y'}, dimensions={0} | all-to-all | bytes 491520 | tf_op jit(solution)/shard_map/all_to_all | solution.py:201
  32.1 42.9 %all_to_all.37 = f32[2,2,40,640]{3,2,1,0:T(8,128)S(1)} all-to-all(f32[2,2,40,640]{3,2,1,0:T(8,128)S(1)} %broadcast_in_dim.6), channel_id=1, replica_groups=mesh['zl'=8,'x'=4,'y'=4,'zh'=2,'c'=2] {'zh'}, dimensions={0} | all-to-all | bytes 819200 | tf_op jit(solution)/shard_map/all_to_all | solution.py:179
  74.9 0.1 broadcast_in_dim.7
  75.0 18.2 %all_to_all.38 = f32[4,2,2,40,640]{4,3,2,1,0:T(8,128)S(1)} all-to-all(f32[4,2,2,40,640]{4,3,2,1,0:T(8,128)S(1)} %broadcast_in_dim.7), channel_id=1, replica_groups=mesh['zl'=8,'x'=4,'y'=4,'zh'=2,'c'=2] {'x'}, dimensions={0} | all-to-all | bytes 3276800 | tf_op jit(solution)/shard_map/all_to_all | solution.py:179
  93.2 0.3 broadcast_in_dim.8
  93.4 6.4 %all_to_all.39.right_ref = f32[2,4,2,2,40,640]{5,4,3,2,1,0:T(8,128)S(1)} all-to-all(f32[2,4,2,2,40,640]{5,4,3,2,1,0:T(8,128)S(1)} %broadcast_in_dim.8), channel_id=1, replica_groups=mesh['zl'=8,'x'=4,'y'=4,'zh'=2,'c'=2] {'c'}, dimensions={0} | all-to-all | bytes 6553600 | tf_op jit(solution)/shard_map/all_to_all | solution.py:179
  99.8 1.3 shard_map.40
  101.1 1.5 copy-done.5
  102.6 1.6 all-gather.3.cloned.1.call-done
  104.2 1.7 %copy-done.6 = bf16[8,256,640]{2,1,0:T(8,128)(2,1)S(1)} copy-done((bf16[8,256,640]{2,1,0:T(8,128)(2,1)S(1)}, bf16[8,256,640]{2,1,0:T(8,128)(2,1)}, u32[]{:S(2)}) %copy-start.6) | copy-done | bytes 2621464
  106.0 1.5 copy-done.7
  107.4 7.4 %shard_map.41 = f32[4,80,640]{2,1,0:T(8,128)S(1)} custom-call(f32[8,4,104,128]{3,2,1,0:T(8,128)S(1)} %bitcast.11, bf16[8,256,640]{2,1,0:T(8,128)(2,1)S(1)} %get-tuple-element.13.hi_ref, bf16[8,256,640]{2,1,0:T(8,128)(2,1)S(1)} %copy-done.6), custom_call_target="tpu_custom_call" | custom-call | flops 3000000000 | bytes 6000000 | tf_op jit(solution)/shard_map/pallas_call | solution.py:29
  114.8 14.6 %all_to_all.40.shares_ref = f32[4,80,640]{2,1,0:T(8,128)S(1)} all-to-all(f32[4,80,640]{2,1,0:T(8,128)S(1)} %shard_map.41), channel_id=1, replica_groups=mesh['zl'=8,'x'=4,'y'=4,'zh'=2,'c'=2] {'y'}, dimensions={0} | all-to-all | bytes 1638400 | tf_op jit(solution)/shard_map/all_to_all | solution.py:216
  129.4 1.1 shard_map.42
  130.5 23.4 %all_to_all.41 = f32[8,1,80]{2,1,0:T(1,128)S(1)} all-to-all(f32[8,1,80]{2,1,0:T(1,128)S(1)} %bitcast.10), channel_id=1, replica_groups=mesh['zl'=8,'x'=4,'y'=4,'zh'=2,'c'=2] {'zl'}, dimensions={0} | all-to-all | bytes 5120 | tf_op jit(solution)/shard_map/all_to_all | solution.py:223
  153.9 0.9 shard_map.43
  (13 shorter events, 0.1 us)
Async XLA Ops:
  6.5 97.7 %all-gather.3.cloned.1.call-start = ((), (), s32[]{:S(2)}) async-start(), calls=%async_computation.7 | async-start | bytes 1916928 | tf_op jit(solution)/shard_map/all_gather | solution.py:198
  6.6 0.9 copy-start
  7.5 0.7 copy-start.2
  20.6 0.9 copy-start.1
  21.5 0.7 copy-start.3
  101.1 1.5 copy-start.5
  104.2 1.7 %copy-start.6 = (bf16[8,256,640]{2,1,0:T(8,128)(2,1)S(1)}, bf16[8,256,640]{2,1,0:T(8,128)(2,1)}, u32[]{:S(2)}) copy-start(bf16[8,256,640]{2,1,0:T(8,128)(2,1)} %copy-done.5) | copy-start | bytes 7864324
  106.0 1.5 copy-start.7
  107.4 22.0 %copy-start.4 = (s32[20,20]{1,0:T(8,128)S(1)}, s32[20,20]{1,0:T(8,128)}, u32[]{:S(2)}) copy-start(s32[20,20]{1,0:T(8,128)} %pattern_ref.5) | copy-start | bytes 4804
Sparse Core Ops, SparseCore 0:
  20.7 83.4 all-gather.2

commit v15 on v12

--- a/solution.py
+++ b/solution.py
@@ -15,6 +15,7 @@
 PIECE = LEFT + 5 * PAD
 VMEM = pl.BlockSpec(memory_space=pltpu.VMEM)
 SMEM = pl.BlockSpec(memory_space=pltpu.SMEM)
+HBM = pl.BlockSpec(memory_space=pltpu.HBM)
 
 
 def split(x):
@@ -26,14 +27,14 @@
     return jnp.dot(a, b, preferred_element_type=jnp.float32)
 
 
-def call(kernel, outs, in_specs, args, scratch=(), flops=10**6, size=10**6):
+def call(kernel, outs, in_specs, args, scratch=(), flops=10**6, size=10**6, vmem=40):
     return pl.pallas_call(
         kernel,
         out_shape=outs,
         in_specs=in_specs,
         out_specs=jax.tree.map(lambda _: VMEM, outs),
         scratch_shapes=scratch,
-        compiler_params=pltpu.CompilerParams(vmem_limit_bytes=40 * 2**20),
+        compiler_params=pltpu.CompilerParams(vmem_limit_bytes=vmem * 2**20),
         cost_estimate=pl.CostEstimate(
             flops=flops, bytes_accessed=size, transcendentals=0
         ),
@@ -50,20 +51,14 @@
     return x * jnp.where(here, low, high)
 
 
-def pack_right(at_ref, owner, pattern_ref, state_ref, masked_ref, out_ref, base):
-    for h in range(5):
-        lanes = slice(128 * h, 128 * h + 128)
-        masked_ref[:, lanes] = masked_block(at_ref, owner, pattern_ref, h, state_ref[:, lanes])
-    out_ref[...] = jnp.zeros_like(out_ref)
-    for y in range(4):
-        for h in range(5):
-            rows = slice(base + PAD * h, base + PAD * h + RUN)
-            out_ref[y, rows] = masked_ref[RUN * y : RUN * y + RUN, 128 * h : 128 * h + 128]
-
-
-def pieces_kernel(at_ref, pattern_ref, state_ref, out_ref, masked_ref):
+def pieces_kernel(
+    at_ref, pattern_hbm, state_hbm, out_ref, pattern_ref, state_ref, masked_ref, sems
+):
+    pattern_copy = pltpu.make_async_copy(pattern_hbm, pattern_ref, sems.at[0])
+    state_copy = pltpu.make_async_copy(state_hbm, state_ref, sems.at[1])
+    pattern_copy.start()
+    state_copy.start()
     zh, c = at_ref[2], at_ref[3]
-    pack_right(at_ref, at_ref[0], pattern_ref, state_ref, masked_ref, out_ref, LEFT)
     n = lax.broadcasted_iota(jnp.int32, (1, 640), 1)
     late = n >= 512
     y = jnp.where(late, (n - 512) // 32, n // 128)
@@ -74,13 +69,26 @@
     source = 80 * (4 * y0 + 2 * zh_of + c_of) + 20 * y + t
     order = lax.broadcasted_iota(jnp.int32, (640, 640), 0) == source
     order = order.astype(jnp.float32).astype(jnp.bfloat16)
+    pattern_copy.wait()
+    state_copy.wait()
+    for h in range(5):
+        lanes = slice(128 * h, 128 * h + 128)
+        masked_ref[:, lanes] = masked_block(
+            at_ref, at_ref[0], pattern_ref, h, state_ref[:, lanes]
+        )
     x = masked_ref[...]
-    hi, rest = x.astype(jnp.bfloat16), x
-    rest = x - hi.astype(jnp.float32)
-    mid, low = split(rest)
+    hi = x.astype(jnp.bfloat16)
+    mid, low = split(x - hi.astype(jnp.float32))
     moved = (dot(hi, order) + dot(mid, order)) + dot(low, order)
     lane = lax.broadcasted_iota(jnp.int32, (8, 128), 1) // 32
     for y in range(4):
+        for h in range(5):
+            out_ref[y, LEFT + PAD * h : LEFT + PAD * h + RUN] = masked_ref[
+                RUN * y : RUN * y + RUN, 128 * h : 128 * h + 128
+            ]
+            out_ref[y, LEFT + PAD * h + RUN : LEFT + PAD * h + PAD] = jnp.zeros(
+                (PAD - RUN, 128), jnp.float32
+            )
         out_ref[y, :MAIN] = moved[:, 128 * y : 128 * y + 128]
         for slot in range(3):
             tile = jnp.zeros((8, 128), jnp.float32)
@@ -93,46 +101,58 @@
             out_ref[y, MAIN + 8 * slot : MAIN + 8 * slot + 8] = tile
 
 
-def unpack_right(got_ref, right_ref, base):
+def unpack_left_kernel(got_ref, left_ref):
+    left_ref[...] = got_ref[:, :LEFT]
+
+
+def unpack_right_kernel(got_ref, right_ref):
     for y in range(4):
         for h in range(5):
             right_ref[y // 2, RUN * (y % 2) : RUN * (y % 2) + RUN, 128 * h : 128 * h + 128] = (
-                got_ref[y, base + PAD * h : base + PAD * h + RUN]
+                got_ref[y, LEFT + PAD * h : LEFT + PAD * h + RUN]
             )
 
 
-def unpack_kernel(got_ref, left_ref, right_ref):
-    left_ref[...] = got_ref[:, :LEFT]
-    unpack_right(got_ref, right_ref, LEFT)
-
-
-def product_kernel(at_ref, left_ref, right_ref, out_ref, hi_ref, lo_ref):
-    for dc in range(2):
-        c = lax.rem(at_ref[3] + dc, 2)
-        for dzh in range(2):
-            rows = slice(40 * (2 * dzh + dc), 40 * (2 * dzh + dc) + 40)
-            for x in range(4):
-                for y1 in range(2):
-                    hi, lo = split(right_ref[c, x, lax.rem(at_ref[2] + dzh, 2), y1])
-                    hi_ref[2 * x + y1, rows] = hi
-                    lo_ref[2 * x + y1, rows] = lo
+def product_kernel(at_ref, left_hbm, right_hbm, out_ref, left_ref, right_ref, sems):
+    def left_copy(block):
+        return pltpu.make_async_copy(left_hbm.at[block], left_ref.at[block], sems.at[0, block])
+
+    def right_copy(c, x):
+        return pltpu.make_async_copy(
+            right_hbm.at[c, x], right_ref.at[c, x], sems.at[1, 2 * x + c]
+        )
+
+    for x in range(4):
+        for part in range(2):
+            right_copy(part, x).start()
+        for part in range(2):
+            left_copy(2 * x + part).start()
     lane = lax.broadcasted_iota(jnp.int32, (8, 128), 1) // 32
+    zh, c = at_ref[2], at_ref[3]
     total = jnp.zeros((320, 640), jnp.float32)
-    for block in range(8):
-        whole = []
-        for y in range(4):
-            rest = []
-            for tile in range(10):
-                rows = MAIN + 8 * (tile // 4)
-                part = left_ref[block, y, rows : rows + 8]
-                rest.append(jnp.where(lane == tile % 4, part, 0.0))
-            rest = jnp.concatenate(rest, axis=0)
-            whole.append(jnp.concatenate([left_ref[block, y, :MAIN], rest], axis=1))
-        left_hi, left_lo = split(jnp.concatenate(whole, axis=0))
-        right_hi, right_lo = hi_ref[block], lo_ref[block]
-        right_hi = jnp.concatenate([right_hi] + [right_hi[128:]] * 3, axis=0)
-        right_lo = jnp.concatenate([right_lo] + [right_lo[128:]] * 3, axis=0)
-        total += dot(left_hi, right_hi) + (dot(left_hi, right_lo) + dot(left_lo, right_hi))
+    for x in range(4):
+        for part in range(2):
+            right_copy(part, x).wait()
+        for y1 in range(2):
+            rows = [
+                right_ref[lax.rem(c + dc, 2), x, lax.rem(zh + dzh, 2), y1]
+                for dzh in range(2)
+                for dc in range(2)
+            ]
+            right_hi, right_lo = split(jnp.concatenate(rows + [rows[3][8:]] * 3, axis=0))
+            block = 2 * x + y1
+            left_copy(block).wait()
+            whole = []
+            for y in range(4):
+                rest = []
+                for tile in range(10):
+                    start = MAIN + 8 * (tile // 4)
+                    part = left_ref[block, y, start : start + 8]
+                    rest.append(jnp.where(lane == tile % 4, part, 0.0))
+                rest = jnp.concatenate(rest, axis=0)
+                whole.append(jnp.concatenate([left_ref[block, y, :MAIN], rest], axis=1))
+            left_hi, left_lo = split(jnp.concatenate(whole, axis=0))
+            total += dot(left_hi, right_hi) + (dot(left_hi, right_lo) + dot(left_lo, right_hi))
     out_ref[...] = total.reshape(4, 80, 640)
 
 
@@ -186,25 +206,36 @@
     pieces = call(
         pieces_kernel,
         f32(4, PIECE, 128),
-        [SMEM, SMEM, VMEM],
+        [SMEM, HBM, HBM],
         (at, in_pattern, state),
-        [pltpu.VMEM((rows, cols), jnp.float32)],
+        [
+            pltpu.SMEM(in_pattern.shape, jnp.int32),
+            pltpu.VMEM((rows, cols), jnp.float32),
+            pltpu.VMEM((rows, cols), jnp.float32),
+            pltpu.SemaphoreType.DMA((2,)),
+        ],
+        vmem=60,
     )
     got = lax.all_to_all(pieces, "y", 0, 0)
-    left, near = call(
-        unpack_kernel, (f32(4, LEFT, 128), f32(2, 2 * RUN, cols)), [VMEM], (got,)
-    )
+    left = call(unpack_left_kernel, f32(4, LEFT, 128), [VMEM], (got,))
+    left, got = lax.optimization_barrier((left, got))
     left = lax.all_gather(left, "zl", axis=0)
+    near = call(unpack_right_kernel, f32(2, 2 * RUN, cols), [VMEM], (got,))
     right = gather(gather(gather(near, "zh"), "x"), "c")
 
     partial = call(
         product_kernel,
         f32(4, rows, cols),
-        [SMEM, VMEM, VMEM],
+        [SMEM, HBM, HBM],
         (at, left, right),
-        [pltpu.VMEM((8, 160, cols), jnp.bfloat16)] * 2,
+        [
+            pltpu.VMEM(left.shape, jnp.float32),
+            pltpu.VMEM(right.shape, jnp.float32),
+            pltpu.SemaphoreType.DMA((2, 8)),
+        ],
         flops=3 * 10**9,
         size=6 * 10**6,
+        vmem=60,
     )
     shares = lax.all_to_all(partial, "y", 0, 0)
     inflated, sums = call(

time: 146 us -> 150 us (1.027)
  Pallas kernels: 7.99 us -> 14.3 us
  local copies, waits for them, and re-layouts: 3.5 us -> 0.41 us
  blocking collectives: 101 us -> 103 us
    pallas_call x5 -> x6, Pallas kernels: 7.99 us -> 14.3 us  [call(): pl.pallas_call(kernel, out_shape=outs, in_specs=in_specs, out_specs=jax.t...]
    unnamed x8 -> x4, local copies, waits for them, and re-layouts: 3.09 us -> 0.01 us
where the time goes in v15:
time: 150 us; the launch traced here: 149 us
  blocking collectives  103 us (69%)
  waiting for transfers between devices  17.7 us (12%)
  Pallas kernels  14.3 us (10%)
  between operations  13.4 us (9%)
    all_to_all x3, blocking collectives, gather(): return lax.all_to_all(copies, axis_name, 0, 0)  58.4 us
    all_gather x1, waiting for transfers between devices, body(): left = lax.all_gather(left, 'zl', axis=0)  17.7 us
    all_to_all x1, blocking collectives, body(): sums = lax.all_to_all(sums.reshape(8, 1, rows), 'zl', 0, 0).reshape(8, rows)  15.8 us
    all_to_all x1, blocking collectives, body(): shares = lax.all_to_all(partial, 'y', 0, 0)  15.3 us
    pallas_call x6, Pallas kernels, call(): pl.pallas_call(kernel, out_shape=outs, in_specs=in_specs, out_specs=jax.t...  14.3 us
    all_to_all x1, blocking collectives, body(): got = lax.all_to_all(pieces, 'y', 0, 0)  13.2 us
  transfers between devices with their start and end apart: 1, of which 1 were waited for; matrix products, arithmetic and copies ran while one was open for 0% of the time, Pallas kernels for 0%

profile of v15, /device:TPU:6, one launch (start us, length us, event | category | flops | bytes accessed | tf_op | source)
XLA Modules:
  0.0 149.2 jit_solution(11394176590847856756)
XLA Ops:
  6.5 0.0 all-gather.3.cloned.1.call-start
  6.5 0.7 pad_add_fusion.at_ref
  7.2 3.1 %shard_map.37 = f32[4,224,128]{2,1,0:T(8,128)} custom-call(s32[4]{0:T(128)} %pad_add_fusion.at_ref, s32[20,20]{1,0:T(8,128)} %pattern_hbm.1, f32[80,640]{1,0:T(8,128)} %state_hbm.1), custom_call_target="tpu_custom_call" | custom-call | flops 1000000 | bytes 1000000 | tf_op jit(solution)/shard_map/pallas_call | solution.py:31
  10.3 13.2 %all_to_all.30.got_ref = f32[4,224,128]{2,1,0:T(8,128)S(1)} all-to-all(f32[4,224,128]{2,1,0:T(8,128)} %shard_map.37), channel_id=1, replica_groups=mesh['zl'=8,'x'=4,'y'=4,'zh'=2,'c'=2] {'y'}, dimensions={0} | all-to-all | bytes 917504 | tf_op jit(solution)/shard_map/all_to_all | solution.py:219
  23.5 0.7 shard_map.38
  24.2 0.0 all-gather.3.cloned.1.call-update
  24.3 31.1 %all_to_all.31 = f32[2,2,40,640]{3,2,1,0:T(8,128)S(1)} all-to-all(f32[2,2,40,640]{3,2,1,0:T(8,128)S(1)} %broadcast_in_dim.6), channel_id=1, replica_groups=mesh['zl'=8,'x'=4,'y'=4,'zh'=2,'c'=2] {'zh'}, dimensions={0} | all-to-all | bytes 819200 | tf_op jit(solution)/shard_map/all_to_all | solution.py:192
  55.4 0.1 broadcast_in_dim.7
  55.5 19.9 %all_to_all.32 = f32[4,2,2,40,640]{4,3,2,1,0:T(8,128)S(1)} all-to-all(f32[4,2,2,40,640]{4,3,2,1,0:T(8,128)S(1)} %broadcast_in_dim.7), channel_id=1, replica_groups=mesh['zl'=8,'x'=4,'y'=4,'zh'=2,'c'=2] {'x'}, dimensions={0} | all-to-all | bytes 3276800 | tf_op jit(solution)/shard_map/all_to_all | solution.py:192
  75.4 0.3 broadcast_in_dim.8
  75.7 7.3 %all_to_all.33.right_hbm = f32[2,4,2,2,40,640]{5,4,3,2,1,0:T(8,128)} all-to-all(f32[2,4,2,2,40,640]{5,4,3,2,1,0:T(8,128)S(1)} %broadcast_in_dim.8), channel_id=1, replica_groups=mesh['zl'=8,'x'=4,'y'=4,'zh'=2,'c'=2] {'c'}, dimensions={0} | all-to-all | bytes 6553600 | tf_op jit(solution)/shard_map/all_to_all | solution.py:192
  83.1 17.7 %all-gather.3.cloned.1.call-done = f32[32,104,128]{2,1,0:T(8,128)} async-done(((f32[4,104,128]{2,1,0:T(8,128)}), f32[32,104,128]{2,1,0:T(8,128)}) %all-gather.3.cloned.1.call-update) | async-done | bytes 1703952 | tf_op jit(solution)/shard_map/all_gather | solution.py:222
  100.7 0.0 copy-start
  100.7 0.0 copy-start.1
  100.7 8.5 %shard_map.40 = f32[4,80,640]{2,1,0:T(8,128)} custom-call(s32[4]{0:T(128)} %pad_add_fusion.at_ref, f32[8,4,104,128]{3,2,1,0:T(8,128)} %bitcast.11, f32[2,4,2,2,40,640]{5,4,3,2,1,0:T(8,128)} %all_to_all.33.right_hbm), custom_call_target="tpu_custom_call" | custom-call | flops 3000000000 | bytes 6000000 | tf_op jit(solution)/shard_map/pallas_call | solution.py:31
  109.2 15.3 %all_to_all.34.shares_ref = f32[4,80,640]{2,1,0:T(8,128)S(1)} all-to-all(f32[4,80,640]{2,1,0:T(8,128)} %shard_map.40), channel_id=1, replica_groups=mesh['zl'=8,'x'=4,'y'=4,'zh'=2,'c'=2] {'y'}, dimensions={0} | all-to-all | bytes 1638400 | tf_op jit(solution)/shard_map/all_to_all | solution.py:240
  124.6 0.0 copy-done
  124.6 0.0 copy-done.1
  124.6 1.1 shard_map.41
  125.6 15.8 %all_to_all.35 = f32[8,1,80]{2,1,0:T(1,128)S(1)} all-to-all(f32[8,1,80]{2,1,0:T(1,128)S(1)} %bitcast.10), channel_id=1, replica_groups=mesh['zl'=8,'x'=4,'y'=4,'zh'=2,'c'=2] {'zl'}, dimensions={0} | all-to-all | bytes 5120 | tf_op jit(solution)/shard_map/all_to_all | solution.py:247
  141.4 0.9 shard_map.42
  (2 shorter events, 0.0 us)
Async XLA Ops:
  6.5 94.2 %all-gather.3.cloned.1.call-start = ((), (), s32[]{:S(2)}) async-start(), calls=%async_computation.6 | async-start | bytes 1916928 | tf_op jit(solution)/shard_map/all_gather | solution.py:222
  100.7 23.8 %copy-start = (s32[20,20]{1,0:T(8,128)S(1)}, s32[20,20]{1,0:T(8,128)}, u32[]{:S(2)}) copy-start(s32[20,20]{1,0:T(8,128)} %pattern_ref.1) | copy-start | bytes 4804
  100.7 23.8 %copy-start.1 = (s32[4]{0:T(128)S(1)}, s32[4]{0:T(128)}, u32[]{:S(2)}) copy-start(s32[4]{0:T(128)} %pad_add_fusion.at_ref) | copy-start | bytes 52
Sparse Core Ops, SparseCore 0:
  24.4 76.3 all-gather.2

commit v16 on v12

--- a/solution.py
+++ b/solution.py
@@ -12,7 +12,6 @@
 MAIN, REST = 80, 24
 LEFT = MAIN + REST
 RUN, PAD = 20, 24
-PIECE = LEFT + 5 * PAD
 VMEM = pl.BlockSpec(memory_space=pltpu.VMEM)
 SMEM = pl.BlockSpec(memory_space=pltpu.SMEM)
 
@@ -50,20 +49,13 @@
     return x * jnp.where(here, low, high)
 
 
-def pack_right(at_ref, owner, pattern_ref, state_ref, masked_ref, out_ref, base):
+def left_kernel(at_ref, pattern_ref, state_ref, out_ref, masked_ref):
+    zh, c = at_ref[2], at_ref[3]
     for h in range(5):
         lanes = slice(128 * h, 128 * h + 128)
-        masked_ref[:, lanes] = masked_block(at_ref, owner, pattern_ref, h, state_ref[:, lanes])
-    out_ref[...] = jnp.zeros_like(out_ref)
-    for y in range(4):
-        for h in range(5):
-            rows = slice(base + PAD * h, base + PAD * h + RUN)
-            out_ref[y, rows] = masked_ref[RUN * y : RUN * y + RUN, 128 * h : 128 * h + 128]
-
-
-def pieces_kernel(at_ref, pattern_ref, state_ref, out_ref, masked_ref):
-    zh, c = at_ref[2], at_ref[3]
-    pack_right(at_ref, at_ref[0], pattern_ref, state_ref, masked_ref, out_ref, LEFT)
+        masked_ref[:, lanes] = masked_block(
+            at_ref, at_ref[0], pattern_ref, h, state_ref[:, lanes]
+        )
     n = lax.broadcasted_iota(jnp.int32, (1, 640), 1)
     late = n >= 512
     y = jnp.where(late, (n - 512) // 32, n // 128)
@@ -75,9 +67,8 @@
     order = lax.broadcasted_iota(jnp.int32, (640, 640), 0) == source
     order = order.astype(jnp.float32).astype(jnp.bfloat16)
     x = masked_ref[...]
-    hi, rest = x.astype(jnp.bfloat16), x
-    rest = x - hi.astype(jnp.float32)
-    mid, low = split(rest)
+    hi = x.astype(jnp.bfloat16)
+    mid, low = split(x - hi.astype(jnp.float32))
     moved = (dot(hi, order) + dot(mid, order)) + dot(low, order)
     lane = lax.broadcasted_iota(jnp.int32, (8, 128), 1) // 32
     for y in range(4):
@@ -93,17 +84,23 @@
             out_ref[y, MAIN + 8 * slot : MAIN + 8 * slot + 8] = tile
 
 
-def unpack_right(got_ref, right_ref, base):
+def pack_kernel(masked_ref, out_ref):
+    out_ref[...] = jnp.zeros_like(out_ref)
     for y in range(4):
-        for h in range(5):
-            right_ref[y // 2, RUN * (y % 2) : RUN * (y % 2) + RUN, 128 * h : 128 * h + 128] = (
-                got_ref[y, base + PAD * h : base + PAD * h + RUN]
-            )
-
-
-def unpack_kernel(got_ref, left_ref, right_ref):
-    left_ref[...] = got_ref[:, :LEFT]
-    unpack_right(got_ref, right_ref, LEFT)
+        for zh in range(2):
+            for h in range(5):
+                out_ref[y, zh, PAD * h : PAD * h + RUN] = masked_ref[
+                    zh, RUN * y : RUN * y + RUN, 128 * h : 128 * h + 128
+                ]
+
+
+def unpack_kernel(got_ref, right_ref):
+    for y in range(4):
+        for zh in range(2):
+            for h in range(5):
+                right_ref[
+                    zh, y // 2, RUN * (y % 2) : RUN * (y % 2) + RUN, 128 * h : 128 * h + 128
+                ] = got_ref[y, zh, PAD * h : PAD * h + RUN]
 
 
 def product_kernel(at_ref, left_ref, right_ref, out_ref, hi_ref, lo_ref):
@@ -183,19 +180,20 @@
         [lax.axis_index(ROWS)] + [lax.axis_index(a) for a in ("zl", "zh", "c")]
     ).astype(jnp.int32)
 
-    pieces = call(
-        pieces_kernel,
-        f32(4, PIECE, 128),
+    left, masked = call(
+        left_kernel,
+        (f32(4, LEFT, 128), f32(rows, cols)),
         [SMEM, SMEM, VMEM],
         (at, in_pattern, state),
-        [pltpu.VMEM((rows, cols), jnp.float32)],
-    )
-    got = lax.all_to_all(pieces, "y", 0, 0)
-    left, near = call(
-        unpack_kernel, (f32(4, LEFT, 128), f32(2, 2 * RUN, cols)), [VMEM], (got,)
-    )
+    )
+    left = lax.all_to_all(left, "y", 0, 0)
+    left, masked = lax.optimization_barrier((left, masked))
     left = lax.all_gather(left, "zl", axis=0)
-    right = gather(gather(gather(near, "zh"), "x"), "c")
+
+    right = call(pack_kernel, f32(4, 2, 5 * PAD, 128), [VMEM], (gather(masked, "zh"),))
+    right = lax.all_to_all(right, "y", 0, 0)
+    right = call(unpack_kernel, f32(2, 2, 2 * RUN, cols), [VMEM], (right,))
+    right = gather(gather(right, "x"), "c")
 
     partial = call(
         product_kernel,

time: 146 us -> 150 us (1.027)
  blocking collectives: 101 us -> 116 us
  waiting for transfers between devices: 18.8 us -> 8.77 us
    all_to_all x1 -> x2, blocking collectives: 13 us -> 23.9 us  [the longest x1 13.1 us: body(): right = lax.all_to_all(right, 'y', 0, 0)]
    all_gather x1, waiting for transfers between devices: 18.8 us -> 8.75 us  [body(): left = lax.all_gather(left, 'zl', axis=0)]
    all_to_all x1, blocking collectives: 16.2 us -> 23.1 us  [body(): sums = lax.all_to_all(sums.reshape(8, 1, rows), 'zl', 0, 0).reshape(8, rows)]
    all_to_all x3, blocking collectives: 57.4 us -> 54.3 us  [gather(): return lax.all_to_all(copies, axis_name, 0, 0)]
    pallas_call x5 -> x6, Pallas kernels: 7.99 us -> 7.38 us  [call(): pl.pallas_call(kernel, out_shape=outs, in_specs=in_specs, out_specs=jax.t...]
where the time goes in v16:
time: 150 us; the launch traced here: 149 us
  blocking collectives  116 us (77%)
  between operations  13.4 us (9%)
  waiting for transfers between devices  8.77 us (6%)
  Pallas kernels  7.38 us (5%)
  local copies, waits for them, and re-layouts  3.5 us (2%)
    all_to_all x3, blocking collectives, gather(): return lax.all_to_all(copies, axis_name, 0, 0)  54.3 us
    all_to_all x1, blocking collectives, body(): sums = lax.all_to_all(sums.reshape(8, 1, rows), 'zl', 0, 0).reshape(8, rows)  23.1 us
    all_to_all x1, blocking collectives, body(): shares = lax.all_to_all(partial, 'y', 0, 0)  14.8 us
    all_to_all x1, blocking collectives, body(): right = lax.all_to_all(right, 'y', 0, 0)  13.1 us
    all_to_all x1, blocking collectives, body(): left = lax.all_to_all(left, 'y', 0, 0)  10.8 us
    all_gather x1, waiting for transfers between devices, body(): left = lax.all_gather(left, 'zl', axis=0)  8.75 us
    pallas_call x6, Pallas kernels, call(): pl.pallas_call(kernel, out_shape=outs, in_specs=in_specs, out_specs=jax.t...  7.38 us
    unnamed x8, local copies, waits for them, and re-layouts  3.09 us
  transfers between devices with their start and end apart: 1, of which 1 were waited for; matrix products, arithmetic and copies ran while one was open for 0% of the time, Pallas kernels for 0%

profile of v16, /device:TPU:6, one launch (start us, length us, event | category | flops | bytes accessed | tf_op | source)
XLA Modules:
  0.0 149.3 jit_solution(4866187038078949345)
XLA Ops:
  6.5 0.0 all-gather.3.cloned.1.call-start
  6.5 0.1 pad_add_fusion.at_ref
  6.6 0.0 copy-start
  6.6 0.9 copy-done
  7.5 0.0 copy-start.1
  7.5 0.7 copy-done.1
  8.3 1.5 %shard_map.37 = (f32[4,104,128]{2,1,0:T(8,128)S(1)}, f32[80,640]{1,0:T(8,128)S(1)}) custom-call(s32[4]{0:T(128)S(1)} %pad_add_fusion.at_ref, s32[20,20]{1,0:T(8,128)S(1)} %copy-done.1, f32[80,640]{1,0:T(8,128)S(1)} %copy-done), custom_call_target="tpu_custom_call" | custom-call | flops 1000000 | bytes 1000000 | tf_op jit(solution)/shard_map/pallas_call | solution.py:29
  9.8 10.8 %all_to_all.35 = f32[4,104,128]{2,1,0:T(8,128)} all-to-all(f32[4,104,128]{2,1,0:T(8,128)S(1)} %get-tuple-element.11), channel_id=1, replica_groups=mesh['zl'=8,'x'=4,'y'=4,'zh'=2,'c'=2] {'y'}, dimensions={0} | all-to-all | bytes 425984 | tf_op jit(solution)/shard_map/all_to_all | solution.py:189
  20.6 0.0 all-gather.3.cloned.1.call-update
  20.6 31.1 %all_to_all.36.masked_ref = f32[2,80,640]{2,1,0:T(8,128)S(1)} all-to-all(f32[2,80,640]{2,1,0:T(8,128)S(1)} %broadcast_in_dim.6), channel_id=1, replica_groups=mesh['zl'=8,'x'=4,'y'=4,'zh'=2,'c'=2] {'zh'}, dimensions={0} | all-to-all | bytes 819200 | tf_op jit(solution)/shard_map/all_to_all | solution.py:169
  51.7 0.1 shard_map.38
  51.8 13.1 %all_to_all.37.got_ref = f32[4,2,120,128]{3,2,1,0:T(8,128)S(1)} all-to-all(f32[4,2,120,128]{3,2,1,0:T(8,128)S(1)} %shard_map.38), channel_id=1, replica_groups=mesh['zl'=8,'x'=4,'y'=4,'zh'=2,'c'=2] {'y'}, dimensions={0} | all-to-all | bytes 983040 | tf_op jit(solution)/shard_map/all_to_all | solution.py:194
  65.0 0.1 broadcast_in_dim.7
  65.1 16.8 %all_to_all.38 = f32[4,2,2,40,640]{4,3,2,1,0:T(8,128)S(1)} all-to-all(f32[4,2,2,40,640]{4,3,2,1,0:T(8,128)S(1)} %broadcast_in_dim.7), channel_id=1, replica_groups=mesh['zl'=8,'x'=4,'y'=4,'zh'=2,'c'=2] {'x'}, dimensions={0} | all-to-all | bytes 3276800 | tf_op jit(solution)/shard_map/all_to_all | solution.py:169
  81.9 0.3 broadcast_in_dim.8
  82.2 6.4 %all_to_all.39.right_ref = f32[2,4,2,2,40,640]{5,4,3,2,1,0:T(8,128)S(1)} all-to-all(f32[2,4,2,2,40,640]{5,4,3,2,1,0:T(8,128)S(1)} %broadcast_in_dim.8), channel_id=1, replica_groups=mesh['zl'=8,'x'=4,'y'=4,'zh'=2,'c'=2] {'c'}, dimensions={0} | all-to-all | bytes 6553600 | tf_op jit(solution)/shard_map/all_to_all | solution.py:169
  88.5 8.8 %all-gather.3.cloned.1.call-done = f32[32,104,128]{2,1,0:T(8,128)} async-done(((f32[4,104,128]{2,1,0:T(8,128)}), f32[32,104,128]{2,1,0:T(8,128)}) %all-gather.3.cloned.1.call-update) | async-done | bytes 1703952 | tf_op jit(solution)/shard_map/all_gather | solution.py:191
  97.3 1.5 copy-done.3
  98.7 3.8 %shard_map.40 = f32[4,80,640]{2,1,0:T(8,128)S(1)} custom-call(s32[4]{0:T(128)S(1)} %pad_add_fusion.at_ref, f32[8,4,104,128]{3,2,1,0:T(8,128)S(1)} %bitcast.11, f32[2,4,2,2,40,640]{5,4,3,2,1,0:T(8,128)S(1)} %all_to_all.39.right_ref), custom_call_target="tpu_custom_call" | custom-call | flops 3000000000 | bytes 6000000 | tf_op jit(solution)/shard_map/pallas_call | solution.py:29
  102.5 14.8 %all_to_all.40.shares_ref = f32[4,80,640]{2,1,0:T(8,128)S(1)} all-to-all(f32[4,80,640]{2,1,0:T(8,128)S(1)} %shard_map.40), channel_id=1, replica_groups=mesh['zl'=8,'x'=4,'y'=4,'zh'=2,'c'=2] {'y'}, dimensions={0} | all-to-all | bytes 1638400 | tf_op jit(solution)/shard_map/all_to_all | solution.py:207
  117.3 0.0 copy-done.2
  117.3 1.1 shard_map.41
  118.4 23.1 %all_to_all.41 = f32[8,1,80]{2,1,0:T(1,128)S(1)} all-to-all(f32[8,1,80]{2,1,0:T(1,128)S(1)} %bitcast.10), channel_id=1, replica_groups=mesh['zl'=8,'x'=4,'y'=4,'zh'=2,'c'=2] {'zl'}, dimensions={0} | all-to-all | bytes 5120 | tf_op jit(solution)/shard_map/all_to_all | solution.py:214
  141.5 0.9 shard_map.42
  (4 shorter events, 0.1 us)
Async XLA Ops:
  6.5 90.7 %all-gather.3.cloned.1.call-start = ((), (), s32[]{:S(2)}) async-start(), calls=%async_computation.7 | async-start | bytes 1916928 | tf_op jit(solution)/shard_map/all_gather | solution.py:191
  6.6 0.9 copy-start
  7.5 0.7 copy-start.1
  97.3 1.5 copy-start.3
  98.7 18.6 %copy-start.2 = (s32[20,20]{1,0:T(8,128)S(1)}, s32[20,20]{1,0:T(8,128)}, u32[]{:S(2)}) copy-start(s32[20,20]{1,0:T(8,128)} %pattern_ref.3) | copy-start | bytes 4804
Sparse Core Ops, SparseCore 0:
  20.7 76.5 all-gather.2

commit v17 on v16

--- a/solution.py
+++ b/solution.py
@@ -11,9 +11,20 @@
 ROWS = ("x", "y", "zh", "c")
 MAIN, REST = 80, 24
 LEFT = MAIN + REST
-RUN, PAD = 20, 24
+SLOTS = 248
+ALL = 400
+UNITS = 32
+EXACT = lax.Precision.HIGHEST
 VMEM = pl.BlockSpec(memory_space=pltpu.VMEM)
 SMEM = pl.BlockSpec(memory_space=pltpu.SMEM)
+
+
+def iota(shape, axis):
+    return lax.broadcasted_iota(jnp.int32, shape, axis)
+
+
+def one_hot(mask):
+    return mask.astype(jnp.float32).astype(jnp.bfloat16)
 
 
 def split(x):
@@ -21,16 +32,27 @@
     return hi, (x - hi.astype(jnp.float32)).astype(jnp.bfloat16)
 
 
-def dot(a, b):
-    return jnp.dot(a, b, preferred_element_type=jnp.float32)
-
-
-def call(kernel, outs, in_specs, args, scratch=(), flops=10**6, size=10**6):
+def split3(x):
+    hi = x.astype(jnp.bfloat16)
+    return (hi, *split(x - hi.astype(jnp.float32)))
+
+
+def dot(a, b, precision=None):
+    return jnp.dot(a, b, preferred_element_type=jnp.float32, precision=precision)
+
+
+def dot_rows(a, b, precision=None):
+    return lax.dot_general(
+        a, b, (((1,), (1,)), ((), ())), precision=precision, preferred_element_type=jnp.float32
+    )
+
+
+def call(kernel, outs, in_specs, args, scratch=(), flops=10**6, size=10**6, out_specs=None):
     return pl.pallas_call(
         kernel,
         out_shape=outs,
         in_specs=in_specs,
-        out_specs=jax.tree.map(lambda _: VMEM, outs),
+        out_specs=out_specs or jax.tree.map(lambda _: VMEM, outs),
         scratch_shapes=scratch,
         compiler_params=pltpu.CompilerParams(vmem_limit_bytes=40 * 2**20),
         cost_estimate=pl.CostEstimate(
@@ -49,8 +71,48 @@
     return x * jnp.where(here, low, high)
 
 
-def left_kernel(at_ref, pattern_ref, state_ref, out_ref, masked_ref):
+def chunk_of(q, zh, c):
+    return 20 * (q // 5) + 10 * zh + 5 * c + q % 5
+
+
+def places(pattern, zh, c):
+    rows = one_hot(chunk_of(iota((80, 1), 0), zh, c) // 16 == iota((80, 20), 1))
+    cols = one_hot(iota((20, 40), 1) // 2 == iota((20, 40), 0))
+    live = dot(dot(rows, pattern).astype(jnp.bfloat16), cols)
+    before = dot(one_hot(iota((80, 80), 1) < iota((80, 80), 0)), live.astype(jnp.bfloat16))
+    total = jnp.broadcast_to(jnp.sum(live, axis=0, keepdims=True), (80, 40))
+    a, b = iota((40, 40), 0), iota((40, 40), 1)
+    earlier = dot(total.astype(jnp.bfloat16), one_hot((a // 5 == b // 5) & (a < b)))
+    return jnp.where(live > 0, before + earlier, -1.0)
+
+
+def places_across(pattern, zh, c):
+    rows = one_hot(chunk_of(iota((1, 80), 1), zh, c) // 16 == iota((20, 80), 0))
+    cols = one_hot(iota((40, 20), 0) // 2 == iota((40, 20), 1))
+    live = dot(dot_rows(cols, pattern).astype(jnp.bfloat16), rows)
+    before = dot(live.astype(jnp.bfloat16), one_hot(iota((80, 80), 0) < iota((80, 80), 1)))
+    total = jnp.broadcast_to(jnp.sum(live, axis=1, keepdims=True), (40, 80))
+    a, b = iota((40, 40), 1), iota((40, 40), 0)
+    earlier = dot(one_hot((a // 5 == b // 5) & (a < b)), total.astype(jnp.bfloat16))
+    return jnp.where(live > 0, before + earlier, -1.0)
+
+
+def most_live(pattern):
+    counts = []
+    for group in range(4):
+        rows = chunk_of(iota((80, 1), 0), group // 2, group % 2) // 16 == iota((80, 20), 1)
+        counts.append(jnp.sum(rows.astype(jnp.float32), axis=0, keepdims=True))
+    counts = jnp.concatenate(counts * 2, axis=0).astype(jnp.bfloat16)
+    wide = jnp.zeros((20, 8), jnp.float32)
+    for h in range(5):
+        wide += ((5 * iota((20, 8), 1) + h) // 2 == iota((20, 8), 0)).astype(jnp.float32)
+    most = dot(dot(counts, pattern).astype(jnp.bfloat16), wide.astype(jnp.bfloat16))
+    return jnp.max(most).astype(jnp.int32)
+
+
+def left_kernel(at_ref, pattern_ref, blocks_ref, state_ref, out_ref, masked_ref, most_ref):
     zh, c = at_ref[2], at_ref[3]
+    most_ref[0, 0] = most_live(blocks_ref[...].astype(jnp.float32).astype(jnp.bfloat16))
     for h in range(5):
         lanes = slice(128 * h, 128 * h + 128)
         masked_ref[:, lanes] = masked_block(
@@ -60,10 +122,10 @@
     late = n >= 512
     y = jnp.where(late, (n - 512) // 32, n // 128)
     m = jnp.where(late, 128 + n % 32, n % 128)
-    dzh, dc, y0, t = m // 80, m // 40 % 2, m // 20 % 2, m % 20
+    dzh, dc, t, y0, e = m // 80, m // 40 % 2, m % 40 // 10, m % 10 // 5, m % 5
     zh_of = jnp.where(dzh == 0, zh, 1 - zh)
     c_of = jnp.where(dc == 0, c, 1 - c)
-    source = 80 * (4 * y0 + 2 * zh_of + c_of) + 20 * y + t
+    source = 80 * (4 * y0 + 2 * zh_of + c_of) + 16 * e + 4 * y + t
     order = lax.broadcasted_iota(jnp.int32, (640, 640), 0) == source
     order = order.astype(jnp.float32).astype(jnp.bfloat16)
     x = masked_ref[...]
@@ -84,35 +146,60 @@
             out_ref[y, MAIN + 8 * slot : MAIN + 8 * slot + 8] = tile
 
 
-def pack_kernel(masked_ref, out_ref):
-    out_ref[...] = jnp.zeros_like(out_ref)
-    for y in range(4):
-        for zh in range(2):
+def units_kernel(masked_ref, out_ref, plain_ref):
+    for h in range(5):
+        plain_ref[h] = masked_ref[:, 128 * h : 128 * h + 128]
+    for x in range(4):
+        for y in range(4):
             for h in range(5):
-                out_ref[y, zh, PAD * h : PAD * h + RUN] = masked_ref[
-                    zh, RUN * y : RUN * y + RUN, 128 * h : 128 * h + 128
+                out_ref[4 * x + y, 5 * h : 5 * h + 5] = plain_ref[
+                    h, pl.ds(4 * y + x, 5, stride=16), :
                 ]
-
-
-def unpack_kernel(got_ref, right_ref):
-    for y in range(4):
-        for zh in range(2):
+            out_ref[4 * x + y, 25:] = jnp.zeros((UNITS - 25, 128), jnp.float32)
+
+
+def pack_kernel(slots, at_ref, pattern_ref, got_ref, right_ref):
+    pattern = pattern_ref[...].astype(jnp.float32).astype(jnp.bfloat16)
+    place = places_across(pattern, at_ref[2], at_ref[3])
+    count = 16 * UNITS
+    units = jnp.concatenate(split3(got_ref[...].reshape(count, 128)), axis=1)
+    row = iota((1, count), 1)
+    j = row % UNITS
+    q = 5 * (row // UNITS) + j % 5
+    expand = (q == iota((80, count), 0)).astype(jnp.float32)
+    spread = dot(place, expand, EXACT)
+    mine = 5 * at_ref[1] + j // 5 == iota((40, count), 0)
+    slot = jnp.sum(jnp.where(mine, spread, 0.0), axis=0, keepdims=True)
+    slot = jnp.where(j < 25, slot, -1.0)
+    pick = one_hot(slot == iota((slots, count), 0).astype(jnp.float32))
+    got = dot(pick, units)
+    right_ref[...] = (got[:, :128] + got[:, 128:256]) + got[:, 256:]
+
+
+def spread_kernel(slots, at_ref, pattern_ref, own_ref, swap_ref, out_ref):
+    pattern = pattern_ref[...].astype(jnp.float32).astype(jnp.bfloat16)
+    zl, zh, c = at_ref[1], at_ref[2], at_ref[3]
+    slot = iota((80, slots), 1).astype(jnp.float32)
+    half = iota((80, 40), 1)
+    for dc, ref in ((0, own_ref), (1, swap_ref)):
+        for dzh in range(2):
+            there = jnp.abs(zh - dzh)
+            place = places(pattern, there, jnp.abs(c - dc))
+            pick = []
             for h in range(5):
-                right_ref[
-                    zh, y // 2, RUN * (y % 2) : RUN * (y % 2) + RUN, 128 * h : 128 * h + 128
-                ] = got_ref[y, zh, PAD * h : PAD * h + RUN]
-
-
-def product_kernel(at_ref, left_ref, right_ref, out_ref, hi_ref, lo_ref):
-    for dc in range(2):
-        c = lax.rem(at_ref[3] + dc, 2)
-        for dzh in range(2):
-            rows = slice(40 * (2 * dzh + dc), 40 * (2 * dzh + dc) + 40)
-            for x in range(4):
-                for y1 in range(2):
-                    hi, lo = split(right_ref[c, x, lax.rem(at_ref[2] + dzh, 2), y1])
-                    hi_ref[2 * x + y1, rows] = hi
-                    lo_ref[2 * x + y1, rows] = lo
+                at = jnp.sum(jnp.where(half == 5 * zl + h, place, 0.0), axis=1, keepdims=True)
+                pick.append(one_hot(at == slot))
+            pick = jnp.concatenate(pick, axis=0)
+            for t in range(4):
+                got = dot(pick, jnp.concatenate(split3(ref[t, there]), axis=1))
+                got = (got[:, :128] + got[:, 128:256]) + got[:, 256:]
+                got = jnp.concatenate([got[80 * h : 80 * h + 80] for h in range(5)], axis=1)
+                base = 40 * (2 * dzh + dc) + 10 * t
+                for block in range(8):
+                    out_ref[block, base : base + 10] = got[10 * block : 10 * block + 10]
+
+
+def product_kernel(left_ref, right_ref, out_ref):
     lane = lax.broadcasted_iota(jnp.int32, (8, 128), 1) // 32
     total = jnp.zeros((320, 640), jnp.float32)
     for block in range(8):
@@ -126,9 +213,8 @@
             rest = jnp.concatenate(rest, axis=0)
             whole.append(jnp.concatenate([left_ref[block, y, :MAIN], rest], axis=1))
         left_hi, left_lo = split(jnp.concatenate(whole, axis=0))
-        right_hi, right_lo = hi_ref[block], lo_ref[block]
-        right_hi = jnp.concatenate([right_hi] + [right_hi[128:]] * 3, axis=0)
-        right_lo = jnp.concatenate([right_lo] + [right_lo[128:]] * 3, axis=0)
+        right = right_ref[block]
+        right_hi, right_lo = split(jnp.concatenate([right] + [right[128:]] * 3, axis=0))
         total += dot(left_hi, right_hi) + (dot(left_hi, right_lo) + dot(left_lo, right_hi))
     out_ref[...] = total.reshape(4, 80, 640)
 
@@ -163,46 +249,82 @@
         out_ref[:, lanes] = inflated_ref[:, lanes] * scale
 
 
-def gather(block, axis_name):
-    size = lax.axis_size(axis_name)
-    copies = jnp.broadcast_to(block[None], (size,) + block.shape)
-    return lax.all_to_all(copies, axis_name, 0, 0)
+def swap(x, axis_name):
+    return lax.ppermute(x, axis_name, [(0, 1), (1, 0)])
+
+
+def gather(x, axis_name, limit):
+    rows = x.shape[-2]
+    parts = -(-rows // limit)
+    size = rows // parts
+    done = [
+        lax.all_gather(x[..., i * size : (i + 1) * size, :], axis_name, axis=0)
+        for i in range(parts)
+    ]
+    return done[0] if parts == 1 else jnp.concatenate(done, axis=-2)
 
 
 def f32(*shape):
     return jax.ShapeDtypeStruct(shape, jnp.float32)
+
+
+def partial_product(slots, at, in_pattern, left, masked):
+    rows, cols = masked.shape
+    left, masked = lax.optimization_barrier((left, masked))
+    left = lax.all_gather(left, "zl", axis=0)
+
+    units = call(
+        units_kernel,
+        f32(16, UNITS, 128),
+        [VMEM],
+        (masked,),
+        [pltpu.VMEM((5, rows, 128), jnp.float32)],
+    )
+    got = lax.all_to_all(units, ("x", "y"), 0, 0)
+    right = call(
+        functools.partial(pack_kernel, slots),
+        f32(slots, 128),
+        [SMEM, VMEM, VMEM],
+        (at, in_pattern, got),
+    )
+    own = gather(gather(right, "zh", SLOTS), "x", SLOTS)
+    right = call(
+        functools.partial(spread_kernel, slots),
+        f32(8, 160, cols),
+        [SMEM, VMEM, VMEM, VMEM],
+        (at, in_pattern, own, swap(own, "c")),
+    )
+    return call(
+        product_kernel,
+        f32(4, rows, cols),
+        [VMEM, VMEM],
+        (left, right),
+        flops=3 * 10**9,
+        size=6 * 10**6,
+    )
 
 
 def body(state, in_pattern, out_pattern):
     rows, cols = state.shape
     nodes = cols * lax.axis_size("zl")
-    at = jnp.stack(
-        [lax.axis_index(ROWS)] + [lax.axis_index(a) for a in ("zl", "zh", "c")]
-    ).astype(jnp.int32)
-
-    left, masked = call(
+    at = jnp.stack([lax.axis_index(ROWS)] + [lax.axis_index(a) for a in ("zl", "zh", "c")])
+    at = at.astype(jnp.int32)
+    left, masked, most = call(
         left_kernel,
-        (f32(4, LEFT, 128), f32(rows, cols)),
-        [SMEM, SMEM, VMEM],
-        (at, in_pattern, state),
+        (f32(4, LEFT, 128), f32(rows, cols), jax.ShapeDtypeStruct((1, 1), jnp.int32)),
+        [SMEM, SMEM, VMEM, VMEM],
+        (at, in_pattern, in_pattern, state),
+        out_specs=(VMEM, VMEM, SMEM),
     )
     left = lax.all_to_all(left, "y", 0, 0)
-    left, masked = lax.optimization_barrier((left, masked))
-    left = lax.all_gather(left, "zl", axis=0)
-
-    right = call(pack_kernel, f32(4, 2, 5 * PAD, 128), [VMEM], (gather(masked, "zh"),))
-    right = lax.all_to_all(right, "y", 0, 0)
-    right = call(unpack_kernel, f32(2, 2, 2 * RUN, cols), [VMEM], (right,))
-    right = gather(gather(right, "x"), "c")
-
-    partial = call(
-        product_kernel,
-        f32(4, rows, cols),
-        [SMEM, VMEM, VMEM],
-        (at, left, right),
-        [pltpu.VMEM((8, 160, cols), jnp.bfloat16)] * 2,
-        flops=3 * 10**9,
-        size=6 * 10**6,
+    partial = lax.cond(
+        most[0, 0] <= SLOTS,
+        functools.partial(partial_product, SLOTS),
+        functools.partial(partial_product, ALL),
+        at,
+        in_pattern,
+        left,
+        masked,
     )
     shares = lax.all_to_all(partial, "y", 0, 0)
     inflated, sums = call(

time: 150 us -> 145 us (0.967)
  blocking collectives: 116 us -> 77.6 us
  waiting for transfers between devices: 8.77 us -> 27.7 us
  Pallas kernels: 7.38 us -> 14.9 us
  starting transfers between devices: 0.01 us -> 6.56 us
    all_to_all x5 -> x1, blocking collectives: 78.2 us -> 13.6 us  [partial_product(): got = lax.all_to_all(units, ('x', 'y'), 0, 0)]
    all_gather x0 -> x2, blocking collectives: none -> 34.1 us  [gather(): lax.all_gather(x[..., i * size:(i + 1) * size, :], axis_name, axis=0)]
    all_gather x1, waiting for transfers between devices: 8.75 us -> 19.5 us  [partial_product(): left = lax.all_gather(left, 'zl', axis=0)]
    all_to_all x1, blocking collectives: 23.1 us -> 14.8 us  [body(): sums = lax.all_to_all(sums.reshape(8, 1, rows), 'zl', 0, 0).reshape(8, rows)]
    pallas_call x6 -> x7, Pallas kernels: 7.38 us -> 14.9 us  [call(): pl.pallas_call(kernel, out_shape=outs, in_specs=in_specs, out_specs=out_s...]
    all_to_all x0 -> x1, waiting for transfers between devices: none -> 5.76 us  [body(): left = lax.all_to_all(left, 'y', 0, 0)]
    all_to_all x0 -> x1, starting transfers between devices: none -> 4.47 us  [body(): left = lax.all_to_all(left, 'y', 0, 0)]
    ppermute x0 -> x1, waiting for transfers between devices: none -> 2.4 us  [swap(): return lax.ppermute(x, axis_name, [(0, 1), (1, 0)])]
  transfers between devices with their start and end apart: 1 -> 3, of which waited for: 1 -> 3; matrix products, arithmetic and copies ran while one was open for 0% -> 0% of each run, Pallas kernels for 0% -> 4%
where the time goes in v17:
time: 145 us; the launch traced here: 144 us
  blocking collectives  77.6 us (54%)
  waiting for transfers between devices  27.7 us (19%)
  Pallas kernels  14.9 us (10%)
  between operations  14 us (10%)
  starting transfers between devices  6.56 us (5%)
  local copies, waits for them, and re-layouts  3.09 us (2%)
    all_gather x2, blocking collectives, gather(): lax.all_gather(x[..., i * size:(i + 1) * size, :], axis_name, axis=0)  34.1 us
    all_gather x1, waiting for transfers between devices, partial_product(): left = lax.all_gather(left, 'zl', axis=0)  19.5 us
    all_to_all x1, blocking collectives, body(): shares = lax.all_to_all(partial, 'y', 0, 0)  15.1 us
    pallas_call x7, Pallas kernels, call(): pl.pallas_call(kernel, out_shape=outs, in_specs=in_specs, out_specs=out_s...  14.9 us
    all_to_all x1, blocking collectives, body(): sums = lax.all_to_all(sums.reshape(8, 1, rows), 'zl', 0, 0).reshape(8, rows)  14.8 us
    all_to_all x1, blocking collectives, partial_product(): got = lax.all_to_all(units, ('x', 'y'), 0, 0)  13.6 us
    all_to_all x1, waiting for transfers between devices, body(): left = lax.all_to_all(left, 'y', 0, 0)  5.76 us
    all_to_all x1, starting transfers between devices, body(): left = lax.all_to_all(left, 'y', 0, 0)  4.47 us
  transfers between devices with their start and end apart: 3, of which 3 were waited for; matrix products, arithmetic and copies ran while one was open for 0% of the time, Pallas kernels for 4%

profile of v17, /device:TPU:6, one launch (start us, length us, event | category | flops | bytes accessed | tf_op | source)
XLA Modules:
  0.0 144.0 jit_solution(1763312005224210294)
XLA Ops:
  6.5 0.1 pad_add_fusion.at_ref
  6.6 0.9 copy-done
  7.5 2.6 %shard_map.37 = (f32[4,104,128]{2,1,0:T(8,128)}, f32[80,640]{1,0:T(8,128)S(1)}, s32[1,1]{1,0:T(1,128)}) custom-call(s32[4]{0:T(128)S(1)} %pad_add_fusion.at_ref, s32[20,20]{1,0:T(8,128)} %blocks_ref.1, s32[20,20]{1,0:T(8,128)} %blocks_ref.1, f32[80,640]{1,0:T(8,128)S(1)} %copy-done), custom_call_target="tpu_custom_call" | custom-call | flops 1000000 | bytes 1000000 | tf_op jit(solution)/shard_map/pallas_call | solution.py:51
  10.1 4.5 %all-to-all-start.2 = ((f32[4,104,128]{2,1,0:T(8,128)}), f32[4,104,128]{2,1,0:T(8,128)S(1)}, u32[]{:S(2)}, u32[]{:S(2)}) async-start(f32[4,104,128]{2,1,0:T(8,128)} %get-tuple-element.42), calls=%async_computation.2 | async-start | bytes 425984 | tf_op jit(solution)/shard_map/all_to_all | solution.py:319
  15.3 5.8 %all-to-all-done.2 = f32[4,104,128]{2,1,0:T(8,128)S(1)} async-done(((f32[4,104,128]{2,1,0:T(8,128)}), f32[4,104,128]{2,1,0:T(8,128)S(1)}, u32[]{:S(2)}, u32[]{:S(2)}) %all-to-all-start.2) | async-done | bytes 213024 | tf_op jit(solution)/shard_map/all_to_all | solution.py:319
  21.0 84.2 %conditional.1 = (f32[4,80,640]{2,1,0:T(8,128)}) conditional(s32[]{:T(128)} %bitcast.12, (f32[4,104,128]{2,1,0:T(8,128)S(1)}, f32[80,640]{1,0:T(8,128)S(1)}, s32[4]{0:T(128)S(1)}, s32[20,20]{1,0:T(8,128)}) %tuple.13, (f32[4,104,128]{2,1,0:T(8,128)S(1)}, f32[80,640]{1,0:T(8,128)S(1)}, s32[4]{0:T(128)S(1)}, s32[20,20]{1,0:T(8,128)}) %tuple.13), branch_computations={%region_0.0_spmd, %region_1.0_spmd} | conditional | flops 3003409664 | bytes 36113932 | solution.py:320
  21.0 0.0 all-gather.13.cloned.1.call-start
  21.0 0.7 copy-done.5
  21.7 0.0 all-gather.13.cloned.1.call-update
  21.7 0.1 branch_1_fun.4
  21.9 13.6 %all_to_all.23.got_ref = f32[16,32,128]{2,1,0:T(8,128)S(1)} all-to-all(f32[16,32,128]{2,1,0:T(8,128)S(1)} %branch_1_fun.4), channel_id=1, replica_groups=mesh['zl'=8,'x'=4,'y'=4,'zh'=2,'c'=2] {'x','y'}, dimensions={0} | all-to-all | bytes 524288 | tf_op jit(solution)/shard_map/cond/branch_1_fun/all_to_all | solution.py:283
  35.5 1.7 %branch_1_fun.5 = f32[248,128]{1,0:T(8,128)S(1)} custom-call(s32[4]{0:T(128)S(1)} %get-tuple-element.33.at_ref, s32[20,20]{1,0:T(8,128)} %get-tuple-element.34.pattern_ref, f32[16,32,128]{2,1,0:T(8,128)S(1)} %all_to_all.23.got_ref), custom_call_target="tpu_custom_call" | custom-call | flops 1000000 | bytes 1000000 | tf_op jit(solution)/shard_map/cond/branch_1_fun/pallas_call | solution.py:51
  37.1 19.1 %all-gather.6 = f32[496,128]{1,0:T(8,128)S(1)} all-gather(f32[248,128]{1,0:T(8,128)S(1)} %branch_1_fun.5), channel_id=8, replica_groups=mesh['zl'=8,'x'=4,'y'=4,'zh'=2,'c'=2] {'zh'}, dimensions={0}, use_global_device_ids=true | all-gather | bytes 380928 | tf_op jit(solution)/shard_map/cond/branch_1_fun/all_gather | solution.py:261
  56.3 14.9 %all-gather.7 = f32[8,248,128]{2,1,0:T(8,128)S(1)} all-gather(f32[2,248,128]{2,1,0:T(8,128)S(1)} %bitcast.25), channel_id=9, replica_groups=mesh['zl'=8,'x'=4,'y'=4,'zh'=2,'c'=2] {'x'}, dimensions={0}, use_global_device_ids=true | all-gather | bytes 1269760 | tf_op jit(solution)/shard_map/cond/branch_1_fun/all_gather | solution.py:261
  71.2 2.1 %collective-permute-start = (f32[4,2,248,128]{3,2,1,0:T(8,128)S(1)}, f32[4,2,248,128]{3,2,1,0:T(8,128)S(1)}, u32[]{:S(2)}, u32[]{:S(2)}) collective-permute-start(f32[4,2,248,128]{3,2,1,0:T(8,128)S(1)} %bitcast.17), channel_id=1, source_target_pairs={{0,1},{1,0},{2,3},{3,2},{4,5},{5,4},{6,7},{7,6},{8,9},{9,8},{10,11... | collective-permute-start | bytes 3047432 | tf_op jit(solution)/shard_map/cond/branch_1_fun/ppermute | solution.py:253
  73.3 2.4 %collective-permute-done.swap_ref = f32[4,2,248,128]{3,2,1,0:T(8,128)S(1)} collective-permute-done((f32[4,2,248,128]{3,2,1,0:T(8,128)S(1)}, f32[4,2,248,128]{3,2,1,0:T(8,128)S(1)}, u32[]{:S(2)}, u32[]{:S(2)}) %collective-permute-start) | collective-permute-done | bytes 1015840 | tf_op jit(solution)/shard_map/cond/branch_1_fun/ppermute | solution.py:253
  75.7 4.4 %branch_1_fun.6.right_ref = f32[8,160,640]{2,1,0:T(8,128)S(1)} custom-call(s32[4]{0:T(128)S(1)} %get-tuple-element.33.at_ref, s32[20,20]{1,0:T(8,128)S(1)} %copy-done.7, f32[4,2,248,128]{3,2,1,0:T(8,128)S(1)} %bitcast.18, f32[4,2,248,128]{3,2,1,0:T(8,128)S(1)} %collective-permute-done.swap_ref), custom_call_target="tpu_custom_call" | custom-call | flops 1000000 | bytes 1000000 | tf_op jit(solution)/shard_map/cond/branch_1_fun/pallas_call | solution.py:51
  80.1 19.5 %all-gather.13.cloned.1.call-done = f32[32,104,128]{2,1,0:T(8,128)} async-done(((f32[4,104,128]{2,1,0:T(8,128)}), f32[32,104,128]{2,1,0:T(8,128)}) %all-gather.13.cloned.1.call-update) | async-done | bytes 1703952 | tf_op jit(solution)/shard_map/cond/branch_1_fun/all_gather | solution.py:274
  99.6 1.5 %copy-done.3 = f32[32,104,128]{2,1,0:T(8,128)S(1)} copy-done((f32[32,104,128]{2,1,0:T(8,128)S(1)}, f32[32,104,128]{2,1,0:T(8,128)}, u32[]{:S(2)}) %copy-start.3) | copy-done | bytes 1703960 | tf_op jit(solution)/shard_map/cond
  101.0 4.2 %branch_1_fun.7 = f32[4,80,640]{2,1,0:T(8,128)} custom-call(f32[8,4,104,128]{3,2,1,0:T(8,128)S(1)} %bitcast.22, f32[8,160,640]{2,1,0:T(8,128)S(1)} %branch_1_fun.6.right_ref), custom_call_target="tpu_custom_call" | custom-call | flops 3000000000 | bytes 6000000 | tf_op jit(solution)/shard_map/cond/branch_1_fun/pallas_call | solution.py:51
  105.2 15.1 %all_to_all.24.shares_ref = f32[4,80,640]{2,1,0:T(8,128)S(1)} all-to-all(f32[4,80,640]{2,1,0:T(8,128)} %get-tuple-element.48), channel_id=1, replica_groups=mesh['zl'=8,'x'=4,'y'=4,'zh'=2,'c'=2] {'y'}, dimensions={0} | all-to-all | bytes 1638400 | tf_op jit(solution)/shard_map/all_to_all | solution.py:329
  120.3 1.1 shard_map.38
  121.4 14.8 %all_to_all.25 = f32[8,1,80]{2,1,0:T(1,128)S(1)} all-to-all(f32[8,1,80]{2,1,0:T(1,128)S(1)} %bitcast.20), channel_id=1, replica_groups=mesh['zl'=8,'x'=4,'y'=4,'zh'=2,'c'=2] {'zl'}, dimensions={0} | all-to-all | bytes 5120 | tf_op jit(solution)/shard_map/all_to_all | solution.py:336
  136.3 0.9 shard_map.39
  (7 shorter events, 0.0 us)
Async XLA Ops:
  6.6 0.9 copy-start
  10.1 10.9 %all-to-all-start.2 = ((f32[4,104,128]{2,1,0:T(8,128)}), f32[4,104,128]{2,1,0:T(8,128)S(1)}, u32[]{:S(2)}, u32[]{:S(2)}) async-start(f32[4,104,128]{2,1,0:T(8,128)} %get-tuple-element.42), calls=%async_computation.2 | async-start | bytes 425984 | tf_op jit(solution)/shard_map/all_to_all | solution.py:319
  21.0 0.7 copy-start.5
  21.0 54.7 %copy-start.7 = (s32[20,20]{1,0:T(8,128)S(1)}, s32[20,20]{1,0:T(8,128)}, u32[]{:S(2)}) copy-start(s32[20,20]{1,0:T(8,128)} %get-tuple-element.34.pattern_ref) | copy-start | bytes 4804 | tf_op jit(solution)/shard_map/cond
  21.0 78.6 %all-gather.13.cloned.1.call-start = ((), (), s32[]{:S(2)}) async-start(), calls=%async_computation.6 | async-start | bytes 1916928 | tf_op jit(solution)/shard_map/cond/branch_1_fun/all_gather | solution.py:274
  71.2 4.5 %collective-permute-start = (f32[4,2,248,128]{3,2,1,0:T(8,128)S(1)}, f32[4,2,248,128]{3,2,1,0:T(8,128)S(1)}, u32[]{:S(2)}, u32[]{:S(2)}) collective-permute-start(f32[4,2,248,128]{3,2,1,0:T(8,128)S(1)} %bitcast.17), channel_id=1, source_target_pairs={{0,1},{1,0},{2,3},{3,2},{4,5},{5,4},{6,7},{7,6},{8,9},{9,8},{10,11... | collective-permute-start | bytes 3047432 | tf_op jit(solution)/shard_map/cond/branch_1_fun/ppermute | solution.py:253
  99.6 1.5 %copy-start.3 = (f32[32,104,128]{2,1,0:T(8,128)S(1)}, f32[32,104,128]{2,1,0:T(8,128)}, u32[]{:S(2)}) copy-start(f32[32,104,128]{2,1,0:T(8,128)} %all-gather.13.cloned.1.call-done) | copy-start | bytes 5111812 | tf_op jit(solution)/shard_map/cond
  105.2 15.1 %copy-start.1 = (s32[20,20]{1,0:T(8,128)S(1)}, s32[20,20]{1,0:T(8,128)}, u32[]{:S(2)}) copy-start(s32[20,20]{1,0:T(8,128)} %pattern_ref.3) | copy-start | bytes 4804
Sparse Core Ops, SparseCore 0:
  23.9 75.6 all-gather.12

commit v18 on v17

--- a/solution.py
+++ b/solution.py
@@ -110,9 +110,8 @@
     return jnp.max(most).astype(jnp.int32)
 
 
-def left_kernel(at_ref, pattern_ref, blocks_ref, state_ref, out_ref, masked_ref, most_ref):
+def left_kernel(at_ref, pattern_ref, state_ref, out_ref, masked_ref):
     zh, c = at_ref[2], at_ref[3]
-    most_ref[0, 0] = most_live(blocks_ref[...].astype(jnp.float32).astype(jnp.bfloat16))
     for h in range(5):
         lanes = slice(128 * h, 128 * h + 128)
         masked_ref[:, lanes] = masked_block(
@@ -146,7 +145,8 @@
             out_ref[y, MAIN + 8 * slot : MAIN + 8 * slot + 8] = tile
 
 
-def units_kernel(masked_ref, out_ref, plain_ref):
+def units_kernel(pattern_ref, masked_ref, out_ref, most_ref, plain_ref):
+    most_ref[0, 0] = most_live(pattern_ref[...].astype(jnp.float32).astype(jnp.bfloat16))
     for h in range(5):
         plain_ref[h] = masked_ref[:, 128 * h : 128 * h + 128]
     for x in range(4):
@@ -176,7 +176,7 @@
     right_ref[...] = (got[:, :128] + got[:, 128:256]) + got[:, 256:]
 
 
-def spread_kernel(slots, at_ref, pattern_ref, own_ref, swap_ref, out_ref):
+def spread_kernel(slots, at_ref, pattern_ref, own_ref, swap_ref, hi_ref, lo_ref, out_ref):
     pattern = pattern_ref[...].astype(jnp.float32).astype(jnp.bfloat16)
     zl, zh, c = at_ref[1], at_ref[2], at_ref[3]
     slot = iota((80, slots), 1).astype(jnp.float32)
@@ -197,9 +197,13 @@
                 base = 40 * (2 * dzh + dc) + 10 * t
                 for block in range(8):
                     out_ref[block, base : base + 10] = got[10 * block : 10 * block + 10]
-
-
-def product_kernel(left_ref, right_ref, out_ref):
+    for block in range(8):
+        rows = out_ref[block]
+        rows = jnp.concatenate([rows] + [rows[128:]] * 3, axis=0)
+        hi_ref[block], lo_ref[block] = split(rows)
+
+
+def product_kernel(left_ref, hi_ref, lo_ref, out_ref):
     lane = lax.broadcasted_iota(jnp.int32, (8, 128), 1) // 32
     total = jnp.zeros((320, 640), jnp.float32)
     for block in range(8):
@@ -213,8 +217,7 @@
             rest = jnp.concatenate(rest, axis=0)
             whole.append(jnp.concatenate([left_ref[block, y, :MAIN], rest], axis=1))
         left_hi, left_lo = split(jnp.concatenate(whole, axis=0))
-        right = right_ref[block]
-        right_hi, right_lo = split(jnp.concatenate([right] + [right[128:]] * 3, axis=0))
+        right_hi, right_lo = hi_ref[block], lo_ref[block]
         total += dot(left_hi, right_hi) + (dot(left_hi, right_lo) + dot(left_lo, right_hi))
     out_ref[...] = total.reshape(4, 80, 640)
 
@@ -268,19 +271,8 @@
     return jax.ShapeDtypeStruct(shape, jnp.float32)
 
 
-def partial_product(slots, at, in_pattern, left, masked):
-    rows, cols = masked.shape
-    left, masked = lax.optimization_barrier((left, masked))
-    left = lax.all_gather(left, "zl", axis=0)
-
-    units = call(
-        units_kernel,
-        f32(16, UNITS, 128),
-        [VMEM],
-        (masked,),
-        [pltpu.VMEM((5, rows, 128), jnp.float32)],
-    )
-    got = lax.all_to_all(units, ("x", "y"), 0, 0)
+def right_halves(slots, at, in_pattern, got):
+    cols = 640
     right = call(
         functools.partial(pack_kernel, slots),
         f32(slots, 128),
@@ -288,19 +280,13 @@
         (at, in_pattern, got),
     )
     own = gather(gather(right, "zh", SLOTS), "x", SLOTS)
-    right = call(
+    half = jax.ShapeDtypeStruct((8, 256, cols), jnp.bfloat16)
+    return call(
         functools.partial(spread_kernel, slots),
-        f32(8, 160, cols),
+        (half, half),
         [SMEM, VMEM, VMEM, VMEM],
         (at, in_pattern, own, swap(own, "c")),
-    )
-    return call(
-        product_kernel,
-        f32(4, rows, cols),
-        [VMEM, VMEM],
-        (left, right),
-        flops=3 * 10**9,
-        size=6 * 10**6,
+        [pltpu.VMEM((8, 160, cols), jnp.float32)],
     )
 
 
@@ -309,22 +295,40 @@
     nodes = cols * lax.axis_size("zl")
     at = jnp.stack([lax.axis_index(ROWS)] + [lax.axis_index(a) for a in ("zl", "zh", "c")])
     at = at.astype(jnp.int32)
-    left, masked, most = call(
+    left, masked = call(
         left_kernel,
-        (f32(4, LEFT, 128), f32(rows, cols), jax.ShapeDtypeStruct((1, 1), jnp.int32)),
-        [SMEM, SMEM, VMEM, VMEM],
-        (at, in_pattern, in_pattern, state),
-        out_specs=(VMEM, VMEM, SMEM),
+        (f32(4, LEFT, 128), f32(rows, cols)),
+        [SMEM, SMEM, VMEM],
+        (at, in_pattern, state),
     )
     left = lax.all_to_all(left, "y", 0, 0)
-    partial = lax.cond(
+    left, masked = lax.optimization_barrier((left, masked))
+    left = lax.all_gather(left, "zl", axis=0)
+
+    units, most = call(
+        units_kernel,
+        (f32(16, UNITS, 128), jax.ShapeDtypeStruct((1, 1), jnp.int32)),
+        [VMEM, VMEM],
+        (in_pattern, masked),
+        [pltpu.VMEM((5, rows, 128), jnp.float32)],
+        out_specs=(VMEM, SMEM),
+    )
+    got = lax.all_to_all(units, ("x", "y"), 0, 0)
+    right_hi, right_lo = lax.cond(
         most[0, 0] <= SLOTS,
-        functools.partial(partial_product, SLOTS),
-        functools.partial(partial_product, ALL),
+        functools.partial(right_halves, SLOTS),
+        functools.partial(right_halves, ALL),
         at,
         in_pattern,
-        left,
-        masked,
+        got,
+    )
+    partial = call(
+        product_kernel,
+        f32(4, rows, cols),
+        [VMEM, VMEM, VMEM],
+        (left, right_hi, right_lo),
+        flops=3 * 10**9,
+        size=6 * 10**6,
     )
     shares = lax.all_to_all(partial, "y", 0, 0)
     inflated, sums = call(

time: 145 us -> 145 us (level)
  blocking collectives: 77.6 us -> 73 us
  Pallas kernels: 14.9 us -> 18.6 us
  starting transfers between devices: 6.56 us -> 9.86 us
  waiting for transfers between devices: 27.7 us -> 24.8 us
    pallas_call x7, Pallas kernels: 14.9 us -> 18.6 us  [call(): pl.pallas_call(kernel, out_shape=outs, in_specs=in_specs, out_specs=out_s...]
    all_to_all x1, starting transfers between devices: 4.47 us -> 7.95 us  [body(): got = lax.all_to_all(units, ('x', 'y'), 0, 0)]
    all_gather x1, waiting for transfers between devices: 19.5 us -> 16.5 us  [body(): left = lax.all_gather(left, 'zl', axis=0)]
    all_to_all x1, blocking collectives: 13.6 us -> 10.8 us  [body(): left = lax.all_to_all(left, 'y', 0, 0)]
    all_to_all x1, blocking collectives: 15.1 us -> 12.9 us  [body(): shares = lax.all_to_all(partial, 'y', 0, 0)]
    cond x6 -> x0, local copies, waits for them, and re-layouts: 2.16 us -> none
    unnamed x4 -> x6, local copies, waits for them, and re-layouts: 0.93 us -> 2.39 us
  transfers between devices with their start and end apart: 3 -> 3, of which waited for: 3 -> 3; matrix products, arithmetic and copies ran while one was open for 0% -> 0% of each run, Pallas kernels for 4% -> 7%
where the time goes in v18:
time: 145 us; the launch traced here: 143 us
  blocking collectives  73 us (50%)
  waiting for transfers between devices  24.8 us (17%)
  Pallas kernels  18.6 us (13%)
  between operations  14.1 us (10%)
  starting transfers between devices  9.86 us (7%)
  local copies, waits for them, and re-layouts  2.39 us (2%)
    all_gather x2, blocking collectives, gather(): lax.all_gather(x[..., i * size:(i + 1) * size, :], axis_name, axis=0)  33.5 us
    pallas_call x7, Pallas kernels, call(): pl.pallas_call(kernel, out_shape=outs, in_specs=in_specs, out_specs=out_s...  18.6 us
    all_gather x1, waiting for transfers between devices, body(): left = lax.all_gather(left, 'zl', axis=0)  16.5 us
    all_to_all x1, blocking collectives, body(): sums = lax.all_to_all(sums.reshape(8, 1, rows), 'zl', 0, 0).reshape(8, rows)  15.8 us
    all_to_all x1, blocking collectives, body(): shares = lax.all_to_all(partial, 'y', 0, 0)  12.9 us
    all_to_all x1, blocking collectives, body(): left = lax.all_to_all(left, 'y', 0, 0)  10.8 us
    all_to_all x1, starting transfers between devices, body(): got = lax.all_to_all(units, ('x', 'y'), 0, 0)  7.95 us
    all_to_all x1, waiting for transfers between devices, body(): got = lax.all_to_all(units, ('x', 'y'), 0, 0)  5.74 us
  transfers between devices with their start and end apart: 3, of which 3 were waited for; matrix products, arithmetic and copies ran while one was open for 0% of the time, Pallas kernels for 7%

profile of v18, /device:TPU:6, one launch (start us, length us, event | category | flops | bytes accessed | tf_op | source)
XLA Modules:
  0.0 142.9 jit_solution(8626858330071130002)
XLA Ops:
  6.5 0.0 all-gather.9.cloned.1.call-start
  6.5 0.1 pad_add_fusion.at_ref
  6.6 0.9 copy-done
  7.5 1.7 %shard_map.37 = (f32[4,104,128]{2,1,0:T(8,128)S(1)}, f32[80,640]{1,0:T(8,128)S(1)}) custom-call(s32[4]{0:T(128)S(1)} %pad_add_fusion.at_ref, s32[20,20]{1,0:T(8,128)} %pattern_ref.4, f32[80,640]{1,0:T(8,128)S(1)} %copy-done), custom_call_target="tpu_custom_call" | custom-call | flops 1000000 | bytes 1000000 | tf_op jit(solution)/shard_map/pallas_call | solution.py:51
  9.2 10.8 %all_to_all.20 = f32[4,104,128]{2,1,0:T(8,128)} all-to-all(f32[4,104,128]{2,1,0:T(8,128)S(1)} %get-tuple-element.33), channel_id=1, replica_groups=mesh['zl'=8,'x'=4,'y'=4,'zh'=2,'c'=2] {'y'}, dimensions={0} | all-to-all | bytes 425984 | tf_op jit(solution)/shard_map/all_to_all | solution.py:304
  20.0 0.0 all-gather.9.cloned.1.call-update
  20.0 1.9 %shard_map.38 = (f32[16,32,128]{2,1,0:T(8,128)}, s32[1,1]{1,0:T(1,128)}) custom-call(s32[20,20]{1,0:T(8,128)} %pattern_ref.4, f32[80,640]{1,0:T(8,128)S(1)} %get-tuple-element.36.masked_ref), custom_call_target="tpu_custom_call" | custom-call | flops 1000000 | bytes 1000000 | tf_op jit(solution)/shard_map/pallas_call | solution.py:51
  21.9 7.9 %all-to-all-start.1 = ((f32[16,32,128]{2,1,0:T(8,128)}), f32[16,32,128]{2,1,0:T(8,128)S(1)}, u32[]{:S(2)}, u32[]{:S(2)}) async-start(f32[16,32,128]{2,1,0:T(8,128)} %get-tuple-element.38), calls=%async_computation.1 | async-start | bytes 524288 | tf_op jit(solution)/shard_map/all_to_all | solution.py:316
  30.5 5.7 %all-to-all-done.1 = f32[16,32,128]{2,1,0:T(8,128)S(1)} async-done(((f32[16,32,128]{2,1,0:T(8,128)}), f32[16,32,128]{2,1,0:T(8,128)S(1)}, u32[]{:S(2)}, u32[]{:S(2)}) %all-to-all-start.1) | async-done | bytes 262176 | tf_op jit(solution)/shard_map/all_to_all | solution.py:316
  36.3 46.1 %conditional.1 = ((bf16[8,256,640]{2,1,0:T(8,128)(2,1)S(1)}, bf16[8,256,640]{2,1,0:T(8,128)(2,1)})) conditional(s32[]{:T(128)} %bitcast.11, (s32[4]{0:T(128)S(1)}, s32[20,20]{1,0:T(8,128)}, f32[16,32,128]{2,1,0:T(8,128)S(1)}) %tuple.13, (s32[4]{0:T(128)S(1)}, s32[20,20]{1,0:T(8,128)}, f32[16,32,128]{2,1,0:T(8,128)S(1)}) %tuple.13), branch_computations={%region_0.0_spmd, %region_1.0_spmd} | conditional | flops 2409600 | bytes 14908876 | solution.py:317
  36.3 1.7 %branch_1_fun.2 = f32[248,128]{1,0:T(8,128)S(1)} custom-call(s32[4]{0:T(128)S(1)} %get-tuple-element.20.at_ref, s32[20,20]{1,0:T(8,128)} %get-tuple-element.21.pattern_ref, f32[16,32,128]{2,1,0:T(8,128)S(1)} %get-tuple-element.22.got_ref), custom_call_target="tpu_custom_call" | custom-call | flops 1000000 | bytes 1000000 | tf_op jit(solution)/shard_map/cond/branch_1_fun/pallas_call | solution.py:51
  37.9 19.5 %all-gather.4 = f32[496,128]{1,0:T(8,128)S(1)} all-gather(f32[248,128]{1,0:T(8,128)S(1)} %branch_1_fun.2), channel_id=6, replica_groups=mesh['zl'=8,'x'=4,'y'=4,'zh'=2,'c'=2] {'zh'}, dimensions={0}, use_global_device_ids=true | all-gather | bytes 380928 | tf_op jit(solution)/shard_map/cond/branch_1_fun/all_gather | solution.py:264
  57.4 14.0 %all-gather.5 = f32[8,248,128]{2,1,0:T(8,128)S(1)} all-gather(f32[2,248,128]{2,1,0:T(8,128)S(1)} %bitcast.23), channel_id=7, replica_groups=mesh['zl'=8,'x'=4,'y'=4,'zh'=2,'c'=2] {'x'}, dimensions={0}, use_global_device_ids=true | all-gather | bytes 1269760 | tf_op jit(solution)/shard_map/cond/branch_1_fun/all_gather | solution.py:264
  71.5 1.9 %collective-permute-start = (f32[4,2,248,128]{3,2,1,0:T(8,128)S(1)}, f32[4,2,248,128]{3,2,1,0:T(8,128)S(1)}, u32[]{:S(2)}, u32[]{:S(2)}) collective-permute-start(f32[4,2,248,128]{3,2,1,0:T(8,128)S(1)} %bitcast.16), channel_id=1, source_target_pairs={{0,1},{1,0},{2,3},{3,2},{4,5},{5,4},{6,7},{7,6},{8,9},{9,8},{10,11... | collective-permute-start | bytes 3047432 | tf_op jit(solution)/shard_map/cond/branch_1_fun/ppermute | solution.py:256
  73.4 2.6 %collective-permute-done.swap_ref = f32[4,2,248,128]{3,2,1,0:T(8,128)S(1)} collective-permute-done((f32[4,2,248,128]{3,2,1,0:T(8,128)S(1)}, f32[4,2,248,128]{3,2,1,0:T(8,128)S(1)}, u32[]{:S(2)}, u32[]{:S(2)}) %collective-permute-start) | collective-permute-done | bytes 1015840 | tf_op jit(solution)/shard_map/cond/branch_1_fun/ppermute | solution.py:256
  76.0 6.4 %branch_1_fun.3 = (bf16[8,256,640]{2,1,0:T(8,128)(2,1)S(1)}, bf16[8,256,640]{2,1,0:T(8,128)(2,1)}) custom-call(s32[4]{0:T(128)S(1)} %get-tuple-element.20.at_ref, s32[20,20]{1,0:T(8,128)} %get-tuple-element.21.pattern_ref, f32[4,2,248,128]{3,2,1,0:T(8,128)S(1)} %bitcast.17, f32[4,2,248,128]{3,2,1,0:T(8,128)S(1)} %collective-permute-done.swap_ref), custom_call_target="tpu_custom_call" | custom-call | flops 1000000 | bytes 1000000 | tf_op jit(solution)/shard_map/cond/branch_1_fun/pallas_call | solution.py:51
  82.3 16.5 %all-gather.9.cloned.1.call-done = f32[32,104,128]{2,1,0:T(8,128)} async-done(((f32[4,104,128]{2,1,0:T(8,128)}), f32[32,104,128]{2,1,0:T(8,128)}) %all-gather.9.cloned.1.call-update) | async-done | bytes 1703952 | tf_op jit(solution)/shard_map/all_gather | solution.py:306
  98.9 1.5 %copy-done.2 = f32[32,104,128]{2,1,0:T(8,128)S(1)} copy-done((f32[32,104,128]{2,1,0:T(8,128)S(1)}, f32[32,104,128]{2,1,0:T(8,128)}, u32[]{:S(2)}) %copy-start.2) | copy-done | bytes 1703960
  100.3 5.0 %shard_map.39 = f32[4,80,640]{2,1,0:T(8,128)S(1)} custom-call(f32[8,4,104,128]{3,2,1,0:T(8,128)S(1)} %bitcast.20, bf16[8,256,640]{2,1,0:T(8,128)(2,1)S(1)} %get-tuple-element.39.hi_ref, bf16[8,256,640]{2,1,0:T(8,128)(2,1)} %get-tuple-element.40.lo_ref), custom_call_target="tpu_custom_call" | custom-call | flops 3000000000 | bytes 6000000 | tf_op jit(solution)/shard_map/pallas_call | solution.py:51
  105.3 12.9 %all_to_all.21.shares_ref = f32[4,80,640]{2,1,0:T(8,128)S(1)} all-to-all(f32[4,80,640]{2,1,0:T(8,128)S(1)} %shard_map.39), channel_id=1, replica_groups=mesh['zl'=8,'x'=4,'y'=4,'zh'=2,'c'=2] {'y'}, dimensions={0} | all-to-all | bytes 1638400 | tf_op jit(solution)/shard_map/all_to_all | solution.py:333
  118.2 0.0 copy-done.1
  118.2 1.1 shard_map.40
  119.3 15.8 %all_to_all.22 = f32[8,1,80]{2,1,0:T(1,128)S(1)} all-to-all(f32[8,1,80]{2,1,0:T(1,128)S(1)} %bitcast.19), channel_id=1, replica_groups=mesh['zl'=8,'x'=4,'y'=4,'zh'=2,'c'=2] {'zl'}, dimensions={0} | all-to-all | bytes 5120 | tf_op jit(solution)/shard_map/all_to_all | solution.py:340
  135.1 0.9 shard_map.41
  (3 shorter events, 0.0 us)
Async XLA Ops:
  6.5 92.3 %all-gather.9.cloned.1.call-start = ((), (), s32[]{:S(2)}) async-start(), calls=%async_computation.4 | async-start | bytes 1916928 | tf_op jit(solution)/shard_map/all_gather | solution.py:306
  6.6 0.9 copy-start
  21.9 14.3 %all-to-all-start.1 = ((f32[16,32,128]{2,1,0:T(8,128)}), f32[16,32,128]{2,1,0:T(8,128)S(1)}, u32[]{:S(2)}, u32[]{:S(2)}) async-start(f32[16,32,128]{2,1,0:T(8,128)} %get-tuple-element.38), calls=%async_computation.1 | async-start | bytes 524288 | tf_op jit(solution)/shard_map/all_to_all | solution.py:316
  71.5 4.5 %collective-permute-start = (f32[4,2,248,128]{3,2,1,0:T(8,128)S(1)}, f32[4,2,248,128]{3,2,1,0:T(8,128)S(1)}, u32[]{:S(2)}, u32[]{:S(2)}) collective-permute-start(f32[4,2,248,128]{3,2,1,0:T(8,128)S(1)} %bitcast.16), channel_id=1, source_target_pairs={{0,1},{1,0},{2,3},{3,2},{4,5},{5,4},{6,7},{7,6},{8,9},{9,8},{10,11... | collective-permute-start | bytes 3047432 | tf_op jit(solution)/shard_map/cond/branch_1_fun/ppermute | solution.py:256
  98.9 1.5 %copy-start.2 = (f32[32,104,128]{2,1,0:T(8,128)S(1)}, f32[32,104,128]{2,1,0:T(8,128)}, u32[]{:S(2)}) copy-start(f32[32,104,128]{2,1,0:T(8,128)} %all-gather.9.cloned.1.call-done) | copy-start | bytes 5111812
  100.3 17.9 %copy-start.1 = (s32[20,20]{1,0:T(8,128)S(1)}, s32[20,20]{1,0:T(8,128)}, u32[]{:S(2)}) copy-start(s32[20,20]{1,0:T(8,128)} %pattern_ref.5) | copy-start | bytes 4804
Sparse Core Ops, SparseCore 0:
  20.2 78.6 all-gather.8

commit v19 on v18

--- a/solution.py
+++ b/solution.py
@@ -54,7 +54,7 @@
         in_specs=in_specs,
         out_specs=out_specs or jax.tree.map(lambda _: VMEM, outs),
         scratch_shapes=scratch,
-        compiler_params=pltpu.CompilerParams(vmem_limit_bytes=40 * 2**20),
+        compiler_params=pltpu.CompilerParams(vmem_limit_bytes=26 * 2**20),
         cost_estimate=pl.CostEstimate(
             flops=flops, bytes_accessed=size, transcendentals=0
         ),
@@ -176,7 +176,7 @@
     right_ref[...] = (got[:, :128] + got[:, 128:256]) + got[:, 256:]
 
 
-def spread_kernel(slots, at_ref, pattern_ref, own_ref, swap_ref, hi_ref, lo_ref, out_ref):
+def spread_kernel(slots, at_ref, pattern_ref, own_ref, swap_ref, out_ref):
     pattern = pattern_ref[...].astype(jnp.float32).astype(jnp.bfloat16)
     zl, zh, c = at_ref[1], at_ref[2], at_ref[3]
     slot = iota((80, slots), 1).astype(jnp.float32)
@@ -197,28 +197,29 @@
                 base = 40 * (2 * dzh + dc) + 10 * t
                 for block in range(8):
                     out_ref[block, base : base + 10] = got[10 * block : 10 * block + 10]
+
+
+def product_kernel(left_ref, right_ref, out_ref, both_ref, hi_ref, lo_ref):
+    lane = iota((8, 128), 1) // 32
     for block in range(8):
-        rows = out_ref[block]
-        rows = jnp.concatenate([rows] + [rows[128:]] * 3, axis=0)
-        hi_ref[block], lo_ref[block] = split(rows)
-
-
-def product_kernel(left_ref, hi_ref, lo_ref, out_ref):
-    lane = lax.broadcasted_iota(jnp.int32, (8, 128), 1) // 32
-    total = jnp.zeros((320, 640), jnp.float32)
-    for block in range(8):
-        whole = []
+        main = slice(256 * block, 256 * block + 128)
+        last = slice(256 * block + 128, 256 * block + 256)
+        rows = slice(256 * block, 256 * block + 256)
+        right = right_ref[block]
+        right = jnp.concatenate([right] + [right[128:]] * 3, axis=0)
+        hi_ref[rows], lo_ref[rows] = split(right)
         for y in range(4):
             rest = []
             for tile in range(10):
-                rows = MAIN + 8 * (tile // 4)
-                part = left_ref[block, y, rows : rows + 8]
+                start = MAIN + 8 * (tile // 4)
+                part = left_ref[block, y, start : start + 8]
                 rest.append(jnp.where(lane == tile % 4, part, 0.0))
-            rest = jnp.concatenate(rest, axis=0)
-            whole.append(jnp.concatenate([left_ref[block, y, :MAIN], rest], axis=1))
-        left_hi, left_lo = split(jnp.concatenate(whole, axis=0))
-        right_hi, right_lo = hi_ref[block], lo_ref[block]
-        total += dot(left_hi, right_hi) + (dot(left_hi, right_lo) + dot(left_lo, right_hi))
+            upper = slice(80 * y, 80 * y + 80)
+            lower = slice(320 + 80 * y, 400 + 80 * y)
+            both_ref[upper, main], both_ref[lower, main] = split(left_ref[block, y, :MAIN])
+            both_ref[upper, last], both_ref[lower, last] = split(jnp.concatenate(rest, axis=0))
+    total = dot(both_ref[...], hi_ref[...])
+    total = total[:320] + (dot(both_ref[:320], lo_ref[...]) + total[320:])
     out_ref[...] = total.reshape(4, 80, 640)
 
 
@@ -271,7 +272,7 @@
     return jax.ShapeDtypeStruct(shape, jnp.float32)
 
 
-def right_halves(slots, at, in_pattern, got):
+def right_blocks(slots, at, in_pattern, got):
     cols = 640
     right = call(
         functools.partial(pack_kernel, slots),
@@ -280,13 +281,11 @@
         (at, in_pattern, got),
     )
     own = gather(gather(right, "zh", SLOTS), "x", SLOTS)
-    half = jax.ShapeDtypeStruct((8, 256, cols), jnp.bfloat16)
     return call(
         functools.partial(spread_kernel, slots),
-        (half, half),
+        f32(8, 160, cols),
         [SMEM, VMEM, VMEM, VMEM],
         (at, in_pattern, own, swap(own, "c")),
-        [pltpu.VMEM((8, 160, cols), jnp.float32)],
     )
 
 
@@ -314,10 +313,10 @@
         out_specs=(VMEM, SMEM),
     )
     got = lax.all_to_all(units, ("x", "y"), 0, 0)
-    right_hi, right_lo = lax.cond(
+    right = lax.cond(
         most[0, 0] <= SLOTS,
-        functools.partial(right_halves, SLOTS),
-        functools.partial(right_halves, ALL),
+        functools.partial(right_blocks, SLOTS),
+        functools.partial(right_blocks, ALL),
         at,
         in_pattern,
         got,
@@ -325,8 +324,9 @@
     partial = call(
         product_kernel,
         f32(4, rows, cols),
-        [VMEM, VMEM, VMEM],
-        (left, right_hi, right_lo),
+        [VMEM, VMEM],
+        (left, right),
+        [pltpu.VMEM((640, 8 * 256), jnp.bfloat16)] + [pltpu.VMEM((8 * 256, cols), jnp.bfloat16)] * 2,
         flops=3 * 10**9,
         size=6 * 10**6,
     )

time: 145 us -> 142 us (0.979)
  Pallas kernels: 18.6 us -> 14.8 us
  waiting for transfers between devices: 24.8 us -> 26.3 us
    pallas_call x7, Pallas kernels: 18.6 us -> 14.8 us  [call(): pl.pallas_call(kernel, out_shape=outs, in_specs=in_specs, out_specs=out_s...]
    all_gather x1, waiting for transfers between devices: 16.5 us -> 18 us  [body(): left = lax.all_gather(left, 'zl', axis=0)]
  transfers between devices with their start and end apart: 3 -> 3, of which waited for: 3 -> 3; matrix products, arithmetic and copies ran while one was open for 0% -> 0% of each run, Pallas kernels for 7% -> 6%
where the time goes in v19:
time: 142 us; the launch traced here: 141 us
  blocking collectives  73.3 us (52%)
  waiting for transfers between devices  26.3 us (19%)
  Pallas kernels  14.8 us (10%)
  between operations  14.1 us (10%)
  starting transfers between devices  9.86 us (7%)
  local copies, waits for them, and re-layouts  2.39 us (2%)
    all_gather x2, blocking collectives, gather(): lax.all_gather(x[..., i * size:(i + 1) * size, :], axis_name, axis=0)  33.4 us
    all_gather x1, waiting for transfers between devices, body(): left = lax.all_gather(left, 'zl', axis=0)  18 us
    all_to_all x1, blocking collectives, body(): sums = lax.all_to_all(sums.reshape(8, 1, rows), 'zl', 0, 0).reshape(8, rows)  15.9 us
    pallas_call x7, Pallas kernels, call(): pl.pallas_call(kernel, out_shape=outs, in_specs=in_specs, out_specs=out_s...  14.8 us
    all_to_all x1, blocking collectives, body(): shares = lax.all_to_all(partial, 'y', 0, 0)  13.2 us
    all_to_all x1, blocking collectives, body(): left = lax.all_to_all(left, 'y', 0, 0)  10.8 us
    all_to_all x1, starting transfers between devices, body(): got = lax.all_to_all(units, ('x', 'y'), 0, 0)  7.95 us
    all_to_all x1, waiting for transfers between devices, body(): got = lax.all_to_all(units, ('x', 'y'), 0, 0)  5.74 us
  transfers between devices with their start and end apart: 3, of which 3 were waited for; matrix products, arithmetic and copies ran while one was open for 0% of the time, Pallas kernels for 6%

profile of v19, /device:TPU:6, one launch (start us, length us, event | category | flops | bytes accessed | tf_op | source)
XLA Modules:
  0.0 141.0 jit_solution(9843763380055182199)
XLA Ops:
  6.5 0.1 pad_add_fusion.at_ref
  6.6 0.9 copy-done
  7.5 1.7 %shard_map.37 = (f32[4,104,128]{2,1,0:T(8,128)S(1)}, f32[80,640]{1,0:T(8,128)S(1)}) custom-call(s32[4]{0:T(128)S(1)} %pad_add_fusion.at_ref, s32[20,20]{1,0:T(8,128)} %pattern_ref.4, f32[80,640]{1,0:T(8,128)S(1)} %copy-done), custom_call_target="tpu_custom_call" | custom-call | flops 1000000 | bytes 1000000 | tf_op jit(solution)/shard_map/pallas_call | solution.py:51
  9.2 10.8 %all_to_all.20 = f32[4,104,128]{2,1,0:T(8,128)} all-to-all(f32[4,104,128]{2,1,0:T(8,128)S(1)} %get-tuple-element.34), channel_id=1, replica_groups=mesh['zl'=8,'x'=4,'y'=4,'zh'=2,'c'=2] {'y'}, dimensions={0} | all-to-all | bytes 425984 | tf_op jit(solution)/shard_map/all_to_all | solution.py:303
  20.0 0.0 all-gather.9.cloned.1.call-update
  20.0 1.9 %shard_map.38 = (f32[16,32,128]{2,1,0:T(8,128)}, s32[1,1]{1,0:T(1,128)}) custom-call(s32[20,20]{1,0:T(8,128)} %pattern_ref.4, f32[80,640]{1,0:T(8,128)S(1)} %get-tuple-element.37.masked_ref), custom_call_target="tpu_custom_call" | custom-call | flops 1000000 | bytes 1000000 | tf_op jit(solution)/shard_map/pallas_call | solution.py:51
  22.0 8.0 %all-to-all-start.1 = ((f32[16,32,128]{2,1,0:T(8,128)}), f32[16,32,128]{2,1,0:T(8,128)S(1)}, u32[]{:S(2)}, u32[]{:S(2)}) async-start(f32[16,32,128]{2,1,0:T(8,128)} %get-tuple-element.39), calls=%async_computation.1 | async-start | bytes 524288 | tf_op jit(solution)/shard_map/all_to_all | solution.py:315
  30.6 5.7 %all-to-all-done.1 = f32[16,32,128]{2,1,0:T(8,128)S(1)} async-done(((f32[16,32,128]{2,1,0:T(8,128)}), f32[16,32,128]{2,1,0:T(8,128)S(1)}, u32[]{:S(2)}, u32[]{:S(2)}) %all-to-all-start.1) | async-done | bytes 262176 | tf_op jit(solution)/shard_map/all_to_all | solution.py:315
  36.3 0.0 copy-done.3
  36.3 44.0 %conditional.1 = (f32[8,160,640]{2,1,0:T(8,128)S(1)}) conditional(s32[]{:T(128)} %bitcast.11, (s32[4]{0:T(128)S(1)}, s32[20,20]{1,0:T(8,128)S(1)}, f32[16,32,128]{2,1,0:T(8,128)S(1)}) %tuple.19, (s32[4]{0:T(128)S(1)}, s32[20,20]{1,0:T(8,128)S(1)}, f32[16,32,128]{2,1,0:T(8,128)S(1)}) %tuple.20), branch_computations={%region_0.0_spmd, %region_1.0_spmd} | conditional | flops 2409600 | bytes 14902448 | solution.py:316
  36.3 1.5 %branch_1_fun.2 = f32[248,128]{1,0:T(8,128)S(1)} custom-call(s32[4]{0:T(128)S(1)} %get-tuple-element.23.at_ref, s32[20,20]{1,0:T(8,128)S(1)} %get-tuple-element.24.pattern_ref, f32[16,32,128]{2,1,0:T(8,128)S(1)} %get-tuple-element.25.got_ref), custom_call_target="tpu_custom_call" | custom-call | flops 1000000 | bytes 1000000 | tf_op jit(solution)/shard_map/cond/branch_1_fun/pallas_call | solution.py:51
  37.8 19.4 %all-gather.4 = f32[496,128]{1,0:T(8,128)S(1)} all-gather(f32[248,128]{1,0:T(8,128)S(1)} %branch_1_fun.2), channel_id=6, replica_groups=mesh['zl'=8,'x'=4,'y'=4,'zh'=2,'c'=2] {'zh'}, dimensions={0}, use_global_device_ids=true | all-gather | bytes 380928 | tf_op jit(solution)/shard_map/cond/branch_1_fun/all_gather | solution.py:265
  57.2 14.0 %all-gather.5 = f32[8,248,128]{2,1,0:T(8,128)S(1)} all-gather(f32[2,248,128]{2,1,0:T(8,128)S(1)} %bitcast.23), channel_id=7, replica_groups=mesh['zl'=8,'x'=4,'y'=4,'zh'=2,'c'=2] {'x'}, dimensions={0}, use_global_device_ids=true | all-gather | bytes 1269760 | tf_op jit(solution)/shard_map/cond/branch_1_fun/all_gather | solution.py:265
  71.2 1.9 %collective-permute-start = (f32[4,2,248,128]{3,2,1,0:T(8,128)S(1)}, f32[4,2,248,128]{3,2,1,0:T(8,128)S(1)}, u32[]{:S(2)}, u32[]{:S(2)}) collective-permute-start(f32[4,2,248,128]{3,2,1,0:T(8,128)S(1)} %bitcast.16), channel_id=1, source_target_pairs={{0,1},{1,0},{2,3},{3,2},{4,5},{5,4},{6,7},{7,6},{8,9},{9,8},{10,11... | collective-permute-start | bytes 3047432 | tf_op jit(solution)/shard_map/cond/branch_1_fun/ppermute | solution.py:257
  73.1 2.6 %collective-permute-done.swap_ref = f32[4,2,248,128]{3,2,1,0:T(8,128)S(1)} collective-permute-done((f32[4,2,248,128]{3,2,1,0:T(8,128)S(1)}, f32[4,2,248,128]{3,2,1,0:T(8,128)S(1)}, u32[]{:S(2)}, u32[]{:S(2)}) %collective-permute-start) | collective-permute-done | bytes 1015840 | tf_op jit(solution)/shard_map/cond/branch_1_fun/ppermute | solution.py:257
  75.7 4.4 %branch_1_fun.3 = f32[8,160,640]{2,1,0:T(8,128)S(1)} custom-call(s32[4]{0:T(128)S(1)} %get-tuple-element.23.at_ref, s32[20,20]{1,0:T(8,128)S(1)} %get-tuple-element.24.pattern_ref, f32[4,2,248,128]{3,2,1,0:T(8,128)S(1)} %bitcast.17, f32[4,2,248,128]{3,2,1,0:T(8,128)S(1)} %collective-permute-done.swap_ref), custom_call_target="tpu_custom_call" | custom-call | flops 1000000 | bytes 1000000 | tf_op jit(solution)/shard_map/cond/branch_1_fun/pallas_call | solution.py:51
  80.3 18.0 %all-gather.9.cloned.1.call-done = f32[32,104,128]{2,1,0:T(8,128)} async-done(((f32[4,104,128]{2,1,0:T(8,128)}), f32[32,104,128]{2,1,0:T(8,128)}) %all-gather.9.cloned.1.call-update) | async-done | bytes 1703952 | tf_op jit(solution)/shard_map/all_gather | solution.py:305
  98.3 1.5 %copy-done.2 = f32[32,104,128]{2,1,0:T(8,128)S(1)} copy-done((f32[32,104,128]{2,1,0:T(8,128)S(1)}, f32[32,104,128]{2,1,0:T(8,128)}, u32[]{:S(2)}) %copy-start.2) | copy-done | bytes 1703960
  99.8 3.3 %shard_map.39 = f32[4,80,640]{2,1,0:T(8,128)S(1)} custom-call(f32[8,4,104,128]{3,2,1,0:T(8,128)S(1)} %bitcast.20, f32[8,160,640]{2,1,0:T(8,128)S(1)} %get-tuple-element.44.right_ref), custom_call_target="tpu_custom_call" | custom-call | flops 3000000000 | bytes 6000000 | tf_op jit(solution)/shard_map/pallas_call | solution.py:51
  103.1 0.0 copy-start.1
  103.1 13.2 %all_to_all.21.shares_ref = f32[4,80,640]{2,1,0:T(8,128)S(1)} all-to-all(f32[4,80,640]{2,1,0:T(8,128)S(1)} %shard_map.39), channel_id=1, replica_groups=mesh['zl'=8,'x'=4,'y'=4,'zh'=2,'c'=2] {'y'}, dimensions={0} | all-to-all | bytes 1638400 | tf_op jit(solution)/shard_map/all_to_all | solution.py:333
  116.3 1.1 shard_map.40
  117.4 15.9 %all_to_all.22 = f32[8,1,80]{2,1,0:T(1,128)S(1)} all-to-all(f32[8,1,80]{2,1,0:T(1,128)S(1)} %bitcast.19), channel_id=1, replica_groups=mesh['zl'=8,'x'=4,'y'=4,'zh'=2,'c'=2] {'zl'}, dimensions={0} | all-to-all | bytes 5120 | tf_op jit(solution)/shard_map/all_to_all | solution.py:340
  133.3 0.9 shard_map.41
  (5 shorter events, 0.0 us)
Async XLA Ops:
  6.5 29.8 %copy-start.3 = (s32[20,20]{1,0:T(8,128)S(1)}, s32[20,20]{1,0:T(8,128)}, u32[]{:S(2)}) copy-start(s32[20,20]{1,0:T(8,128)} %pattern_ref.4) | copy-start | bytes 4804
  6.5 91.8 %all-gather.9.cloned.1.call-start = ((), (), s32[]{:S(2)}) async-start(), calls=%async_computation.4 | async-start | bytes 1916928 | tf_op jit(solution)/shard_map/all_gather | solution.py:305
  6.6 0.9 copy-start
  22.0 14.3 %all-to-all-start.1 = ((f32[16,32,128]{2,1,0:T(8,128)}), f32[16,32,128]{2,1,0:T(8,128)S(1)}, u32[]{:S(2)}, u32[]{:S(2)}) async-start(f32[16,32,128]{2,1,0:T(8,128)} %get-tuple-element.39), calls=%async_computation.1 | async-start | bytes 524288 | tf_op jit(solution)/shard_map/all_to_all | solution.py:315
  71.2 4.5 %collective-permute-start = (f32[4,2,248,128]{3,2,1,0:T(8,128)S(1)}, f32[4,2,248,128]{3,2,1,0:T(8,128)S(1)}, u32[]{:S(2)}, u32[]{:S(2)}) collective-permute-start(f32[4,2,248,128]{3,2,1,0:T(8,128)S(1)} %bitcast.16), channel_id=1, source_target_pairs={{0,1},{1,0},{2,3},{3,2},{4,5},{5,4},{6,7},{7,6},{8,9},{9,8},{10,11... | collective-permute-start | bytes 3047432 | tf_op jit(solution)/shard_map/cond/branch_1_fun/ppermute | solution.py:257
  98.3 1.5 %copy-start.2 = (f32[32,104,128]{2,1,0:T(8,128)S(1)}, f32[32,104,128]{2,1,0:T(8,128)}, u32[]{:S(2)}) copy-start(f32[32,104,128]{2,1,0:T(8,128)} %all-gather.9.cloned.1.call-done) | copy-start | bytes 5111812
  103.1 13.3 %copy-start.1 = (s32[20,20]{1,0:T(8,128)S(1)}, s32[20,20]{1,0:T(8,128)}, u32[]{:S(2)}) copy-start(s32[20,20]{1,0:T(8,128)} %pattern_ref.5) | copy-start | bytes 4804
Sparse Core Ops, SparseCore 0:
  20.2 78.0 all-gather.8

commit v20 on v19

--- a/solution.py
+++ b/solution.py
@@ -280,7 +280,7 @@
         [SMEM, VMEM, VMEM],
         (at, in_pattern, got),
     )
-    own = gather(gather(right, "zh", SLOTS), "x", SLOTS)
+    own = gather(gather(right, "zh", ALL), "x", SLOTS)
     return call(
         functools.partial(spread_kernel, slots),
         f32(8, 160, cols),

time: 142 us -> 142 us (level)
  no operation moved by 1% of the time
where the time goes in v20:
time: 142 us; the launch traced here: 141 us
  blocking collectives  73.3 us (52%)
  waiting for transfers between devices  26.3 us (19%)
  Pallas kernels  14.8 us (10%)
  between operations  14.1 us (10%)
  starting transfers between devices  9.86 us (7%)
  local copies, waits for them, and re-layouts  2.39 us (2%)
    all_gather x2, blocking collectives, gather(): lax.all_gather(x[..., i * size:(i + 1) * size, :], axis_name, axis=0)  33.4 us
    all_gather x1, waiting for transfers between devices, body(): left = lax.all_gather(left, 'zl', axis=0)  18 us
    all_to_all x1, blocking collectives, body(): sums = lax.all_to_all(sums.reshape(8, 1, rows), 'zl', 0, 0).reshape(8, rows)  15.9 us
    pallas_call x7, Pallas kernels, call(): pl.pallas_call(kernel, out_shape=outs, in_specs=in_specs, out_specs=out_s...  14.8 us
    all_to_all x1, blocking collectives, body(): shares = lax.all_to_all(partial, 'y', 0, 0)  13.2 us
    all_to_all x1, blocking collectives, body(): left = lax.all_to_all(left, 'y', 0, 0)  10.8 us
    all_to_all x1, starting transfers between devices, body(): got = lax.all_to_all(units, ('x', 'y'), 0, 0)  7.95 us
    all_to_all x1, waiting for transfers between devices, body(): got = lax.all_to_all(units, ('x', 'y'), 0, 0)  5.74 us
  transfers between devices with their start and end apart: 3, of which 3 were waited for; matrix products, arithmetic and copies ran while one was open for 0% of the time, Pallas kernels for 6%

profile of v20, /device:TPU:6, one launch (start us, length us, event | category | flops | bytes accessed | tf_op | source)
XLA Modules:
  0.0 141.0 jit_solution(3197327522854856195)
XLA Ops:
  6.5 0.1 pad_add_fusion.at_ref
  6.6 0.9 copy-done
  7.5 1.7 %shard_map.37 = (f32[4,104,128]{2,1,0:T(8,128)S(1)}, f32[80,640]{1,0:T(8,128)S(1)}) custom-call(s32[4]{0:T(128)S(1)} %pad_add_fusion.at_ref, s32[20,20]{1,0:T(8,128)} %pattern_ref.4, f32[80,640]{1,0:T(8,128)S(1)} %copy-done), custom_call_target="tpu_custom_call" | custom-call | flops 1000000 | bytes 1000000 | tf_op jit(solution)/shard_map/pallas_call | solution.py:51
  9.2 10.8 %all_to_all.20 = f32[4,104,128]{2,1,0:T(8,128)} all-to-all(f32[4,104,128]{2,1,0:T(8,128)S(1)} %get-tuple-element.34), channel_id=1, replica_groups=mesh['zl'=8,'x'=4,'y'=4,'zh'=2,'c'=2] {'y'}, dimensions={0} | all-to-all | bytes 425984 | tf_op jit(solution)/shard_map/all_to_all | solution.py:303
  20.0 0.0 all-gather.8.cloned.1.call-update
  20.0 1.9 %shard_map.38 = (f32[16,32,128]{2,1,0:T(8,128)}, s32[1,1]{1,0:T(1,128)}) custom-call(s32[20,20]{1,0:T(8,128)} %pattern_ref.4, f32[80,640]{1,0:T(8,128)S(1)} %get-tuple-element.37.masked_ref), custom_call_target="tpu_custom_call" | custom-call | flops 1000000 | bytes 1000000 | tf_op jit(solution)/shard_map/pallas_call | solution.py:51
  22.0 8.0 %all-to-all-start.1 = ((f32[16,32,128]{2,1,0:T(8,128)}), f32[16,32,128]{2,1,0:T(8,128)S(1)}, u32[]{:S(2)}, u32[]{:S(2)}) async-start(f32[16,32,128]{2,1,0:T(8,128)} %get-tuple-element.39), calls=%async_computation.1 | async-start | bytes 524288 | tf_op jit(solution)/shard_map/all_to_all | solution.py:315
  30.6 5.7 %all-to-all-done.1 = f32[16,32,128]{2,1,0:T(8,128)S(1)} async-done(((f32[16,32,128]{2,1,0:T(8,128)}), f32[16,32,128]{2,1,0:T(8,128)S(1)}, u32[]{:S(2)}, u32[]{:S(2)}) %all-to-all-start.1) | async-done | bytes 262176 | tf_op jit(solution)/shard_map/all_to_all | solution.py:315
  36.3 0.0 copy-done.3
  36.3 44.0 %conditional.1 = (f32[8,160,640]{2,1,0:T(8,128)S(1)}) conditional(s32[]{:T(128)} %bitcast.10, (s32[4]{0:T(128)S(1)}, s32[20,20]{1,0:T(8,128)S(1)}, f32[16,32,128]{2,1,0:T(8,128)S(1)}) %tuple.19, (s32[4]{0:T(128)S(1)}, s32[20,20]{1,0:T(8,128)S(1)}, f32[16,32,128]{2,1,0:T(8,128)S(1)}) %tuple.20), branch_computations={%region_0.0_spmd, %region_1.0_spmd} | conditional | flops 2409600 | bytes 15312048 | solution.py:316
  36.3 1.5 %branch_1_fun.2 = f32[248,128]{1,0:T(8,128)S(1)} custom-call(s32[4]{0:T(128)S(1)} %get-tuple-element.23.at_ref, s32[20,20]{1,0:T(8,128)S(1)} %get-tuple-element.24.pattern_ref, f32[16,32,128]{2,1,0:T(8,128)S(1)} %get-tuple-element.25.got_ref), custom_call_target="tpu_custom_call" | custom-call | flops 1000000 | bytes 1000000 | tf_op jit(solution)/shard_map/cond/branch_1_fun/pallas_call | solution.py:51
  37.8 19.4 %all-gather.3 = f32[496,128]{1,0:T(8,128)S(1)} all-gather(f32[248,128]{1,0:T(8,128)S(1)} %branch_1_fun.2), channel_id=5, replica_groups=mesh['zl'=8,'x'=4,'y'=4,'zh'=2,'c'=2] {'zh'}, dimensions={0}, use_global_device_ids=true | all-gather | bytes 380928 | tf_op jit(solution)/shard_map/cond/branch_1_fun/all_gather | solution.py:265
  57.2 14.0 %all-gather.4 = f32[8,248,128]{2,1,0:T(8,128)S(1)} all-gather(f32[2,248,128]{2,1,0:T(8,128)S(1)} %bitcast.23), channel_id=6, replica_groups=mesh['zl'=8,'x'=4,'y'=4,'zh'=2,'c'=2] {'x'}, dimensions={0}, use_global_device_ids=true | all-gather | bytes 1269760 | tf_op jit(solution)/shard_map/cond/branch_1_fun/all_gather | solution.py:265
  71.2 1.9 %collective-permute-start = (f32[4,2,248,128]{3,2,1,0:T(8,128)S(1)}, f32[4,2,248,128]{3,2,1,0:T(8,128)S(1)}, u32[]{:S(2)}, u32[]{:S(2)}) collective-permute-start(f32[4,2,248,128]{3,2,1,0:T(8,128)S(1)} %bitcast.15), channel_id=1, source_target_pairs={{0,1},{1,0},{2,3},{3,2},{4,5},{5,4},{6,7},{7,6},{8,9},{9,8},{10,11... | collective-permute-start | bytes 3047432 | tf_op jit(solution)/shard_map/cond/branch_1_fun/ppermute | solution.py:257
  73.1 2.6 %collective-permute-done.swap_ref = f32[4,2,248,128]{3,2,1,0:T(8,128)S(1)} collective-permute-done((f32[4,2,248,128]{3,2,1,0:T(8,128)S(1)}, f32[4,2,248,128]{3,2,1,0:T(8,128)S(1)}, u32[]{:S(2)}, u32[]{:S(2)}) %collective-permute-start) | collective-permute-done | bytes 1015840 | tf_op jit(solution)/shard_map/cond/branch_1_fun/ppermute | solution.py:257
  75.7 4.4 %branch_1_fun.3 = f32[8,160,640]{2,1,0:T(8,128)S(1)} custom-call(s32[4]{0:T(128)S(1)} %get-tuple-element.23.at_ref, s32[20,20]{1,0:T(8,128)S(1)} %get-tuple-element.24.pattern_ref, f32[4,2,248,128]{3,2,1,0:T(8,128)S(1)} %bitcast.16, f32[4,2,248,128]{3,2,1,0:T(8,128)S(1)} %collective-permute-done.swap_ref), custom_call_target="tpu_custom_call" | custom-call | flops 1000000 | bytes 1000000 | tf_op jit(solution)/shard_map/cond/branch_1_fun/pallas_call | solution.py:51
  80.3 18.0 %all-gather.8.cloned.1.call-done = f32[32,104,128]{2,1,0:T(8,128)} async-done(((f32[4,104,128]{2,1,0:T(8,128)}), f32[32,104,128]{2,1,0:T(8,128)}) %all-gather.8.cloned.1.call-update) | async-done | bytes 1703952 | tf_op jit(solution)/shard_map/all_gather | solution.py:305
  98.3 1.5 %copy-done.2 = f32[32,104,128]{2,1,0:T(8,128)S(1)} copy-done((f32[32,104,128]{2,1,0:T(8,128)S(1)}, f32[32,104,128]{2,1,0:T(8,128)}, u32[]{:S(2)}) %copy-start.2) | copy-done | bytes 1703960
  99.8 3.3 %shard_map.39 = f32[4,80,640]{2,1,0:T(8,128)S(1)} custom-call(f32[8,4,104,128]{3,2,1,0:T(8,128)S(1)} %bitcast.19, f32[8,160,640]{2,1,0:T(8,128)S(1)} %get-tuple-element.44.right_ref), custom_call_target="tpu_custom_call" | custom-call | flops 3000000000 | bytes 6000000 | tf_op jit(solution)/shard_map/pallas_call | solution.py:51
  103.1 0.0 copy-start.1
  103.1 13.2 %all_to_all.21.shares_ref = f32[4,80,640]{2,1,0:T(8,128)S(1)} all-to-all(f32[4,80,640]{2,1,0:T(8,128)S(1)} %shard_map.39), channel_id=1, replica_groups=mesh['zl'=8,'x'=4,'y'=4,'zh'=2,'c'=2] {'y'}, dimensions={0} | all-to-all | bytes 1638400 | tf_op jit(solution)/shard_map/all_to_all | solution.py:333
  116.3 1.1 shard_map.40
  117.4 15.9 %all_to_all.22 = f32[8,1,80]{2,1,0:T(1,128)S(1)} all-to-all(f32[8,1,80]{2,1,0:T(1,128)S(1)} %bitcast.18), channel_id=1, replica_groups=mesh['zl'=8,'x'=4,'y'=4,'zh'=2,'c'=2] {'zl'}, dimensions={0} | all-to-all | bytes 5120 | tf_op jit(solution)/shard_map/all_to_all | solution.py:340
  133.3 0.9 shard_map.41
  (5 shorter events, 0.0 us)
Async XLA Ops:
  6.5 29.8 %copy-start.3 = (s32[20,20]{1,0:T(8,128)S(1)}, s32[20,20]{1,0:T(8,128)}, u32[]{:S(2)}) copy-start(s32[20,20]{1,0:T(8,128)} %pattern_ref.4) | copy-start | bytes 4804
  6.5 91.8 %all-gather.8.cloned.1.call-start = ((), (), s32[]{:S(2)}) async-start(), calls=%async_computation.4 | async-start | bytes 1916928 | tf_op jit(solution)/shard_map/all_gather | solution.py:305
  6.6 0.9 copy-start
  22.0 14.3 %all-to-all-start.1 = ((f32[16,32,128]{2,1,0:T(8,128)}), f32[16,32,128]{2,1,0:T(8,128)S(1)}, u32[]{:S(2)}, u32[]{:S(2)}) async-start(f32[16,32,128]{2,1,0:T(8,128)} %get-tuple-element.39), calls=%async_computation.1 | async-start | bytes 524288 | tf_op jit(solution)/shard_map/all_to_all | solution.py:315
  71.2 4.5 %collective-permute-start = (f32[4,2,248,128]{3,2,1,0:T(8,128)S(1)}, f32[4,2,248,128]{3,2,1,0:T(8,128)S(1)}, u32[]{:S(2)}, u32[]{:S(2)}) collective-permute-start(f32[4,2,248,128]{3,2,1,0:T(8,128)S(1)} %bitcast.15), channel_id=1, source_target_pairs={{0,1},{1,0},{2,3},{3,2},{4,5},{5,4},{6,7},{7,6},{8,9},{9,8},{10,11... | collective-permute-start | bytes 3047432 | tf_op jit(solution)/shard_map/cond/branch_1_fun/ppermute | solution.py:257
  98.3 1.5 %copy-start.2 = (f32[32,104,128]{2,1,0:T(8,128)S(1)}, f32[32,104,128]{2,1,0:T(8,128)}, u32[]{:S(2)}) copy-start(f32[32,104,128]{2,1,0:T(8,128)} %all-gather.8.cloned.1.call-done) | copy-start | bytes 5111812
  103.1 13.3 %copy-start.1 = (s32[20,20]{1,0:T(8,128)S(1)}, s32[20,20]{1,0:T(8,128)}, u32[]{:S(2)}) copy-start(s32[20,20]{1,0:T(8,128)} %pattern_ref.5) | copy-start | bytes 4804
Sparse Core Ops, SparseCore 0:
  20.2 78.0 all-gather.7

commit v21 on v20

--- a/solution.py
+++ b/solution.py
@@ -128,9 +128,8 @@
     order = lax.broadcasted_iota(jnp.int32, (640, 640), 0) == source
     order = order.astype(jnp.float32).astype(jnp.bfloat16)
     x = masked_ref[...]
-    hi = x.astype(jnp.bfloat16)
-    mid, low = split(x - hi.astype(jnp.float32))
-    moved = (dot(hi, order) + dot(mid, order)) + dot(low, order)
+    hi, lo = split(x)
+    moved = dot(hi, order) + dot(lo, order)
     lane = lax.broadcasted_iota(jnp.int32, (8, 128), 1) // 32
     for y in range(4):
         out_ref[y, :MAIN] = moved[:, 128 * y : 128 * y + 128]

time: 142 us -> 142 us (level)
  no operation moved by 1% of the time
where the time goes in v21:
time: 142 us; the launch traced here: 141 us
  blocking collectives  73 us (51%)
  waiting for transfers between devices  26.6 us (19%)
  Pallas kernels  14.7 us (10%)
  between operations  14.1 us (10%)
  starting transfers between devices  9.86 us (7%)
  local copies, waits for them, and re-layouts  2.39 us (2%)
    all_gather x2, blocking collectives, gather(): lax.all_gather(x[..., i * size:(i + 1) * size, :], axis_name, axis=0)  33.4 us
    all_gather x1, waiting for transfers between devices, body(): left = lax.all_gather(left, 'zl', axis=0)  18.2 us
    all_to_all x1, blocking collectives, body(): sums = lax.all_to_all(sums.reshape(8, 1, rows), 'zl', 0, 0).reshape(8, rows)  15.7 us
    pallas_call x7, Pallas kernels, call(): pl.pallas_call(kernel, out_shape=outs, in_specs=in_specs, out_specs=out_s...  14.7 us
    all_to_all x1, blocking collectives, body(): shares = lax.all_to_all(partial, 'y', 0, 0)  13.1 us
    all_to_all x1, blocking collectives, body(): left = lax.all_to_all(left, 'y', 0, 0)  10.8 us
    all_to_all x1, starting transfers between devices, body(): got = lax.all_to_all(units, ('x', 'y'), 0, 0)  7.95 us
    all_to_all x1, waiting for transfers between devices, body(): got = lax.all_to_all(units, ('x', 'y'), 0, 0)  5.74 us
  transfers between devices with their start and end apart: 3, of which 3 were waited for; matrix products, arithmetic and copies ran while one was open for 0% of the time, Pallas kernels for 6%

profile of v21, /device:TPU:6, one launch (start us, length us, event | category | flops | bytes accessed | tf_op | source)
XLA Modules:
  0.0 140.9 jit_solution(5813554810939343397)
XLA Ops:
  6.5 0.0 all-gather.8.cloned.1.call-start
  6.5 0.1 pad_add_fusion.at_ref
  6.6 0.9 copy-done
  7.5 1.6 %shard_map.37 = (f32[4,104,128]{2,1,0:T(8,128)S(1)}, f32[80,640]{1,0:T(8,128)S(1)}) custom-call(s32[4]{0:T(128)S(1)} %pad_add_fusion.at_ref, s32[20,20]{1,0:T(8,128)} %pattern_ref.4, f32[80,640]{1,0:T(8,128)S(1)} %copy-done), custom_call_target="tpu_custom_call" | custom-call | flops 1000000 | bytes 1000000 | tf_op jit(solution)/shard_map/pallas_call | solution.py:51
  9.2 10.8 %all_to_all.20 = f32[4,104,128]{2,1,0:T(8,128)} all-to-all(f32[4,104,128]{2,1,0:T(8,128)S(1)} %get-tuple-element.34), channel_id=1, replica_groups=mesh['zl'=8,'x'=4,'y'=4,'zh'=2,'c'=2] {'y'}, dimensions={0} | all-to-all | bytes 425984 | tf_op jit(solution)/shard_map/all_to_all | solution.py:302
  19.9 0.0 all-gather.8.cloned.1.call-update
  20.0 1.9 %shard_map.38 = (f32[16,32,128]{2,1,0:T(8,128)}, s32[1,1]{1,0:T(1,128)}) custom-call(s32[20,20]{1,0:T(8,128)} %pattern_ref.4, f32[80,640]{1,0:T(8,128)S(1)} %get-tuple-element.37.masked_ref), custom_call_target="tpu_custom_call" | custom-call | flops 1000000 | bytes 1000000 | tf_op jit(solution)/shard_map/pallas_call | solution.py:51
  21.9 8.0 %all-to-all-start.1 = ((f32[16,32,128]{2,1,0:T(8,128)}), f32[16,32,128]{2,1,0:T(8,128)S(1)}, u32[]{:S(2)}, u32[]{:S(2)}) async-start(f32[16,32,128]{2,1,0:T(8,128)} %get-tuple-element.39), calls=%async_computation.1 | async-start | bytes 524288 | tf_op jit(solution)/shard_map/all_to_all | solution.py:314
  30.5 5.7 %all-to-all-done.1 = f32[16,32,128]{2,1,0:T(8,128)S(1)} async-done(((f32[16,32,128]{2,1,0:T(8,128)}), f32[16,32,128]{2,1,0:T(8,128)S(1)}, u32[]{:S(2)}, u32[]{:S(2)}) %all-to-all-start.1) | async-done | bytes 262176 | tf_op jit(solution)/shard_map/all_to_all | solution.py:314
  36.2 44.0 %conditional.1 = (f32[8,160,640]{2,1,0:T(8,128)S(1)}) conditional(s32[]{:T(128)} %bitcast.10, (s32[4]{0:T(128)S(1)}, s32[20,20]{1,0:T(8,128)S(1)}, f32[16,32,128]{2,1,0:T(8,128)S(1)}) %tuple.19, (s32[4]{0:T(128)S(1)}, s32[20,20]{1,0:T(8,128)S(1)}, f32[16,32,128]{2,1,0:T(8,128)S(1)}) %tuple.20), branch_computations={%region_0.0_spmd, %region_1.0_spmd} | conditional | flops 2409600 | bytes 15312048 | solution.py:315
  36.2 1.5 %branch_1_fun.2 = f32[248,128]{1,0:T(8,128)S(1)} custom-call(s32[4]{0:T(128)S(1)} %get-tuple-element.23.at_ref, s32[20,20]{1,0:T(8,128)S(1)} %get-tuple-element.24.pattern_ref, f32[16,32,128]{2,1,0:T(8,128)S(1)} %get-tuple-element.25.got_ref), custom_call_target="tpu_custom_call" | custom-call | flops 1000000 | bytes 1000000 | tf_op jit(solution)/shard_map/cond/branch_1_fun/pallas_call | solution.py:51
  37.7 19.4 %all-gather.3 = f32[496,128]{1,0:T(8,128)S(1)} all-gather(f32[248,128]{1,0:T(8,128)S(1)} %branch_1_fun.2), channel_id=5, replica_groups=mesh['zl'=8,'x'=4,'y'=4,'zh'=2,'c'=2] {'zh'}, dimensions={0}, use_global_device_ids=true | all-gather | bytes 380928 | tf_op jit(solution)/shard_map/cond/branch_1_fun/all_gather | solution.py:264
  57.1 14.0 %all-gather.4 = f32[8,248,128]{2,1,0:T(8,128)S(1)} all-gather(f32[2,248,128]{2,1,0:T(8,128)S(1)} %bitcast.23), channel_id=6, replica_groups=mesh['zl'=8,'x'=4,'y'=4,'zh'=2,'c'=2] {'x'}, dimensions={0}, use_global_device_ids=true | all-gather | bytes 1269760 | tf_op jit(solution)/shard_map/cond/branch_1_fun/all_gather | solution.py:264
  71.1 1.9 %collective-permute-start = (f32[4,2,248,128]{3,2,1,0:T(8,128)S(1)}, f32[4,2,248,128]{3,2,1,0:T(8,128)S(1)}, u32[]{:S(2)}, u32[]{:S(2)}) collective-permute-start(f32[4,2,248,128]{3,2,1,0:T(8,128)S(1)} %bitcast.15), channel_id=1, source_target_pairs={{0,1},{1,0},{2,3},{3,2},{4,5},{5,4},{6,7},{7,6},{8,9},{9,8},{10,11... | collective-permute-start | bytes 3047432 | tf_op jit(solution)/shard_map/cond/branch_1_fun/ppermute | solution.py:256
  73.0 2.6 %collective-permute-done.swap_ref = f32[4,2,248,128]{3,2,1,0:T(8,128)S(1)} collective-permute-done((f32[4,2,248,128]{3,2,1,0:T(8,128)S(1)}, f32[4,2,248,128]{3,2,1,0:T(8,128)S(1)}, u32[]{:S(2)}, u32[]{:S(2)}) %collective-permute-start) | collective-permute-done | bytes 1015840 | tf_op jit(solution)/shard_map/cond/branch_1_fun/ppermute | solution.py:256
  75.6 4.4 %branch_1_fun.3 = f32[8,160,640]{2,1,0:T(8,128)S(1)} custom-call(s32[4]{0:T(128)S(1)} %get-tuple-element.23.at_ref, s32[20,20]{1,0:T(8,128)S(1)} %get-tuple-element.24.pattern_ref, f32[4,2,248,128]{3,2,1,0:T(8,128)S(1)} %bitcast.16, f32[4,2,248,128]{3,2,1,0:T(8,128)S(1)} %collective-permute-done.swap_ref), custom_call_target="tpu_custom_call" | custom-call | flops 1000000 | bytes 1000000 | tf_op jit(solution)/shard_map/cond/branch_1_fun/pallas_call | solution.py:51
  80.2 18.2 %all-gather.8.cloned.1.call-done = f32[32,104,128]{2,1,0:T(8,128)} async-done(((f32[4,104,128]{2,1,0:T(8,128)}), f32[32,104,128]{2,1,0:T(8,128)}) %all-gather.8.cloned.1.call-update) | async-done | bytes 1703952 | tf_op jit(solution)/shard_map/all_gather | solution.py:304
  98.5 1.5 %copy-done.2 = f32[32,104,128]{2,1,0:T(8,128)S(1)} copy-done((f32[32,104,128]{2,1,0:T(8,128)S(1)}, f32[32,104,128]{2,1,0:T(8,128)}, u32[]{:S(2)}) %copy-start.2) | copy-done | bytes 1703960
  99.9 3.3 %shard_map.39 = f32[4,80,640]{2,1,0:T(8,128)S(1)} custom-call(f32[8,4,104,128]{3,2,1,0:T(8,128)S(1)} %bitcast.19, f32[8,160,640]{2,1,0:T(8,128)S(1)} %get-tuple-element.44.right_ref), custom_call_target="tpu_custom_call" | custom-call | flops 3000000000 | bytes 6000000 | tf_op jit(solution)/shard_map/pallas_call | solution.py:51
  103.2 0.0 copy-start.1
  103.2 13.1 %all_to_all.21.shares_ref = f32[4,80,640]{2,1,0:T(8,128)S(1)} all-to-all(f32[4,80,640]{2,1,0:T(8,128)S(1)} %shard_map.39), channel_id=1, replica_groups=mesh['zl'=8,'x'=4,'y'=4,'zh'=2,'c'=2] {'y'}, dimensions={0} | all-to-all | bytes 1638400 | tf_op jit(solution)/shard_map/all_to_all | solution.py:332
  116.3 1.1 shard_map.40
  117.4 15.7 %all_to_all.22 = f32[8,1,80]{2,1,0:T(1,128)S(1)} all-to-all(f32[8,1,80]{2,1,0:T(1,128)S(1)} %bitcast.18), channel_id=1, replica_groups=mesh['zl'=8,'x'=4,'y'=4,'zh'=2,'c'=2] {'zl'}, dimensions={0} | all-to-all | bytes 5120 | tf_op jit(solution)/shard_map/all_to_all | solution.py:339
  133.1 0.9 shard_map.41
  (5 shorter events, 0.0 us)
Async XLA Ops:
  6.5 29.7 %copy-start.3 = (s32[20,20]{1,0:T(8,128)S(1)}, s32[20,20]{1,0:T(8,128)}, u32[]{:S(2)}) copy-start(s32[20,20]{1,0:T(8,128)} %pattern_ref.4) | copy-start | bytes 4804
  6.5 91.9 %all-gather.8.cloned.1.call-start = ((), (), s32[]{:S(2)}) async-start(), calls=%async_computation.4 | async-start | bytes 1916928 | tf_op jit(solution)/shard_map/all_gather | solution.py:304
  6.6 0.9 copy-start
  21.9 14.3 %all-to-all-start.1 = ((f32[16,32,128]{2,1,0:T(8,128)}), f32[16,32,128]{2,1,0:T(8,128)S(1)}, u32[]{:S(2)}, u32[]{:S(2)}) async-start(f32[16,32,128]{2,1,0:T(8,128)} %get-tuple-element.39), calls=%async_computation.1 | async-start | bytes 524288 | tf_op jit(solution)/shard_map/all_to_all | solution.py:314
  71.1 4.5 %collective-permute-start = (f32[4,2,248,128]{3,2,1,0:T(8,128)S(1)}, f32[4,2,248,128]{3,2,1,0:T(8,128)S(1)}, u32[]{:S(2)}, u32[]{:S(2)}) collective-permute-start(f32[4,2,248,128]{3,2,1,0:T(8,128)S(1)} %bitcast.15), channel_id=1, source_target_pairs={{0,1},{1,0},{2,3},{3,2},{4,5},{5,4},{6,7},{7,6},{8,9},{9,8},{10,11... | collective-permute-start | bytes 3047432 | tf_op jit(solution)/shard_map/cond/branch_1_fun/ppermute | solution.py:256
  98.5 1.5 %copy-start.2 = (f32[32,104,128]{2,1,0:T(8,128)S(1)}, f32[32,104,128]{2,1,0:T(8,128)}, u32[]{:S(2)}) copy-start(f32[32,104,128]{2,1,0:T(8,128)} %all-gather.8.cloned.1.call-done) | copy-start | bytes 5111812
  103.2 13.1 %copy-start.1 = (s32[20,20]{1,0:T(8,128)S(1)}, s32[20,20]{1,0:T(8,128)}, u32[]{:S(2)}) copy-start(s32[20,20]{1,0:T(8,128)} %pattern_ref.5) | copy-start | bytes 4804
Sparse Core Ops, SparseCore 0:
  20.1 78.3 all-gather.7
